TPU v7x, 32 devices: a whole 2x2x4 slice. The times are simulated.
32 devices in a mesh: gx: 4 (over x, core), gy: 8 (over z, y).
Axes of the slice: x: 2, y: 2, z: 4, core: 2. Of those that a mesh axis runs over, the one named last changes fastest.
Arguments:
- state: float32 [2, 8, 128, 512], P(None, None, 'gy', 'gx'), may hold values from 0 to 1, as said below
- previous: float32 [2, 8, 128, 512], P(None, None, 'gy', 'gx'), may hold values from 0 to 1
- feed: float32 [8, 128, 512], P(None, 'gy', 'gx'), may hold values from 0.01 to 0.1
- kill: float32 [8, 128, 512], P(None, 'gy', 'gx'), may hold values from 0.03 to 0.1
Outputs:
- correction: float32 [2, 8, 128, 512], P(None, None, 'gy', 'gx')
Inputs may be any that keep to these rules, and one draw needn't show every extreme that they name: `state`: u and v of every cell lie in the stated range.
All inputs are finite; a program needn't handle non-finite values.
Results may differ from a plain program's by a relative error of at most 0.0001.
Values sent between devices are 32-bit elements; how exact they have to be, the bound alone decides.
No kernel may reach another device: no remote copies, remote signals or barrier semaphores. Data moves between devices by JAX's collectives and lax.ppermute only.
A program may use at most 128 MiB of HBM per device.

v0:
```python
import functools

import jax
import jax.numpy as jnp
from jax import lax
from jax.experimental import pallas as pl
from jax.experimental.pallas import tpu as pltpu
from jax.sharding import PartitionSpec as P

DIFF = (40.0, 20.0)
INV_STEP = 2.0
LOWER = 0.25

_CENTRE = (1.0 + LOWER) / 2.0
_HALF = (1.0 - LOWER) / 2.0
_SIGMA = _CENTRE / _HALF
_RHO0 = 1.0 / _SIGMA
_RHO1 = 1.0 / (2.0 * _SIGMA - _RHO0)
_RHO2 = 1.0 / (2.0 * _SIGMA - _RHO1)

Z = 8
X = 128
HALO0 = 4
HALOS = (4, 4, 3, 3, 3, 3)
STARTS = tuple(sum(HALOS[:i]) for i in range(6))
FIELDS1 = sum(HALOS)
FIELDS2 = FIELDS1 + 8
PACKET = FIELDS2 + 1
WIDE = 42
PER = X // WIDE
EDGE = 3
CHUNK = 4

LO1, HI1 = -4, 8
LO2, HI2 = -2, 3
LO_UP, HI_UP = -3, 7
SIZE1, SIZE2, SIZE_UP = HI1 - LO1 + 2, HI2 - LO2 + 2, HI_UP - LO_UP + 2
OWN = 4


def lane_of():
    return lax.broadcasted_iota(jnp.int32, (1, Z, X), 2)


def sub_of():
    return lax.broadcasted_iota(jnp.int32, (1, Z, X), 1)


def roll_x(tile, shift):
    shift = shift % X
    return pltpu.roll(tile, shift, 2) if shift else tile


def roll_z(tile, shift):
    shift = shift % Z
    return pltpu.roll(tile, shift, 1) if shift else tile


def rows_loop(lo, hi, body, step=CHUNK):
    full = (hi - lo) // step
    if full == 1:
        body(lo, step)
    elif full > 1:

        def trip(i, carry):
            body(lo + i * step, step)
            return carry

        lax.fori_loop(0, full, trip, 0)
    rest = hi - lo - full * step
    if rest:
        body(hi - rest, rest)


def neighbour_sums(read, r, n, k):
    lane = lane_of()
    low, high = lane < k, lane >= X - k
    centre = [read(t, r, n) for t in (0, 1)]
    right = [roll_x(c, k) for c in centre]
    left = [roll_x(c, -k) for c in centre]
    sums = []
    for t in (0, 1):
        c = centre[t]
        along_x = jnp.where(low, right[1 - t], right[t]) + jnp.where(high, left[1 - t], left[t])
        along_y = read(t, r - 1, n) + read(t, r + 1, n)
        along_z = 2.0 * roll_z(c, k) if 2 * k == Z else roll_z(c, k) + roll_z(c, -k)
        sums.append(along_x + along_y + along_z)
    return centre, sums


def jacobian(u, v, f, k, level):
    scale = 0.25**level
    product = u * v
    squared = v * v
    first = INV_STEP + squared + f + 6.0 * DIFF[0] * scale
    second = INV_STEP + f + k - 2.0 * product + 6.0 * DIFF[1] * scale
    return 2.0 * product, squared, 1.0 / first, 1.0 / second, first, second


def cheb_step(level, keep, source, target, d, r, n, carry, gain):
    scale = 0.25**level
    k = 1 << level
    u, nb_u = neighbour_sums(lambda t, a, m: source[0, t, pl.ds(a, m)], r, n, k)
    v, nb_v = neighbour_sums(lambda t, a, m: source[1, t, pl.ds(a, m)], r, n, k)
    rows = pl.ds(r, n)
    for t in (0, 1):
        cross, squared, inv_u, inv_v = (keep[i, t, rows] for i in range(4))
        res_u = inv_u * (keep[4, t, rows] - cross * v[t] + DIFF[0] * scale * nb_u[t]) - u[t]
        res_v = inv_v * (keep[5, t, rows] + squared * u[t] + DIFF[1] * scale * nb_v[t]) - v[t]
        du, dv = gain * res_u, gain * res_v
        if carry is not None:
            du = du + carry * d[0, t, rows]
            dv = dv + carry * d[1, t, rows]
        d[0, t, rows] = du
        d[1, t, rows] = dv
        target[0, t, rows] = u[t] + du
        target[1, t, rows] = v[t] + dv


def residual(level, keep, diag, source, r, n):
    scale = 0.25**level
    k = 1 << level
    u, nb_u = neighbour_sums(lambda t, a, m: source[0, t, pl.ds(a, m)], r, n, k)
    v, nb_v = neighbour_sums(lambda t, a, m: source[1, t, pl.ds(a, m)], r, n, k)
    rows = pl.ds(r, n)
    first, second = [], []
    for t in (0, 1):
        first.append(
            keep[4, t, rows] - diag[0, t, rows] * u[t] - keep[0, t, rows] * v[t] + DIFF[0] * scale * nb_u[t]
        )
        second.append(
            keep[5, t, rows] - diag[1, t, rows] * v[t] + keep[1, t, rows] * u[t] + DIFF[1] * scale * nb_v[t]
        )
    return first, second


CARRY1 = _RHO1 * _RHO0
CARRY2 = _RHO2 * _RHO1


def write_gains(spread, out):
    lane = lax.broadcasted_iota(jnp.int32, (1, X), 1)
    for level in range(3):
        top = jnp.max(jnp.where(lane == level, spread, 0.0), axis=1, keepdims=True)
        tau = 1.0 / (1.0 + jnp.broadcast_to(top, (Z, X)))
        for i, factor in enumerate((1.0 / _CENTRE, 2.0 * _RHO1 / _HALF, 2.0 * _RHO2 / _HALF)):
            out[3 * level + i] = factor * tau


def pair_rows(value):
    n = value.shape[0] // 2
    pairs = value.reshape(n, 2, Z, X)
    return pairs[:, 0] + pairs[:, 1]


def restrict_01(first, second):
    lane, sub = lane_of(), sub_of()
    across = []
    for value in (first, second):
        a, b = value[0:1], value[1:2]
        across.append(jnp.where((lane & 1) == 0, a + roll_x(a, -1), b + roll_x(b, 1)))
    a, b = across
    return 0.125 * jnp.where((sub & 1) == 0, a + roll_z(a, -1), b + roll_z(b, 1))


def restrict_12(groups):
    lane, sub = lane_of(), sub_of()
    out = None
    for p, value in enumerate(groups):
        value = value + roll_x(value, 1 if p & 1 else -1)
        value = value + roll_x(value, 2 if p & 2 else -2)
        out = value if out is None else jnp.where((lane & 3) == p, value, out)
    return 0.125 * (out + jnp.where((sub & 2) == 0, roll_z(out, -2), roll_z(out, 2)))


def spread_x(tile, k, phase):
    return jnp.where((lane_of() & k) == phase, tile, roll_x(tile, -k if phase else k))


def packed_jacobian(uv, fk, level):
    scale = 0.25**level
    even = (sub_of() & 1) == 0
    u, v = jnp.where(even, uv, roll_z(uv, 1)), jnp.where(even, roll_z(uv, -1), uv)
    f, k = jnp.where(even, fk, roll_z(fk, 1)), jnp.where(even, roll_z(fk, -1), fk)
    product, squared = u * v, v * v
    diag = jnp.where(
        even,
        INV_STEP + squared + f + 6.0 * DIFF[0] * scale,
        INV_STEP + f + k - 2.0 * product + 6.0 * DIFF[1] * scale,
    )
    return 1.0 / diag, jnp.where(even, -2.0 * product, squared), diag


def packed_spread(uv, fk, level):
    scale = 0.25**level
    even = (sub_of() & 1) == 0
    inverse, other, _ = packed_jacobian(uv, fk, level)
    return jnp.where(even, 6.0 * DIFF[0] * scale - other, 6.0 * DIFF[1] * scale + other) * inverse


def packed_terms(source, g, n, level):
    k = 1 << level
    lane, sub = lane_of(), sub_of()
    even = (sub & 1) == 0
    first, last = (lane & (k - 1)) == 0, (lane & (k - 1)) == k - 1
    low, high = lane < k, lane >= X - k
    diff = jnp.where(even, DIFF[0] * 0.25**level, DIFF[1] * 0.25**level)
    wide = [source[t, pl.ds(g - 1, n + 2)] for t in (0, 1)]
    centre = [w[1 : n + 1] for w in wide]
    right = [roll_x(c, k) for c in centre]
    left = [roll_x(c, -k) for c in centre]
    out = []
    for t in (0, 1):
        c, w = centre[t], wide[t]
        total = jnp.where(low, right[1 - t], right[t]) + jnp.where(high, left[1 - t], left[t])
        if k == 2:
            ahead, back = roll_x(w, 1), roll_x(w, -1)
            total = total + jnp.where(first, back[0:n], ahead[1 : n + 1])
            total = total + jnp.where(last, ahead[2 : n + 2], back[1 : n + 1])
            total = total + roll_z(c, 2) + roll_z(c, -2)
        else:
            total = total + jnp.where(first, roll_x(w[0:n], -(k - 1)), roll_x(c, 1))
            total = total + jnp.where(last, roll_x(w[2 : n + 2], k - 1), roll_x(c, -1))
            total = total + 2.0 * roll_z(c, 4)
        other = jnp.where(even, roll_z(c, -1), roll_z(c, 1))
        out.append((c, other, diff * total))
    return out


def packed_first(coef, shift, b, target, d, g, n, gain):
    for t in (0, 1):
        value = gain * coef[0, t, pl.ds(g + shift, n)] * b[t, pl.ds(g + shift, n)]
        d[t, pl.ds(g, n)] = value
        target[t, pl.ds(g, n)] = value


def packed_step(level, coef, shift, b, source, target, d, g, n, carry, gain):
    for t, (c, other, spread) in enumerate(packed_terms(source, g, n, level)):
        at = pl.ds(g + shift, n)
        res = coef[0, t, at] * (b[t, at] + coef[1, t, at] * other + spread) - c
        delta = gain * res
        if carry is not None:
            delta = delta + carry * d[t, pl.ds(g, n)]
        d[t, pl.ds(g, n)] = delta
        target[t, pl.ds(g, n)] = c + delta


def plane(ref, f, y, rows):
    return ref[pl.ds(f * Z * rows + y, Z, stride=rows), :]


def is_even(axis):
    return lax.rem(lax.axis_index(axis), 2) == 0


def prev_of(even, first, second, at):
    return jnp.where(even, first[at], second[at])


def next_of(even, first, second, at):
    return jnp.where(even, second[at], first[at])


def first_kernel(rows, state, previous, feed, kill, first, second, main, coarse, *scratch):
    sources, sems = scratch[:4], scratch[4]
    copies = [
        pltpu.make_async_copy(ref, held, sems.at[i])
        for i, (ref, held) in enumerate(zip((state, previous, feed, kill), sources))
    ]
    for copy in copies:
        copy.start()
    for copy in copies:
        copy.wait()
    even = is_even("gy")
    state, previous, feed, kill = sources
    fields = [(state, 0), (state, 1), (previous, 0), (previous, 1), (feed, 0), (kill, 0)]
    for i, (ref, f) in enumerate(fields):
        for y in range(rows):
            main[i, y] = plane(ref, f, y, rows)
        top, bottom = main[i, 0 : HALOS[i]], main[i, rows - HALOS[i] : rows]
        at = slice(STARTS[i], STARTS[i] + HALOS[i])
        first[at] = jnp.where(even, top, bottom)
        second[at] = jnp.where(even, bottom, top)
    u, v, f, k = (main[i] for i in (0, 1, 4, 5))
    sums = [pair_rows(value) for value in (u, v, f, k)]
    pairs = []
    for p in (0, 1):
        values = [
            restrict_01(sums[2 * p][2 * g : 2 * g + 2], sums[2 * p + 1][2 * g : 2 * g + 2]) for g in range(OWN)
        ]
        pairs.append(jnp.concatenate(values, axis=0))
        coarse[p * OWN : (p + 1) * OWN] = pairs[p]
        for ref in (first, second):
            ref[FIELDS1 + p * OWN : FIELDS1 + (p + 1) * OWN] = pairs[p]

    uv, fk = (restrict_12([pair[j : j + 1] for j in range(OWN)]) for pair in pairs)
    both = jnp.where((sub_of() & 2) == 0, uv, fk)
    coarse[2 * OWN : 2 * OWN + 1] = both
    for ref in (first, second):
        ref[FIELDS2 : FIELDS2 + 1] = both


def split_fields2(both):
    low = (sub_of() & 2) == 0
    return jnp.where(low, both, roll_z(both, 2)), jnp.where(low, roll_z(both, -2), both)


def spread_kernel(main, coarse, out):
    lane = lax.broadcasted_iota(jnp.int32, (1, X), 1)
    u, v, f, k = (main[i] for i in (0, 1, 4, 5))
    cross, squared, inv_u, inv_v, _, _ = jacobian(u, v, f, k, 0)
    tops = [jnp.max(jnp.maximum((6.0 * DIFF[0] + cross) * inv_u, (6.0 * DIFF[1] + squared) * inv_v), axis=0)]
    tops.append(jnp.max(packed_spread(coarse[0:OWN], coarse[OWN : 2 * OWN], 1), axis=0))
    tops.append(packed_spread(*split_fields2(coarse[2 * OWN : 2 * OWN + 1]), 2)[0])
    result = jnp.zeros((1, X), jnp.float32)
    for level, top in enumerate(tops):
        top = jnp.max(jnp.max(top, axis=0, keepdims=True), axis=1, keepdims=True)
        result = jnp.where(lane == level, jnp.broadcast_to(top, (1, X)), result)
    out[...] = jnp.broadcast_to(result[None], out.shape)


GROUPS1 = HI1 - LO1
GROUPS2 = HI2 - LO2


def tiles_for(entries):
    return -(-entries // PER)


def pack_edges(entries, even, first, second):
    lane = lane_of()
    share = first.shape[0]
    left, right = None, None
    for j in range(PER):
        part = entries[j * share : (j + 1) * share]
        a, b = roll_x(part, WIDE * j), roll_x(part, WIDE + WIDE * j)
        left = a if left is None else jnp.where(lane >= WIDE * j, a, left)
        right = b if right is None else jnp.where(lane >= WIDE * j, b, right)
    first[...] = jnp.where(even, left, right)
    second[...] = jnp.where(even, right, left)


def halo_tiles(even, packets, lo, hi):
    first, second = packets
    share = first.shape[0]
    lane = lane_of()
    out = []
    for j in range(PER):
        a, b = max(lo, j * share), min(hi, (j + 1) * share)
        if a < b:
            strip = slice(a - j * share, b - j * share)
            left, right = prev_of(even, first, second, strip), next_of(even, first, second, strip)
            value = jnp.where(lane < X // 2, roll_x(right, -WIDE * j), roll_x(left, X - WIDE - WIDE * j))
            out.append((a - lo, b - lo, value))
    return out


def pack_own_kernel(rows, main, coarse, first, second, held):
    for i in range(6):
        held[i * rows : (i + 1) * rows] = main[i]
    held[6 * rows : 6 * rows + 2 * OWN + 1] = coarse[...]
    pack_edges(held, is_even("gx"), first, second)


def pack_corner_kernel(y_first, y_second, first, second, held):
    even = is_even("gy")
    every = slice(0, PACKET)
    held[0:PACKET] = prev_of(even, y_first, y_second, every)
    held[PACKET : 2 * PACKET] = next_of(even, y_first, y_second, every)
    pack_edges(held, is_even("gx"), first, second)


EDGES = 2 * OWN
FAR = EDGES + 2 * EDGE + 1


def level0_kernel(
    rows, main, y_first, y_second, own_a, own_b, corner_a, corner_b, gathered, own, first, second, keep, gain_out, fields, other, d, diag
):
    even, even_x = is_even("gy"), is_even("gx")
    total = rows + 2 * HALO0
    own_x, corner_x = (own_a, own_b), (corner_a, corner_b)
    top = jnp.max(gathered[...], axis=0)
    write_gains(top[0:1], gain_out)
    g0, g1, g2 = (gain_out[i] for i in range(3))
    for i, halo in enumerate(HALOS):
        strip = slice(STARTS[i], STARTS[i] + halo)
        skip = HALO0 - halo
        fields[i, 0, skip:HALO0] = prev_of(even, y_first, y_second, strip)
        fields[i, 0, HALO0 : HALO0 + rows] = main[i]
        fields[i, 0, HALO0 + rows : total - skip] = next_of(even, y_first, y_second, strip)
        for packets, lo, n, at in (
            (corner_x, STARTS[i], halo, skip),
            (own_x, i * rows, rows, HALO0),
            (corner_x, PACKET + STARTS[i], halo, HALO0 + rows),
        ):
            for a, b, value in halo_tiles(even_x, packets, lo, lo + n):
                fields[i, 1, at + a : at + b] = value
    here = keep.at[6:8]

    def setup(r, n):
        at = pl.ds(r, n)
        u, nb_u = neighbour_sums(lambda t, a, m: fields[0, t, pl.ds(a, m)], r, n, 1)
        v, nb_v = neighbour_sums(lambda t, a, m: fields[1, t, pl.ds(a, m)], r, n, 1)
        for t in (0, 1):
            f, k = fields[4, t, at], fields[5, t, at]
            cross, squared, inv_u, inv_v, first, second = jacobian(u[t], v[t], f, k, 0)
            react = u[t] * squared
            b_u = (
                DIFF[0] * (nb_u[t] - 6.0 * u[t])
                - INV_STEP * (u[t] - fields[2, t, at])
                - react
                + f * (1.0 - u[t])
            )
            b_v = (
                DIFF[1] * (nb_v[t] - 6.0 * v[t]) - INV_STEP * (v[t] - fields[3, t, at]) + react - (f + k) * v[t]
            )
            for i, value in enumerate((cross, squared, inv_u, inv_v, b_u, b_v)):
                keep[i, t, at] = value
            diag[0, t, at] = first
            diag[1, t, at] = second
            for i, value in enumerate((g0 * inv_u * b_u, g0 * inv_v * b_v)):
                d[i, t, at] = value
                keep[6 + i, t, at] = value

    rows_loop(1, total - 1, setup)
    rows_loop(2, total - 2, lambda r, n: cheb_step(0, keep, here, other, d, r, n, CARRY1, g1))
    rows_loop(3, total - 3, lambda r, n: cheb_step(0, keep, other, here, d, r, n, CARRY2, g2))

    def down(r, n):
        res = residual(0, keep, diag, here, r, n)
        out = (r - HALO0) // 4
        for t in (0, 1):
            value = restrict_01(pair_rows(res[0][t]), pair_rows(res[1][t]))
            own[t, pl.ds(out, 1)] = value
            if t == 0:
                first[pl.ds(out, 1)] = value
                second[pl.ds(out, 1)] = value

    rows_loop(HALO0, HALO0 + rows, down, 4)

    lane = lane_of()
    edges = []
    for start in (HALO0, HALO0 + rows - EDGE):
        halo = None
        for i in (0, 1):
            for j in range(EDGE):
                at = i * EDGE + j
                value = roll_x(keep[6 + i, 1, start + j : start + j + 1], 4 + 8 * at)
                halo = value if halo is None else jnp.where((lane >> 3) == at, value, halo)
        edges.append([keep[6, 0, start : start + EDGE], keep[7, 0, start : start + EDGE], halo])
    top, bottom = (jnp.concatenate(parts, axis=0) for parts in edges)
    for ref in (first, second):
        ref[OWN : 2 * OWN] = own[1]
    strip = slice(FIELDS2, FIELDS2 + 1)
    for t in (0, 1):
        if t == 0:
            before, after = prev_of(even, y_first, y_second, strip), next_of(even, y_first, y_second, strip)
        else:
            before, after = (
                halo_tiles(even_x, corner_x, at + FIELDS2, at + FIELDS2 + 1)[0][2] for at in (0, PACKET)
            )
        first[FAR + t : FAR + t + 1] = jnp.where(even, after, before)
        second[FAR + t : FAR + t + 1] = jnp.where(even, before, after)
    first[EDGES : EDGES + 2 * EDGE + 1] = jnp.where(even, top, bottom)
    second[EDGES : EDGES + 2 * EDGE + 1] = jnp.where(even, bottom, top)


def coarse1_kernel(
    rows, coarse, y_first, y_second, own_a, own_b, corner_a, corner_b, gain, coef, fields
):
    del gain
    even, even_x = is_even("gy"), is_even("gx")
    own_x, corner_x = (own_a, own_b), (corner_a, corner_b)
    for p in (0, 1):
        to = p * GROUPS1
        strip = slice(FIELDS1 + p * OWN, FIELDS1 + (p + 1) * OWN)
        fields[0, to : to + OWN] = prev_of(even, y_first, y_second, strip)
        fields[0, to + OWN : to + 2 * OWN] = coarse[p * OWN : (p + 1) * OWN]
        fields[0, to + 2 * OWN : to + 3 * OWN] = next_of(even, y_first, y_second, strip)
        for part, (packets, lo) in enumerate(
            ((corner_x, FIELDS1), (own_x, 6 * rows), (corner_x, PACKET + FIELDS1))
        ):
            lo += p * OWN
            for a, b, value in halo_tiles(even_x, packets, lo, lo + OWN):
                fields[1, to + part * OWN + a : to + part * OWN + b] = value
    for t in (0, 1):
        for i, value in enumerate(packed_jacobian(fields[t, 0:GROUPS1], fields[t, GROUPS1 : 2 * GROUPS1], 1)):
            coef[i, t, 1 : SIZE1 - 1] = value


def coarse2_kernel(
    rows, coarse, y_first, y_second, own_a, own_b, corner_a, corner_b, b_first, b_second, coef
):
    even, even_x = is_even("gy"), is_even("gx")
    own_x, corner_x = (own_a, own_b), (corner_a, corner_b)
    near = slice(FIELDS2, FIELDS2 + 1)
    for t in (0, 1):
        far = slice(FAR + t, FAR + t + 1)
        if t == 0:
            middle = [
                prev_of(even, y_first, y_second, near),
                coarse[2 * OWN : 2 * OWN + 1],
                next_of(even, y_first, y_second, near),
            ]
        else:
            middle = [
                halo_tiles(even_x, packets, lo, lo + 1)[0][2]
                for packets, lo in ((corner_x, FIELDS2), (own_x, 6 * rows + 2 * OWN), (corner_x, PACKET + FIELDS2))
            ]
        parts = [prev_of(even, b_first, b_second, far), *middle, next_of(even, b_first, b_second, far)]
        inverse, other, _ = packed_jacobian(*split_fields2(jnp.concatenate(parts, axis=0)), 2)
        coef[0, t, 1 : SIZE2 - 1] = inverse
        coef[1, t, 1 : SIZE2 - 1] = other


def level1_kernel(own, first, second, coef1, gain, packet, keep, y1, d1):
    b1, x1 = keep.at[0], keep.at[1]
    even = is_even("gy")
    for t in (0, 1):
        b1[t, 1 + OWN : 1 + 2 * OWN] = own[t]
        strip = slice(t * OWN, (t + 1) * OWN)
        b1[t, 1 : 1 + OWN] = prev_of(even, first, second, strip)
        b1[t, 1 + 2 * OWN : 1 + 3 * OWN] = next_of(even, first, second, strip)
    g0, g1, g2 = (gain[3 + i] for i in range(3))
    n = GROUPS1
    packed_first(coef1, 0, b1, x1, d1, 1, n, g0)
    packed_step(1, coef1, 0, b1, x1, y1, d1, 1, n, CARRY1, g1)
    packed_step(1, coef1, 0, b1, y1, x1, d1, 1, n, CARRY2, g2)
    here = pl.ds(1 + OWN, OWN)
    for t, (c, other, spread) in enumerate(packed_terms(x1, 1 + OWN, OWN, 1)):
        res = b1[t, here] - coef1[2, t, here] * c + coef1[1, t, here] * other + spread
        packet[t : t + 1] = restrict_12([res[j : j + 1] for j in range(OWN)])


def rest_kernel(
    own2, near_a, near_b, far_a, far_b, gain, coef1, coef2, keep0, keep1, first, second, out, d1, b2, x2, y2, d2, xu, yu, x0, y0, d0
):
    rows = out.shape[0] // (2 * Z)
    even = (sub_of() & 1) == 0
    b1, x1 = keep1.at[0], keep1.at[1]

    even_y, low = is_even("gy"), lax.rem(lax.axis_index("gy"), 4) < 2
    for t in (0, 1):
        at = slice(t, t + 1)
        parts = [
            next_of(low, far_a, far_b, at),
            prev_of(even_y, near_a, near_b, at),
            own2[at],
            next_of(even_y, near_a, near_b, at),
            prev_of(low, far_a, far_b, at),
        ]
        b2[t, 1 : SIZE2 - 1] = jnp.concatenate(parts, axis=0)

    n = HI2 - LO2
    g0, g1, g2 = (gain[6 + i] for i in range(3))
    packed_first(coef2, 0, b2, x2, d2, 1, n, g0)
    packed_step(2, coef2, 0, b2, x2, y2, d2, 1, n, CARRY1, g1)
    packed_step(2, coef2, 0, b2, y2, x2, d2, 1, n, CARRY2, g2)
    packed_step(2, coef2, 0, b2, x2, y2, d2, 1, n, None, g0)
    packed_step(2, coef2, 0, b2, y2, x2, d2, 1, n, CARRY1, g1)
    packed_step(2, coef2, 0, b2, x2, y2, d2, 1, n, CARRY2, g2)

    g0, g1, g2 = (gain[3 + i] for i in range(3))
    shift = LO_UP - LO1
    for t in (0, 1):
        for g in range(LO_UP, HI_UP):
            p = g % 4
            value = y2[t, g // 4 - LO2 + 1 : g // 4 - LO2 + 2]
            value = spread_x(spread_x(value, 1, p & 1), 2, p & 2)
            at = g - LO_UP + 1
            xu[t, at : at + 1] = x1[t, at + shift : at + shift + 1] + value
    n = HI_UP - LO_UP
    packed_step(1, coef1, shift, b1, xu, yu, d1, 1, n, None, g0)
    packed_step(1, coef1, shift, b1, yu, xu, d1, 1, n, CARRY1, g1)
    packed_step(1, coef1, shift, b1, xu, yu, d1, 1, n, CARRY2, g2)

    g0, g1, g2 = (gain[i] for i in range(3))
    last = EDGES + 2 * EDGE
    for i in (0, 1):
        for at, take in ((HALO0 - EDGE, prev_of), (HALO0 + rows, next_of)):
            strip = slice(EDGES + i * EDGE, EDGES + (i + 1) * EDGE)
            x0[i, 0, at : at + EDGE] = take(even_y, first, second, strip)
            sides = take(even_y, first, second, slice(last, last + 1))
            for j in range(EDGE):
                x0[i, 1, at + j : at + j + 1] = roll_x(sides, -(4 + 8 * (i * EDGE + j)))
        for t in (0, 1):
            x0[i, t, HALO0 : HALO0 + rows] = keep0[6 + i, t, HALO0 : HALO0 + rows]
    for t in (0, 1):
        for row in range(-2, rows // 2 + 2):
            at = row // 2 - LO_UP + 1
            value = spread_x(yu[t, at : at + 1], 1, row & 1)
            for i, fine in enumerate((jnp.where(even, value, roll_z(value, 1)), jnp.where(even, roll_z(value, -1), value))):
                for y in (2 * row, 2 * row + 1):
                    if -EDGE <= y < rows + EDGE:
                        x0[i, t, y + HALO0 : y + HALO0 + 1] = x0[i, t, y + HALO0 : y + HALO0 + 1] + fine
    total = rows + 2 * HALO0
    rows_loop(2, total - 2, lambda r, n: cheb_step(0, keep0, x0, y0, d0, r, n, None, g0))
    rows_loop(3, total - 3, lambda r, n: cheb_step(0, keep0, y0, x0, d0, r, n, CARRY1, g1))
    rows_loop(4, total - 4, lambda r, n: cheb_step(0, keep0, x0, y0, d0, r, n, CARRY2, g2))
    for i in (0, 1):
        for y in range(rows):
            out[pl.ds(i * Z * rows + y, Z, stride=rows), :] = y0[i, 0, HALO0 + y]


def call(kernel, out_shapes, scratch, *args, space=pltpu.VMEM):
    out = [jax.ShapeDtypeStruct(shape, jnp.float32) for shape in out_shapes]
    return pl.pallas_call(
        kernel,
        out_shape=out,
        in_specs=[pl.BlockSpec(memory_space=space)] * len(args),
        out_specs=[pl.BlockSpec(memory_space=pltpu.VMEM)] * len(out),
        scratch_shapes=[pltpu.VMEM(s, jnp.float32) if isinstance(s, tuple) else s for s in scratch],
        compiler_params=pltpu.CompilerParams(vmem_limit_bytes=24 * 2**20),
    )(*args)


def swap(value, axis, step):
    count = lax.axis_size(axis)
    assert count % 2 == 0
    pairs = [(i, (i + step) % count) for i in range(0, count, 2)]
    return lax.ppermute(value, axis, pairs + [(j, i) for i, j in pairs])


def swap_far(value, axis, step):
    count = lax.axis_size(axis)
    assert count % 4 == 0
    pairs = [(i + j, (i + j + 2 * step) % count) for i in range(0, count, 4) for j in (0, 1)]
    return lax.ppermute(value, axis, pairs + [(j, i) for i, j in pairs])


def exchange(first, second, axis):
    return swap(first, axis, -1), swap(second, axis, 1)


def body(state, previous, feed, kill):
    _, depth, rows, cols = state.shape
    assert depth == Z and cols == X and rows == 4 * OWN
    across, count = lax.axis_size("gx"), lax.axis_size("gy")
    total0 = rows + 2 * HALO0
    state = state.reshape(2 * Z * rows, X)
    previous = previous.reshape(2 * Z * rows, X)
    feed = feed.reshape(Z * rows, X)
    kill = kill.reshape(Z * rows, X)
    inputs = (state, previous, feed, kill)

    strip = (FIELDS2 + 1, Z, X)
    first, second, main, coarse = call(
        functools.partial(first_kernel, rows),
        [strip, strip, (6, rows, Z, X), (2 * OWN + 1, Z, X)],
        [*(a.shape for a in inputs), pltpu.SemaphoreType.DMA((4,))],
        *(pltpu.with_memory_space_constraint(a, pltpu.HBM) for a in inputs),
        space=pltpu.HBM,
    )
    y_packets = exchange(first, second, "gy")
    (spread,) = call(spread_kernel, [(across * count, Z // 2, X)], [], main, coarse)
    spread = lax.all_to_all(spread, ("gx", "gy"), 0, 0, tiled=True)

    tiles = tiles_for(6 * rows + 2 * OWN + 1)
    own_x = exchange(
        *call(
            functools.partial(pack_own_kernel, rows),
            [(tiles, Z, X), (tiles, Z, X)],
            [(PER * tiles, Z, X)],
            main,
            coarse,
        ),
        "gx",
    )
    tiles = tiles_for(2 * PACKET)
    corner_x = exchange(
        *call(pack_corner_kernel, [(tiles, Z, X), (tiles, Z, X)], [(PER * tiles, Z, X)], *y_packets), "gx"
    )

    strip = (FAR + 2, Z, X)
    pair0 = (2, 2, total0, Z, X)
    own, first, second, keep0, gain = call(
        functools.partial(level0_kernel, rows),
        [(2, OWN, Z, X), strip, strip, (8, 2, total0, Z, X), (9, Z, X)],
        [(6, 2, total0, Z, X), pair0, pair0, pair0],
        main,
        *y_packets,
        *own_x,
        *corner_x,
        spread,
    )
    (coef1,) = call(
        functools.partial(coarse1_kernel, rows),
        [(3, 2, SIZE1, Z, X)],
        [(2, 2 * GROUPS1, Z, X)],
        coarse,
        *y_packets,
        *own_x,
        *corner_x,
        gain,
    )
    b_packets = exchange(first, second, "gy")

    one, two, up = (2, SIZE1, Z, X), (2, SIZE2, Z, X), (2, SIZE_UP, Z, X)
    packet, keep1 = call(
        level1_kernel, [(2, Z, X), (2, *one)], [one, one], own, *b_packets, coef1, gain
    )
    near = exchange(packet, packet, "gy")
    far = (swap_far(packet, "gy", 1), swap_far(packet, "gy", -1))
    (coef2,) = call(
        functools.partial(coarse2_kernel, rows),
        [(2, 2, SIZE2, Z, X)],
        [],
        coarse,
        *y_packets,
        *own_x,
        *corner_x,
        *b_packets,
    )

    (out,) = call(
        rest_kernel,
        [(2 * Z * rows, X)],
        [one, two, two, two, two, up, up, pair0, pair0, pair0],
        packet,
        *near,
        *far,
        gain,
        coef1,
        coef2,
        keep0,
        keep1,
        *b_packets,
    )
    return out.reshape(2, Z, rows, X)


def solution(mesh):
    placed = (
        P(None, None, "gy", "gx"),
        P(None, None, "gy", "gx"),
        P(None, "gy", "gx"),
        P(None, "gy", "gx"),
    )
    return jax.shard_map(
        body, mesh=mesh, in_specs=placed, out_specs=P(None, None, "gy", "gx"), check_vma=False
    )
```

profile of v0, /device:TPU:0, one launch (start us, length us, event | category | flops | bytes accessed | tf_op | source)
XLA Modules:
  0.0 44.4 jit_solution(7813597991504338003)
XLA Ops:
  0.0 1.4 %shard_map.46 = (f32[29,8,128]{2,1,0:T(8,128)S(1)}, f32[29,8,128]{2,1,0:T(8,128)S(1)}, f32[6,16,8,128]{3,2,1,0:T(8,128)S(1)}, f32[9,8,128]{2,1,0:T(8,128)S(1)}) custom-call(f32[256,128]{1,0:T(8,128)} %bitcast.5, f32[256,128]{1,0:T(8,128)} %bitcast.6, f32[128,128]{1,0:T(8,128)} %bitcast.7, f32[128,128]{1,0:T(8,128)} %bitcast.8), custom_call_target="tpu_custom_call" | custom-call | tf_op jit(solution)/shard_map/pallas_call | solution.py:608
  1.4 6.1 %collective-permute-start = (f32[29,8,128]{2,1,0:T(8,128)S(1)}, f32[29,8,128]{2,1,0:T(8,128)S(1)}, u32[]{:S(2)}, u32[]{:S(2)}) collective-permute-start(f32[29,8,128]{2,1,0:T(8,128)S(1)} %get-tuple-element.21), channel_id=1, source_target_pairs={{0,7},{2,1},{4,3},{6,5},{7,0},{1,2},{3,4},{5,6},{8,15},{10,9},{12,... | collective-permute-start | bytes 356360 | tf_op jit(solution)/shard_map/ppermute | solution.py:622
  7.5 0.2 shard_map.47
  7.7 0.7 %collective-permute-start.2 = (f32[35,8,128]{2,1,0:T(8,128)S(1)}, f32[35,8,128]{2,1,0:T(8,128)S(1)}, u32[]{:S(2)}, u32[]{:S(2)}) collective-permute-start(f32[35,8,128]{2,1,0:T(8,128)S(1)} %get-tuple-element.24), channel_id=1, source_target_pairs={{0,24},{16,8},{24,0},{8,16},{1,25},{17,9},{25,1},{9,17},{2,26},{18... | collective-permute-start | bytes 430088 | tf_op jit(solution)/shard_map/ppermute | solution.py:622
  8.4 1.0 %collective-permute-start.3 = (f32[35,8,128]{2,1,0:T(8,128)S(1)}, f32[35,8,128]{2,1,0:T(8,128)S(1)}, u32[]{:S(2)}, u32[]{:S(2)}) collective-permute-start(f32[35,8,128]{2,1,0:T(8,128)S(1)} %get-tuple-element.25), channel_id=1, source_target_pairs={{0,8},{16,24},{8,0},{24,16},{1,9},{17,25},{9,1},{25,17},{2,10},{18... | collective-permute-start | bytes 430088 | tf_op jit(solution)/shard_map/ppermute | solution.py:622
  9.4 0.8 %shard_map.49 = f32[32,4,128]{2,1,0:T(4,128)} custom-call(f32[6,16,8,128]{3,2,1,0:T(8,128)S(1)} %get-tuple-element.20.main, f32[9,8,128]{2,1,0:T(8,128)S(1)} %get-tuple-element.23.coarse), custom_call_target="tpu_custom_call" | custom-call | tf_op jit(solution)/shard_map/pallas_call | solution.py:608
  10.2 2.6 %all-to-all-start = ((f32[32,4,128]{2,1,0:T(4,128)}), f32[32,4,128]{2,1,0:T(4,128)S(1)}, u32[]{:S(2)}, u32[]{:S(2)}) async-start(f32[32,4,128]{2,1,0:T(4,128)} %shard_map.49), calls=%async_computation | async-start | bytes 131072 | tf_op jit(solution)/shard_map/all_to_all | solution.py:657
  12.8 0.5 %collective-permute-done.1.y_second = f32[29,8,128]{2,1,0:T(8,128)S(1)} collective-permute-done((f32[29,8,128]{2,1,0:T(8,128)S(1)}, f32[29,8,128]{2,1,0:T(8,128)S(1)}, u32[]{:S(2)}, u32[]{:S(2)}) %collective-permute-start.1) | collective-permute-done | bytes 118816 | tf_op jit(solution)/shard_map/ppermute | solution.py:622
  13.2 0.2 shard_map.48
  13.4 1.0 %collective-permute-start.4 = (f32[20,8,128]{2,1,0:T(8,128)S(1)}, f32[20,8,128]{2,1,0:T(8,128)S(1)}, u32[]{:S(2)}, u32[]{:S(2)}) collective-permute-start(f32[20,8,128]{2,1,0:T(8,128)S(1)} %get-tuple-element.26), channel_id=1, source_target_pairs={{0,24},{16,8},{24,0},{8,16},{1,25},{17,9},{25,1},{9,17},{2,26},{18... | collective-permute-start | bytes 245768 | tf_op jit(solution)/shard_map/ppermute | solution.py:622
  14.4 0.7 %collective-permute-start.5 = (f32[20,8,128]{2,1,0:T(8,128)S(1)}, f32[20,8,128]{2,1,0:T(8,128)S(1)}, u32[]{:S(2)}, u32[]{:S(2)}) collective-permute-start(f32[20,8,128]{2,1,0:T(8,128)S(1)} %get-tuple-element.27), channel_id=1, source_target_pairs={{0,8},{16,24},{8,0},{24,16},{1,9},{17,25},{9,1},{25,17},{2,10},{18... | collective-permute-start | bytes 245768 | tf_op jit(solution)/shard_map/ppermute | solution.py:622
  15.1 4.9 %all-to-all-done.gathered = f32[32,4,128]{2,1,0:T(4,128)S(1)} async-done(((f32[32,4,128]{2,1,0:T(4,128)}), f32[32,4,128]{2,1,0:T(4,128)S(1)}, u32[]{:S(2)}, u32[]{:S(2)}) %all-to-all-start) | async-done | bytes 65568 | tf_op jit(solution)/shard_map/all_to_all | solution.py:657
  20.1 3.0 %shard_map.50 = (f32[2,4,8,128]{3,2,1,0:T(8,128)S(1)}, f32[17,8,128]{2,1,0:T(8,128)S(1)}, f32[17,8,128]{2,1,0:T(8,128)S(1)}, f32[8,2,24,8,128]{4,3,2,1,0:T(8,128)S(1)}, f32[9,8,128]{2,1,0:T(8,128)S(1)}) custom-call(f32[6,16,8,128]{3,2,1,0:T(8,128)S(1)} %get-tuple-element.20.main, f32[29,8,128]{2,1,0:T(8,128)S(1)} %collective-permute-done.y_first, ...), custom_call_target="tpu_custom_call" | custom-call | tf_op jit(solution)/shard_map/pallas_call | solution.py:608
  23.1 2.2 %collective-permute-start.6 = (f32[17,8,128]{2,1,0:T(8,128)S(1)}, f32[17,8,128]{2,1,0:T(8,128)S(1)}, u32[]{:S(2)}, u32[]{:S(2)}) collective-permute-start(f32[17,8,128]{2,1,0:T(8,128)S(1)} %get-tuple-element.29), channel_id=1, source_target_pairs={{0,7},{2,1},{4,3},{6,5},{7,0},{1,2},{3,4},{5,6},{8,15},{10,9},{12,... | collective-permute-start | bytes 208904 | tf_op jit(solution)/shard_map/ppermute | solution.py:622
  25.3 0.2 shard_map.51.coef1
  25.5 4.7 %collective-permute-done.6.first.b_first = f32[17,8,128]{2,1,0:T(8,128)S(1)} collective-permute-done((f32[17,8,128]{2,1,0:T(8,128)S(1)}, f32[17,8,128]{2,1,0:T(8,128)S(1)}, u32[]{:S(2)}, u32[]{:S(2)}) %collective-permute-start.6) | collective-permute-done | bytes 69664 | tf_op jit(solution)/shard_map/ppermute | solution.py:622
  30.2 0.6 %collective-permute-done.7.second.b_second = f32[17,8,128]{2,1,0:T(8,128)S(1)} collective-permute-done((f32[17,8,128]{2,1,0:T(8,128)S(1)}, f32[17,8,128]{2,1,0:T(8,128)S(1)}, u32[]{:S(2)}, u32[]{:S(2)}) %collective-permute-start.7) | collective-permute-done | bytes 69664 | tf_op jit(solution)/shard_map/ppermute | solution.py:622
  30.7 0.6 %shard_map.52 = (f32[2,8,128]{2,1,0:T(8,128)S(1)}, f32[2,2,14,8,128]{4,3,2,1,0:T(8,128)S(1)}) custom-call(f32[2,4,8,128]{3,2,1,0:T(8,128)S(1)} %get-tuple-element.28.own, f32[17,8,128]{2,1,0:T(8,128)S(1)} %collective-permute-done.6.first.b_first, f32[17,8,128]{2,1,0:T(8,128)S(1)} %collective-permute-done.7.second.b_second, ...), custom_call_target="tpu_custom_call" | custom-call | tf_op jit(solution)/shard_map/pallas_call | solution.py:608
  31.3 0.6 %collective-permute-start.11 = (f32[2,8,128]{2,1,0:T(8,128)S(1)}, f32[2,8,128]{2,1,0:T(8,128)S(1)}, u32[]{:S(2)}, u32[]{:S(2)}) collective-permute-start(f32[2,8,128]{2,1,0:T(8,128)S(1)} %get-tuple-element.32.own2), channel_id=1, source_target_pairs={{0,6},{1,7},{4,2},{5,3},{6,0},{7,1},{2,4},{3,5},{8,14},{9,15},{12,... | collective-permute-start | bytes 24584 | tf_op jit(solution)/shard_map/ppermute | solution.py:629
  32.0 2.5 %collective-permute-start.9 = (f32[2,8,128]{2,1,0:T(8,128)S(1)}, f32[2,8,128]{2,1,0:T(8,128)S(1)}, u32[]{:S(2)}, u32[]{:S(2)}) collective-permute-start(f32[2,8,128]{2,1,0:T(8,128)S(1)} %get-tuple-element.32.own2), channel_id=1, source_target_pairs={{0,1},{2,3},{4,5},{6,7},{1,0},{3,2},{5,4},{7,6},{8,9},{10,11},{12,... | collective-permute-start | bytes 24584 | tf_op jit(solution)/shard_map/ppermute | solution.py:622
  34.4 2.2 %collective-permute-start.8 = (f32[2,8,128]{2,1,0:T(8,128)S(1)}, f32[2,8,128]{2,1,0:T(8,128)S(1)}, u32[]{:S(2)}, u32[]{:S(2)}) collective-permute-start(f32[2,8,128]{2,1,0:T(8,128)S(1)} %get-tuple-element.32.own2), channel_id=1, source_target_pairs={{0,7},{2,1},{4,3},{6,5},{7,0},{1,2},{3,4},{5,6},{8,15},{10,9},{12,... | collective-permute-start | bytes 24584 | tf_op jit(solution)/shard_map/ppermute | solution.py:622
  36.7 0.1 shard_map.53.coef2
  36.9 3.9 %collective-permute-done.8.near_a = f32[2,8,128]{2,1,0:T(8,128)S(1)} collective-permute-done((f32[2,8,128]{2,1,0:T(8,128)S(1)}, f32[2,8,128]{2,1,0:T(8,128)S(1)}, u32[]{:S(2)}, u32[]{:S(2)}) %collective-permute-start.8) | collective-permute-done | bytes 8224 | tf_op jit(solution)/shard_map/ppermute | solution.py:622
  40.8 3.7 %shard_map.54 = f32[256,128]{1,0:T(8,128)} custom-call(f32[2,8,128]{2,1,0:T(8,128)S(1)} %get-tuple-element.32.own2, f32[2,8,128]{2,1,0:T(8,128)S(1)} %collective-permute-done.8.near_a, f32[2,8,128]{2,1,0:T(8,128)S(1)} %collective-permute-done.9.near_b, f32[2,8,128]{2,1,0:T(8,128)S(1)} %collective-permute-done.10.far_a, ...), custom_call_target="tpu_custom_call" | custom-call | tf_op jit(solution)/shard_map/pallas_call | solution.py:608
  (11 shorter events, 0.1 us)
Async XLA Ops:
  1.4 11.4 %collective-permute-start = (f32[29,8,128]{2,1,0:T(8,128)S(1)}, f32[29,8,128]{2,1,0:T(8,128)S(1)}, u32[]{:S(2)}, u32[]{:S(2)}) collective-permute-start(f32[29,8,128]{2,1,0:T(8,128)S(1)} %get-tuple-element.21), channel_id=1, source_target_pairs={{0,7},{2,1},{4,3},{6,5},{7,0},{1,2},{3,4},{5,6},{8,15},{10,9},{12,... | collective-permute-start | bytes 356360 | tf_op jit(solution)/shard_map/ppermute | solution.py:622
  7.5 5.8 %collective-permute-start.1 = (f32[29,8,128]{2,1,0:T(8,128)S(1)}, f32[29,8,128]{2,1,0:T(8,128)S(1)}, u32[]{:S(2)}, u32[]{:S(2)}) collective-permute-start(f32[29,8,128]{2,1,0:T(8,128)S(1)} %get-tuple-element.22), channel_id=1, source_target_pairs={{0,1},{2,3},{4,5},{6,7},{1,0},{3,2},{5,4},{7,6},{8,9},{10,11},{12,... | collective-permute-start | bytes 356360 | tf_op jit(solution)/shard_map/ppermute | solution.py:622
  7.7 12.3 %collective-permute-start.2 = (f32[35,8,128]{2,1,0:T(8,128)S(1)}, f32[35,8,128]{2,1,0:T(8,128)S(1)}, u32[]{:S(2)}, u32[]{:S(2)}) collective-permute-start(f32[35,8,128]{2,1,0:T(8,128)S(1)} %get-tuple-element.24), channel_id=1, source_target_pairs={{0,24},{16,8},{24,0},{8,16},{1,25},{17,9},{25,1},{9,17},{2,26},{18... | collective-permute-start | bytes 430088 | tf_op jit(solution)/shard_map/ppermute | solution.py:622
  8.4 11.6 %collective-permute-start.3 = (f32[35,8,128]{2,1,0:T(8,128)S(1)}, f32[35,8,128]{2,1,0:T(8,128)S(1)}, u32[]{:S(2)}, u32[]{:S(2)}) collective-permute-start(f32[35,8,128]{2,1,0:T(8,128)S(1)} %get-tuple-element.25), channel_id=1, source_target_pairs={{0,8},{16,24},{8,0},{24,16},{1,9},{17,25},{9,1},{25,17},{2,10},{18... | collective-permute-start | bytes 430088 | tf_op jit(solution)/shard_map/ppermute | solution.py:622
  10.2 9.9 %all-to-all-start = ((f32[32,4,128]{2,1,0:T(4,128)}), f32[32,4,128]{2,1,0:T(4,128)S(1)}, u32[]{:S(2)}, u32[]{:S(2)}) async-start(f32[32,4,128]{2,1,0:T(4,128)} %shard_map.49), calls=%async_computation | async-start | bytes 131072 | tf_op jit(solution)/shard_map/all_to_all | solution.py:657
  13.4 6.6 %collective-permute-start.4 = (f32[20,8,128]{2,1,0:T(8,128)S(1)}, f32[20,8,128]{2,1,0:T(8,128)S(1)}, u32[]{:S(2)}, u32[]{:S(2)}) collective-permute-start(f32[20,8,128]{2,1,0:T(8,128)S(1)} %get-tuple-element.26), channel_id=1, source_target_pairs={{0,24},{16,8},{24,0},{8,16},{1,25},{17,9},{25,1},{9,17},{2,26},{18... | collective-permute-start | bytes 245768 | tf_op jit(solution)/shard_map/ppermute | solution.py:622
  14.4 5.6 %collective-permute-start.5 = (f32[20,8,128]{2,1,0:T(8,128)S(1)}, f32[20,8,128]{2,1,0:T(8,128)S(1)}, u32[]{:S(2)}, u32[]{:S(2)}) collective-permute-start(f32[20,8,128]{2,1,0:T(8,128)S(1)} %get-tuple-element.27), channel_id=1, source_target_pairs={{0,8},{16,24},{8,0},{24,16},{1,9},{17,25},{9,1},{25,17},{2,10},{18... | collective-permute-start | bytes 245768 | tf_op jit(solution)/shard_map/ppermute | solution.py:622
  23.1 7.1 %collective-permute-start.6 = (f32[17,8,128]{2,1,0:T(8,128)S(1)}, f32[17,8,128]{2,1,0:T(8,128)S(1)}, u32[]{:S(2)}, u32[]{:S(2)}) collective-permute-start(f32[17,8,128]{2,1,0:T(8,128)S(1)} %get-tuple-element.29), channel_id=1, source_target_pairs={{0,7},{2,1},{4,3},{6,5},{7,0},{1,2},{3,4},{5,6},{8,15},{10,9},{12,... | collective-permute-start | bytes 208904 | tf_op jit(solution)/shard_map/ppermute | solution.py:622
  25.3 5.4 %collective-permute-start.7 = (f32[17,8,128]{2,1,0:T(8,128)S(1)}, f32[17,8,128]{2,1,0:T(8,128)S(1)}, u32[]{:S(2)}, u32[]{:S(2)}) collective-permute-start(f32[17,8,128]{2,1,0:T(8,128)S(1)} %get-tuple-element.30), channel_id=1, source_target_pairs={{0,1},{2,3},{4,5},{6,7},{1,0},{3,2},{5,4},{7,6},{8,9},{10,11},{12,... | collective-permute-start | bytes 208904 | tf_op jit(solution)/shard_map/ppermute | solution.py:622
  31.3 5.5 %collective-permute-start.11 = (f32[2,8,128]{2,1,0:T(8,128)S(1)}, f32[2,8,128]{2,1,0:T(8,128)S(1)}, u32[]{:S(2)}, u32[]{:S(2)}) collective-permute-start(f32[2,8,128]{2,1,0:T(8,128)S(1)} %get-tuple-element.32.own2), channel_id=1, source_target_pairs={{0,6},{1,7},{4,2},{5,3},{6,0},{7,1},{2,4},{3,5},{8,14},{9,15},{12,... | collective-permute-start | bytes 24584 | tf_op jit(solution)/shard_map/ppermute | solution.py:629
  31.9 4.9 %collective-permute-start.10 = (f32[2,8,128]{2,1,0:T(8,128)S(1)}, f32[2,8,128]{2,1,0:T(8,128)S(1)}, u32[]{:S(2)}, u32[]{:S(2)}) collective-permute-start(f32[2,8,128]{2,1,0:T(8,128)S(1)} %get-tuple-element.32.own2), channel_id=1, source_target_pairs={{0,2},{1,3},{4,6},{5,7},{2,0},{3,1},{6,4},{7,5},{8,10},{9,11},{12,... | collective-permute-start | bytes 24584 | tf_op jit(solution)/shard_map/ppermute | solution.py:629
  32.0 4.9 %collective-permute-start.9 = (f32[2,8,128]{2,1,0:T(8,128)S(1)}, f32[2,8,128]{2,1,0:T(8,128)S(1)}, u32[]{:S(2)}, u32[]{:S(2)}) collective-permute-start(f32[2,8,128]{2,1,0:T(8,128)S(1)} %get-tuple-element.32.own2), channel_id=1, source_target_pairs={{0,1},{2,3},{4,5},{6,7},{1,0},{3,2},{5,4},{7,6},{8,9},{10,11},{12,... | collective-permute-start | bytes 24584 | tf_op jit(solution)/shard_map/ppermute | solution.py:622
  34.4 6.3 %collective-permute-start.8 = (f32[2,8,128]{2,1,0:T(8,128)S(1)}, f32[2,8,128]{2,1,0:T(8,128)S(1)}, u32[]{:S(2)}, u32[]{:S(2)}) collective-permute-start(f32[2,8,128]{2,1,0:T(8,128)S(1)} %get-tuple-element.32.own2), channel_id=1, source_target_pairs={{0,7},{2,1},{4,3},{6,5},{7,0},{1,2},{3,4},{5,6},{8,15},{10,9},{12,... | collective-permute-start | bytes 24584 | tf_op jit(solution)/shard_map/ppermute | solution.py:622
where the time goes:
time: 44.6 us; the launch traced here: 44.4 us
  starting transfers between devices  19.6 us (44%)
  waiting for transfers between devices  14.7 us (33%)
  Pallas kernels  10.1 us (23%)
    ppermute x10, starting transfers between devices, swap(): return lax.ppermute(value, axis, pairs + [(j, i) for i, j in pairs])  16.4 us
    pallas_call x9, Pallas kernels, call(): pl.pallas_call(kernel, out_shape=out, in_specs=[pl.BlockSpec(memory_space...  10.1 us
    ppermute x10, waiting for transfers between devices, swap(): return lax.ppermute(value, axis, pairs + [(j, i) for i, j in pairs])  9.65 us
    all_to_all x1, waiting for transfers between devices, body(): spread = lax.all_to_all(spread, ('gx', 'gy'), 0, 0, tiled=True)  4.94 us
    all_to_all x1, starting transfers between devices, body(): spread = lax.all_to_all(spread, ('gx', 'gy'), 0, 0, tiled=True)  2.57 us
  transfers between devices with their start and end apart: 13, of which 6 were waited for; matrix products, arithmetic and copies ran while one was open for 0% of the time, Pallas kernels for 3%

commit v1 on v0

--- a/solution.py
+++ b/solution.py
@@ -530,27 +530,23 @@
     here = pl.ds(1 + OWN, OWN)
     for t, (c, other, spread) in enumerate(packed_terms(x1, 1 + OWN, OWN, 1)):
         res = b1[t, here] - coef1[2, t, here] * c + coef1[1, t, here] * other + spread
-        packet[t : t + 1] = restrict_12([res[j : j + 1] for j in range(OWN)])
+        value = restrict_12([res[j : j + 1] for j in range(OWN)])
+        for c in range(packet.shape[0] // 2):
+            packet[2 * c + t : 2 * c + t + 1] = value
 
 
 def rest_kernel(
-    own2, near_a, near_b, far_a, far_b, gain, coef1, coef2, keep0, keep1, first, second, out, d1, b2, x2, y2, d2, xu, yu, x0, y0, d0
+    count, gathered, gain, coef1, coef2, keep0, keep1, first, second, out, d1, b2, x2, y2, d2, xu, yu, x0, y0, d0
 ):
     rows = out.shape[0] // (2 * Z)
     even = (sub_of() & 1) == 0
     b1, x1 = keep1.at[0], keep1.at[1]
 
-    even_y, low = is_even("gy"), lax.rem(lax.axis_index("gy"), 4) < 2
-    for t in (0, 1):
-        at = slice(t, t + 1)
-        parts = [
-            next_of(low, far_a, far_b, at),
-            prev_of(even_y, near_a, near_b, at),
-            own2[at],
-            next_of(even_y, near_a, near_b, at),
-            prev_of(low, far_a, far_b, at),
-        ]
-        b2[t, 1 : SIZE2 - 1] = jnp.concatenate(parts, axis=0)
+    even_y, me = is_even("gy"), lax.axis_index("gy")
+    for q in range(GROUPS2):
+        at = lax.rem(me + LO2 + q + 4 * count, count) * 2
+        for t in (0, 1):
+            b2[t, 1 + q : 2 + q] = gathered[pl.ds(at + t, 1)]
 
     n = HI2 - LO2
     g0, g1, g2 = (gain[6 + i] for i in range(3))
@@ -622,13 +618,6 @@
     return lax.ppermute(value, axis, pairs + [(j, i) for i, j in pairs])
 
 
-def swap_far(value, axis, step):
-    count = lax.axis_size(axis)
-    assert count % 4 == 0
-    pairs = [(i + j, (i + j + 2 * step) % count) for i in range(0, count, 4) for j in (0, 1)]
-    return lax.ppermute(value, axis, pairs + [(j, i) for i, j in pairs])
-
-
 def exchange(first, second, axis):
     return swap(first, axis, -1), swap(second, axis, 1)
 
@@ -653,7 +642,7 @@
         space=pltpu.HBM,
     )
     y_packets = exchange(first, second, "gy")
-    (spread,) = call(spread_kernel, [(across * count, Z // 2, X)], [], main, coarse)
+    (spread,) = call(spread_kernel, [(across * count, 6, X)], [], main, coarse)
     spread = lax.all_to_all(spread, ("gx", "gy"), 0, 0, tiled=True)
 
     tiles = tiles_for(6 * rows + 2 * OWN + 1)
@@ -698,10 +687,9 @@
 
     one, two, up = (2, SIZE1, Z, X), (2, SIZE2, Z, X), (2, SIZE_UP, Z, X)
     packet, keep1 = call(
-        level1_kernel, [(2, Z, X), (2, *one)], [one, one], own, *b_packets, coef1, gain
-    )
-    near = exchange(packet, packet, "gy")
-    far = (swap_far(packet, "gy", 1), swap_far(packet, "gy", -1))
+        level1_kernel, [(2 * count, Z, X), (2, *one)], [one, one], own, *b_packets, coef1, gain
+    )
+    gathered = lax.all_to_all(packet, "gy", 0, 0, tiled=True)
     (coef2,) = call(
         functools.partial(coarse2_kernel, rows),
         [(2, 2, SIZE2, Z, X)],
@@ -714,12 +702,10 @@
     )
 
     (out,) = call(
-        rest_kernel,
+        functools.partial(rest_kernel, count),
         [(2 * Z * rows, X)],
         [one, two, two, two, two, up, up, pair0, pair0, pair0],
-        packet,
-        *near,
-        *far,
+        gathered,
         gain,
         coef1,
         coef2,

time: 44.6 us -> 48.2 us (1.081)
  waiting for transfers between devices: 14.7 us -> 16.7 us
  starting transfers between devices: 19.6 us -> 20.4 us
  Pallas kernels: 10.1 us -> 10.8 us
    all_to_all x0 -> x1, waiting for transfers between devices: none -> 6.8 us  [body(): gathered = lax.all_to_all(packet, 'gy', 0, 0, tiled=True)]
    all_to_all x1, waiting for transfers between devices: 4.94 us -> 0.49 us  [body(): spread = lax.all_to_all(spread, ('gx', 'gy'), 0, 0, tiled=True)]
    all_to_all x0 -> x1, starting transfers between devices: none -> 3.88 us  [body(): gathered = lax.all_to_all(packet, 'gy', 0, 0, tiled=True)]
    ppermute x10 -> x8, starting transfers between devices: 16.4 us -> 13.2 us  [swap(): return lax.ppermute(value, axis, pairs + [(j, i) for i, j in pairs])]
    all_to_all x1, starting transfers between devices: 2.57 us -> 3.31 us  [body(): spread = lax.all_to_all(spread, ('gx', 'gy'), 0, 0, tiled=True)]
    pallas_call x9, Pallas kernels: 10.1 us -> 10.8 us  [call(): pl.pallas_call(kernel, out_shape=out, in_specs=[pl.BlockSpec(memory_space...]
    ppermute x2 -> x0, starting transfers between devices: 0.64 us -> none  [swap_far(): return lax.ppermute(value, axis, pairs + [(j, i) for i, j in pairs])]
    ppermute x10 -> x8, waiting for transfers between devices: 9.65 us -> 9.36 us  [swap(): return lax.ppermute(value, axis, pairs + [(j, i) for i, j in pairs])]
  transfers between devices with their start and end apart: 13 -> 10, of which waited for: 6 -> 6; matrix products, arithmetic and copies ran while one was open for 0% -> 0% of each run, Pallas kernels for 3% -> 3%
where the time goes in v1:
time: 48.2 us; the launch traced here: 47.9 us
  starting transfers between devices  20.4 us (42%)
  waiting for transfers between devices  16.7 us (35%)
  Pallas kernels  10.8 us (22%)
    ppermute x8, starting transfers between devices, swap(): return lax.ppermute(value, axis, pairs + [(j, i) for i, j in pairs])  13.2 us
    pallas_call x9, Pallas kernels, call(): pl.pallas_call(kernel, out_shape=out, in_specs=[pl.BlockSpec(memory_space...  10.8 us
    ppermute x8, waiting for transfers between devices, swap(): return lax.ppermute(value, axis, pairs + [(j, i) for i, j in pairs])  9.36 us
    all_to_all x1, waiting for transfers between devices, body(): gathered = lax.all_to_all(packet, 'gy', 0, 0, tiled=True)  6.8 us
    all_to_all x1, starting transfers between devices, body(): gathered = lax.all_to_all(packet, 'gy', 0, 0, tiled=True)  3.88 us
    all_to_all x1, starting transfers between devices, body(): spread = lax.all_to_all(spread, ('gx', 'gy'), 0, 0, tiled=True)  3.31 us
  transfers between devices with their start and end apart: 10, of which 6 were waited for; matrix products, arithmetic and copies ran while one was open for 0% of the time, Pallas kernels for 3%

profile of v1, /device:TPU:0, one launch (start us, length us, event | category | flops | bytes accessed | tf_op | source)
XLA Modules:
  0.0 47.9 jit_solution(6422989675211983227)
XLA Ops:
  0.0 1.4 %shard_map.46 = (f32[29,8,128]{2,1,0:T(8,128)S(1)}, f32[29,8,128]{2,1,0:T(8,128)S(1)}, f32[6,16,8,128]{3,2,1,0:T(8,128)S(1)}, f32[9,8,128]{2,1,0:T(8,128)S(1)}) custom-call(f32[256,128]{1,0:T(8,128)} %bitcast.5, f32[256,128]{1,0:T(8,128)} %bitcast.6, f32[128,128]{1,0:T(8,128)} %bitcast.7, f32[128,128]{1,0:T(8,128)} %bitcast.8), custom_call_target="tpu_custom_call" | custom-call | tf_op jit(solution)/shard_map/pallas_call | solution.py:604
  1.4 6.1 %collective-permute-start = (f32[29,8,128]{2,1,0:T(8,128)S(1)}, f32[29,8,128]{2,1,0:T(8,128)S(1)}, u32[]{:S(2)}, u32[]{:S(2)}) collective-permute-start(f32[29,8,128]{2,1,0:T(8,128)S(1)} %get-tuple-element.21), channel_id=1, source_target_pairs={{0,7},{2,1},{4,3},{6,5},{7,0},{1,2},{3,4},{5,6},{8,15},{10,9},{12,... | collective-permute-start | bytes 356360 | tf_op jit(solution)/shard_map/ppermute | solution.py:618
  7.5 0.0 collective-permute-start.1
  7.5 0.8 %shard_map.49 = f32[32,6,128]{2,1,0:T(8,128)} custom-call(f32[6,16,8,128]{3,2,1,0:T(8,128)S(1)} %get-tuple-element.20.main, f32[9,8,128]{2,1,0:T(8,128)S(1)} %get-tuple-element.23.coarse), custom_call_target="tpu_custom_call" | custom-call | tf_op jit(solution)/shard_map/pallas_call | solution.py:604
  8.3 3.3 %all-to-all-start = ((f32[32,6,128]{2,1,0:T(8,128)}), f32[32,6,128]{2,1,0:T(8,128)S(1)}, u32[]{:S(2)}, u32[]{:S(2)}) async-start(f32[32,6,128]{2,1,0:T(8,128)} %shard_map.49), calls=%async_computation | async-start | bytes 262144 | tf_op jit(solution)/shard_map/all_to_all | solution.py:646
  11.6 0.3 shard_map.47
  11.9 1.6 %collective-permute-start.2 = (f32[35,8,128]{2,1,0:T(8,128)S(1)}, f32[35,8,128]{2,1,0:T(8,128)S(1)}, u32[]{:S(2)}, u32[]{:S(2)}) collective-permute-start(f32[35,8,128]{2,1,0:T(8,128)S(1)} %get-tuple-element.24), channel_id=1, source_target_pairs={{0,24},{16,8},{24,0},{8,16},{1,25},{17,9},{25,1},{9,17},{2,26},{18... | collective-permute-start | bytes 430088 | tf_op jit(solution)/shard_map/ppermute | solution.py:618
  13.4 0.4 collective-permute-start.3
  13.8 0.2 shard_map.48
  14.0 0.4 collective-permute-start.4
  14.4 0.7 %collective-permute-start.5 = (f32[20,8,128]{2,1,0:T(8,128)S(1)}, f32[20,8,128]{2,1,0:T(8,128)S(1)}, u32[]{:S(2)}, u32[]{:S(2)}) collective-permute-start(f32[20,8,128]{2,1,0:T(8,128)S(1)} %get-tuple-element.27), channel_id=1, source_target_pairs={{0,8},{16,24},{8,0},{24,16},{1,9},{17,25},{9,1},{25,17},{2,10},{18... | collective-permute-start | bytes 245768 | tf_op jit(solution)/shard_map/ppermute | solution.py:618
  15.1 3.7 %collective-permute-done.2.own_a = f32[35,8,128]{2,1,0:T(8,128)S(1)} collective-permute-done((f32[35,8,128]{2,1,0:T(8,128)S(1)}, f32[35,8,128]{2,1,0:T(8,128)S(1)}, u32[]{:S(2)}, u32[]{:S(2)}) %collective-permute-start.2) | collective-permute-done | bytes 143392 | tf_op jit(solution)/shard_map/ppermute | solution.py:618
  18.9 0.5 %all-to-all-done.gathered = f32[32,6,128]{2,1,0:T(8,128)S(1)} async-done(((f32[32,6,128]{2,1,0:T(8,128)}), f32[32,6,128]{2,1,0:T(8,128)S(1)}, u32[]{:S(2)}, u32[]{:S(2)}) %all-to-all-start) | async-done | bytes 98336 | tf_op jit(solution)/shard_map/all_to_all | solution.py:646
  19.3 1.4 %collective-permute-done.4.corner_a = f32[20,8,128]{2,1,0:T(8,128)S(1)} collective-permute-done((f32[20,8,128]{2,1,0:T(8,128)S(1)}, f32[20,8,128]{2,1,0:T(8,128)S(1)}, u32[]{:S(2)}, u32[]{:S(2)}) %collective-permute-start.4) | collective-permute-done | bytes 81952 | tf_op jit(solution)/shard_map/ppermute | solution.py:618
  20.7 3.0 %shard_map.50 = (f32[2,4,8,128]{3,2,1,0:T(8,128)S(1)}, f32[17,8,128]{2,1,0:T(8,128)S(1)}, f32[17,8,128]{2,1,0:T(8,128)S(1)}, f32[8,2,24,8,128]{4,3,2,1,0:T(8,128)S(1)}, f32[9,8,128]{2,1,0:T(8,128)S(1)}) custom-call(f32[6,16,8,128]{3,2,1,0:T(8,128)S(1)} %get-tuple-element.20.main, f32[29,8,128]{2,1,0:T(8,128)S(1)} %collective-permute-done.y_first, ...), custom_call_target="tpu_custom_call" | custom-call | tf_op jit(solution)/shard_map/pallas_call | solution.py:604
  23.7 4.1 %collective-permute-start.6 = (f32[17,8,128]{2,1,0:T(8,128)S(1)}, f32[17,8,128]{2,1,0:T(8,128)S(1)}, u32[]{:S(2)}, u32[]{:S(2)}) collective-permute-start(f32[17,8,128]{2,1,0:T(8,128)S(1)} %get-tuple-element.29), channel_id=1, source_target_pairs={{0,7},{2,1},{4,3},{6,5},{7,0},{1,2},{3,4},{5,6},{8,15},{10,9},{12,... | collective-permute-start | bytes 208904 | tf_op jit(solution)/shard_map/ppermute | solution.py:618
  27.8 0.2 shard_map.51.coef1
  28.0 2.8 %collective-permute-done.6.first.b_first = f32[17,8,128]{2,1,0:T(8,128)S(1)} collective-permute-done((f32[17,8,128]{2,1,0:T(8,128)S(1)}, f32[17,8,128]{2,1,0:T(8,128)S(1)}, u32[]{:S(2)}, u32[]{:S(2)}) %collective-permute-start.6) | collective-permute-done | bytes 69664 | tf_op jit(solution)/shard_map/ppermute | solution.py:618
  30.8 1.4 %collective-permute-done.7.second.b_second = f32[17,8,128]{2,1,0:T(8,128)S(1)} collective-permute-done((f32[17,8,128]{2,1,0:T(8,128)S(1)}, f32[17,8,128]{2,1,0:T(8,128)S(1)}, u32[]{:S(2)}, u32[]{:S(2)}) %collective-permute-start.7) | collective-permute-done | bytes 69664 | tf_op jit(solution)/shard_map/ppermute | solution.py:618
  32.2 1.2 %shard_map.52 = (f32[16,8,128]{2,1,0:T(8,128)}, f32[2,2,14,8,128]{4,3,2,1,0:T(8,128)S(1)}) custom-call(f32[2,4,8,128]{3,2,1,0:T(8,128)S(1)} %get-tuple-element.28.own, f32[17,8,128]{2,1,0:T(8,128)S(1)} %collective-permute-done.6.first.b_first, f32[17,8,128]{2,1,0:T(8,128)S(1)} %collective-permute-done.7.second.b_second, ...), custom_call_target="tpu_custom_call" | custom-call | tf_op jit(solution)/shard_map/pallas_call | solution.py:604
  33.4 3.9 %all-to-all-start.1 = ((f32[16,8,128]{2,1,0:T(8,128)}), f32[16,8,128]{2,1,0:T(8,128)S(1)}, u32[]{:S(2)}, u32[]{:S(2)}) async-start(f32[16,8,128]{2,1,0:T(8,128)} %get-tuple-element.32), calls=%async_computation.1 | async-start | bytes 131072 | tf_op jit(solution)/shard_map/all_to_all | solution.py:692
  37.3 0.1 shard_map.53.coef2
  37.4 6.8 %all-to-all-done.1.gathered = f32[16,8,128]{2,1,0:T(8,128)S(1)} async-done(((f32[16,8,128]{2,1,0:T(8,128)}), f32[16,8,128]{2,1,0:T(8,128)S(1)}, u32[]{:S(2)}, u32[]{:S(2)}) %all-to-all-start.1) | async-done | bytes 65568 | tf_op jit(solution)/shard_map/all_to_all | solution.py:692
  44.2 3.7 %shard_map.54 = f32[256,128]{1,0:T(8,128)} custom-call(f32[16,8,128]{2,1,0:T(8,128)S(1)} %all-to-all-done.1.gathered, f32[9,8,128]{2,1,0:T(8,128)S(1)} %get-tuple-element.31.gain, f32[3,2,14,8,128]{4,3,2,1,0:T(8,128)S(1)} %shard_map.51.coef1, f32[2,2,7,8,128]{4,3,2,1,0:T(8,128)S(1)} %shard_map.53.coef2, f32[8,2,24,8,128]{4,3,2,1,0:T(8,128)S(1)} %get-tuple-element.33.keep0, ...), custom_call_target="tpu_custom_call" | custom-call | tf_op jit(solution)/shard_map/pallas_call | solution.py:604
  (5 shorter events, 0.0 us)
Async XLA Ops:
  1.4 12.4 %collective-permute-start = (f32[29,8,128]{2,1,0:T(8,128)S(1)}, f32[29,8,128]{2,1,0:T(8,128)S(1)}, u32[]{:S(2)}, u32[]{:S(2)}) collective-permute-start(f32[29,8,128]{2,1,0:T(8,128)S(1)} %get-tuple-element.21), channel_id=1, source_target_pairs={{0,7},{2,1},{4,3},{6,5},{7,0},{1,2},{3,4},{5,6},{8,15},{10,9},{12,... | collective-permute-start | bytes 356360 | tf_op jit(solution)/shard_map/ppermute | solution.py:618
  7.5 6.4 %collective-permute-start.1 = (f32[29,8,128]{2,1,0:T(8,128)S(1)}, f32[29,8,128]{2,1,0:T(8,128)S(1)}, u32[]{:S(2)}, u32[]{:S(2)}) collective-permute-start(f32[29,8,128]{2,1,0:T(8,128)S(1)} %get-tuple-element.22), channel_id=1, source_target_pairs={{0,1},{2,3},{4,5},{6,7},{1,0},{3,2},{5,4},{7,6},{8,9},{10,11},{12,... | collective-permute-start | bytes 356360 | tf_op jit(solution)/shard_map/ppermute | solution.py:618
  8.3 11.1 %all-to-all-start = ((f32[32,6,128]{2,1,0:T(8,128)}), f32[32,6,128]{2,1,0:T(8,128)S(1)}, u32[]{:S(2)}, u32[]{:S(2)}) async-start(f32[32,6,128]{2,1,0:T(8,128)} %shard_map.49), calls=%async_computation | async-start | bytes 262144 | tf_op jit(solution)/shard_map/all_to_all | solution.py:646
  11.9 7.0 %collective-permute-start.2 = (f32[35,8,128]{2,1,0:T(8,128)S(1)}, f32[35,8,128]{2,1,0:T(8,128)S(1)}, u32[]{:S(2)}, u32[]{:S(2)}) collective-permute-start(f32[35,8,128]{2,1,0:T(8,128)S(1)} %get-tuple-element.24), channel_id=1, source_target_pairs={{0,24},{16,8},{24,0},{8,16},{1,25},{17,9},{25,1},{9,17},{2,26},{18... | collective-permute-start | bytes 430088 | tf_op jit(solution)/shard_map/ppermute | solution.py:618
  13.4 5.4 %collective-permute-start.3 = (f32[35,8,128]{2,1,0:T(8,128)S(1)}, f32[35,8,128]{2,1,0:T(8,128)S(1)}, u32[]{:S(2)}, u32[]{:S(2)}) collective-permute-start(f32[35,8,128]{2,1,0:T(8,128)S(1)} %get-tuple-element.25), channel_id=1, source_target_pairs={{0,8},{16,24},{8,0},{24,16},{1,9},{17,25},{9,1},{25,17},{2,10},{18... | collective-permute-start | bytes 430088 | tf_op jit(solution)/shard_map/ppermute | solution.py:618
  14.0 6.7 %collective-permute-start.4 = (f32[20,8,128]{2,1,0:T(8,128)S(1)}, f32[20,8,128]{2,1,0:T(8,128)S(1)}, u32[]{:S(2)}, u32[]{:S(2)}) collective-permute-start(f32[20,8,128]{2,1,0:T(8,128)S(1)} %get-tuple-element.26), channel_id=1, source_target_pairs={{0,24},{16,8},{24,0},{8,16},{1,25},{17,9},{25,1},{9,17},{2,26},{18... | collective-permute-start | bytes 245768 | tf_op jit(solution)/shard_map/ppermute | solution.py:618
  14.4 6.3 %collective-permute-start.5 = (f32[20,8,128]{2,1,0:T(8,128)S(1)}, f32[20,8,128]{2,1,0:T(8,128)S(1)}, u32[]{:S(2)}, u32[]{:S(2)}) collective-permute-start(f32[20,8,128]{2,1,0:T(8,128)S(1)} %get-tuple-element.27), channel_id=1, source_target_pairs={{0,8},{16,24},{8,0},{24,16},{1,9},{17,25},{9,1},{25,17},{2,10},{18... | collective-permute-start | bytes 245768 | tf_op jit(solution)/shard_map/ppermute | solution.py:618
  23.7 7.1 %collective-permute-start.6 = (f32[17,8,128]{2,1,0:T(8,128)S(1)}, f32[17,8,128]{2,1,0:T(8,128)S(1)}, u32[]{:S(2)}, u32[]{:S(2)}) collective-permute-start(f32[17,8,128]{2,1,0:T(8,128)S(1)} %get-tuple-element.29), channel_id=1, source_target_pairs={{0,7},{2,1},{4,3},{6,5},{7,0},{1,2},{3,4},{5,6},{8,15},{10,9},{12,... | collective-permute-start | bytes 208904 | tf_op jit(solution)/shard_map/ppermute | solution.py:618
  27.8 4.4 %collective-permute-start.7 = (f32[17,8,128]{2,1,0:T(8,128)S(1)}, f32[17,8,128]{2,1,0:T(8,128)S(1)}, u32[]{:S(2)}, u32[]{:S(2)}) collective-permute-start(f32[17,8,128]{2,1,0:T(8,128)S(1)} %get-tuple-element.30), channel_id=1, source_target_pairs={{0,1},{2,3},{4,5},{6,7},{1,0},{3,2},{5,4},{7,6},{8,9},{10,11},{12,... | collective-permute-start | bytes 208904 | tf_op jit(solution)/shard_map/ppermute | solution.py:618
  33.4 10.8 %all-to-all-start.1 = ((f32[16,8,128]{2,1,0:T(8,128)}), f32[16,8,128]{2,1,0:T(8,128)S(1)}, u32[]{:S(2)}, u32[]{:S(2)}) async-start(f32[16,8,128]{2,1,0:T(8,128)} %get-tuple-element.32), calls=%async_computation.1 | async-start | bytes 131072 | tf_op jit(solution)/shard_map/all_to_all | solution.py:692

commit v2 on v0

--- a/solution.py
+++ b/solution.py
@@ -29,7 +29,6 @@
 WIDE = 42
 PER = X // WIDE
 EDGE = 3
-CHUNK = 4
 
 LO1, HI1 = -4, 8
 LO2, HI2 = -2, 3
@@ -56,7 +55,8 @@
     return pltpu.roll(tile, shift, 1) if shift else tile
 
 
-def rows_loop(lo, hi, body, step=CHUNK):
+def rows_loop(lo, hi, body, step=None):
+    step = step or (hi - lo) // 2
     full = (hi - lo) // step
     if full == 1:
         body(lo, step)
@@ -370,12 +370,13 @@
     pack_edges(held, is_even("gx"), first, second)
 
 
-EDGES = 2 * OWN
-FAR = EDGES + 2 * EDGE + 1
+FAR = 2 * OWN
+EDGES = 2
+EDGE_TILES = 2 * EDGE + 1
 
 
 def level0_kernel(
-    rows, main, y_first, y_second, own_a, own_b, corner_a, corner_b, gathered, own, first, second, keep, gain_out, fields, other, d, diag
+    rows, main, y_first, y_second, own_a, own_b, corner_a, corner_b, gathered, own, first, second, edge_first, edge_second, keep, gain_out, fields, other, d, diag
 ):
     even, even_x = is_even("gy"), is_even("gx")
     total = rows + 2 * HALO0
@@ -429,15 +430,14 @@
 
     def down(r, n):
         res = residual(0, keep, diag, here, r, n)
-        out = (r - HALO0) // 4
         for t in (0, 1):
-            value = restrict_01(pair_rows(res[0][t]), pair_rows(res[1][t]))
-            own[t, pl.ds(out, 1)] = value
-            if t == 0:
-                first[pl.ds(out, 1)] = value
-                second[pl.ds(out, 1)] = value
-
-    rows_loop(HALO0, HALO0 + rows, down, 4)
+            u, v = pair_rows(res[0][t]), pair_rows(res[1][t])
+            for j in range(n // 4):
+                value = restrict_01(u[2 * j : 2 * j + 2], v[2 * j : 2 * j + 2])
+                for ref, at in ((own.at[t], 0), (first, t * OWN), (second, t * OWN)):
+                    ref[pl.ds(at + (r - HALO0) // 4 + j, 1)] = value
+
+    rows_loop(HALO0, HALO0 + rows, down, 8)
 
     lane = lane_of()
     edges = []
@@ -450,8 +450,6 @@
                 halo = value if halo is None else jnp.where((lane >> 3) == at, value, halo)
         edges.append([keep[6, 0, start : start + EDGE], keep[7, 0, start : start + EDGE], halo])
     top, bottom = (jnp.concatenate(parts, axis=0) for parts in edges)
-    for ref in (first, second):
-        ref[OWN : 2 * OWN] = own[1]
     strip = slice(FIELDS2, FIELDS2 + 1)
     for t in (0, 1):
         if t == 0:
@@ -462,8 +460,8 @@
             )
         first[FAR + t : FAR + t + 1] = jnp.where(even, after, before)
         second[FAR + t : FAR + t + 1] = jnp.where(even, before, after)
-    first[EDGES : EDGES + 2 * EDGE + 1] = jnp.where(even, top, bottom)
-    second[EDGES : EDGES + 2 * EDGE + 1] = jnp.where(even, bottom, top)
+    edge_first[...] = jnp.where(even, top, bottom)
+    edge_second[...] = jnp.where(even, bottom, top)
 
 
 def coarse1_kernel(
@@ -514,7 +512,7 @@
         coef[1, t, 1 : SIZE2 - 1] = other
 
 
-def level1_kernel(own, first, second, coef1, gain, packet, keep, y1, d1):
+def level1_kernel(own, first, second, edge_a, edge_b, coef1, gain, packet, to_first, to_second, keep, y1, d1):
     b1, x1 = keep.at[0], keep.at[1]
     even = is_even("gy")
     for t in (0, 1):
@@ -530,11 +528,15 @@
     here = pl.ds(1 + OWN, OWN)
     for t, (c, other, spread) in enumerate(packed_terms(x1, 1 + OWN, OWN, 1)):
         res = b1[t, here] - coef1[2, t, here] * c + coef1[1, t, here] * other + spread
-        packet[t : t + 1] = restrict_12([res[j : j + 1] for j in range(OWN)])
+        value = restrict_12([res[j : j + 1] for j in range(OWN)])
+        for ref in (packet, to_first, to_second):
+            ref[t : t + 1] = value
+    to_first[EDGES : EDGES + EDGE_TILES] = edge_a[...]
+    to_second[EDGES : EDGES + EDGE_TILES] = edge_b[...]
 
 
 def rest_kernel(
-    own2, near_a, near_b, far_a, far_b, gain, coef1, coef2, keep0, keep1, first, second, out, d1, b2, x2, y2, d2, xu, yu, x0, y0, d0
+    own2, near_a, near_b, far_a, far_b, gain, coef1, coef2, keep0, keep1, out, d1, b2, x2, y2, d2, xu, yu, x0, y0, d0
 ):
     rows = out.shape[0] // (2 * Z)
     even = (sub_of() & 1) == 0
@@ -580,8 +582,8 @@
     for i in (0, 1):
         for at, take in ((HALO0 - EDGE, prev_of), (HALO0 + rows, next_of)):
             strip = slice(EDGES + i * EDGE, EDGES + (i + 1) * EDGE)
-            x0[i, 0, at : at + EDGE] = take(even_y, first, second, strip)
-            sides = take(even_y, first, second, slice(last, last + 1))
+            x0[i, 0, at : at + EDGE] = take(even_y, near_a, near_b, strip)
+            sides = take(even_y, near_a, near_b, slice(last, last + 1))
             for j in range(EDGE):
                 x0[i, 1, at + j : at + j + 1] = roll_x(sides, -(4 + 8 * (i * EDGE + j)))
         for t in (0, 1):
@@ -672,11 +674,11 @@
         *call(pack_corner_kernel, [(tiles, Z, X), (tiles, Z, X)], [(PER * tiles, Z, X)], *y_packets), "gx"
     )
 
-    strip = (FAR + 2, Z, X)
+    strip, edge = (FAR + 2, Z, X), (EDGE_TILES, Z, X)
     pair0 = (2, 2, total0, Z, X)
-    own, first, second, keep0, gain = call(
+    own, first, second, edge_a, edge_b, keep0, gain = call(
         functools.partial(level0_kernel, rows),
-        [(2, OWN, Z, X), strip, strip, (8, 2, total0, Z, X), (9, Z, X)],
+        [(2, OWN, Z, X), strip, strip, edge, edge, (8, 2, total0, Z, X), (9, Z, X)],
         [(6, 2, total0, Z, X), pair0, pair0, pair0],
         main,
         *y_packets,
@@ -697,11 +699,20 @@
     b_packets = exchange(first, second, "gy")
 
     one, two, up = (2, SIZE1, Z, X), (2, SIZE2, Z, X), (2, SIZE_UP, Z, X)
-    packet, keep1 = call(
-        level1_kernel, [(2, Z, X), (2, *one)], [one, one], own, *b_packets, coef1, gain
-    )
-    near = exchange(packet, packet, "gy")
+    near = (EDGES + EDGE_TILES, Z, X)
+    packet, first, second, keep1 = call(
+        level1_kernel,
+        [(2, Z, X), near, near, (2, *one)],
+        [one, one],
+        own,
+        *b_packets,
+        edge_a,
+        edge_b,
+        coef1,
+        gain,
+    )
     far = (swap_far(packet, "gy", 1), swap_far(packet, "gy", -1))
+    near = exchange(first, second, "gy")
     (coef2,) = call(
         functools.partial(coarse2_kernel, rows),
         [(2, 2, SIZE2, Z, X)],
@@ -725,7 +736,6 @@
         coef2,
         keep0,
         keep1,
-        *b_packets,
     )
     return out.reshape(2, Z, rows, X)
 

time: 44.6 us -> 41.9 us (0.939)
  waiting for transfers between devices: 14.7 us -> 13.3 us
  Pallas kernels: 10.1 us -> 8.73 us
    ppermute x10, waiting for transfers between devices: 9.65 us -> 4.82 us  [swap(): return lax.ppermute(value, axis, pairs + [(j, i) for i, j in pairs])]
    ppermute x2, waiting for transfers between devices: 0.09 us -> 3.55 us  [swap_far(): return lax.ppermute(value, axis, pairs + [(j, i) for i, j in pairs])]
    ppermute x2, starting transfers between devices: 0.64 us -> 2.85 us  [swap_far(): return lax.ppermute(value, axis, pairs + [(j, i) for i, j in pairs])]
    ppermute x10, starting transfers between devices: 16.4 us -> 14.2 us  [swap(): return lax.ppermute(value, axis, pairs + [(j, i) for i, j in pairs])]
    pallas_call x9, Pallas kernels: 10.1 us -> 8.73 us  [call(): pl.pallas_call(kernel, out_shape=out, in_specs=[pl.BlockSpec(memory_space...]
  transfers between devices with their start and end apart: 13 -> 13, of which waited for: 6 -> 5; matrix products, arithmetic and copies ran while one was open for 0% -> 0% of each run, Pallas kernels for 3% -> 4%
where the time goes in v2:
time: 41.9 us; the launch traced here: 41.8 us
  starting transfers between devices  19.6 us (47%)
  waiting for transfers between devices  13.3 us (32%)
  Pallas kernels  8.73 us (21%)
    ppermute x10, starting transfers between devices, swap(): return lax.ppermute(value, axis, pairs + [(j, i) for i, j in pairs])  14.2 us
    pallas_call x9, Pallas kernels, call(): pl.pallas_call(kernel, out_shape=out, in_specs=[pl.BlockSpec(memory_space...  8.73 us
    all_to_all x1, waiting for transfers between devices, body(): spread = lax.all_to_all(spread, ('gx', 'gy'), 0, 0, tiled=True)  4.94 us
    ppermute x10, waiting for transfers between devices, swap(): return lax.ppermute(value, axis, pairs + [(j, i) for i, j in pairs])  4.82 us
    ppermute x2, waiting for transfers between devices, swap_far(): return lax.ppermute(value, axis, pairs + [(j, i) for i, j in pairs])  3.55 us
    ppermute x2, starting transfers between devices, swap_far(): return lax.ppermute(value, axis, pairs + [(j, i) for i, j in pairs])  2.85 us
    all_to_all x1, starting transfers between devices, body(): spread = lax.all_to_all(spread, ('gx', 'gy'), 0, 0, tiled=True)  2.57 us
  transfers between devices with their start and end apart: 13, of which 5 were waited for; matrix products, arithmetic and copies ran while one was open for 0% of the time, Pallas kernels for 4%

profile of v2, /device:TPU:0, one launch (start us, length us, event | category | flops | bytes accessed | tf_op | source)
XLA Modules:
  0.0 41.8 jit_solution(13558971239900097511)
XLA Ops:
  0.0 1.4 %shard_map.46 = (f32[29,8,128]{2,1,0:T(8,128)S(1)}, f32[29,8,128]{2,1,0:T(8,128)S(1)}, f32[6,16,8,128]{3,2,1,0:T(8,128)S(1)}, f32[9,8,128]{2,1,0:T(8,128)S(1)}) custom-call(f32[256,128]{1,0:T(8,128)} %bitcast.5, f32[256,128]{1,0:T(8,128)} %bitcast.6, f32[128,128]{1,0:T(8,128)} %bitcast.7, f32[128,128]{1,0:T(8,128)} %bitcast.8), custom_call_target="tpu_custom_call" | custom-call | tf_op jit(solution)/shard_map/pallas_call | solution.py:610
  1.4 6.1 %collective-permute-start = (f32[29,8,128]{2,1,0:T(8,128)S(1)}, f32[29,8,128]{2,1,0:T(8,128)S(1)}, u32[]{:S(2)}, u32[]{:S(2)}) collective-permute-start(f32[29,8,128]{2,1,0:T(8,128)S(1)} %get-tuple-element.25), channel_id=1, source_target_pairs={{0,7},{2,1},{4,3},{6,5},{7,0},{1,2},{3,4},{5,6},{8,15},{10,9},{12,... | collective-permute-start | bytes 356360 | tf_op jit(solution)/shard_map/ppermute | solution.py:624
  7.5 0.0 collective-permute-start.1
  7.5 0.2 shard_map.47
  7.7 0.7 %collective-permute-start.2 = (f32[35,8,128]{2,1,0:T(8,128)S(1)}, f32[35,8,128]{2,1,0:T(8,128)S(1)}, u32[]{:S(2)}, u32[]{:S(2)}) collective-permute-start(f32[35,8,128]{2,1,0:T(8,128)S(1)} %get-tuple-element.28), channel_id=1, source_target_pairs={{0,24},{16,8},{24,0},{8,16},{1,25},{17,9},{25,1},{9,17},{2,26},{18... | collective-permute-start | bytes 430088 | tf_op jit(solution)/shard_map/ppermute | solution.py:624
  8.4 1.0 %collective-permute-start.3 = (f32[35,8,128]{2,1,0:T(8,128)S(1)}, f32[35,8,128]{2,1,0:T(8,128)S(1)}, u32[]{:S(2)}, u32[]{:S(2)}) collective-permute-start(f32[35,8,128]{2,1,0:T(8,128)S(1)} %get-tuple-element.29), channel_id=1, source_target_pairs={{0,8},{16,24},{8,0},{24,16},{1,9},{17,25},{9,1},{25,17},{2,10},{18... | collective-permute-start | bytes 430088 | tf_op jit(solution)/shard_map/ppermute | solution.py:624
  9.4 0.8 %shard_map.49 = f32[32,4,128]{2,1,0:T(4,128)} custom-call(f32[6,16,8,128]{3,2,1,0:T(8,128)S(1)} %get-tuple-element.24.main, f32[9,8,128]{2,1,0:T(8,128)S(1)} %get-tuple-element.27.coarse), custom_call_target="tpu_custom_call" | custom-call | tf_op jit(solution)/shard_map/pallas_call | solution.py:610
  10.2 2.6 %all-to-all-start = ((f32[32,4,128]{2,1,0:T(4,128)}), f32[32,4,128]{2,1,0:T(4,128)S(1)}, u32[]{:S(2)}, u32[]{:S(2)}) async-start(f32[32,4,128]{2,1,0:T(4,128)} %shard_map.49), calls=%async_computation | async-start | bytes 131072 | tf_op jit(solution)/shard_map/all_to_all | solution.py:659
  12.8 0.5 %collective-permute-done.1.y_second = f32[29,8,128]{2,1,0:T(8,128)S(1)} collective-permute-done((f32[29,8,128]{2,1,0:T(8,128)S(1)}, f32[29,8,128]{2,1,0:T(8,128)S(1)}, u32[]{:S(2)}, u32[]{:S(2)}) %collective-permute-start.1) | collective-permute-done | bytes 118816 | tf_op jit(solution)/shard_map/ppermute | solution.py:624
  13.2 0.2 shard_map.48
  13.4 1.0 %collective-permute-start.4 = (f32[20,8,128]{2,1,0:T(8,128)S(1)}, f32[20,8,128]{2,1,0:T(8,128)S(1)}, u32[]{:S(2)}, u32[]{:S(2)}) collective-permute-start(f32[20,8,128]{2,1,0:T(8,128)S(1)} %get-tuple-element.30), channel_id=1, source_target_pairs={{0,24},{16,8},{24,0},{8,16},{1,25},{17,9},{25,1},{9,17},{2,26},{18... | collective-permute-start | bytes 245768 | tf_op jit(solution)/shard_map/ppermute | solution.py:624
  14.4 0.7 %collective-permute-start.5 = (f32[20,8,128]{2,1,0:T(8,128)S(1)}, f32[20,8,128]{2,1,0:T(8,128)S(1)}, u32[]{:S(2)}, u32[]{:S(2)}) collective-permute-start(f32[20,8,128]{2,1,0:T(8,128)S(1)} %get-tuple-element.31), channel_id=1, source_target_pairs={{0,8},{16,24},{8,0},{24,16},{1,9},{17,25},{9,1},{25,17},{2,10},{18... | collective-permute-start | bytes 245768 | tf_op jit(solution)/shard_map/ppermute | solution.py:624
  15.1 4.9 %all-to-all-done.gathered = f32[32,4,128]{2,1,0:T(4,128)S(1)} async-done(((f32[32,4,128]{2,1,0:T(4,128)}), f32[32,4,128]{2,1,0:T(4,128)S(1)}, u32[]{:S(2)}, u32[]{:S(2)}) %all-to-all-start) | async-done | bytes 65568 | tf_op jit(solution)/shard_map/all_to_all | solution.py:659
  20.1 2.1 %shard_map.50 = (f32[2,4,8,128]{3,2,1,0:T(8,128)S(1)}, f32[10,8,128]{2,1,0:T(8,128)S(1)}, f32[10,8,128]{2,1,0:T(8,128)S(1)}, f32[7,8,128]{2,1,0:T(8,128)S(1)}, f...) custom-call(f32[6,16,8,128]{3,2,1,0:T(8,128)S(1)} %get-tuple-element.24.main, ...), custom_call_target="tpu_custom_call" | custom-call | tf_op jit(solution)/shard_map/pallas_call | solution.py:610
  22.2 2.3 %collective-permute-start.6 = (f32[10,8,128]{2,1,0:T(8,128)S(1)}, f32[10,8,128]{2,1,0:T(8,128)S(1)}, u32[]{:S(2)}, u32[]{:S(2)}) collective-permute-start(f32[10,8,128]{2,1,0:T(8,128)S(1)} %get-tuple-element.33), channel_id=1, source_target_pairs={{0,7},{2,1},{4,3},{6,5},{7,0},{1,2},{3,4},{5,6},{8,15},{10,9},{12,... | collective-permute-start | bytes 122888 | tf_op jit(solution)/shard_map/ppermute | solution.py:624
  24.5 0.2 shard_map.51.coef1
  24.7 4.3 %collective-permute-done.6.first.b_first = f32[10,8,128]{2,1,0:T(8,128)S(1)} collective-permute-done((f32[10,8,128]{2,1,0:T(8,128)S(1)}, f32[10,8,128]{2,1,0:T(8,128)S(1)}, u32[]{:S(2)}, u32[]{:S(2)}) %collective-permute-start.6) | collective-permute-done | bytes 40992 | tf_op jit(solution)/shard_map/ppermute | solution.py:624
  29.0 0.6 %shard_map.52 = (f32[2,8,128]{2,1,0:T(8,128)S(1)}, f32[9,8,128]{2,1,0:T(8,128)S(1)}, f32[9,8,128]{2,1,0:T(8,128)S(1)}, f32[2,2,14,8,128]{4,3,2,1,0:T(8,128)S(1)}) custom-call(f32[2,4,8,128]{3,2,1,0:T(8,128)S(1)} %get-tuple-element.32.own, f32[10,8,128]{2,1,0:T(8,128)S(1)} %collective-permute-done.6.first.b_first, ...), custom_call_target="tpu_custom_call" | custom-call | tf_op jit(solution)/shard_map/pallas_call | solution.py:610
  29.6 2.5 %collective-permute-start.8 = (f32[9,8,128]{2,1,0:T(8,128)S(1)}, f32[9,8,128]{2,1,0:T(8,128)S(1)}, u32[]{:S(2)}, u32[]{:S(2)}) collective-permute-start(f32[9,8,128]{2,1,0:T(8,128)S(1)} %get-tuple-element.39), channel_id=1, source_target_pairs={{0,7},{2,1},{4,3},{6,5},{7,0},{1,2},{3,4},{5,6},{8,15},{10,9},{12,... | collective-permute-start | bytes 110600 | tf_op jit(solution)/shard_map/ppermute | solution.py:624
  32.1 2.8 %collective-permute-start.11 = (f32[2,8,128]{2,1,0:T(8,128)S(1)}, f32[2,8,128]{2,1,0:T(8,128)S(1)}, u32[]{:S(2)}, u32[]{:S(2)}) collective-permute-start(f32[2,8,128]{2,1,0:T(8,128)S(1)} %get-tuple-element.38.own2), channel_id=1, source_target_pairs={{0,6},{1,7},{4,2},{5,3},{6,0},{7,1},{2,4},{3,5},{8,14},{9,15},{12,... | collective-permute-start | bytes 24584 | tf_op jit(solution)/shard_map/ppermute | solution.py:631
  34.9 0.1 shard_map.53.coef2
  35.0 2.5 %collective-permute-done.11.far_b = f32[2,8,128]{2,1,0:T(8,128)S(1)} collective-permute-done((f32[2,8,128]{2,1,0:T(8,128)S(1)}, f32[2,8,128]{2,1,0:T(8,128)S(1)}, u32[]{:S(2)}, u32[]{:S(2)}) %collective-permute-start.11) | collective-permute-done | bytes 8224 | tf_op jit(solution)/shard_map/ppermute | solution.py:631
  37.5 1.0 %collective-permute-done.10.far_a = f32[2,8,128]{2,1,0:T(8,128)S(1)} collective-permute-done((f32[2,8,128]{2,1,0:T(8,128)S(1)}, f32[2,8,128]{2,1,0:T(8,128)S(1)}, u32[]{:S(2)}, u32[]{:S(2)}) %collective-permute-start.10) | collective-permute-done | bytes 8224 | tf_op jit(solution)/shard_map/ppermute | solution.py:631
  38.6 3.2 %shard_map.54 = f32[256,128]{1,0:T(8,128)} custom-call(f32[2,8,128]{2,1,0:T(8,128)S(1)} %get-tuple-element.38.own2, f32[9,8,128]{2,1,0:T(8,128)S(1)} %collective-permute-done.8.near_a, f32[9,8,128]{2,1,0:T(8,128)S(1)} %collective-permute-done.9.near_b, f32[2,8,128]{2,1,0:T(8,128)S(1)} %collective-permute-done.10.far_a, ...), custom_call_target="tpu_custom_call" | custom-call | tf_op jit(solution)/shard_map/pallas_call | solution.py:610
  (11 shorter events, 0.0 us)
Async XLA Ops:
  1.4 11.4 %collective-permute-start = (f32[29,8,128]{2,1,0:T(8,128)S(1)}, f32[29,8,128]{2,1,0:T(8,128)S(1)}, u32[]{:S(2)}, u32[]{:S(2)}) collective-permute-start(f32[29,8,128]{2,1,0:T(8,128)S(1)} %get-tuple-element.25), channel_id=1, source_target_pairs={{0,7},{2,1},{4,3},{6,5},{7,0},{1,2},{3,4},{5,6},{8,15},{10,9},{12,... | collective-permute-start | bytes 356360 | tf_op jit(solution)/shard_map/ppermute | solution.py:624
  7.5 5.8 %collective-permute-start.1 = (f32[29,8,128]{2,1,0:T(8,128)S(1)}, f32[29,8,128]{2,1,0:T(8,128)S(1)}, u32[]{:S(2)}, u32[]{:S(2)}) collective-permute-start(f32[29,8,128]{2,1,0:T(8,128)S(1)} %get-tuple-element.26), channel_id=1, source_target_pairs={{0,1},{2,3},{4,5},{6,7},{1,0},{3,2},{5,4},{7,6},{8,9},{10,11},{12,... | collective-permute-start | bytes 356360 | tf_op jit(solution)/shard_map/ppermute | solution.py:624
  7.7 12.3 %collective-permute-start.2 = (f32[35,8,128]{2,1,0:T(8,128)S(1)}, f32[35,8,128]{2,1,0:T(8,128)S(1)}, u32[]{:S(2)}, u32[]{:S(2)}) collective-permute-start(f32[35,8,128]{2,1,0:T(8,128)S(1)} %get-tuple-element.28), channel_id=1, source_target_pairs={{0,24},{16,8},{24,0},{8,16},{1,25},{17,9},{25,1},{9,17},{2,26},{18... | collective-permute-start | bytes 430088 | tf_op jit(solution)/shard_map/ppermute | solution.py:624
  8.4 11.6 %collective-permute-start.3 = (f32[35,8,128]{2,1,0:T(8,128)S(1)}, f32[35,8,128]{2,1,0:T(8,128)S(1)}, u32[]{:S(2)}, u32[]{:S(2)}) collective-permute-start(f32[35,8,128]{2,1,0:T(8,128)S(1)} %get-tuple-element.29), channel_id=1, source_target_pairs={{0,8},{16,24},{8,0},{24,16},{1,9},{17,25},{9,1},{25,17},{2,10},{18... | collective-permute-start | bytes 430088 | tf_op jit(solution)/shard_map/ppermute | solution.py:624
  10.2 9.9 %all-to-all-start = ((f32[32,4,128]{2,1,0:T(4,128)}), f32[32,4,128]{2,1,0:T(4,128)S(1)}, u32[]{:S(2)}, u32[]{:S(2)}) async-start(f32[32,4,128]{2,1,0:T(4,128)} %shard_map.49), calls=%async_computation | async-start | bytes 131072 | tf_op jit(solution)/shard_map/all_to_all | solution.py:659
  13.4 6.6 %collective-permute-start.4 = (f32[20,8,128]{2,1,0:T(8,128)S(1)}, f32[20,8,128]{2,1,0:T(8,128)S(1)}, u32[]{:S(2)}, u32[]{:S(2)}) collective-permute-start(f32[20,8,128]{2,1,0:T(8,128)S(1)} %get-tuple-element.30), channel_id=1, source_target_pairs={{0,24},{16,8},{24,0},{8,16},{1,25},{17,9},{25,1},{9,17},{2,26},{18... | collective-permute-start | bytes 245768 | tf_op jit(solution)/shard_map/ppermute | solution.py:624
  14.4 5.6 %collective-permute-start.5 = (f32[20,8,128]{2,1,0:T(8,128)S(1)}, f32[20,8,128]{2,1,0:T(8,128)S(1)}, u32[]{:S(2)}, u32[]{:S(2)}) collective-permute-start(f32[20,8,128]{2,1,0:T(8,128)S(1)} %get-tuple-element.31), channel_id=1, source_target_pairs={{0,8},{16,24},{8,0},{24,16},{1,9},{17,25},{9,1},{25,17},{2,10},{18... | collective-permute-start | bytes 245768 | tf_op jit(solution)/shard_map/ppermute | solution.py:624
  22.2 6.8 %collective-permute-start.6 = (f32[10,8,128]{2,1,0:T(8,128)S(1)}, f32[10,8,128]{2,1,0:T(8,128)S(1)}, u32[]{:S(2)}, u32[]{:S(2)}) collective-permute-start(f32[10,8,128]{2,1,0:T(8,128)S(1)} %get-tuple-element.33), channel_id=1, source_target_pairs={{0,7},{2,1},{4,3},{6,5},{7,0},{1,2},{3,4},{5,6},{8,15},{10,9},{12,... | collective-permute-start | bytes 122888 | tf_op jit(solution)/shard_map/ppermute | solution.py:624
  24.5 4.5 %collective-permute-start.7 = (f32[10,8,128]{2,1,0:T(8,128)S(1)}, f32[10,8,128]{2,1,0:T(8,128)S(1)}, u32[]{:S(2)}, u32[]{:S(2)}) collective-permute-start(f32[10,8,128]{2,1,0:T(8,128)S(1)} %get-tuple-element.34), channel_id=1, source_target_pairs={{0,1},{2,3},{4,5},{6,7},{1,0},{3,2},{5,4},{7,6},{8,9},{10,11},{12,... | collective-permute-start | bytes 122888 | tf_op jit(solution)/shard_map/ppermute | solution.py:624
  29.6 9.0 %collective-permute-start.8 = (f32[9,8,128]{2,1,0:T(8,128)S(1)}, f32[9,8,128]{2,1,0:T(8,128)S(1)}, u32[]{:S(2)}, u32[]{:S(2)}) collective-permute-start(f32[9,8,128]{2,1,0:T(8,128)S(1)} %get-tuple-element.39), channel_id=1, source_target_pairs={{0,7},{2,1},{4,3},{6,5},{7,0},{1,2},{3,4},{5,6},{8,15},{10,9},{12,... | collective-permute-start | bytes 110600 | tf_op jit(solution)/shard_map/ppermute | solution.py:624
  32.1 6.5 %collective-permute-start.9 = (f32[9,8,128]{2,1,0:T(8,128)S(1)}, f32[9,8,128]{2,1,0:T(8,128)S(1)}, u32[]{:S(2)}, u32[]{:S(2)}) collective-permute-start(f32[9,8,128]{2,1,0:T(8,128)S(1)} %get-tuple-element.40), channel_id=1, source_target_pairs={{0,1},{2,3},{4,5},{6,7},{1,0},{3,2},{5,4},{7,6},{8,9},{10,11},{12,... | collective-permute-start | bytes 110600 | tf_op jit(solution)/shard_map/ppermute | solution.py:624
  32.1 5.4 %collective-permute-start.11 = (f32[2,8,128]{2,1,0:T(8,128)S(1)}, f32[2,8,128]{2,1,0:T(8,128)S(1)}, u32[]{:S(2)}, u32[]{:S(2)}) collective-permute-start(f32[2,8,128]{2,1,0:T(8,128)S(1)} %get-tuple-element.38.own2), channel_id=1, source_target_pairs={{0,6},{1,7},{4,2},{5,3},{6,0},{7,1},{2,4},{3,5},{8,14},{9,15},{12,... | collective-permute-start | bytes 24584 | tf_op jit(solution)/shard_map/ppermute | solution.py:631
  34.9 3.7 %collective-permute-start.10 = (f32[2,8,128]{2,1,0:T(8,128)S(1)}, f32[2,8,128]{2,1,0:T(8,128)S(1)}, u32[]{:S(2)}, u32[]{:S(2)}) collective-permute-start(f32[2,8,128]{2,1,0:T(8,128)S(1)} %get-tuple-element.38.own2), channel_id=1, source_target_pairs={{0,2},{1,3},{4,6},{5,7},{2,0},{3,1},{6,4},{7,5},{8,10},{9,11},{12,... | collective-permute-start | bytes 24584 | tf_op jit(solution)/shard_map/ppermute | solution.py:631

commit v3 on v2

--- a/solution.py
+++ b/solution.py
@@ -117,25 +117,23 @@
         target[1, t, rows] = v[t] + dv
 
 
-def residual(level, keep, diag, source, r, n):
-    scale = 0.25**level
-    k = 1 << level
-    u, nb_u = neighbour_sums(lambda t, a, m: source[0, t, pl.ds(a, m)], r, n, k)
-    v, nb_v = neighbour_sums(lambda t, a, m: source[1, t, pl.ds(a, m)], r, n, k)
+def next_power(keep, source, r, n):
+    u, nb_u = neighbour_sums(lambda t, a, m: source[0, t, pl.ds(a, m)], r, n, 1)
+    v, nb_v = neighbour_sums(lambda t, a, m: source[1, t, pl.ds(a, m)], r, n, 1)
     rows = pl.ds(r, n)
     first, second = [], []
     for t in (0, 1):
-        first.append(
-            keep[4, t, rows] - diag[0, t, rows] * u[t] - keep[0, t, rows] * v[t] + DIFF[0] * scale * nb_u[t]
-        )
-        second.append(
-            keep[5, t, rows] - diag[1, t, rows] * v[t] + keep[1, t, rows] * u[t] + DIFF[1] * scale * nb_v[t]
-        )
+        cross, squared, inv_u, inv_v = (keep[i, t, rows] for i in range(4))
+        first.append(u[t] + inv_u * (cross * v[t] - DIFF[0] * nb_u[t]))
+        second.append(v[t] - inv_v * (squared * u[t] + DIFF[1] * nb_v[t]))
     return first, second
 
 
 CARRY1 = _RHO1 * _RHO0
 CARRY2 = _RHO2 * _RHO1
+
+
+POWERS = 9
 
 
 def write_gains(spread, out):
@@ -145,6 +143,11 @@
         tau = 1.0 / (1.0 + jnp.broadcast_to(top, (Z, X)))
         for i, factor in enumerate((1.0 / _CENTRE, 2.0 * _RHO1 / _HALF, 2.0 * _RHO2 / _HALF)):
             out[3 * level + i] = factor * tau
+    g0, g1, g2 = (out[i] for i in range(3))
+    first, second = g0 + CARRY1 * g0 + g1, g1 * g0
+    out[POWERS] = first + CARRY2 * (CARRY1 * g0 + g1) + g2
+    out[POWERS + 1] = second + CARRY2 * second + g2 * first
+    out[POWERS + 2] = g2 * second
 
 
 def pair_rows(value):
@@ -376,14 +379,11 @@
 
 
 def level0_kernel(
-    rows, main, y_first, y_second, own_a, own_b, corner_a, corner_b, gathered, own, first, second, edge_first, edge_second, keep, gain_out, fields, other, d, diag
+    rows, main, y_first, y_second, own_a, own_b, corner_a, corner_b, keep, powers, sources, fields, diag
 ):
     even, even_x = is_even("gy"), is_even("gx")
     total = rows + 2 * HALO0
     own_x, corner_x = (own_a, own_b), (corner_a, corner_b)
-    top = jnp.max(gathered[...], axis=0)
-    write_gains(top[0:1], gain_out)
-    g0, g1, g2 = (gain_out[i] for i in range(3))
     for i, halo in enumerate(HALOS):
         strip = slice(STARTS[i], STARTS[i] + halo)
         skip = HALO0 - halo
@@ -397,7 +397,6 @@
         ):
             for a, b, value in halo_tiles(even_x, packets, lo, lo + n):
                 fields[i, 1, at + a : at + b] = value
-    here = keep.at[6:8]
 
     def setup(r, n):
         at = pl.ds(r, n)
@@ -420,54 +419,60 @@
                 keep[i, t, at] = value
             diag[0, t, at] = first
             diag[1, t, at] = second
-            for i, value in enumerate((g0 * inv_u * b_u, g0 * inv_v * b_v)):
-                d[i, t, at] = value
-                keep[6 + i, t, at] = value
+            powers[0, 0, t, at] = inv_u * b_u
+            powers[0, 1, t, at] = inv_v * b_v
 
     rows_loop(1, total - 1, setup)
-    rows_loop(2, total - 2, lambda r, n: cheb_step(0, keep, here, other, d, r, n, CARRY1, g1))
-    rows_loop(3, total - 3, lambda r, n: cheb_step(0, keep, other, here, d, r, n, CARRY2, g2))
+    for p in (0, 1):
+
+        def power(r, n, p=p):
+            for i, values in enumerate(next_power(keep, powers.at[p], r, n)):
+                for t in (0, 1):
+                    powers[p + 1, i, t, pl.ds(r, n)] = values[t]
+
+        rows_loop(2 + p, total - 2 - p, power)
 
     def down(r, n):
-        res = residual(0, keep, diag, here, r, n)
+        at = pl.ds(r, n)
+        last = next_power(keep, powers.at[2], r, n)
         for t in (0, 1):
-            u, v = pair_rows(res[0][t]), pair_rows(res[1][t])
-            for j in range(n // 4):
-                value = restrict_01(u[2 * j : 2 * j + 2], v[2 * j : 2 * j + 2])
-                for ref, at in ((own.at[t], 0), (first, t * OWN), (second, t * OWN)):
-                    ref[pl.ds(at + (r - HALO0) // 4 + j, 1)] = value
+            both = [diag[i, t, at] for i in (0, 1)]
+            parts = [[keep[4 + i, t, at] for i in (0, 1)]]
+            parts += [[both[i] * powers[p, i, t, at] for i in (0, 1)] for p in (1, 2)]
+            parts.append([both[i] * last[i][t] for i in (0, 1)])
+            for q, part in enumerate(parts):
+                u, v = (pair_rows(value) for value in part)
+                for j in range(n // 4):
+                    value = restrict_01(u[2 * j : 2 * j + 2], v[2 * j : 2 * j + 2])
+                    sources[q, t, pl.ds((r - HALO0) // 4 + j, 1)] = value
 
     rows_loop(HALO0, HALO0 + rows, down, 8)
 
-    lane = lane_of()
-    edges = []
-    for start in (HALO0, HALO0 + rows - EDGE):
-        halo = None
-        for i in (0, 1):
-            for j in range(EDGE):
-                at = i * EDGE + j
-                value = roll_x(keep[6 + i, 1, start + j : start + j + 1], 4 + 8 * at)
-                halo = value if halo is None else jnp.where((lane >> 3) == at, value, halo)
-        edges.append([keep[6, 0, start : start + EDGE], keep[7, 0, start : start + EDGE], halo])
-    top, bottom = (jnp.concatenate(parts, axis=0) for parts in edges)
+
+def combine_kernel(sources, y_first, y_second, corner_a, corner_b, spread, own, first, second, gain):
+    even, even_x = is_even("gy"), is_even("gx")
+    write_gains(jnp.max(spread[...], axis=0)[0:1], gain)
+    p0, p1, p2 = (gain[POWERS + i] for i in range(3))
+    for t in (0, 1):
+        value = sources[0, t] - p0 * sources[1, t] + p1 * sources[2, t] - p2 * sources[3, t]
+        own[t] = value
+        for ref in (first, second):
+            ref[t * OWN : (t + 1) * OWN] = value
     strip = slice(FIELDS2, FIELDS2 + 1)
     for t in (0, 1):
         if t == 0:
             before, after = prev_of(even, y_first, y_second, strip), next_of(even, y_first, y_second, strip)
         else:
             before, after = (
-                halo_tiles(even_x, corner_x, at + FIELDS2, at + FIELDS2 + 1)[0][2] for at in (0, PACKET)
+                halo_tiles(even_x, (corner_a, corner_b), at + FIELDS2, at + FIELDS2 + 1)[0][2] for at in (0, PACKET)
             )
         first[FAR + t : FAR + t + 1] = jnp.where(even, after, before)
         second[FAR + t : FAR + t + 1] = jnp.where(even, before, after)
-    edge_first[...] = jnp.where(even, top, bottom)
-    edge_second[...] = jnp.where(even, bottom, top)
 
 
 def coarse1_kernel(
-    rows, coarse, y_first, y_second, own_a, own_b, corner_a, corner_b, gain, coef, fields
+    rows, coarse, y_first, y_second, own_a, own_b, corner_a, corner_b, gain, powers, coef, x0, edge_first, edge_second, fields
 ):
-    del gain
     even, even_x = is_even("gy"), is_even("gx")
     own_x, corner_x = (own_a, own_b), (corner_a, corner_b)
     for p in (0, 1):
@@ -485,6 +490,25 @@
     for t in (0, 1):
         for i, value in enumerate(packed_jacobian(fields[t, 0:GROUPS1], fields[t, GROUPS1 : 2 * GROUPS1], 1)):
             coef[i, t, 1 : SIZE1 - 1] = value
+
+    p0, p1, p2 = (gain[POWERS + i] for i in range(3))
+    for i in (0, 1):
+        for t in (0, 1):
+            y0, y1, y2 = (powers[p, i, t, HALO0 : HALO0 + rows] for p in range(3))
+            x0[i, t] = p0 * y0 - p1 * y1 + p2 * y2
+    lane = lane_of()
+    edges = []
+    for start in (0, rows - EDGE):
+        halo = None
+        for i in (0, 1):
+            for j in range(EDGE):
+                at = i * EDGE + j
+                value = roll_x(x0[i, 1, start + j : start + j + 1], 4 + 8 * at)
+                halo = value if halo is None else jnp.where((lane >> 3) == at, value, halo)
+        edges.append([x0[0, 0, start : start + EDGE], x0[1, 0, start : start + EDGE], halo])
+    top, bottom = (jnp.concatenate(parts, axis=0) for parts in edges)
+    edge_first[...] = jnp.where(even, top, bottom)
+    edge_second[...] = jnp.where(even, bottom, top)
 
 
 def coarse2_kernel(
@@ -536,7 +560,7 @@
 
 
 def rest_kernel(
-    own2, near_a, near_b, far_a, far_b, gain, coef1, coef2, keep0, keep1, out, d1, b2, x2, y2, d2, xu, yu, x0, y0, d0
+    own2, near_a, near_b, far_a, far_b, gain, coef1, coef2, keep0, iterate, keep1, out, d1, b2, x2, y2, d2, xu, yu, x0, y0, d0
 ):
     rows = out.shape[0] // (2 * Z)
     even = (sub_of() & 1) == 0
@@ -587,7 +611,7 @@
             for j in range(EDGE):
                 x0[i, 1, at + j : at + j + 1] = roll_x(sides, -(4 + 8 * (i * EDGE + j)))
         for t in (0, 1):
-            x0[i, t, HALO0 : HALO0 + rows] = keep0[6 + i, t, HALO0 : HALO0 + rows]
+            x0[i, t, HALO0 : HALO0 + rows] = iterate[i, t]
     for t in (0, 1):
         for row in range(-2, rows // 2 + 2):
             at = row // 2 - LO_UP + 1
@@ -676,25 +700,34 @@
 
     strip, edge = (FAR + 2, Z, X), (EDGE_TILES, Z, X)
     pair0 = (2, 2, total0, Z, X)
-    own, first, second, edge_a, edge_b, keep0, gain = call(
+    keep0, powers, sources = call(
         functools.partial(level0_kernel, rows),
-        [(2, OWN, Z, X), strip, strip, edge, edge, (8, 2, total0, Z, X), (9, Z, X)],
-        [(6, 2, total0, Z, X), pair0, pair0, pair0],
+        [(6, 2, total0, Z, X), (3, *pair0), (4, 2, OWN, Z, X)],
+        [(6, 2, total0, Z, X), pair0],
         main,
         *y_packets,
         *own_x,
         *corner_x,
+    )
+    own, first, second, gain = call(
+        combine_kernel,
+        [(2, OWN, Z, X), strip, strip, (POWERS + 3, Z, X)],
+        [],
+        sources,
+        *y_packets,
+        *corner_x,
         spread,
     )
-    (coef1,) = call(
+    coef1, iterate, edge_a, edge_b = call(
         functools.partial(coarse1_kernel, rows),
-        [(3, 2, SIZE1, Z, X)],
+        [(3, 2, SIZE1, Z, X), (2, 2, rows, Z, X), edge, edge],
         [(2, 2 * GROUPS1, Z, X)],
         coarse,
         *y_packets,
         *own_x,
         *corner_x,
         gain,
+        powers,
     )
     b_packets = exchange(first, second, "gy")
 
@@ -735,6 +768,7 @@
         coef1,
         coef2,
         keep0,
+        iterate,
         keep1,
     )
     return out.reshape(2, Z, rows, X)

time: 41.9 us -> 42.9 us (1.024)
  waiting for transfers between devices: 13.3 us -> 11.3 us
  local copies, waits for them, and re-layouts: 0 us -> 1.55 us
  starting transfers between devices: 19.6 us -> 21.1 us
    all_to_all x1, waiting for transfers between devices: 4.94 us -> 0.01 us  [body(): spread = lax.all_to_all(spread, ('gx', 'gy'), 0, 0, tiled=True)]
    ppermute x10, waiting for transfers between devices: 4.82 us -> 7.74 us  [swap(): return lax.ppermute(value, axis, pairs + [(j, i) for i, j in pairs])]
    ppermute x10, starting transfers between devices: 14.2 us -> 16 us  [swap(): return lax.ppermute(value, axis, pairs + [(j, i) for i, j in pairs])]
    unnamed x0 -> x4, local copies, waits for them, and re-layouts: none -> 1.55 us
    pallas_call x9 -> x10, Pallas kernels: 8.73 us -> 8.62 us  [call(): pl.pallas_call(kernel, out_shape=out, in_specs=[pl.BlockSpec(memory_space...]
  transfers between devices with their start and end apart: 13 -> 13, of which waited for: 5 -> 6; matrix products, arithmetic and copies ran while one was open for 0% -> 0% of each run, Pallas kernels for 4% -> 8%
where the time goes in v3:
time: 42.9 us; the launch traced here: 42.7 us
  starting transfers between devices  21.1 us (49%)
  waiting for transfers between devices  11.3 us (26%)
  Pallas kernels  8.62 us (20%)
  local copies, waits for them, and re-layouts  1.55 us (4%)
    ppermute x10, starting transfers between devices, swap(): return lax.ppermute(value, axis, pairs + [(j, i) for i, j in pairs])  16 us
    pallas_call x10, Pallas kernels, call(): pl.pallas_call(kernel, out_shape=out, in_specs=[pl.BlockSpec(memory_space...  8.62 us
    ppermute x10, waiting for transfers between devices, swap(): return lax.ppermute(value, axis, pairs + [(j, i) for i, j in pairs])  7.74 us
    ppermute x2, waiting for transfers between devices, swap_far(): return lax.ppermute(value, axis, pairs + [(j, i) for i, j in pairs])  3.55 us
    ppermute x2, starting transfers between devices, swap_far(): return lax.ppermute(value, axis, pairs + [(j, i) for i, j in pairs])  2.59 us
    all_to_all x1, starting transfers between devices, body(): spread = lax.all_to_all(spread, ('gx', 'gy'), 0, 0, tiled=True)  2.55 us
    unnamed x4, local copies, waits for them, and re-layouts  1.55 us
  transfers between devices with their start and end apart: 13, of which 6 were waited for; matrix products, arithmetic and copies ran while one was open for 0% of the time, Pallas kernels for 8%

profile of v3, /device:TPU:0, one launch (start us, length us, event | category | flops | bytes accessed | tf_op | source)
XLA Modules:
  0.0 42.7 jit_solution(4033525055657012693)
XLA Ops:
  0.0 1.4 %shard_map.46 = (f32[29,8,128]{2,1,0:T(8,128)S(1)}, f32[29,8,128]{2,1,0:T(8,128)S(1)}, f32[6,16,8,128]{3,2,1,0:T(8,128)S(1)}, f32[9,8,128]{2,1,0:T(8,128)S(1)}) custom-call(f32[256,128]{1,0:T(8,128)} %bitcast.5, f32[256,128]{1,0:T(8,128)} %bitcast.6, f32[128,128]{1,0:T(8,128)} %bitcast.7, f32[128,128]{1,0:T(8,128)} %bitcast.8), custom_call_target="tpu_custom_call" | custom-call | tf_op jit(solution)/shard_map/pallas_call | solution.py:634
  1.4 6.1 %collective-permute-start = (f32[29,8,128]{2,1,0:T(8,128)S(1)}, f32[29,8,128]{2,1,0:T(8,128)S(1)}, u32[]{:S(2)}, u32[]{:S(2)}) collective-permute-start(f32[29,8,128]{2,1,0:T(8,128)S(1)} %get-tuple-element.29), channel_id=1, source_target_pairs={{0,7},{2,1},{4,3},{6,5},{7,0},{1,2},{3,4},{5,6},{8,15},{10,9},{12,... | collective-permute-start | bytes 356360 | tf_op jit(solution)/shard_map/ppermute | solution.py:648
  7.5 0.2 shard_map.47
  7.7 0.7 %collective-permute-start.2 = (f32[35,8,128]{2,1,0:T(8,128)S(1)}, f32[35,8,128]{2,1,0:T(8,128)S(1)}, u32[]{:S(2)}, u32[]{:S(2)}) collective-permute-start(f32[35,8,128]{2,1,0:T(8,128)S(1)} %get-tuple-element.32), channel_id=1, source_target_pairs={{0,24},{16,8},{24,0},{8,16},{1,25},{17,9},{25,1},{9,17},{2,26},{18... | collective-permute-start | bytes 430088 | tf_op jit(solution)/shard_map/ppermute | solution.py:648
  8.4 1.0 %collective-permute-start.3 = (f32[35,8,128]{2,1,0:T(8,128)S(1)}, f32[35,8,128]{2,1,0:T(8,128)S(1)}, u32[]{:S(2)}, u32[]{:S(2)}) collective-permute-start(f32[35,8,128]{2,1,0:T(8,128)S(1)} %get-tuple-element.33), channel_id=1, source_target_pairs={{0,8},{16,24},{8,0},{24,16},{1,9},{17,25},{9,1},{25,17},{2,10},{18... | collective-permute-start | bytes 430088 | tf_op jit(solution)/shard_map/ppermute | solution.py:648
  9.4 0.8 %shard_map.50 = f32[32,4,128]{2,1,0:T(4,128)} custom-call(f32[6,16,8,128]{3,2,1,0:T(8,128)S(1)} %get-tuple-element.28.main, f32[9,8,128]{2,1,0:T(8,128)S(1)} %get-tuple-element.31.coarse), custom_call_target="tpu_custom_call" | custom-call | tf_op jit(solution)/shard_map/pallas_call | solution.py:634
  10.2 2.6 %all-to-all-start = ((f32[32,4,128]{2,1,0:T(4,128)}), f32[32,4,128]{2,1,0:T(4,128)S(1)}, u32[]{:S(2)}, u32[]{:S(2)}) async-start(f32[32,4,128]{2,1,0:T(4,128)} %shard_map.50), calls=%async_computation | async-start | bytes 131072 | tf_op jit(solution)/shard_map/all_to_all | solution.py:683
  12.7 0.5 %collective-permute-done.1.y_second = f32[29,8,128]{2,1,0:T(8,128)S(1)} collective-permute-done((f32[29,8,128]{2,1,0:T(8,128)S(1)}, f32[29,8,128]{2,1,0:T(8,128)S(1)}, u32[]{:S(2)}, u32[]{:S(2)}) %collective-permute-start.1) | collective-permute-done | bytes 118816 | tf_op jit(solution)/shard_map/ppermute | solution.py:648
  13.2 0.2 shard_map.48
  13.4 1.0 %collective-permute-start.4 = (f32[20,8,128]{2,1,0:T(8,128)S(1)}, f32[20,8,128]{2,1,0:T(8,128)S(1)}, u32[]{:S(2)}, u32[]{:S(2)}) collective-permute-start(f32[20,8,128]{2,1,0:T(8,128)S(1)} %get-tuple-element.34), channel_id=1, source_target_pairs={{0,24},{16,8},{24,0},{8,16},{1,25},{17,9},{25,1},{9,17},{2,26},{18... | collective-permute-start | bytes 245768 | tf_op jit(solution)/shard_map/ppermute | solution.py:648
  14.4 0.7 %collective-permute-start.5 = (f32[20,8,128]{2,1,0:T(8,128)S(1)}, f32[20,8,128]{2,1,0:T(8,128)S(1)}, u32[]{:S(2)}, u32[]{:S(2)}) collective-permute-start(f32[20,8,128]{2,1,0:T(8,128)S(1)} %get-tuple-element.35), channel_id=1, source_target_pairs={{0,8},{16,24},{8,0},{24,16},{1,9},{17,25},{9,1},{25,17},{2,10},{18... | collective-permute-start | bytes 245768 | tf_op jit(solution)/shard_map/ppermute | solution.py:648
  15.1 3.4 %collective-permute-done.4.corner_a = f32[20,8,128]{2,1,0:T(8,128)S(1)} collective-permute-done((f32[20,8,128]{2,1,0:T(8,128)S(1)}, f32[20,8,128]{2,1,0:T(8,128)S(1)}, u32[]{:S(2)}, u32[]{:S(2)}) %collective-permute-start.4) | collective-permute-done | bytes 81952 | tf_op jit(solution)/shard_map/ppermute | solution.py:648
  18.5 2.0 %shard_map.49 = (f32[6,2,24,8,128]{4,3,2,1,0:T(8,128)S(1)}, f32[3,2,2,24,8,128]{5,4,3,2,1,0:T(8,128)S(1)}, f32[4,2,4,8,128]{4,3,2,1,0:T(8,128)S(1)}) custom-call(f32[6,16,8,128]{3,2,1,0:T(8,128)S(1)} %get-tuple-element.28.main, f32[29,8,128]{2,1,0:T(8,128)S(1)} %collective-permute-done.y_first, f32[29,8,128]{2,1,0:T(8,128)S(1)} %collective-permute-done.1.y_second, ...), custom_call_target="tpu_custom_call" | custom-call | tf_op jit(solution)/shard_map/pallas_call | solution.py:634
  20.5 0.6 %copy-done = f32[4,2,4,8,128]{4,3,2,1,0:T(8,128)} copy-done((f32[4,2,4,8,128]{4,3,2,1,0:T(8,128)}, f32[4,2,4,8,128]{4,3,2,1,0:T(8,128)S(1)}, u32[]{:S(2)}) %copy-start) | copy-done | bytes 131096
  21.2 0.9 %copy-done.1 = f32[4,2,4,8,128]{4,3,2,1,0:T(8,128)S(1)} copy-done((f32[4,2,4,8,128]{4,3,2,1,0:T(8,128)S(1)}, f32[4,2,4,8,128]{4,3,2,1,0:T(8,128)}, u32[]{:S(2)}) %copy-start.1) | copy-done | bytes 131096
  22.2 3.8 %collective-permute-start.6 = (f32[10,8,128]{2,1,0:T(8,128)S(1)}, f32[10,8,128]{2,1,0:T(8,128)S(1)}, u32[]{:S(2)}, u32[]{:S(2)}) collective-permute-start(f32[10,8,128]{2,1,0:T(8,128)S(1)} %get-tuple-element.38), channel_id=1, source_target_pairs={{0,7},{2,1},{4,3},{6,5},{7,0},{1,2},{3,4},{5,6},{8,15},{10,9},{12,... | collective-permute-start | bytes 122888 | tf_op jit(solution)/shard_map/ppermute | solution.py:648
  26.2 2.9 %collective-permute-done.6.first.b_first = f32[10,8,128]{2,1,0:T(8,128)S(1)} collective-permute-done((f32[10,8,128]{2,1,0:T(8,128)S(1)}, f32[10,8,128]{2,1,0:T(8,128)S(1)}, u32[]{:S(2)}, u32[]{:S(2)}) %collective-permute-start.6) | collective-permute-done | bytes 40992 | tf_op jit(solution)/shard_map/ppermute | solution.py:648
  29.1 0.9 %collective-permute-done.7.second.b_second = f32[10,8,128]{2,1,0:T(8,128)S(1)} collective-permute-done((f32[10,8,128]{2,1,0:T(8,128)S(1)}, f32[10,8,128]{2,1,0:T(8,128)S(1)}, u32[]{:S(2)}, u32[]{:S(2)}) %collective-permute-start.7) | collective-permute-done | bytes 40992 | tf_op jit(solution)/shard_map/ppermute | solution.py:648
  30.0 0.6 %shard_map.53 = (f32[2,8,128]{2,1,0:T(8,128)S(1)}, f32[9,8,128]{2,1,0:T(8,128)S(1)}, f32[9,8,128]{2,1,0:T(8,128)S(1)}, f32[2,2,14,8,128]{4,3,2,1,0:T(8,128)S(1)}) custom-call(f32[2,4,8,128]{3,2,1,0:T(8,128)S(1)} %get-tuple-element.37.own, f32[10,8,128]{2,1,0:T(8,128)S(1)} %collective-permute-done.6.first.b_first, ...), custom_call_target="tpu_custom_call" | custom-call | tf_op jit(solution)/shard_map/pallas_call | solution.py:634
  30.6 2.8 %collective-permute-start.8 = (f32[9,8,128]{2,1,0:T(8,128)S(1)}, f32[9,8,128]{2,1,0:T(8,128)S(1)}, u32[]{:S(2)}, u32[]{:S(2)}) collective-permute-start(f32[9,8,128]{2,1,0:T(8,128)S(1)} %get-tuple-element.46), channel_id=1, source_target_pairs={{0,7},{2,1},{4,3},{6,5},{7,0},{1,2},{3,4},{5,6},{8,15},{10,9},{12,... | collective-permute-start | bytes 110600 | tf_op jit(solution)/shard_map/ppermute | solution.py:648
  33.3 2.6 %collective-permute-start.11 = (f32[2,8,128]{2,1,0:T(8,128)S(1)}, f32[2,8,128]{2,1,0:T(8,128)S(1)}, u32[]{:S(2)}, u32[]{:S(2)}) collective-permute-start(f32[2,8,128]{2,1,0:T(8,128)S(1)} %get-tuple-element.45.own2), channel_id=1, source_target_pairs={{0,6},{1,7},{4,2},{5,3},{6,0},{7,1},{2,4},{3,5},{8,14},{9,15},{12,... | collective-permute-start | bytes 24584 | tf_op jit(solution)/shard_map/ppermute | solution.py:655
  36.0 2.8 %collective-permute-done.11.far_b = f32[2,8,128]{2,1,0:T(8,128)S(1)} collective-permute-done((f32[2,8,128]{2,1,0:T(8,128)S(1)}, f32[2,8,128]{2,1,0:T(8,128)S(1)}, u32[]{:S(2)}, u32[]{:S(2)}) %collective-permute-start.11) | collective-permute-done | bytes 8224 | tf_op jit(solution)/shard_map/ppermute | solution.py:655
  38.8 0.8 %collective-permute-done.10.far_a = f32[2,8,128]{2,1,0:T(8,128)S(1)} collective-permute-done((f32[2,8,128]{2,1,0:T(8,128)S(1)}, f32[2,8,128]{2,1,0:T(8,128)S(1)}, u32[]{:S(2)}, u32[]{:S(2)}) %collective-permute-start.10) | collective-permute-done | bytes 8224 | tf_op jit(solution)/shard_map/ppermute | solution.py:655
  39.6 3.1 %shard_map.55 = f32[256,128]{1,0:T(8,128)} custom-call(f32[2,8,128]{2,1,0:T(8,128)S(1)} %get-tuple-element.45.own2, f32[9,8,128]{2,1,0:T(8,128)S(1)} %collective-permute-done.8.near_a, f32[9,8,128]{2,1,0:T(8,128)S(1)} %collective-permute-done.9.near_b, f32[2,8,128]{2,1,0:T(8,128)S(1)} %collective-permute-done.10.far_a, ...), custom_call_target="tpu_custom_call" | custom-call | tf_op jit(solution)/shard_map/pallas_call | solution.py:634
  (16 shorter events, 0.4 us)
Async XLA Ops:
  1.4 11.4 %collective-permute-start = (f32[29,8,128]{2,1,0:T(8,128)S(1)}, f32[29,8,128]{2,1,0:T(8,128)S(1)}, u32[]{:S(2)}, u32[]{:S(2)}) collective-permute-start(f32[29,8,128]{2,1,0:T(8,128)S(1)} %get-tuple-element.29), channel_id=1, source_target_pairs={{0,7},{2,1},{4,3},{6,5},{7,0},{1,2},{3,4},{5,6},{8,15},{10,9},{12,... | collective-permute-start | bytes 356360 | tf_op jit(solution)/shard_map/ppermute | solution.py:648
  7.5 5.8 %collective-permute-start.1 = (f32[29,8,128]{2,1,0:T(8,128)S(1)}, f32[29,8,128]{2,1,0:T(8,128)S(1)}, u32[]{:S(2)}, u32[]{:S(2)}) collective-permute-start(f32[29,8,128]{2,1,0:T(8,128)S(1)} %get-tuple-element.30), channel_id=1, source_target_pairs={{0,1},{2,3},{4,5},{6,7},{1,0},{3,2},{5,4},{7,6},{8,9},{10,11},{12,... | collective-permute-start | bytes 356360 | tf_op jit(solution)/shard_map/ppermute | solution.py:648
  7.7 7.4 %collective-permute-start.2 = (f32[35,8,128]{2,1,0:T(8,128)S(1)}, f32[35,8,128]{2,1,0:T(8,128)S(1)}, u32[]{:S(2)}, u32[]{:S(2)}) collective-permute-start(f32[35,8,128]{2,1,0:T(8,128)S(1)} %get-tuple-element.32), channel_id=1, source_target_pairs={{0,24},{16,8},{24,0},{8,16},{1,25},{17,9},{25,1},{9,17},{2,26},{18... | collective-permute-start | bytes 430088 | tf_op jit(solution)/shard_map/ppermute | solution.py:648
  8.4 6.7 %collective-permute-start.3 = (f32[35,8,128]{2,1,0:T(8,128)S(1)}, f32[35,8,128]{2,1,0:T(8,128)S(1)}, u32[]{:S(2)}, u32[]{:S(2)}) collective-permute-start(f32[35,8,128]{2,1,0:T(8,128)S(1)} %get-tuple-element.33), channel_id=1, source_target_pairs={{0,8},{16,24},{8,0},{24,16},{1,9},{17,25},{9,1},{25,17},{2,10},{18... | collective-permute-start | bytes 430088 | tf_op jit(solution)/shard_map/ppermute | solution.py:648
  10.2 11.0 %all-to-all-start = ((f32[32,4,128]{2,1,0:T(4,128)}), f32[32,4,128]{2,1,0:T(4,128)S(1)}, u32[]{:S(2)}, u32[]{:S(2)}) async-start(f32[32,4,128]{2,1,0:T(4,128)} %shard_map.50), calls=%async_computation | async-start | bytes 131072 | tf_op jit(solution)/shard_map/all_to_all | solution.py:683
  13.4 5.1 %collective-permute-start.4 = (f32[20,8,128]{2,1,0:T(8,128)S(1)}, f32[20,8,128]{2,1,0:T(8,128)S(1)}, u32[]{:S(2)}, u32[]{:S(2)}) collective-permute-start(f32[20,8,128]{2,1,0:T(8,128)S(1)} %get-tuple-element.34), channel_id=1, source_target_pairs={{0,24},{16,8},{24,0},{8,16},{1,25},{17,9},{25,1},{9,17},{2,26},{18... | collective-permute-start | bytes 245768 | tf_op jit(solution)/shard_map/ppermute | solution.py:648
  14.4 4.1 %collective-permute-start.5 = (f32[20,8,128]{2,1,0:T(8,128)S(1)}, f32[20,8,128]{2,1,0:T(8,128)S(1)}, u32[]{:S(2)}, u32[]{:S(2)}) collective-permute-start(f32[20,8,128]{2,1,0:T(8,128)S(1)} %get-tuple-element.35), channel_id=1, source_target_pairs={{0,8},{16,24},{8,0},{24,16},{1,9},{17,25},{9,1},{25,17},{2,10},{18... | collective-permute-start | bytes 245768 | tf_op jit(solution)/shard_map/ppermute | solution.py:648
  20.5 0.7 %copy-start = (f32[4,2,4,8,128]{4,3,2,1,0:T(8,128)}, f32[4,2,4,8,128]{4,3,2,1,0:T(8,128)S(1)}, u32[]{:S(2)}) copy-start(f32[4,2,4,8,128]{4,3,2,1,0:T(8,128)S(1)} %get-tuple-element.36.sources) | copy-start | bytes 393220
  21.2 0.9 %copy-start.1 = (f32[4,2,4,8,128]{4,3,2,1,0:T(8,128)S(1)}, f32[4,2,4,8,128]{4,3,2,1,0:T(8,128)}, u32[]{:S(2)}) copy-start(f32[4,2,4,8,128]{4,3,2,1,0:T(8,128)} %copy-done) | copy-start | bytes 393220
  22.2 6.9 %collective-permute-start.6 = (f32[10,8,128]{2,1,0:T(8,128)S(1)}, f32[10,8,128]{2,1,0:T(8,128)S(1)}, u32[]{:S(2)}, u32[]{:S(2)}) collective-permute-start(f32[10,8,128]{2,1,0:T(8,128)S(1)} %get-tuple-element.38), channel_id=1, source_target_pairs={{0,7},{2,1},{4,3},{6,5},{7,0},{1,2},{3,4},{5,6},{8,15},{10,9},{12,... | collective-permute-start | bytes 122888 | tf_op jit(solution)/shard_map/ppermute | solution.py:648
  26.0 4.0 %collective-permute-start.7 = (f32[10,8,128]{2,1,0:T(8,128)S(1)}, f32[10,8,128]{2,1,0:T(8,128)S(1)}, u32[]{:S(2)}, u32[]{:S(2)}) collective-permute-start(f32[10,8,128]{2,1,0:T(8,128)S(1)} %get-tuple-element.39), channel_id=1, source_target_pairs={{0,1},{2,3},{4,5},{6,7},{1,0},{3,2},{5,4},{7,6},{8,9},{10,11},{12,... | collective-permute-start | bytes 122888 | tf_op jit(solution)/shard_map/ppermute | solution.py:648
  30.6 9.0 %collective-permute-start.8 = (f32[9,8,128]{2,1,0:T(8,128)S(1)}, f32[9,8,128]{2,1,0:T(8,128)S(1)}, u32[]{:S(2)}, u32[]{:S(2)}) collective-permute-start(f32[9,8,128]{2,1,0:T(8,128)S(1)} %get-tuple-element.46), channel_id=1, source_target_pairs={{0,7},{2,1},{4,3},{6,5},{7,0},{1,2},{3,4},{5,6},{8,15},{10,9},{12,... | collective-permute-start | bytes 110600 | tf_op jit(solution)/shard_map/ppermute | solution.py:648
  33.3 6.2 %collective-permute-start.9 = (f32[9,8,128]{2,1,0:T(8,128)S(1)}, f32[9,8,128]{2,1,0:T(8,128)S(1)}, u32[]{:S(2)}, u32[]{:S(2)}) collective-permute-start(f32[9,8,128]{2,1,0:T(8,128)S(1)} %get-tuple-element.47), channel_id=1, source_target_pairs={{0,1},{2,3},{4,5},{6,7},{1,0},{3,2},{5,4},{7,6},{8,9},{10,11},{12,... | collective-permute-start | bytes 110600 | tf_op jit(solution)/shard_map/ppermute | solution.py:648
  33.3 5.4 %collective-permute-start.11 = (f32[2,8,128]{2,1,0:T(8,128)S(1)}, f32[2,8,128]{2,1,0:T(8,128)S(1)}, u32[]{:S(2)}, u32[]{:S(2)}) collective-permute-start(f32[2,8,128]{2,1,0:T(8,128)S(1)} %get-tuple-element.45.own2), channel_id=1, source_target_pairs={{0,6},{1,7},{4,2},{5,3},{6,0},{7,1},{2,4},{3,5},{8,14},{9,15},{12,... | collective-permute-start | bytes 24584 | tf_op jit(solution)/shard_map/ppermute | solution.py:655
  35.9 3.7 %collective-permute-start.10 = (f32[2,8,128]{2,1,0:T(8,128)S(1)}, f32[2,8,128]{2,1,0:T(8,128)S(1)}, u32[]{:S(2)}, u32[]{:S(2)}) collective-permute-start(f32[2,8,128]{2,1,0:T(8,128)S(1)} %get-tuple-element.45.own2), channel_id=1, source_target_pairs={{0,2},{1,3},{4,6},{5,7},{2,0},{3,1},{6,4},{7,5},{8,10},{9,11},{12,... | collective-permute-start | bytes 24584 | tf_op jit(solution)/shard_map/ppermute | solution.py:655

commit v4 on v3

--- a/solution.py
+++ b/solution.py
@@ -379,7 +379,7 @@
 
 
 def level0_kernel(
-    rows, main, y_first, y_second, own_a, own_b, corner_a, corner_b, keep, powers, sources, fields, diag
+    rows, main, y_first, y_second, own_a, own_b, corner_a, corner_b, keep, powers, sources, fields, diag, y0
 ):
     even, even_x = is_even("gy"), is_even("gx")
     total = rows + 2 * HALO0
@@ -419,26 +419,26 @@
                 keep[i, t, at] = value
             diag[0, t, at] = first
             diag[1, t, at] = second
-            powers[0, 0, t, at] = inv_u * b_u
-            powers[0, 1, t, at] = inv_v * b_v
+            y0[0, t, at] = inv_u * b_u
+            y0[1, t, at] = inv_v * b_v
 
     rows_loop(1, total - 1, setup)
     for p in (0, 1):
 
         def power(r, n, p=p):
-            for i, values in enumerate(next_power(keep, powers.at[p], r, n)):
+            for i, values in enumerate(next_power(keep, powers.at[0] if p else y0, r, n)):
                 for t in (0, 1):
-                    powers[p + 1, i, t, pl.ds(r, n)] = values[t]
+                    powers[p, i, t, pl.ds(r, n)] = values[t]
 
         rows_loop(2 + p, total - 2 - p, power)
 
     def down(r, n):
         at = pl.ds(r, n)
-        last = next_power(keep, powers.at[2], r, n)
+        last = next_power(keep, powers.at[1], r, n)
         for t in (0, 1):
             both = [diag[i, t, at] for i in (0, 1)]
             parts = [[keep[4 + i, t, at] for i in (0, 1)]]
-            parts += [[both[i] * powers[p, i, t, at] for i in (0, 1)] for p in (1, 2)]
+            parts += [[both[i] * powers[p, i, t, at] for i in (0, 1)] for p in (0, 1)]
             parts.append([both[i] * last[i][t] for i in (0, 1)])
             for q, part in enumerate(parts):
                 u, v = (pair_rows(value) for value in part)
@@ -471,7 +471,7 @@
 
 
 def coarse1_kernel(
-    rows, coarse, y_first, y_second, own_a, own_b, corner_a, corner_b, gain, powers, coef, x0, edge_first, edge_second, fields
+    rows, coarse, y_first, y_second, own_a, own_b, corner_a, corner_b, gain, keep0, powers, coef, x0, edge_first, edge_second, fields
 ):
     even, even_x = is_even("gy"), is_even("gx")
     own_x, corner_x = (own_a, own_b), (corner_a, corner_b)
@@ -494,7 +494,8 @@
     p0, p1, p2 = (gain[POWERS + i] for i in range(3))
     for i in (0, 1):
         for t in (0, 1):
-            y0, y1, y2 = (powers[p, i, t, HALO0 : HALO0 + rows] for p in range(3))
+            y0 = keep0[2 + i, t, HALO0 : HALO0 + rows] * keep0[4 + i, t, HALO0 : HALO0 + rows]
+            y1, y2 = (powers[p, i, t, HALO0 : HALO0 + rows] for p in (0, 1))
             x0[i, t] = p0 * y0 - p1 * y1 + p2 * y2
     lane = lane_of()
     edges = []
@@ -702,8 +703,8 @@
     pair0 = (2, 2, total0, Z, X)
     keep0, powers, sources = call(
         functools.partial(level0_kernel, rows),
-        [(6, 2, total0, Z, X), (3, *pair0), (4, 2, OWN, Z, X)],
-        [(6, 2, total0, Z, X), pair0],
+        [(6, 2, total0, Z, X), (2, *pair0), (4, 2, OWN, Z, X)],
+        [(6, 2, total0, Z, X), pair0, pair0],
         main,
         *y_packets,
         *own_x,
@@ -727,6 +728,7 @@
         *own_x,
         *corner_x,
         gain,
+        keep0,
         powers,
     )
     b_packets = exchange(first, second, "gy")

time: 42.9 us -> 40.5 us (0.944)
  local copies, waits for them, and re-layouts: 1.55 us -> 0 us
  waiting for transfers between devices: 11.3 us -> 10.5 us
    unnamed x4 -> x0, local copies, waits for them, and re-layouts: 1.55 us -> none
    ppermute x2, waiting for transfers between devices: 3.55 us -> 2.77 us  [swap_far(): return lax.ppermute(value, axis, pairs + [(j, i) for i, j in pairs])]
  transfers between devices with their start and end apart: 13 -> 13, of which waited for: 6 -> 6; matrix products, arithmetic and copies ran while one was open for 0% -> 0% of each run, Pallas kernels for 8% -> 9%
where the time goes in v4:
time: 40.5 us; the launch traced here: 40.4 us
  starting transfers between devices  21.1 us (52%)
  waiting for transfers between devices  10.5 us (26%)
  Pallas kernels  8.63 us (21%)
    ppermute x10, starting transfers between devices, swap(): return lax.ppermute(value, axis, pairs + [(j, i) for i, j in pairs])  16 us
    pallas_call x10, Pallas kernels, call(): pl.pallas_call(kernel, out_shape=out, in_specs=[pl.BlockSpec(memory_space...  8.63 us
    ppermute x10, waiting for transfers between devices, swap(): return lax.ppermute(value, axis, pairs + [(j, i) for i, j in pairs])  7.75 us
    ppermute x2, waiting for transfers between devices, swap_far(): return lax.ppermute(value, axis, pairs + [(j, i) for i, j in pairs])  2.77 us
    ppermute x2, starting transfers between devices, swap_far(): return lax.ppermute(value, axis, pairs + [(j, i) for i, j in pairs])  2.59 us
    all_to_all x1, starting transfers between devices, body(): spread = lax.all_to_all(spread, ('gx', 'gy'), 0, 0, tiled=True)  2.57 us
  transfers between devices with their start and end apart: 13, of which 6 were waited for; matrix products, arithmetic and copies ran while one was open for 0% of the time, Pallas kernels for 9%

profile of v4, /device:TPU:0, one launch (start us, length us, event | category | flops | bytes accessed | tf_op | source)
XLA Modules:
  0.0 40.4 jit_solution(17642490291105768155)
XLA Ops:
  0.0 1.4 %shard_map.46 = (f32[29,8,128]{2,1,0:T(8,128)S(1)}, f32[29,8,128]{2,1,0:T(8,128)S(1)}, f32[6,16,8,128]{3,2,1,0:T(8,128)S(1)}, f32[9,8,128]{2,1,0:T(8,128)S(1)}) custom-call(f32[256,128]{1,0:T(8,128)} %bitcast.5, f32[256,128]{1,0:T(8,128)} %bitcast.6, f32[128,128]{1,0:T(8,128)} %bitcast.7, f32[128,128]{1,0:T(8,128)} %bitcast.8), custom_call_target="tpu_custom_call" | custom-call | tf_op jit(solution)/shard_map/pallas_call | solution.py:635
  1.4 6.1 %collective-permute-start = (f32[29,8,128]{2,1,0:T(8,128)S(1)}, f32[29,8,128]{2,1,0:T(8,128)S(1)}, u32[]{:S(2)}, u32[]{:S(2)}) collective-permute-start(f32[29,8,128]{2,1,0:T(8,128)S(1)} %get-tuple-element.29), channel_id=1, source_target_pairs={{0,7},{2,1},{4,3},{6,5},{7,0},{1,2},{3,4},{5,6},{8,15},{10,9},{12,... | collective-permute-start | bytes 356360 | tf_op jit(solution)/shard_map/ppermute | solution.py:649
  7.5 0.2 shard_map.47
  7.7 0.7 %collective-permute-start.2 = (f32[35,8,128]{2,1,0:T(8,128)S(1)}, f32[35,8,128]{2,1,0:T(8,128)S(1)}, u32[]{:S(2)}, u32[]{:S(2)}) collective-permute-start(f32[35,8,128]{2,1,0:T(8,128)S(1)} %get-tuple-element.32), channel_id=1, source_target_pairs={{0,24},{16,8},{24,0},{8,16},{1,25},{17,9},{25,1},{9,17},{2,26},{18... | collective-permute-start | bytes 430088 | tf_op jit(solution)/shard_map/ppermute | solution.py:649
  8.4 1.0 %collective-permute-start.3 = (f32[35,8,128]{2,1,0:T(8,128)S(1)}, f32[35,8,128]{2,1,0:T(8,128)S(1)}, u32[]{:S(2)}, u32[]{:S(2)}) collective-permute-start(f32[35,8,128]{2,1,0:T(8,128)S(1)} %get-tuple-element.33), channel_id=1, source_target_pairs={{0,8},{16,24},{8,0},{24,16},{1,9},{17,25},{9,1},{25,17},{2,10},{18... | collective-permute-start | bytes 430088 | tf_op jit(solution)/shard_map/ppermute | solution.py:649
  9.4 0.8 %shard_map.50 = f32[32,4,128]{2,1,0:T(4,128)} custom-call(f32[6,16,8,128]{3,2,1,0:T(8,128)S(1)} %get-tuple-element.28.main, f32[9,8,128]{2,1,0:T(8,128)S(1)} %get-tuple-element.31.coarse), custom_call_target="tpu_custom_call" | custom-call | tf_op jit(solution)/shard_map/pallas_call | solution.py:635
  10.2 2.6 %all-to-all-start = ((f32[32,4,128]{2,1,0:T(4,128)}), f32[32,4,128]{2,1,0:T(4,128)S(1)}, u32[]{:S(2)}, u32[]{:S(2)}) async-start(f32[32,4,128]{2,1,0:T(4,128)} %shard_map.50), calls=%async_computation | async-start | bytes 131072 | tf_op jit(solution)/shard_map/all_to_all | solution.py:684
  12.8 0.5 %collective-permute-done.1.y_second = f32[29,8,128]{2,1,0:T(8,128)S(1)} collective-permute-done((f32[29,8,128]{2,1,0:T(8,128)S(1)}, f32[29,8,128]{2,1,0:T(8,128)S(1)}, u32[]{:S(2)}, u32[]{:S(2)}) %collective-permute-start.1) | collective-permute-done | bytes 118816 | tf_op jit(solution)/shard_map/ppermute | solution.py:649
  13.2 0.2 shard_map.48
  13.4 1.0 %collective-permute-start.4 = (f32[20,8,128]{2,1,0:T(8,128)S(1)}, f32[20,8,128]{2,1,0:T(8,128)S(1)}, u32[]{:S(2)}, u32[]{:S(2)}) collective-permute-start(f32[20,8,128]{2,1,0:T(8,128)S(1)} %get-tuple-element.34), channel_id=1, source_target_pairs={{0,24},{16,8},{24,0},{8,16},{1,25},{17,9},{25,1},{9,17},{2,26},{18... | collective-permute-start | bytes 245768 | tf_op jit(solution)/shard_map/ppermute | solution.py:649
  14.4 0.7 %collective-permute-start.5 = (f32[20,8,128]{2,1,0:T(8,128)S(1)}, f32[20,8,128]{2,1,0:T(8,128)S(1)}, u32[]{:S(2)}, u32[]{:S(2)}) collective-permute-start(f32[20,8,128]{2,1,0:T(8,128)S(1)} %get-tuple-element.35), channel_id=1, source_target_pairs={{0,8},{16,24},{8,0},{24,16},{1,9},{17,25},{9,1},{25,17},{2,10},{18... | collective-permute-start | bytes 245768 | tf_op jit(solution)/shard_map/ppermute | solution.py:649
  15.1 3.5 %collective-permute-done.4.corner_a = f32[20,8,128]{2,1,0:T(8,128)S(1)} collective-permute-done((f32[20,8,128]{2,1,0:T(8,128)S(1)}, f32[20,8,128]{2,1,0:T(8,128)S(1)}, u32[]{:S(2)}, u32[]{:S(2)}) %collective-permute-start.4) | collective-permute-done | bytes 81952 | tf_op jit(solution)/shard_map/ppermute | solution.py:649
  18.6 2.0 %shard_map.49 = (f32[6,2,24,8,128]{4,3,2,1,0:T(8,128)S(1)}, f32[2,2,2,24,8,128]{5,4,3,2,1,0:T(8,128)S(1)}, f32[4,2,4,8,128]{4,3,2,1,0:T(8,128)S(1)}) custom-call(f32[6,16,8,128]{3,2,1,0:T(8,128)S(1)} %get-tuple-element.28.main, f32[29,8,128]{2,1,0:T(8,128)S(1)} %collective-permute-done.y_first, f32[29,8,128]{2,1,0:T(8,128)S(1)} %collective-permute-done.1.y_second, ...), custom_call_target="tpu_custom_call" | custom-call | tf_op jit(solution)/shard_map/pallas_call | solution.py:635
  20.5 0.1 shard_map.51
  20.7 3.8 %collective-permute-start.6 = (f32[10,8,128]{2,1,0:T(8,128)S(1)}, f32[10,8,128]{2,1,0:T(8,128)S(1)}, u32[]{:S(2)}, u32[]{:S(2)}) collective-permute-start(f32[10,8,128]{2,1,0:T(8,128)S(1)} %get-tuple-element.38), channel_id=1, source_target_pairs={{0,7},{2,1},{4,3},{6,5},{7,0},{1,2},{3,4},{5,6},{8,15},{10,9},{12,... | collective-permute-start | bytes 122888 | tf_op jit(solution)/shard_map/ppermute | solution.py:649
  24.5 0.2 shard_map.52
  24.6 2.9 %collective-permute-done.6.first.b_first = f32[10,8,128]{2,1,0:T(8,128)S(1)} collective-permute-done((f32[10,8,128]{2,1,0:T(8,128)S(1)}, f32[10,8,128]{2,1,0:T(8,128)S(1)}, u32[]{:S(2)}, u32[]{:S(2)}) %collective-permute-start.6) | collective-permute-done | bytes 40992 | tf_op jit(solution)/shard_map/ppermute | solution.py:649
  27.5 0.9 %collective-permute-done.7.second.b_second = f32[10,8,128]{2,1,0:T(8,128)S(1)} collective-permute-done((f32[10,8,128]{2,1,0:T(8,128)S(1)}, f32[10,8,128]{2,1,0:T(8,128)S(1)}, u32[]{:S(2)}, u32[]{:S(2)}) %collective-permute-start.7) | collective-permute-done | bytes 40992 | tf_op jit(solution)/shard_map/ppermute | solution.py:649
  28.5 0.6 %shard_map.53 = (f32[2,8,128]{2,1,0:T(8,128)S(1)}, f32[9,8,128]{2,1,0:T(8,128)S(1)}, f32[9,8,128]{2,1,0:T(8,128)S(1)}, f32[2,2,14,8,128]{4,3,2,1,0:T(8,128)S(1)}) custom-call(f32[2,4,8,128]{3,2,1,0:T(8,128)S(1)} %get-tuple-element.37.own, f32[10,8,128]{2,1,0:T(8,128)S(1)} %collective-permute-done.6.first.b_first, ...), custom_call_target="tpu_custom_call" | custom-call | tf_op jit(solution)/shard_map/pallas_call | solution.py:635
  29.0 2.8 %collective-permute-start.8 = (f32[9,8,128]{2,1,0:T(8,128)S(1)}, f32[9,8,128]{2,1,0:T(8,128)S(1)}, u32[]{:S(2)}, u32[]{:S(2)}) collective-permute-start(f32[9,8,128]{2,1,0:T(8,128)S(1)} %get-tuple-element.47), channel_id=1, source_target_pairs={{0,7},{2,1},{4,3},{6,5},{7,0},{1,2},{3,4},{5,6},{8,15},{10,9},{12,... | collective-permute-start | bytes 110600 | tf_op jit(solution)/shard_map/ppermute | solution.py:649
  31.8 2.6 %collective-permute-start.11 = (f32[2,8,128]{2,1,0:T(8,128)S(1)}, f32[2,8,128]{2,1,0:T(8,128)S(1)}, u32[]{:S(2)}, u32[]{:S(2)}) collective-permute-start(f32[2,8,128]{2,1,0:T(8,128)S(1)} %get-tuple-element.46.own2), channel_id=1, source_target_pairs={{0,6},{1,7},{4,2},{5,3},{6,0},{7,1},{2,4},{3,5},{8,14},{9,15},{12,... | collective-permute-start | bytes 24584 | tf_op jit(solution)/shard_map/ppermute | solution.py:656
  34.5 1.0 %collective-permute-done.10.far_a = f32[2,8,128]{2,1,0:T(8,128)S(1)} collective-permute-done((f32[2,8,128]{2,1,0:T(8,128)S(1)}, f32[2,8,128]{2,1,0:T(8,128)S(1)}, u32[]{:S(2)}, u32[]{:S(2)}) %collective-permute-start.10) | collective-permute-done | bytes 8224 | tf_op jit(solution)/shard_map/ppermute | solution.py:656
  35.4 1.8 %collective-permute-done.11.far_b = f32[2,8,128]{2,1,0:T(8,128)S(1)} collective-permute-done((f32[2,8,128]{2,1,0:T(8,128)S(1)}, f32[2,8,128]{2,1,0:T(8,128)S(1)}, u32[]{:S(2)}, u32[]{:S(2)}) %collective-permute-start.11) | collective-permute-done | bytes 8224 | tf_op jit(solution)/shard_map/ppermute | solution.py:656
  37.2 3.1 %shard_map.55 = f32[256,128]{1,0:T(8,128)} custom-call(f32[2,8,128]{2,1,0:T(8,128)S(1)} %get-tuple-element.46.own2, f32[9,8,128]{2,1,0:T(8,128)S(1)} %collective-permute-done.8.near_a, f32[9,8,128]{2,1,0:T(8,128)S(1)} %collective-permute-done.9.near_b, f32[2,8,128]{2,1,0:T(8,128)S(1)} %collective-permute-done.10.far_a, ...), custom_call_target="tpu_custom_call" | custom-call | tf_op jit(solution)/shard_map/pallas_call | solution.py:635
  (12 shorter events, 0.1 us)
Async XLA Ops:
  1.4 11.4 %collective-permute-start = (f32[29,8,128]{2,1,0:T(8,128)S(1)}, f32[29,8,128]{2,1,0:T(8,128)S(1)}, u32[]{:S(2)}, u32[]{:S(2)}) collective-permute-start(f32[29,8,128]{2,1,0:T(8,128)S(1)} %get-tuple-element.29), channel_id=1, source_target_pairs={{0,7},{2,1},{4,3},{6,5},{7,0},{1,2},{3,4},{5,6},{8,15},{10,9},{12,... | collective-permute-start | bytes 356360 | tf_op jit(solution)/shard_map/ppermute | solution.py:649
  7.5 5.8 %collective-permute-start.1 = (f32[29,8,128]{2,1,0:T(8,128)S(1)}, f32[29,8,128]{2,1,0:T(8,128)S(1)}, u32[]{:S(2)}, u32[]{:S(2)}) collective-permute-start(f32[29,8,128]{2,1,0:T(8,128)S(1)} %get-tuple-element.30), channel_id=1, source_target_pairs={{0,1},{2,3},{4,5},{6,7},{1,0},{3,2},{5,4},{7,6},{8,9},{10,11},{12,... | collective-permute-start | bytes 356360 | tf_op jit(solution)/shard_map/ppermute | solution.py:649
  7.7 7.4 %collective-permute-start.2 = (f32[35,8,128]{2,1,0:T(8,128)S(1)}, f32[35,8,128]{2,1,0:T(8,128)S(1)}, u32[]{:S(2)}, u32[]{:S(2)}) collective-permute-start(f32[35,8,128]{2,1,0:T(8,128)S(1)} %get-tuple-element.32), channel_id=1, source_target_pairs={{0,24},{16,8},{24,0},{8,16},{1,25},{17,9},{25,1},{9,17},{2,26},{18... | collective-permute-start | bytes 430088 | tf_op jit(solution)/shard_map/ppermute | solution.py:649
  8.4 6.7 %collective-permute-start.3 = (f32[35,8,128]{2,1,0:T(8,128)S(1)}, f32[35,8,128]{2,1,0:T(8,128)S(1)}, u32[]{:S(2)}, u32[]{:S(2)}) collective-permute-start(f32[35,8,128]{2,1,0:T(8,128)S(1)} %get-tuple-element.33), channel_id=1, source_target_pairs={{0,8},{16,24},{8,0},{24,16},{1,9},{17,25},{9,1},{25,17},{2,10},{18... | collective-permute-start | bytes 430088 | tf_op jit(solution)/shard_map/ppermute | solution.py:649
  10.2 10.4 %all-to-all-start = ((f32[32,4,128]{2,1,0:T(4,128)}), f32[32,4,128]{2,1,0:T(4,128)S(1)}, u32[]{:S(2)}, u32[]{:S(2)}) async-start(f32[32,4,128]{2,1,0:T(4,128)} %shard_map.50), calls=%async_computation | async-start | bytes 131072 | tf_op jit(solution)/shard_map/all_to_all | solution.py:684
  13.4 5.1 %collective-permute-start.4 = (f32[20,8,128]{2,1,0:T(8,128)S(1)}, f32[20,8,128]{2,1,0:T(8,128)S(1)}, u32[]{:S(2)}, u32[]{:S(2)}) collective-permute-start(f32[20,8,128]{2,1,0:T(8,128)S(1)} %get-tuple-element.34), channel_id=1, source_target_pairs={{0,24},{16,8},{24,0},{8,16},{1,25},{17,9},{25,1},{9,17},{2,26},{18... | collective-permute-start | bytes 245768 | tf_op jit(solution)/shard_map/ppermute | solution.py:649
  14.4 4.1 %collective-permute-start.5 = (f32[20,8,128]{2,1,0:T(8,128)S(1)}, f32[20,8,128]{2,1,0:T(8,128)S(1)}, u32[]{:S(2)}, u32[]{:S(2)}) collective-permute-start(f32[20,8,128]{2,1,0:T(8,128)S(1)} %get-tuple-element.35), channel_id=1, source_target_pairs={{0,8},{16,24},{8,0},{24,16},{1,9},{17,25},{9,1},{25,17},{2,10},{18... | collective-permute-start | bytes 245768 | tf_op jit(solution)/shard_map/ppermute | solution.py:649
  20.7 6.9 %collective-permute-start.6 = (f32[10,8,128]{2,1,0:T(8,128)S(1)}, f32[10,8,128]{2,1,0:T(8,128)S(1)}, u32[]{:S(2)}, u32[]{:S(2)}) collective-permute-start(f32[10,8,128]{2,1,0:T(8,128)S(1)} %get-tuple-element.38), channel_id=1, source_target_pairs={{0,7},{2,1},{4,3},{6,5},{7,0},{1,2},{3,4},{5,6},{8,15},{10,9},{12,... | collective-permute-start | bytes 122888 | tf_op jit(solution)/shard_map/ppermute | solution.py:649
  24.5 4.0 %collective-permute-start.7 = (f32[10,8,128]{2,1,0:T(8,128)S(1)}, f32[10,8,128]{2,1,0:T(8,128)S(1)}, u32[]{:S(2)}, u32[]{:S(2)}) collective-permute-start(f32[10,8,128]{2,1,0:T(8,128)S(1)} %get-tuple-element.39), channel_id=1, source_target_pairs={{0,1},{2,3},{4,5},{6,7},{1,0},{3,2},{5,4},{7,6},{8,9},{10,11},{12,... | collective-permute-start | bytes 122888 | tf_op jit(solution)/shard_map/ppermute | solution.py:649
  29.0 8.2 %collective-permute-start.8 = (f32[9,8,128]{2,1,0:T(8,128)S(1)}, f32[9,8,128]{2,1,0:T(8,128)S(1)}, u32[]{:S(2)}, u32[]{:S(2)}) collective-permute-start(f32[9,8,128]{2,1,0:T(8,128)S(1)} %get-tuple-element.47), channel_id=1, source_target_pairs={{0,7},{2,1},{4,3},{6,5},{7,0},{1,2},{3,4},{5,6},{8,15},{10,9},{12,... | collective-permute-start | bytes 110600 | tf_op jit(solution)/shard_map/ppermute | solution.py:649
  31.8 5.5 %collective-permute-start.9 = (f32[9,8,128]{2,1,0:T(8,128)S(1)}, f32[9,8,128]{2,1,0:T(8,128)S(1)}, u32[]{:S(2)}, u32[]{:S(2)}) collective-permute-start(f32[9,8,128]{2,1,0:T(8,128)S(1)} %get-tuple-element.48), channel_id=1, source_target_pairs={{0,1},{2,3},{4,5},{6,7},{1,0},{3,2},{5,4},{7,6},{8,9},{10,11},{12,... | collective-permute-start | bytes 110600 | tf_op jit(solution)/shard_map/ppermute | solution.py:649
  31.8 3.7 %collective-permute-start.10 = (f32[2,8,128]{2,1,0:T(8,128)S(1)}, f32[2,8,128]{2,1,0:T(8,128)S(1)}, u32[]{:S(2)}, u32[]{:S(2)}) collective-permute-start(f32[2,8,128]{2,1,0:T(8,128)S(1)} %get-tuple-element.46.own2), channel_id=1, source_target_pairs={{0,2},{1,3},{4,6},{5,7},{2,0},{3,1},{6,4},{7,5},{8,10},{9,11},{12,... | collective-permute-start | bytes 24584 | tf_op jit(solution)/shard_map/ppermute | solution.py:656
  31.8 5.4 %collective-permute-start.11 = (f32[2,8,128]{2,1,0:T(8,128)S(1)}, f32[2,8,128]{2,1,0:T(8,128)S(1)}, u32[]{:S(2)}, u32[]{:S(2)}) collective-permute-start(f32[2,8,128]{2,1,0:T(8,128)S(1)} %get-tuple-element.46.own2), channel_id=1, source_target_pairs={{0,6},{1,7},{4,2},{5,3},{6,0},{7,1},{2,4},{3,5},{8,14},{9,15},{12,... | collective-permute-start | bytes 24584 | tf_op jit(solution)/shard_map/ppermute | solution.py:656

commit v5 on v4

--- a/solution.py
+++ b/solution.py
@@ -56,7 +56,7 @@
 
 
 def rows_loop(lo, hi, body, step=None):
-    step = step or (hi - lo) // 2
+    step = step or hi - lo
     full = (hi - lo) // step
     if full == 1:
         body(lo, step)
@@ -373,8 +373,8 @@
     pack_edges(held, is_even("gx"), first, second)
 
 
-FAR = 2 * OWN
-EDGES = 2
+FAR = 2
+EDGES = 4
 EDGE_TILES = 2 * EDGE + 1
 
 
@@ -446,11 +446,10 @@
                     value = restrict_01(u[2 * j : 2 * j + 2], v[2 * j : 2 * j + 2])
                     sources[q, t, pl.ds((r - HALO0) // 4 + j, 1)] = value
 
-    rows_loop(HALO0, HALO0 + rows, down, 8)
-
-
-def combine_kernel(sources, y_first, y_second, corner_a, corner_b, spread, own, first, second, gain):
-    even, even_x = is_even("gy"), is_even("gx")
+    rows_loop(HALO0, HALO0 + rows, down)
+
+
+def combine_kernel(sources, spread, own, first, second, gain):
     write_gains(jnp.max(spread[...], axis=0)[0:1], gain)
     p0, p1, p2 = (gain[POWERS + i] for i in range(3))
     for t in (0, 1):
@@ -458,16 +457,6 @@
         own[t] = value
         for ref in (first, second):
             ref[t * OWN : (t + 1) * OWN] = value
-    strip = slice(FIELDS2, FIELDS2 + 1)
-    for t in (0, 1):
-        if t == 0:
-            before, after = prev_of(even, y_first, y_second, strip), next_of(even, y_first, y_second, strip)
-        else:
-            before, after = (
-                halo_tiles(even_x, (corner_a, corner_b), at + FIELDS2, at + FIELDS2 + 1)[0][2] for at in (0, PACKET)
-            )
-        first[FAR + t : FAR + t + 1] = jnp.where(even, after, before)
-        second[FAR + t : FAR + t + 1] = jnp.where(even, before, after)
 
 
 def coarse1_kernel(
@@ -508,33 +497,31 @@
                 halo = value if halo is None else jnp.where((lane >> 3) == at, value, halo)
         edges.append([x0[0, 0, start : start + EDGE], x0[1, 0, start : start + EDGE], halo])
     top, bottom = (jnp.concatenate(parts, axis=0) for parts in edges)
-    edge_first[...] = jnp.where(even, top, bottom)
-    edge_second[...] = jnp.where(even, bottom, top)
-
-
-def coarse2_kernel(
-    rows, coarse, y_first, y_second, own_a, own_b, corner_a, corner_b, b_first, b_second, coef
-):
+    edge_first[2:] = jnp.where(even, top, bottom)
+    edge_second[2:] = jnp.where(even, bottom, top)
+    strip = slice(FIELDS2, FIELDS2 + 1)
+    for t in (0, 1):
+        if t == 0:
+            before, after = prev_of(even, y_first, y_second, strip), next_of(even, y_first, y_second, strip)
+        else:
+            before, after = (
+                halo_tiles(even_x, corner_x, at + FIELDS2, at + FIELDS2 + 1)[0][2] for at in (0, PACKET)
+            )
+        edge_first[t : t + 1] = jnp.where(even, after, before)
+        edge_second[t : t + 1] = jnp.where(even, before, after)
+
+
+def fields2_kernel(rows, coarse, y_first, y_second, own_a, own_b, corner_a, corner_b, out):
     even, even_x = is_even("gy"), is_even("gx")
     own_x, corner_x = (own_a, own_b), (corner_a, corner_b)
     near = slice(FIELDS2, FIELDS2 + 1)
-    for t in (0, 1):
-        far = slice(FAR + t, FAR + t + 1)
-        if t == 0:
-            middle = [
-                prev_of(even, y_first, y_second, near),
-                coarse[2 * OWN : 2 * OWN + 1],
-                next_of(even, y_first, y_second, near),
-            ]
-        else:
-            middle = [
-                halo_tiles(even_x, packets, lo, lo + 1)[0][2]
-                for packets, lo in ((corner_x, FIELDS2), (own_x, 6 * rows + 2 * OWN), (corner_x, PACKET + FIELDS2))
-            ]
-        parts = [prev_of(even, b_first, b_second, far), *middle, next_of(even, b_first, b_second, far)]
-        inverse, other, _ = packed_jacobian(*split_fields2(jnp.concatenate(parts, axis=0)), 2)
-        coef[0, t, 1 : SIZE2 - 1] = inverse
-        coef[1, t, 1 : SIZE2 - 1] = other
+    out[0, 0:1] = prev_of(even, y_first, y_second, near)
+    out[0, 1:2] = coarse[2 * OWN : 2 * OWN + 1]
+    out[0, 2:3] = next_of(even, y_first, y_second, near)
+    for q, (packets, lo) in enumerate(
+        ((corner_x, FIELDS2), (own_x, 6 * rows + 2 * OWN), (corner_x, PACKET + FIELDS2))
+    ):
+        out[1, q : q + 1] = halo_tiles(even_x, packets, lo, lo + 1)[0][2]
 
 
 def level1_kernel(own, first, second, edge_a, edge_b, coef1, gain, packet, to_first, to_second, keep, y1, d1):
@@ -556,12 +543,12 @@
         value = restrict_12([res[j : j + 1] for j in range(OWN)])
         for ref in (packet, to_first, to_second):
             ref[t : t + 1] = value
-    to_first[EDGES : EDGES + EDGE_TILES] = edge_a[...]
-    to_second[EDGES : EDGES + EDGE_TILES] = edge_b[...]
+    to_first[FAR:] = edge_a[...]
+    to_second[FAR:] = edge_b[...]
 
 
 def rest_kernel(
-    own2, near_a, near_b, far_a, far_b, gain, coef1, coef2, keep0, iterate, keep1, out, d1, b2, x2, y2, d2, xu, yu, x0, y0, d0
+    own2, near_a, near_b, far_a, far_b, gain, coef1, fields2, keep0, iterate, keep1, out, coef2, d1, b2, x2, y2, d2, xu, yu, x0, y0, d0
 ):
     rows = out.shape[0] // (2 * Z)
     even = (sub_of() & 1) == 0
@@ -578,6 +565,11 @@
             prev_of(low, far_a, far_b, at),
         ]
         b2[t, 1 : SIZE2 - 1] = jnp.concatenate(parts, axis=0)
+        far = slice(FAR + t, FAR + t + 1)
+        parts = [prev_of(even_y, near_a, near_b, far), fields2[t], next_of(even_y, near_a, near_b, far)]
+        inverse, other, _ = packed_jacobian(*split_fields2(jnp.concatenate(parts, axis=0)), 2)
+        coef2[0, t, 1 : SIZE2 - 1] = inverse
+        coef2[1, t, 1 : SIZE2 - 1] = other
 
     n = HI2 - LO2
     g0, g1, g2 = (gain[6 + i] for i in range(3))
@@ -699,7 +691,7 @@
         *call(pack_corner_kernel, [(tiles, Z, X), (tiles, Z, X)], [(PER * tiles, Z, X)], *y_packets), "gx"
     )
 
-    strip, edge = (FAR + 2, Z, X), (EDGE_TILES, Z, X)
+    strip, edge = (2 * OWN, Z, X), (2 + EDGE_TILES, Z, X)
     pair0 = (2, 2, total0, Z, X)
     keep0, powers, sources = call(
         functools.partial(level0_kernel, rows),
@@ -715,8 +707,6 @@
         [(2, OWN, Z, X), strip, strip, (POWERS + 3, Z, X)],
         [],
         sources,
-        *y_packets,
-        *corner_x,
         spread,
     )
     coef1, iterate, edge_a, edge_b = call(
@@ -730,6 +720,9 @@
         gain,
         keep0,
         powers,
+    )
+    (fields2,) = call(
+        functools.partial(fields2_kernel, rows), [(2, 3, Z, X)], [], coarse, *y_packets, *own_x, *corner_x
     )
     b_packets = exchange(first, second, "gy")
 
@@ -748,27 +741,17 @@
     )
     far = (swap_far(packet, "gy", 1), swap_far(packet, "gy", -1))
     near = exchange(first, second, "gy")
-    (coef2,) = call(
-        functools.partial(coarse2_kernel, rows),
-        [(2, 2, SIZE2, Z, X)],
-        [],
-        coarse,
-        *y_packets,
-        *own_x,
-        *corner_x,
-        *b_packets,
-    )
 
     (out,) = call(
         rest_kernel,
         [(2 * Z * rows, X)],
-        [one, two, two, two, two, up, up, pair0, pair0, pair0],
+        [(2, *two), one, two, two, two, two, up, up, pair0, pair0, pair0],
         packet,
         *near,
         *far,
         gain,
         coef1,
-        coef2,
+        fields2,
         keep0,
         iterate,
         keep1,

time: 40.5 us -> 39.4 us (0.973)
  Pallas kernels: 8.63 us -> 7.51 us
    pallas_call x10, Pallas kernels: 8.63 us -> 7.51 us  [call(): pl.pallas_call(kernel, out_shape=out, in_specs=[pl.BlockSpec(memory_space...]
  transfers between devices with their start and end apart: 13 -> 13, of which waited for: 6 -> 7; matrix products, arithmetic and copies ran while one was open for 0% -> 0% of each run, Pallas kernels for 9% -> 7%
where the time goes in v5:
time: 39.4 us; the launch traced here: 39.2 us
  starting transfers between devices  21 us (53%)
  waiting for transfers between devices  10.6 us (27%)
  Pallas kernels  7.51 us (19%)
    ppermute x10, starting transfers between devices, swap(): return lax.ppermute(value, axis, pairs + [(j, i) for i, j in pairs])  15.9 us
    ppermute x10, waiting for transfers between devices, swap(): return lax.ppermute(value, axis, pairs + [(j, i) for i, j in pairs])  7.66 us
    pallas_call x10, Pallas kernels, call(): pl.pallas_call(kernel, out_shape=out, in_specs=[pl.BlockSpec(memory_space...  7.51 us
    ppermute x2, waiting for transfers between devices, swap_far(): return lax.ppermute(value, axis, pairs + [(j, i) for i, j in pairs])  2.79 us
    ppermute x2, starting transfers between devices, swap_far(): return lax.ppermute(value, axis, pairs + [(j, i) for i, j in pairs])  2.59 us
    all_to_all x1, starting transfers between devices, body(): spread = lax.all_to_all(spread, ('gx', 'gy'), 0, 0, tiled=True)  2.57 us
  transfers between devices with their start and end apart: 13, of which 7 were waited for; matrix products, arithmetic and copies ran while one was open for 0% of the time, Pallas kernels for 7%

profile of v5, /device:TPU:0, one launch (start us, length us, event | category | flops | bytes accessed | tf_op | source)
XLA Modules:
  0.0 39.2 jit_solution(8867110497931348215)
XLA Ops:
  0.0 1.4 %shard_map.46 = (f32[29,8,128]{2,1,0:T(8,128)S(1)}, f32[29,8,128]{2,1,0:T(8,128)S(1)}, f32[6,16,8,128]{3,2,1,0:T(8,128)S(1)}, f32[9,8,128]{2,1,0:T(8,128)S(1)}) custom-call(f32[256,128]{1,0:T(8,128)} %bitcast.5, f32[256,128]{1,0:T(8,128)} %bitcast.6, f32[128,128]{1,0:T(8,128)} %bitcast.7, f32[128,128]{1,0:T(8,128)} %bitcast.8), custom_call_target="tpu_custom_call" | custom-call | tf_op jit(solution)/shard_map/pallas_call | solution.py:627
  1.4 6.1 %collective-permute-start = (f32[29,8,128]{2,1,0:T(8,128)S(1)}, f32[29,8,128]{2,1,0:T(8,128)S(1)}, u32[]{:S(2)}, u32[]{:S(2)}) collective-permute-start(f32[29,8,128]{2,1,0:T(8,128)S(1)} %get-tuple-element.29), channel_id=1, source_target_pairs={{0,7},{2,1},{4,3},{6,5},{7,0},{1,2},{3,4},{5,6},{8,15},{10,9},{12,... | collective-permute-start | bytes 356360 | tf_op jit(solution)/shard_map/ppermute | solution.py:641
  7.5 0.2 shard_map.47
  7.7 0.7 %collective-permute-start.2 = (f32[35,8,128]{2,1,0:T(8,128)S(1)}, f32[35,8,128]{2,1,0:T(8,128)S(1)}, u32[]{:S(2)}, u32[]{:S(2)}) collective-permute-start(f32[35,8,128]{2,1,0:T(8,128)S(1)} %get-tuple-element.32), channel_id=1, source_target_pairs={{0,24},{16,8},{24,0},{8,16},{1,25},{17,9},{25,1},{9,17},{2,26},{18... | collective-permute-start | bytes 430088 | tf_op jit(solution)/shard_map/ppermute | solution.py:641
  8.4 1.0 %collective-permute-start.3 = (f32[35,8,128]{2,1,0:T(8,128)S(1)}, f32[35,8,128]{2,1,0:T(8,128)S(1)}, u32[]{:S(2)}, u32[]{:S(2)}) collective-permute-start(f32[35,8,128]{2,1,0:T(8,128)S(1)} %get-tuple-element.33), channel_id=1, source_target_pairs={{0,8},{16,24},{8,0},{24,16},{1,9},{17,25},{9,1},{25,17},{2,10},{18... | collective-permute-start | bytes 430088 | tf_op jit(solution)/shard_map/ppermute | solution.py:641
  9.4 0.8 %shard_map.50 = f32[32,4,128]{2,1,0:T(4,128)} custom-call(f32[6,16,8,128]{3,2,1,0:T(8,128)S(1)} %get-tuple-element.28.main, f32[9,8,128]{2,1,0:T(8,128)S(1)} %get-tuple-element.31.coarse), custom_call_target="tpu_custom_call" | custom-call | tf_op jit(solution)/shard_map/pallas_call | solution.py:627
  10.2 2.6 %all-to-all-start = ((f32[32,4,128]{2,1,0:T(4,128)}), f32[32,4,128]{2,1,0:T(4,128)S(1)}, u32[]{:S(2)}, u32[]{:S(2)}) async-start(f32[32,4,128]{2,1,0:T(4,128)} %shard_map.50), calls=%async_computation | async-start | bytes 131072 | tf_op jit(solution)/shard_map/all_to_all | solution.py:676
  12.8 0.5 %collective-permute-done.1.y_second = f32[29,8,128]{2,1,0:T(8,128)S(1)} collective-permute-done((f32[29,8,128]{2,1,0:T(8,128)S(1)}, f32[29,8,128]{2,1,0:T(8,128)S(1)}, u32[]{:S(2)}, u32[]{:S(2)}) %collective-permute-start.1) | collective-permute-done | bytes 118816 | tf_op jit(solution)/shard_map/ppermute | solution.py:641
  13.2 0.2 shard_map.48
  13.4 1.0 %collective-permute-start.4 = (f32[20,8,128]{2,1,0:T(8,128)S(1)}, f32[20,8,128]{2,1,0:T(8,128)S(1)}, u32[]{:S(2)}, u32[]{:S(2)}) collective-permute-start(f32[20,8,128]{2,1,0:T(8,128)S(1)} %get-tuple-element.34), channel_id=1, source_target_pairs={{0,24},{16,8},{24,0},{8,16},{1,25},{17,9},{25,1},{9,17},{2,26},{18... | collective-permute-start | bytes 245768 | tf_op jit(solution)/shard_map/ppermute | solution.py:641
  14.4 0.7 %collective-permute-start.5 = (f32[20,8,128]{2,1,0:T(8,128)S(1)}, f32[20,8,128]{2,1,0:T(8,128)S(1)}, u32[]{:S(2)}, u32[]{:S(2)}) collective-permute-start(f32[20,8,128]{2,1,0:T(8,128)S(1)} %get-tuple-element.35), channel_id=1, source_target_pairs={{0,8},{16,24},{8,0},{24,16},{1,9},{17,25},{9,1},{25,17},{2,10},{18... | collective-permute-start | bytes 245768 | tf_op jit(solution)/shard_map/ppermute | solution.py:641
  15.1 3.5 %collective-permute-done.4.corner_a = f32[20,8,128]{2,1,0:T(8,128)S(1)} collective-permute-done((f32[20,8,128]{2,1,0:T(8,128)S(1)}, f32[20,8,128]{2,1,0:T(8,128)S(1)}, u32[]{:S(2)}, u32[]{:S(2)}) %collective-permute-start.4) | collective-permute-done | bytes 81952 | tf_op jit(solution)/shard_map/ppermute | solution.py:641
  18.6 1.3 %shard_map.49 = (f32[6,2,24,8,128]{4,3,2,1,0:T(8,128)S(1)}, f32[2,2,2,24,8,128]{5,4,3,2,1,0:T(8,128)S(1)}, f32[4,2,4,8,128]{4,3,2,1,0:T(8,128)S(1)}) custom-call(f32[6,16,8,128]{3,2,1,0:T(8,128)S(1)} %get-tuple-element.28.main, f32[29,8,128]{2,1,0:T(8,128)S(1)} %collective-permute-done.y_first, f32[29,8,128]{2,1,0:T(8,128)S(1)} %collective-permute-done.1.y_second, ...), custom_call_target="tpu_custom_call" | custom-call | tf_op jit(solution)/shard_map/pallas_call | solution.py:627
  19.9 0.1 all-to-all-done.spread
  20.2 3.7 %collective-permute-start.6 = (f32[8,8,128]{2,1,0:T(8,128)S(1)}, f32[8,8,128]{2,1,0:T(8,128)S(1)}, u32[]{:S(2)}, u32[]{:S(2)}) collective-permute-start(f32[8,8,128]{2,1,0:T(8,128)S(1)} %get-tuple-element.38), channel_id=1, source_target_pairs={{0,7},{2,1},{4,3},{6,5},{7,0},{1,2},{3,4},{5,6},{8,15},{10,9},{12,... | collective-permute-start | bytes 98312 | tf_op jit(solution)/shard_map/ppermute | solution.py:641
  23.8 0.2 shard_map.52
  24.0 2.9 %collective-permute-done.6.first = f32[8,8,128]{2,1,0:T(8,128)S(1)} collective-permute-done((f32[8,8,128]{2,1,0:T(8,128)S(1)}, f32[8,8,128]{2,1,0:T(8,128)S(1)}, u32[]{:S(2)}, u32[]{:S(2)}) %collective-permute-start.6) | collective-permute-done | bytes 32800 | tf_op jit(solution)/shard_map/ppermute | solution.py:641
  26.9 0.8 %collective-permute-done.7.second = f32[8,8,128]{2,1,0:T(8,128)S(1)} collective-permute-done((f32[8,8,128]{2,1,0:T(8,128)S(1)}, f32[8,8,128]{2,1,0:T(8,128)S(1)}, u32[]{:S(2)}, u32[]{:S(2)}) %collective-permute-start.7) | collective-permute-done | bytes 32800 | tf_op jit(solution)/shard_map/ppermute | solution.py:641
  27.7 0.6 %shard_map.53 = (f32[2,8,128]{2,1,0:T(8,128)S(1)}, f32[11,8,128]{2,1,0:T(8,128)S(1)}, f32[11,8,128]{2,1,0:T(8,128)S(1)}, f32[2,2,14,8,128]{4,3,2,1,0:T(8,128)S(1)}) custom-call(f32[2,4,8,128]{3,2,1,0:T(8,128)S(1)} %get-tuple-element.37.own, f32[8,8,128]{2,1,0:T(8,128)S(1)} %collective-permute-done.6.first, f32[8,8,128]{2,1,0:T(8,128)S(1)} %collective-permute-done.7.second, ...), custom_call_target="tpu_custom_call" | custom-call | tf_op jit(solution)/shard_map/pallas_call | solution.py:627
  28.3 2.8 %collective-permute-start.8 = (f32[11,8,128]{2,1,0:T(8,128)S(1)}, f32[11,8,128]{2,1,0:T(8,128)S(1)}, u32[]{:S(2)}, u32[]{:S(2)}) collective-permute-start(f32[11,8,128]{2,1,0:T(8,128)S(1)} %get-tuple-element.47), channel_id=1, source_target_pairs={{0,7},{2,1},{4,3},{6,5},{7,0},{1,2},{3,4},{5,6},{8,15},{10,9},{12,... | collective-permute-start | bytes 135176 | tf_op jit(solution)/shard_map/ppermute | solution.py:641
  31.1 2.6 %collective-permute-start.11 = (f32[2,8,128]{2,1,0:T(8,128)S(1)}, f32[2,8,128]{2,1,0:T(8,128)S(1)}, u32[]{:S(2)}, u32[]{:S(2)}) collective-permute-start(f32[2,8,128]{2,1,0:T(8,128)S(1)} %get-tuple-element.46.own2), channel_id=1, source_target_pairs={{0,6},{1,7},{4,2},{5,3},{6,0},{7,1},{2,4},{3,5},{8,14},{9,15},{12,... | collective-permute-start | bytes 24584 | tf_op jit(solution)/shard_map/ppermute | solution.py:648
  33.7 1.0 %collective-permute-done.10.far_a = f32[2,8,128]{2,1,0:T(8,128)S(1)} collective-permute-done((f32[2,8,128]{2,1,0:T(8,128)S(1)}, f32[2,8,128]{2,1,0:T(8,128)S(1)}, u32[]{:S(2)}, u32[]{:S(2)}) %collective-permute-start.10) | collective-permute-done | bytes 8224 | tf_op jit(solution)/shard_map/ppermute | solution.py:648
  34.7 1.8 %collective-permute-done.11.far_b = f32[2,8,128]{2,1,0:T(8,128)S(1)} collective-permute-done((f32[2,8,128]{2,1,0:T(8,128)S(1)}, f32[2,8,128]{2,1,0:T(8,128)S(1)}, u32[]{:S(2)}, u32[]{:S(2)}) %collective-permute-start.11) | collective-permute-done | bytes 8224 | tf_op jit(solution)/shard_map/ppermute | solution.py:648
  36.5 2.6 %shard_map.55 = f32[256,128]{1,0:T(8,128)} custom-call(f32[2,8,128]{2,1,0:T(8,128)S(1)} %get-tuple-element.46.own2, f32[11,8,128]{2,1,0:T(8,128)S(1)} %collective-permute-done.8.near_a, f32[11,8,128]{2,1,0:T(8,128)S(1)} %collective-permute-done.9.near_b, f32[2,8,128]{2,1,0:T(8,128)S(1)} %collective-permute-done.10.far_a, ...), custom_call_target="tpu_custom_call" | custom-call | tf_op jit(solution)/shard_map/pallas_call | solution.py:627
  (12 shorter events, 0.2 us)
Async XLA Ops:
  1.4 11.4 %collective-permute-start = (f32[29,8,128]{2,1,0:T(8,128)S(1)}, f32[29,8,128]{2,1,0:T(8,128)S(1)}, u32[]{:S(2)}, u32[]{:S(2)}) collective-permute-start(f32[29,8,128]{2,1,0:T(8,128)S(1)} %get-tuple-element.29), channel_id=1, source_target_pairs={{0,7},{2,1},{4,3},{6,5},{7,0},{1,2},{3,4},{5,6},{8,15},{10,9},{12,... | collective-permute-start | bytes 356360 | tf_op jit(solution)/shard_map/ppermute | solution.py:641
  7.5 5.8 %collective-permute-start.1 = (f32[29,8,128]{2,1,0:T(8,128)S(1)}, f32[29,8,128]{2,1,0:T(8,128)S(1)}, u32[]{:S(2)}, u32[]{:S(2)}) collective-permute-start(f32[29,8,128]{2,1,0:T(8,128)S(1)} %get-tuple-element.30), channel_id=1, source_target_pairs={{0,1},{2,3},{4,5},{6,7},{1,0},{3,2},{5,4},{7,6},{8,9},{10,11},{12,... | collective-permute-start | bytes 356360 | tf_op jit(solution)/shard_map/ppermute | solution.py:641
  7.7 7.4 %collective-permute-start.2 = (f32[35,8,128]{2,1,0:T(8,128)S(1)}, f32[35,8,128]{2,1,0:T(8,128)S(1)}, u32[]{:S(2)}, u32[]{:S(2)}) collective-permute-start(f32[35,8,128]{2,1,0:T(8,128)S(1)} %get-tuple-element.32), channel_id=1, source_target_pairs={{0,24},{16,8},{24,0},{8,16},{1,25},{17,9},{25,1},{9,17},{2,26},{18... | collective-permute-start | bytes 430088 | tf_op jit(solution)/shard_map/ppermute | solution.py:641
  8.4 6.7 %collective-permute-start.3 = (f32[35,8,128]{2,1,0:T(8,128)S(1)}, f32[35,8,128]{2,1,0:T(8,128)S(1)}, u32[]{:S(2)}, u32[]{:S(2)}) collective-permute-start(f32[35,8,128]{2,1,0:T(8,128)S(1)} %get-tuple-element.33), channel_id=1, source_target_pairs={{0,8},{16,24},{8,0},{24,16},{1,9},{17,25},{9,1},{25,17},{2,10},{18... | collective-permute-start | bytes 430088 | tf_op jit(solution)/shard_map/ppermute | solution.py:641
  10.2 9.9 %all-to-all-start = ((f32[32,4,128]{2,1,0:T(4,128)}), f32[32,4,128]{2,1,0:T(4,128)S(1)}, u32[]{:S(2)}, u32[]{:S(2)}) async-start(f32[32,4,128]{2,1,0:T(4,128)} %shard_map.50), calls=%async_computation | async-start | bytes 131072 | tf_op jit(solution)/shard_map/all_to_all | solution.py:676
  13.4 5.1 %collective-permute-start.4 = (f32[20,8,128]{2,1,0:T(8,128)S(1)}, f32[20,8,128]{2,1,0:T(8,128)S(1)}, u32[]{:S(2)}, u32[]{:S(2)}) collective-permute-start(f32[20,8,128]{2,1,0:T(8,128)S(1)} %get-tuple-element.34), channel_id=1, source_target_pairs={{0,24},{16,8},{24,0},{8,16},{1,25},{17,9},{25,1},{9,17},{2,26},{18... | collective-permute-start | bytes 245768 | tf_op jit(solution)/shard_map/ppermute | solution.py:641
  14.4 4.1 %collective-permute-start.5 = (f32[20,8,128]{2,1,0:T(8,128)S(1)}, f32[20,8,128]{2,1,0:T(8,128)S(1)}, u32[]{:S(2)}, u32[]{:S(2)}) collective-permute-start(f32[20,8,128]{2,1,0:T(8,128)S(1)} %get-tuple-element.35), channel_id=1, source_target_pairs={{0,8},{16,24},{8,0},{24,16},{1,9},{17,25},{9,1},{25,17},{2,10},{18... | collective-permute-start | bytes 245768 | tf_op jit(solution)/shard_map/ppermute | solution.py:641
  20.2 6.8 %collective-permute-start.6 = (f32[8,8,128]{2,1,0:T(8,128)S(1)}, f32[8,8,128]{2,1,0:T(8,128)S(1)}, u32[]{:S(2)}, u32[]{:S(2)}) collective-permute-start(f32[8,8,128]{2,1,0:T(8,128)S(1)} %get-tuple-element.38), channel_id=1, source_target_pairs={{0,7},{2,1},{4,3},{6,5},{7,0},{1,2},{3,4},{5,6},{8,15},{10,9},{12,... | collective-permute-start | bytes 98312 | tf_op jit(solution)/shard_map/ppermute | solution.py:641
  23.8 3.9 %collective-permute-start.7 = (f32[8,8,128]{2,1,0:T(8,128)S(1)}, f32[8,8,128]{2,1,0:T(8,128)S(1)}, u32[]{:S(2)}, u32[]{:S(2)}) collective-permute-start(f32[8,8,128]{2,1,0:T(8,128)S(1)} %get-tuple-element.39), channel_id=1, source_target_pairs={{0,1},{2,3},{4,5},{6,7},{1,0},{3,2},{5,4},{7,6},{8,9},{10,11},{12,... | collective-permute-start | bytes 98312 | tf_op jit(solution)/shard_map/ppermute | solution.py:641
  28.3 8.2 %collective-permute-start.8 = (f32[11,8,128]{2,1,0:T(8,128)S(1)}, f32[11,8,128]{2,1,0:T(8,128)S(1)}, u32[]{:S(2)}, u32[]{:S(2)}) collective-permute-start(f32[11,8,128]{2,1,0:T(8,128)S(1)} %get-tuple-element.47), channel_id=1, source_target_pairs={{0,7},{2,1},{4,3},{6,5},{7,0},{1,2},{3,4},{5,6},{8,15},{10,9},{12,... | collective-permute-start | bytes 135176 | tf_op jit(solution)/shard_map/ppermute | solution.py:641
  31.1 5.5 %collective-permute-start.9 = (f32[11,8,128]{2,1,0:T(8,128)S(1)}, f32[11,8,128]{2,1,0:T(8,128)S(1)}, u32[]{:S(2)}, u32[]{:S(2)}) collective-permute-start(f32[11,8,128]{2,1,0:T(8,128)S(1)} %get-tuple-element.48), channel_id=1, source_target_pairs={{0,1},{2,3},{4,5},{6,7},{1,0},{3,2},{5,4},{7,6},{8,9},{10,11},{12,... | collective-permute-start | bytes 135176 | tf_op jit(solution)/shard_map/ppermute | solution.py:641
  31.1 3.7 %collective-permute-start.10 = (f32[2,8,128]{2,1,0:T(8,128)S(1)}, f32[2,8,128]{2,1,0:T(8,128)S(1)}, u32[]{:S(2)}, u32[]{:S(2)}) collective-permute-start(f32[2,8,128]{2,1,0:T(8,128)S(1)} %get-tuple-element.46.own2), channel_id=1, source_target_pairs={{0,2},{1,3},{4,6},{5,7},{2,0},{3,1},{6,4},{7,5},{8,10},{9,11},{12,... | collective-permute-start | bytes 24584 | tf_op jit(solution)/shard_map/ppermute | solution.py:648
  31.1 5.4 %collective-permute-start.11 = (f32[2,8,128]{2,1,0:T(8,128)S(1)}, f32[2,8,128]{2,1,0:T(8,128)S(1)}, u32[]{:S(2)}, u32[]{:S(2)}) collective-permute-start(f32[2,8,128]{2,1,0:T(8,128)S(1)} %get-tuple-element.46.own2), channel_id=1, source_target_pairs={{0,6},{1,7},{4,2},{5,3},{6,0},{7,1},{2,4},{3,5},{8,14},{9,15},{12,... | collective-permute-start | bytes 24584 | tf_op jit(solution)/shard_map/ppermute | solution.py:648

commit v6 on v5

--- a/solution.py
+++ b/solution.py
@@ -373,8 +373,6 @@
     pack_edges(held, is_even("gx"), first, second)
 
 
-FAR = 2
-EDGES = 4
 EDGE_TILES = 2 * EDGE + 1
 
 
@@ -497,18 +495,8 @@
                 halo = value if halo is None else jnp.where((lane >> 3) == at, value, halo)
         edges.append([x0[0, 0, start : start + EDGE], x0[1, 0, start : start + EDGE], halo])
     top, bottom = (jnp.concatenate(parts, axis=0) for parts in edges)
-    edge_first[2:] = jnp.where(even, top, bottom)
-    edge_second[2:] = jnp.where(even, bottom, top)
-    strip = slice(FIELDS2, FIELDS2 + 1)
-    for t in (0, 1):
-        if t == 0:
-            before, after = prev_of(even, y_first, y_second, strip), next_of(even, y_first, y_second, strip)
-        else:
-            before, after = (
-                halo_tiles(even_x, corner_x, at + FIELDS2, at + FIELDS2 + 1)[0][2] for at in (0, PACKET)
-            )
-        edge_first[t : t + 1] = jnp.where(even, after, before)
-        edge_second[t : t + 1] = jnp.where(even, before, after)
+    edge_first[...] = jnp.where(even, top, bottom)
+    edge_second[...] = jnp.where(even, bottom, top)
 
 
 def fields2_kernel(rows, coarse, y_first, y_second, own_a, own_b, corner_a, corner_b, out):
@@ -524,7 +512,9 @@
         out[1, q : q + 1] = halo_tiles(even_x, packets, lo, lo + 1)[0][2]
 
 
-def level1_kernel(own, first, second, edge_a, edge_b, coef1, gain, packet, to_first, to_second, keep, y1, d1):
+def level1_kernel(
+    own, first, second, edge, edge_in, fields2, coef1, gain, packet, to_first, to_far, to_far2, edge_out, keep, y1, d1
+):
     b1, x1 = keep.at[0], keep.at[1]
     even = is_even("gy")
     for t in (0, 1):
@@ -541,14 +531,17 @@
     for t, (c, other, spread) in enumerate(packed_terms(x1, 1 + OWN, OWN, 1)):
         res = b1[t, here] - coef1[2, t, here] * c + coef1[1, t, here] * other + spread
         value = restrict_12([res[j : j + 1] for j in range(OWN)])
-        for ref in (packet, to_first, to_second):
+        for ref in (packet, to_first, to_far, to_far2):
             ref[t : t + 1] = value
-    to_first[FAR:] = edge_a[...]
-    to_second[FAR:] = edge_b[...]
+            if ref is to_far or ref is to_far2:
+                ref[2 + t : 3 + t] = fields2[t, 1:2]
+    to_far2[4:] = value
+    to_first[2:] = edge[...]
+    edge_out[...] = edge_in[...]
 
 
 def rest_kernel(
-    own2, near_a, near_b, far_a, far_b, gain, coef1, fields2, keep0, iterate, keep1, out, coef2, d1, b2, x2, y2, d2, xu, yu, x0, y0, d0
+    own2, near_a, near_b, far_a, far_b, edge_b, gain, coef1, fields2, keep0, iterate, keep1, out, coef2, d1, b2, x2, y2, d2, xu, yu, x0, y0, d0
 ):
     rows = out.shape[0] // (2 * Z)
     even = (sub_of() & 1) == 0
@@ -565,8 +558,8 @@
             prev_of(low, far_a, far_b, at),
         ]
         b2[t, 1 : SIZE2 - 1] = jnp.concatenate(parts, axis=0)
-        far = slice(FAR + t, FAR + t + 1)
-        parts = [prev_of(even_y, near_a, near_b, far), fields2[t], next_of(even_y, near_a, near_b, far)]
+        at = slice(2 + t, 3 + t)
+        parts = [next_of(low, far_a, far_b, at), fields2[t], prev_of(low, far_a, far_b, at)]
         inverse, other, _ = packed_jacobian(*split_fields2(jnp.concatenate(parts, axis=0)), 2)
         coef2[0, t, 1 : SIZE2 - 1] = inverse
         coef2[1, t, 1 : SIZE2 - 1] = other
@@ -595,14 +588,12 @@
     packed_step(1, coef1, shift, b1, xu, yu, d1, 1, n, CARRY2, g2)
 
     g0, g1, g2 = (gain[i] for i in range(3))
-    last = EDGES + 2 * EDGE
     for i in (0, 1):
         for at, take in ((HALO0 - EDGE, prev_of), (HALO0 + rows, next_of)):
-            strip = slice(EDGES + i * EDGE, EDGES + (i + 1) * EDGE)
-            x0[i, 0, at : at + EDGE] = take(even_y, near_a, near_b, strip)
-            sides = take(even_y, near_a, near_b, slice(last, last + 1))
+            whole = take(even_y, near_a.at[2:], edge_b, slice(0, EDGE_TILES))
+            x0[i, 0, at : at + EDGE] = whole[i * EDGE : (i + 1) * EDGE]
             for j in range(EDGE):
-                x0[i, 1, at + j : at + j + 1] = roll_x(sides, -(4 + 8 * (i * EDGE + j)))
+                x0[i, 1, at + j : at + j + 1] = roll_x(whole[2 * EDGE :], -(4 + 8 * (i * EDGE + j)))
         for t in (0, 1):
             x0[i, t, HALO0 : HALO0 + rows] = iterate[i, t]
     for t in (0, 1):
@@ -691,7 +682,7 @@
         *call(pack_corner_kernel, [(tiles, Z, X), (tiles, Z, X)], [(PER * tiles, Z, X)], *y_packets), "gx"
     )
 
-    strip, edge = (2 * OWN, Z, X), (2 + EDGE_TILES, Z, X)
+    strip, edge = (2 * OWN, Z, X), (EDGE_TILES, Z, X)
     pair0 = (2, 2, total0, Z, X)
     keep0, powers, sources = call(
         functools.partial(level0_kernel, rows),
@@ -727,20 +718,21 @@
     b_packets = exchange(first, second, "gy")
 
     one, two, up = (2, SIZE1, Z, X), (2, SIZE2, Z, X), (2, SIZE_UP, Z, X)
-    near = (EDGES + EDGE_TILES, Z, X)
-    packet, first, second, keep1 = call(
+    edge_in = swap(edge_b, "gy", 1)
+    packet, first, to_far, to_far2, edge_out, keep1 = call(
         level1_kernel,
-        [(2, Z, X), near, near, (2, *one)],
+        [(2, Z, X), (2 + EDGE_TILES, Z, X), (4, Z, X), (5, Z, X), edge, (2, *one)],
         [one, one],
         own,
         *b_packets,
         edge_a,
-        edge_b,
+        edge_in,
+        fields2,
         coef1,
         gain,
     )
-    far = (swap_far(packet, "gy", 1), swap_far(packet, "gy", -1))
-    near = exchange(first, second, "gy")
+    near = (swap(first, "gy", -1), swap(packet, "gy", 1))
+    far = (swap_far(to_far, "gy", 1), swap_far(to_far2, "gy", -1))
 
     (out,) = call(
         rest_kernel,
@@ -749,6 +741,7 @@
         packet,
         *near,
         *far,
+        edge_out,
         gain,
         coef1,
         fields2,

time: 39.4 us -> 39.5 us (level)
  starting transfers between devices: 21 us -> 23.1 us
  waiting for transfers between devices: 10.6 us -> 8.61 us
    ppermute x10 -> x11, starting transfers between devices: 15.9 us -> 19.5 us  [swap(): return lax.ppermute(value, axis, pairs + [(j, i) for i, j in pairs])]
    ppermute x2, waiting for transfers between devices: 2.79 us -> 0.93 us  [swap_far(): return lax.ppermute(value, axis, pairs + [(j, i) for i, j in pairs])]
    ppermute x2, starting transfers between devices: 2.59 us -> 0.99 us  [swap_far(): return lax.ppermute(value, axis, pairs + [(j, i) for i, j in pairs])]
    ppermute x10 -> x11, waiting for transfers between devices: 7.66 us -> 7.56 us  [swap(): return lax.ppermute(value, axis, pairs + [(j, i) for i, j in pairs])]
  transfers between devices with their start and end apart: 13 -> 14, of which waited for: 7 -> 6; matrix products, arithmetic and copies ran while one was open for 0% -> 0% of each run, Pallas kernels for 7% -> 7%
where the time goes in v6:
time: 39.5 us; the launch traced here: 39.3 us
  starting transfers between devices  23.1 us (58%)
  waiting for transfers between devices  8.61 us (22%)
  Pallas kernels  7.51 us (19%)
    ppermute x11, starting transfers between devices, swap(): return lax.ppermute(value, axis, pairs + [(j, i) for i, j in pairs])  19.5 us
    ppermute x11, waiting for transfers between devices, swap(): return lax.ppermute(value, axis, pairs + [(j, i) for i, j in pairs])  7.56 us
    pallas_call x10, Pallas kernels, call(): pl.pallas_call(kernel, out_shape=out, in_specs=[pl.BlockSpec(memory_space...  7.51 us
    all_to_all x1, starting transfers between devices, body(): spread = lax.all_to_all(spread, ('gx', 'gy'), 0, 0, tiled=True)  2.57 us
    ppermute x2, starting transfers between devices, swap_far(): return lax.ppermute(value, axis, pairs + [(j, i) for i, j in pairs])  0.99 us
    ppermute x2, waiting for transfers between devices, swap_far(): return lax.ppermute(value, axis, pairs + [(j, i) for i, j in pairs])  0.93 us
  transfers between devices with their start and end apart: 14, of which 6 were waited for; matrix products, arithmetic and copies ran while one was open for 0% of the time, Pallas kernels for 7%

profile of v6, /device:TPU:0, one launch (start us, length us, event | category | flops | bytes accessed | tf_op | source)
XLA Modules:
  0.0 39.3 jit_solution(4010734709798840020)
XLA Ops:
  0.0 1.4 %shard_map.46 = (f32[29,8,128]{2,1,0:T(8,128)S(1)}, f32[29,8,128]{2,1,0:T(8,128)S(1)}, f32[6,16,8,128]{3,2,1,0:T(8,128)S(1)}, f32[9,8,128]{2,1,0:T(8,128)S(1)}) custom-call(f32[256,128]{1,0:T(8,128)} %bitcast.5, f32[256,128]{1,0:T(8,128)} %bitcast.6, f32[128,128]{1,0:T(8,128)} %bitcast.7, f32[128,128]{1,0:T(8,128)} %bitcast.8), custom_call_target="tpu_custom_call" | custom-call | tf_op jit(solution)/shard_map/pallas_call | solution.py:618
  1.4 6.1 %collective-permute-start = (f32[29,8,128]{2,1,0:T(8,128)S(1)}, f32[29,8,128]{2,1,0:T(8,128)S(1)}, u32[]{:S(2)}, u32[]{:S(2)}) collective-permute-start(f32[29,8,128]{2,1,0:T(8,128)S(1)} %get-tuple-element.31), channel_id=1, source_target_pairs={{0,7},{2,1},{4,3},{6,5},{7,0},{1,2},{3,4},{5,6},{8,15},{10,9},{12,... | collective-permute-start | bytes 356360 | tf_op jit(solution)/shard_map/ppermute | solution.py:632
  7.5 0.2 shard_map.47
  7.7 0.7 %collective-permute-start.2 = (f32[35,8,128]{2,1,0:T(8,128)S(1)}, f32[35,8,128]{2,1,0:T(8,128)S(1)}, u32[]{:S(2)}, u32[]{:S(2)}) collective-permute-start(f32[35,8,128]{2,1,0:T(8,128)S(1)} %get-tuple-element.34), channel_id=1, source_target_pairs={{0,24},{16,8},{24,0},{8,16},{1,25},{17,9},{25,1},{9,17},{2,26},{18... | collective-permute-start | bytes 430088 | tf_op jit(solution)/shard_map/ppermute | solution.py:632
  8.4 1.0 %collective-permute-start.3 = (f32[35,8,128]{2,1,0:T(8,128)S(1)}, f32[35,8,128]{2,1,0:T(8,128)S(1)}, u32[]{:S(2)}, u32[]{:S(2)}) collective-permute-start(f32[35,8,128]{2,1,0:T(8,128)S(1)} %get-tuple-element.35), channel_id=1, source_target_pairs={{0,8},{16,24},{8,0},{24,16},{1,9},{17,25},{9,1},{25,17},{2,10},{18... | collective-permute-start | bytes 430088 | tf_op jit(solution)/shard_map/ppermute | solution.py:632
  9.4 0.8 %shard_map.50 = f32[32,4,128]{2,1,0:T(4,128)} custom-call(f32[6,16,8,128]{3,2,1,0:T(8,128)S(1)} %get-tuple-element.30.main, f32[9,8,128]{2,1,0:T(8,128)S(1)} %get-tuple-element.33.coarse), custom_call_target="tpu_custom_call" | custom-call | tf_op jit(solution)/shard_map/pallas_call | solution.py:618
  10.2 2.6 %all-to-all-start = ((f32[32,4,128]{2,1,0:T(4,128)}), f32[32,4,128]{2,1,0:T(4,128)S(1)}, u32[]{:S(2)}, u32[]{:S(2)}) async-start(f32[32,4,128]{2,1,0:T(4,128)} %shard_map.50), calls=%async_computation | async-start | bytes 131072 | tf_op jit(solution)/shard_map/all_to_all | solution.py:667
  12.8 0.5 %collective-permute-done.1.y_second = f32[29,8,128]{2,1,0:T(8,128)S(1)} collective-permute-done((f32[29,8,128]{2,1,0:T(8,128)S(1)}, f32[29,8,128]{2,1,0:T(8,128)S(1)}, u32[]{:S(2)}, u32[]{:S(2)}) %collective-permute-start.1) | collective-permute-done | bytes 118816 | tf_op jit(solution)/shard_map/ppermute | solution.py:632
  13.2 0.2 shard_map.48
  13.4 1.0 %collective-permute-start.4 = (f32[20,8,128]{2,1,0:T(8,128)S(1)}, f32[20,8,128]{2,1,0:T(8,128)S(1)}, u32[]{:S(2)}, u32[]{:S(2)}) collective-permute-start(f32[20,8,128]{2,1,0:T(8,128)S(1)} %get-tuple-element.36), channel_id=1, source_target_pairs={{0,24},{16,8},{24,0},{8,16},{1,25},{17,9},{25,1},{9,17},{2,26},{18... | collective-permute-start | bytes 245768 | tf_op jit(solution)/shard_map/ppermute | solution.py:632
  14.4 0.7 %collective-permute-start.5 = (f32[20,8,128]{2,1,0:T(8,128)S(1)}, f32[20,8,128]{2,1,0:T(8,128)S(1)}, u32[]{:S(2)}, u32[]{:S(2)}) collective-permute-start(f32[20,8,128]{2,1,0:T(8,128)S(1)} %get-tuple-element.37), channel_id=1, source_target_pairs={{0,8},{16,24},{8,0},{24,16},{1,9},{17,25},{9,1},{25,17},{2,10},{18... | collective-permute-start | bytes 245768 | tf_op jit(solution)/shard_map/ppermute | solution.py:632
  15.1 3.5 %collective-permute-done.4.corner_a = f32[20,8,128]{2,1,0:T(8,128)S(1)} collective-permute-done((f32[20,8,128]{2,1,0:T(8,128)S(1)}, f32[20,8,128]{2,1,0:T(8,128)S(1)}, u32[]{:S(2)}, u32[]{:S(2)}) %collective-permute-start.4) | collective-permute-done | bytes 81952 | tf_op jit(solution)/shard_map/ppermute | solution.py:632
  18.6 1.3 %shard_map.49 = (f32[6,2,24,8,128]{4,3,2,1,0:T(8,128)S(1)}, f32[2,2,2,24,8,128]{5,4,3,2,1,0:T(8,128)S(1)}, f32[4,2,4,8,128]{4,3,2,1,0:T(8,128)S(1)}) custom-call(f32[6,16,8,128]{3,2,1,0:T(8,128)S(1)} %get-tuple-element.30.main, f32[29,8,128]{2,1,0:T(8,128)S(1)} %collective-permute-done.y_first, f32[29,8,128]{2,1,0:T(8,128)S(1)} %collective-permute-done.1.y_second, ...), custom_call_target="tpu_custom_call" | custom-call | tf_op jit(solution)/shard_map/pallas_call | solution.py:618
  20.2 3.7 %collective-permute-start.6 = (f32[8,8,128]{2,1,0:T(8,128)S(1)}, f32[8,8,128]{2,1,0:T(8,128)S(1)}, u32[]{:S(2)}, u32[]{:S(2)}) collective-permute-start(f32[8,8,128]{2,1,0:T(8,128)S(1)} %get-tuple-element.40), channel_id=1, source_target_pairs={{0,7},{2,1},{4,3},{6,5},{7,0},{1,2},{3,4},{5,6},{8,15},{10,9},{12,... | collective-permute-start | bytes 98312 | tf_op jit(solution)/shard_map/ppermute | solution.py:632
  24.0 2.1 %collective-permute-start.8 = (f32[7,8,128]{2,1,0:T(8,128)S(1)}, f32[7,8,128]{2,1,0:T(8,128)S(1)}, u32[]{:S(2)}, u32[]{:S(2)}) collective-permute-start(f32[7,8,128]{2,1,0:T(8,128)S(1)} %get-tuple-element.46), channel_id=1, source_target_pairs={{0,1},{2,3},{4,5},{6,7},{1,0},{3,2},{5,4},{7,6},{8,9},{10,11},{12,... | collective-permute-start | bytes 86024 | tf_op jit(solution)/shard_map/ppermute | solution.py:632
  26.2 1.9 %collective-permute-done.8.edge_in = f32[7,8,128]{2,1,0:T(8,128)S(1)} collective-permute-done((f32[7,8,128]{2,1,0:T(8,128)S(1)}, f32[7,8,128]{2,1,0:T(8,128)S(1)}, u32[]{:S(2)}, u32[]{:S(2)}) %collective-permute-start.8) | collective-permute-done | bytes 28704 | tf_op jit(solution)/shard_map/ppermute | solution.py:632
  28.1 0.6 %shard_map.54 = (f32[2,8,128]{2,1,0:T(8,128)S(1)}, f32[9,8,128]{2,1,0:T(8,128)S(1)}, f32[4,8,128]{2,1,0:T(8,128)S(1)}, f32[5,8,128]{2,1,0:T(8,128)S(1)}, f32[7,8...) custom-call(f32[2,4,8,128]{3,2,1,0:T(8,128)S(1)} %get-tuple-element.39.own, ...), custom_call_target="tpu_custom_call" | custom-call | tf_op jit(solution)/shard_map/pallas_call | solution.py:618
  28.6 2.5 %collective-permute-start.9 = (f32[9,8,128]{2,1,0:T(8,128)S(1)}, f32[9,8,128]{2,1,0:T(8,128)S(1)}, u32[]{:S(2)}, u32[]{:S(2)}) collective-permute-start(f32[9,8,128]{2,1,0:T(8,128)S(1)} %get-tuple-element.49), channel_id=1, source_target_pairs={{0,7},{2,1},{4,3},{6,5},{7,0},{1,2},{3,4},{5,6},{8,15},{10,9},{12,... | collective-permute-start | bytes 110600 | tf_op jit(solution)/shard_map/ppermute | solution.py:632
  31.1 0.2 collective-permute-start.12
  31.3 0.8 %collective-permute-start.11 = (f32[4,8,128]{2,1,0:T(8,128)S(1)}, f32[4,8,128]{2,1,0:T(8,128)S(1)}, u32[]{:S(2)}, u32[]{:S(2)}) collective-permute-start(f32[4,8,128]{2,1,0:T(8,128)S(1)} %get-tuple-element.50), channel_id=1, source_target_pairs={{0,2},{1,3},{4,6},{5,7},{2,0},{3,1},{6,4},{7,5},{8,10},{9,11},{12,... | collective-permute-start | bytes 49160 | tf_op jit(solution)/shard_map/ppermute | solution.py:639
  32.1 1.9 %collective-permute-start.10 = (f32[2,8,128]{2,1,0:T(8,128)S(1)}, f32[2,8,128]{2,1,0:T(8,128)S(1)}, u32[]{:S(2)}, u32[]{:S(2)}) collective-permute-start(f32[2,8,128]{2,1,0:T(8,128)S(1)} %get-tuple-element.48.own2), channel_id=1, source_target_pairs={{0,1},{2,3},{4,5},{6,7},{1,0},{3,2},{5,4},{7,6},{8,9},{10,11},{12,... | collective-permute-start | bytes 24584 | tf_op jit(solution)/shard_map/ppermute | solution.py:632
  34.0 1.7 %collective-permute-done.10.near_b = f32[2,8,128]{2,1,0:T(8,128)S(1)} collective-permute-done((f32[2,8,128]{2,1,0:T(8,128)S(1)}, f32[2,8,128]{2,1,0:T(8,128)S(1)}, u32[]{:S(2)}, u32[]{:S(2)}) %collective-permute-start.10) | collective-permute-done | bytes 8224 | tf_op jit(solution)/shard_map/ppermute | solution.py:632
  35.7 0.9 %collective-permute-done.12.far_b = f32[5,8,128]{2,1,0:T(8,128)S(1)} collective-permute-done((f32[5,8,128]{2,1,0:T(8,128)S(1)}, f32[5,8,128]{2,1,0:T(8,128)S(1)}, u32[]{:S(2)}, u32[]{:S(2)}) %collective-permute-start.12) | collective-permute-done | bytes 20512 | tf_op jit(solution)/shard_map/ppermute | solution.py:639
  36.7 2.6 %shard_map.55 = f32[256,128]{1,0:T(8,128)} custom-call(f32[2,8,128]{2,1,0:T(8,128)S(1)} %get-tuple-element.48.own2, f32[9,8,128]{2,1,0:T(8,128)S(1)} %collective-permute-done.9.near_a, f32[2,8,128]{2,1,0:T(8,128)S(1)} %collective-permute-done.10.near_b, f32[4,8,128]{2,1,0:T(8,128)S(1)} %collective-permute-done.11.far_a, ...), custom_call_target="tpu_custom_call" | custom-call | tf_op jit(solution)/shard_map/pallas_call | solution.py:618
  (14 shorter events, 0.5 us)
Async XLA Ops:
  1.4 11.4 %collective-permute-start = (f32[29,8,128]{2,1,0:T(8,128)S(1)}, f32[29,8,128]{2,1,0:T(8,128)S(1)}, u32[]{:S(2)}, u32[]{:S(2)}) collective-permute-start(f32[29,8,128]{2,1,0:T(8,128)S(1)} %get-tuple-element.31), channel_id=1, source_target_pairs={{0,7},{2,1},{4,3},{6,5},{7,0},{1,2},{3,4},{5,6},{8,15},{10,9},{12,... | collective-permute-start | bytes 356360 | tf_op jit(solution)/shard_map/ppermute | solution.py:632
  7.5 5.8 %collective-permute-start.1 = (f32[29,8,128]{2,1,0:T(8,128)S(1)}, f32[29,8,128]{2,1,0:T(8,128)S(1)}, u32[]{:S(2)}, u32[]{:S(2)}) collective-permute-start(f32[29,8,128]{2,1,0:T(8,128)S(1)} %get-tuple-element.32), channel_id=1, source_target_pairs={{0,1},{2,3},{4,5},{6,7},{1,0},{3,2},{5,4},{7,6},{8,9},{10,11},{12,... | collective-permute-start | bytes 356360 | tf_op jit(solution)/shard_map/ppermute | solution.py:632
  7.7 7.4 %collective-permute-start.2 = (f32[35,8,128]{2,1,0:T(8,128)S(1)}, f32[35,8,128]{2,1,0:T(8,128)S(1)}, u32[]{:S(2)}, u32[]{:S(2)}) collective-permute-start(f32[35,8,128]{2,1,0:T(8,128)S(1)} %get-tuple-element.34), channel_id=1, source_target_pairs={{0,24},{16,8},{24,0},{8,16},{1,25},{17,9},{25,1},{9,17},{2,26},{18... | collective-permute-start | bytes 430088 | tf_op jit(solution)/shard_map/ppermute | solution.py:632
  8.4 6.7 %collective-permute-start.3 = (f32[35,8,128]{2,1,0:T(8,128)S(1)}, f32[35,8,128]{2,1,0:T(8,128)S(1)}, u32[]{:S(2)}, u32[]{:S(2)}) collective-permute-start(f32[35,8,128]{2,1,0:T(8,128)S(1)} %get-tuple-element.35), channel_id=1, source_target_pairs={{0,8},{16,24},{8,0},{24,16},{1,9},{17,25},{9,1},{25,17},{2,10},{18... | collective-permute-start | bytes 430088 | tf_op jit(solution)/shard_map/ppermute | solution.py:632
  10.2 9.9 %all-to-all-start = ((f32[32,4,128]{2,1,0:T(4,128)}), f32[32,4,128]{2,1,0:T(4,128)S(1)}, u32[]{:S(2)}, u32[]{:S(2)}) async-start(f32[32,4,128]{2,1,0:T(4,128)} %shard_map.50), calls=%async_computation | async-start | bytes 131072 | tf_op jit(solution)/shard_map/all_to_all | solution.py:667
  13.4 5.1 %collective-permute-start.4 = (f32[20,8,128]{2,1,0:T(8,128)S(1)}, f32[20,8,128]{2,1,0:T(8,128)S(1)}, u32[]{:S(2)}, u32[]{:S(2)}) collective-permute-start(f32[20,8,128]{2,1,0:T(8,128)S(1)} %get-tuple-element.36), channel_id=1, source_target_pairs={{0,24},{16,8},{24,0},{8,16},{1,25},{17,9},{25,1},{9,17},{2,26},{18... | collective-permute-start | bytes 245768 | tf_op jit(solution)/shard_map/ppermute | solution.py:632
  14.4 4.1 %collective-permute-start.5 = (f32[20,8,128]{2,1,0:T(8,128)S(1)}, f32[20,8,128]{2,1,0:T(8,128)S(1)}, u32[]{:S(2)}, u32[]{:S(2)}) collective-permute-start(f32[20,8,128]{2,1,0:T(8,128)S(1)} %get-tuple-element.37), channel_id=1, source_target_pairs={{0,8},{16,24},{8,0},{24,16},{1,9},{17,25},{9,1},{25,17},{2,10},{18... | collective-permute-start | bytes 245768 | tf_op jit(solution)/shard_map/ppermute | solution.py:632
  20.2 7.9 %collective-permute-start.6 = (f32[8,8,128]{2,1,0:T(8,128)S(1)}, f32[8,8,128]{2,1,0:T(8,128)S(1)}, u32[]{:S(2)}, u32[]{:S(2)}) collective-permute-start(f32[8,8,128]{2,1,0:T(8,128)S(1)} %get-tuple-element.40), channel_id=1, source_target_pairs={{0,7},{2,1},{4,3},{6,5},{7,0},{1,2},{3,4},{5,6},{8,15},{10,9},{12,... | collective-permute-start | bytes 98312 | tf_op jit(solution)/shard_map/ppermute | solution.py:632
  23.8 4.2 %collective-permute-start.7 = (f32[8,8,128]{2,1,0:T(8,128)S(1)}, f32[8,8,128]{2,1,0:T(8,128)S(1)}, u32[]{:S(2)}, u32[]{:S(2)}) collective-permute-start(f32[8,8,128]{2,1,0:T(8,128)S(1)} %get-tuple-element.41), channel_id=1, source_target_pairs={{0,1},{2,3},{4,5},{6,7},{1,0},{3,2},{5,4},{7,6},{8,9},{10,11},{12,... | collective-permute-start | bytes 98312 | tf_op jit(solution)/shard_map/ppermute | solution.py:632
  24.0 4.0 %collective-permute-start.8 = (f32[7,8,128]{2,1,0:T(8,128)S(1)}, f32[7,8,128]{2,1,0:T(8,128)S(1)}, u32[]{:S(2)}, u32[]{:S(2)}) collective-permute-start(f32[7,8,128]{2,1,0:T(8,128)S(1)} %get-tuple-element.46), channel_id=1, source_target_pairs={{0,1},{2,3},{4,5},{6,7},{1,0},{3,2},{5,4},{7,6},{8,9},{10,11},{12,... | collective-permute-start | bytes 86024 | tf_op jit(solution)/shard_map/ppermute | solution.py:632
  28.6 8.0 %collective-permute-start.9 = (f32[9,8,128]{2,1,0:T(8,128)S(1)}, f32[9,8,128]{2,1,0:T(8,128)S(1)}, u32[]{:S(2)}, u32[]{:S(2)}) collective-permute-start(f32[9,8,128]{2,1,0:T(8,128)S(1)} %get-tuple-element.49), channel_id=1, source_target_pairs={{0,7},{2,1},{4,3},{6,5},{7,0},{1,2},{3,4},{5,6},{8,15},{10,9},{12,... | collective-permute-start | bytes 110600 | tf_op jit(solution)/shard_map/ppermute | solution.py:632
  31.1 5.6 %collective-permute-start.12 = (f32[5,8,128]{2,1,0:T(8,128)S(1)}, f32[5,8,128]{2,1,0:T(8,128)S(1)}, u32[]{:S(2)}, u32[]{:S(2)}) collective-permute-start(f32[5,8,128]{2,1,0:T(8,128)S(1)} %get-tuple-element.51), channel_id=1, source_target_pairs={{0,6},{1,7},{4,2},{5,3},{6,0},{7,1},{2,4},{3,5},{8,14},{9,15},{12,... | collective-permute-start | bytes 61448 | tf_op jit(solution)/shard_map/ppermute | solution.py:639
  31.3 4.4 %collective-permute-start.11 = (f32[4,8,128]{2,1,0:T(8,128)S(1)}, f32[4,8,128]{2,1,0:T(8,128)S(1)}, u32[]{:S(2)}, u32[]{:S(2)}) collective-permute-start(f32[4,8,128]{2,1,0:T(8,128)S(1)} %get-tuple-element.50), channel_id=1, source_target_pairs={{0,2},{1,3},{4,6},{5,7},{2,0},{3,1},{6,4},{7,5},{8,10},{9,11},{12,... | collective-permute-start | bytes 49160 | tf_op jit(solution)/shard_map/ppermute | solution.py:639
  32.1 3.7 %collective-permute-start.10 = (f32[2,8,128]{2,1,0:T(8,128)S(1)}, f32[2,8,128]{2,1,0:T(8,128)S(1)}, u32[]{:S(2)}, u32[]{:S(2)}) collective-permute-start(f32[2,8,128]{2,1,0:T(8,128)S(1)} %get-tuple-element.48.own2), channel_id=1, source_target_pairs={{0,1},{2,3},{4,5},{6,7},{1,0},{3,2},{5,4},{7,6},{8,9},{10,11},{12,... | collective-permute-start | bytes 24584 | tf_op jit(solution)/shard_map/ppermute | solution.py:632

commit v7 on v6

--- a/solution.py
+++ b/solution.py
@@ -308,7 +308,7 @@
     return jnp.where(low, both, roll_z(both, 2)), jnp.where(low, roll_z(both, -2), both)
 
 
-def spread_kernel(main, coarse, out):
+def write_spread(main, coarse, out):
     lane = lax.broadcasted_iota(jnp.int32, (1, X), 1)
     u, v, f, k = (main[i] for i in (0, 1, 4, 5))
     cross, squared, inv_u, inv_v, _, _ = jacobian(u, v, f, k, 0)
@@ -358,11 +358,15 @@
     return out
 
 
-def pack_own_kernel(rows, main, coarse, first, second, held):
+def pack_own_kernel(rows, main, coarse, first, second, spread, held, copies, sem):
+    write_spread(main, coarse, copies)
+    copy = pltpu.make_async_copy(copies, spread, sem)
+    copy.start()
     for i in range(6):
         held[i * rows : (i + 1) * rows] = main[i]
     held[6 * rows : 6 * rows + 2 * OWN + 1] = coarse[...]
     pack_edges(held, is_even("gx"), first, second)
+    copy.wait()
 
 
 def pack_corner_kernel(y_first, y_second, first, second, held):
@@ -376,78 +380,174 @@
 EDGE_TILES = 2 * EDGE + 1
 
 
-def level0_kernel(
-    rows, main, y_first, y_second, own_a, own_b, corner_a, corner_b, keep, powers, sources, fields, diag, y0
+def level0_setup(fields, keep, diag, power, r, n):
+    at = pl.ds(r, n)
+    u, nb_u = neighbour_sums(lambda t, a, m: fields[0, t, pl.ds(a, m)], r, n, 1)
+    v, nb_v = neighbour_sums(lambda t, a, m: fields[1, t, pl.ds(a, m)], r, n, 1)
+    for t in (0, 1):
+        f, k = fields[4, t, at], fields[5, t, at]
+        cross, squared, inv_u, inv_v, first, second = jacobian(u[t], v[t], f, k, 0)
+        react = u[t] * squared
+        b_u = DIFF[0] * (nb_u[t] - 6.0 * u[t]) - INV_STEP * (u[t] - fields[2, t, at]) - react + f * (1.0 - u[t])
+        b_v = DIFF[1] * (nb_v[t] - 6.0 * v[t]) - INV_STEP * (v[t] - fields[3, t, at]) + react - (f + k) * v[t]
+        for i, value in enumerate((cross, squared, inv_u, inv_v, b_u, b_v)):
+            keep[i, t, at] = value
+        for i, value in enumerate((first, second)):
+            diag[i, t, at] = value
+        for i, value in enumerate((inv_u * b_u, inv_v * b_v)):
+            power[i, t, at] = value
+
+
+def level0_power(keep, source, target, r, n):
+    for i, values in enumerate(next_power(keep, source, r, n)):
+        for t in (0, 1):
+            target[i, t, pl.ds(r, n)] = values[t]
+
+
+def level0_down(keep, diag, y1, y2, sources, r, n):
+    at = pl.ds(r, n)
+    last = next_power(keep, y2, r, n)
+    for t in (0, 1):
+        both = [diag[i, t, at] for i in (0, 1)]
+        parts = [[keep[4 + i, t, at] for i in (0, 1)]]
+        parts += [[both[i] * power[i, t, at] for i in (0, 1)] for power in (y1, y2)]
+        parts.append([both[i] * last[i][t] for i in (0, 1)])
+        for q, part in enumerate(parts):
+            u, v = (pair_rows(value) for value in part)
+            for j in range(n // 4):
+                value = restrict_01(u[2 * j : 2 * j + 2], v[2 * j : 2 * j + 2])
+                sources[q, t, pl.ds((r - HALO0) // 4 + j, 1)] = value
+
+
+def inner(rows, lost):
+    return slice(HALO0 + lost, HALO0 + rows - lost)
+
+
+def ends(rows, lo, hi):
+    total = rows + 2 * HALO0
+    return slice(lo, hi), slice(total - hi, total - lo)
+
+
+def put_ends(target, rows, lo, hi, source):
+    n = hi - lo
+    for at, part in zip(ends(rows, lo, hi), (slice(0, n), slice(n, 2 * n))):
+        for i in range(target.shape[0]):
+            for t in (0, 1):
+                target[i, t, at] = source[i, t, part]
+
+
+def take_ends(source, rows, lo, hi, target):
+    n = hi - lo
+    for at, part in zip(ends(rows, lo, hi), (slice(0, n), slice(n, 2 * n))):
+        for i in range(source.shape[0]):
+            for t in (0, 1):
+                target[i, t, part] = source[i, t, at]
+
+
+def level0_inner_kernel(rows, main, own_a, own_b, keep_in, y0_in, y1_in, y2_in, diag_in, sources_in, *scratch):
+    fields, keep, diag, y0, y1, y2 = scratch
+    even_x = is_even("gx")
+    for i in range(6):
+        fields[i, 0, HALO0 : HALO0 + rows] = main[i]
+        for a, b, value in halo_tiles(even_x, (own_a, own_b), i * rows, (i + 1) * rows):
+            fields[i, 1, HALO0 + a : HALO0 + b] = value
+    first = HALO0 + 1
+    level0_setup(fields, keep, diag, y0, first, rows - 2)
+    level0_power(keep, y0, y1, first + 1, rows - 4)
+    level0_power(keep, y1, y2, first + 2, rows - 6)
+    level0_down(keep, diag, y1, y2, sources_in, first + 3, rows - 8)
+    for source, target, lost in ((keep, keep_in, 1), (y1, y1_in, 2), (y2, y2_in, 3)):
+        for i in range(source.shape[0]):
+            for t in (0, 1):
+                target[i, t] = source[i, t, inner(rows, lost)]
+    take_ends(y0, rows, HALO0 + 1, HALO0 + 3, y0_in)
+    take_ends(diag, rows, HALO0 + 1, HALO0 + 4, diag_in)
+
+
+def level0_outer_kernel(
+    rows,
+    main,
+    y_first,
+    y_second,
+    own_a,
+    own_b,
+    corner_a,
+    corner_b,
+    keep_in,
+    y0_in,
+    y1_in,
+    y2_in,
+    diag_in,
+    sources_in,
+    keep_out,
+    y1_out,
+    y2_out,
+    sources,
+    edges,
+    *scratch,
 ):
+    fields, keep, diag, y0, y1, y2 = scratch
     even, even_x = is_even("gy"), is_even("gx")
     total = rows + 2 * HALO0
-    own_x, corner_x = (own_a, own_b), (corner_a, corner_b)
+    near = HALO0 + 2
     for i, halo in enumerate(HALOS):
         strip = slice(STARTS[i], STARTS[i] + halo)
         skip = HALO0 - halo
         fields[i, 0, skip:HALO0] = prev_of(even, y_first, y_second, strip)
-        fields[i, 0, HALO0 : HALO0 + rows] = main[i]
+        fields[i, 0, HALO0:near] = main[i, 0:2]
+        fields[i, 0, total - near : total - HALO0] = main[i, rows - 2 : rows]
         fields[i, 0, HALO0 + rows : total - skip] = next_of(even, y_first, y_second, strip)
         for packets, lo, n, at in (
-            (corner_x, STARTS[i], halo, skip),
-            (own_x, i * rows, rows, HALO0),
-            (corner_x, PACKET + STARTS[i], halo, HALO0 + rows),
+            ((corner_a, corner_b), STARTS[i], halo, skip),
+            ((own_a, own_b), i * rows, 2, HALO0),
+            ((own_a, own_b), (i + 1) * rows - 2, 2, total - near),
+            ((corner_a, corner_b), PACKET + STARTS[i], halo, HALO0 + rows),
         ):
             for a, b, value in halo_tiles(even_x, packets, lo, lo + n):
                 fields[i, 1, at + a : at + b] = value
-
-    def setup(r, n):
-        at = pl.ds(r, n)
-        u, nb_u = neighbour_sums(lambda t, a, m: fields[0, t, pl.ds(a, m)], r, n, 1)
-        v, nb_v = neighbour_sums(lambda t, a, m: fields[1, t, pl.ds(a, m)], r, n, 1)
+    for at, part in zip(ends(rows, 5, 8), (slice(0, 3), slice(rows - 5, rows - 2))):
+        for i in range(6):
+            for t in (0, 1):
+                keep[i, t, at] = keep_in[i, t, part]
+    put_ends(diag, rows, 5, 8, diag_in)
+    put_ends(y0, rows, 5, 7, y0_in)
+    for target, source, lost in ((y1, y1_in, 2), (y2, y2_in, 3)):
+        n = rows - 2 * lost
+        for at, part in zip(ends(rows, HALO0 + lost, HALO0 + lost + 2), (slice(0, 2), slice(n - 2, n))):
+            for i in (0, 1):
+                for t in (0, 1):
+                    target[i, t, at] = source[i, t, part]
+    for r in (1, total - 5):
+        level0_setup(fields, keep, diag, y0, r, 4)
+    for r in (2, total - 6):
+        level0_power(keep, y0, y1, r, 4)
+    for r in (3, total - 7):
+        level0_power(keep, y1, y2, r, 4)
+    for r in (4, total - 8):
+        level0_down(keep, diag, y1, y2, sources, r, 4)
+    for q in range(4):
         for t in (0, 1):
-            f, k = fields[4, t, at], fields[5, t, at]
-            cross, squared, inv_u, inv_v, first, second = jacobian(u[t], v[t], f, k, 0)
-            react = u[t] * squared
-            b_u = (
-                DIFF[0] * (nb_u[t] - 6.0 * u[t])
-                - INV_STEP * (u[t] - fields[2, t, at])
-                - react
-                + f * (1.0 - u[t])
-            )
-            b_v = (
-                DIFF[1] * (nb_v[t] - 6.0 * v[t]) - INV_STEP * (v[t] - fields[3, t, at]) + react - (f + k) * v[t]
-            )
-            for i, value in enumerate((cross, squared, inv_u, inv_v, b_u, b_v)):
-                keep[i, t, at] = value
-            diag[0, t, at] = first
-            diag[1, t, at] = second
-            y0[0, t, at] = inv_u * b_u
-            y0[1, t, at] = inv_v * b_v
-
-    rows_loop(1, total - 1, setup)
-    for p in (0, 1):
-
-        def power(r, n, p=p):
-            for i, values in enumerate(next_power(keep, powers.at[0] if p else y0, r, n)):
-                for t in (0, 1):
-                    powers[p, i, t, pl.ds(r, n)] = values[t]
-
-        rows_loop(2 + p, total - 2 - p, power)
-
-    def down(r, n):
-        at = pl.ds(r, n)
-        last = next_power(keep, powers.at[1], r, n)
-        for t in (0, 1):
-            both = [diag[i, t, at] for i in (0, 1)]
-            parts = [[keep[4 + i, t, at] for i in (0, 1)]]
-            parts += [[both[i] * powers[p, i, t, at] for i in (0, 1)] for p in (0, 1)]
-            parts.append([both[i] * last[i][t] for i in (0, 1)])
-            for q, part in enumerate(parts):
-                u, v = (pair_rows(value) for value in part)
-                for j in range(n // 4):
-                    value = restrict_01(u[2 * j : 2 * j + 2], v[2 * j : 2 * j + 2])
-                    sources[q, t, pl.ds((r - HALO0) // 4 + j, 1)] = value
-
-    rows_loop(HALO0, HALO0 + rows, down)
-
-
-def combine_kernel(sources, spread, own, first, second, gain):
+            sources[q, t, 1 : OWN - 1] = sources_in[q, t, 1 : OWN - 1]
+    take_ends(keep, rows, 1, 5, keep_out)
+    take_ends(y1, rows, 4, 6, y1_out)
+    take_ends(y2, rows, 4, 7, y2_out)
+    for p, power in enumerate((y0, y1, y2)):
+        for side, start in enumerate((HALO0, HALO0 + rows - EDGE)):
+            edges[p, side] = pack_rows(power, start)
+
+
+def pack_rows(x, start):
+    lane = lane_of()
+    halo = None
+    for i in (0, 1):
+        for j in range(EDGE):
+            at = i * EDGE + j
+            value = roll_x(x[i, 1, start + j : start + j + 1], 4 + 8 * at)
+            halo = value if halo is None else jnp.where((lane >> 3) == at, value, halo)
+    return jnp.concatenate([x[i, 0, start : start + EDGE] for i in (0, 1)] + [halo], axis=0)
+
+
+def combine_kernel(sources, edges, spread, own, first, second, edge_first, edge_second, gain):
     write_gains(jnp.max(spread[...], axis=0)[0:1], gain)
     p0, p1, p2 = (gain[POWERS + i] for i in range(3))
     for t in (0, 1):
@@ -455,10 +555,15 @@
         own[t] = value
         for ref in (first, second):
             ref[t * OWN : (t + 1) * OWN] = value
+    even = is_even("gy")
+    top, bottom = (p0 * edges[0, side] - p1 * edges[1, side] + p2 * edges[2, side] for side in (0, 1))
+    edge_first[...] = jnp.where(even, top, bottom)
+    edge_second[...] = jnp.where(even, bottom, top)
 
 
 def coarse1_kernel(
-    rows, coarse, y_first, y_second, own_a, own_b, corner_a, corner_b, gain, keep0, powers, coef, x0, edge_first, edge_second, fields
+    rows, coarse, y_first, y_second, own_a, own_b, corner_a, corner_b, gain, keep_in, y1_in, y2_in, keep_out, y1_out, y2_out,
+    coef, keep0, x0, fields
 ):
     even, even_x = is_even("gy"), is_even("gx")
     own_x, corner_x = (own_a, own_b), (corner_a, corner_b)
@@ -478,25 +583,19 @@
         for i, value in enumerate(packed_jacobian(fields[t, 0:GROUPS1], fields[t, GROUPS1 : 2 * GROUPS1], 1)):
             coef[i, t, 1 : SIZE1 - 1] = value
 
+    def whole(inside, outside):
+        n = outside.shape[0] // 2
+        return jnp.concatenate([outside[0:n], inside, outside[n:]], axis=0)
+
+    for i in range(6):
+        for t in (0, 1):
+            keep0[i, t, 1 : rows + 2 * HALO0 - 1] = whole(keep_in[i, t], keep_out[i, t])
     p0, p1, p2 = (gain[POWERS + i] for i in range(3))
     for i in (0, 1):
         for t in (0, 1):
             y0 = keep0[2 + i, t, HALO0 : HALO0 + rows] * keep0[4 + i, t, HALO0 : HALO0 + rows]
-            y1, y2 = (powers[p, i, t, HALO0 : HALO0 + rows] for p in (0, 1))
+            y1, y2 = (whole(a[i, t], b[i, t]) for a, b in ((y1_in, y1_out), (y2_in, y2_out)))
             x0[i, t] = p0 * y0 - p1 * y1 + p2 * y2
-    lane = lane_of()
-    edges = []
-    for start in (0, rows - EDGE):
-        halo = None
-        for i in (0, 1):
-            for j in range(EDGE):
-                at = i * EDGE + j
-                value = roll_x(x0[i, 1, start + j : start + j + 1], 4 + 8 * at)
-                halo = value if halo is None else jnp.where((lane >> 3) == at, value, halo)
-        edges.append([x0[0, 0, start : start + EDGE], x0[1, 0, start : start + EDGE], halo])
-    top, bottom = (jnp.concatenate(parts, axis=0) for parts in edges)
-    edge_first[...] = jnp.where(even, top, bottom)
-    edge_second[...] = jnp.where(even, bottom, top)
 
 
 def fields2_kernel(rows, coarse, y_first, y_second, own_a, own_b, corner_a, corner_b, out):
@@ -513,7 +612,7 @@
 
 
 def level1_kernel(
-    own, first, second, edge, edge_in, fields2, coef1, gain, packet, to_first, to_far, to_far2, edge_out, keep, y1, d1
+    own, first, second, edge_a, edge_b, fields2, coef1, gain, packet, to_first, to_second, to_far, keep, y1, d1
 ):
     b1, x1 = keep.at[0], keep.at[1]
     even = is_even("gy")
@@ -531,17 +630,15 @@
     for t, (c, other, spread) in enumerate(packed_terms(x1, 1 + OWN, OWN, 1)):
         res = b1[t, here] - coef1[2, t, here] * c + coef1[1, t, here] * other + spread
         value = restrict_12([res[j : j + 1] for j in range(OWN)])
-        for ref in (packet, to_first, to_far, to_far2):
+        for ref in (packet, to_first, to_second, to_far):
             ref[t : t + 1] = value
-            if ref is to_far or ref is to_far2:
-                ref[2 + t : 3 + t] = fields2[t, 1:2]
-    to_far2[4:] = value
-    to_first[2:] = edge[...]
-    edge_out[...] = edge_in[...]
+        to_far[2 + t : 3 + t] = fields2[t, 1:2]
+    to_first[2:] = edge_a[...]
+    to_second[2:] = edge_b[...]
 
 
 def rest_kernel(
-    own2, near_a, near_b, far_a, far_b, edge_b, gain, coef1, fields2, keep0, iterate, keep1, out, coef2, d1, b2, x2, y2, d2, xu, yu, x0, y0, d0
+    own2, near_a, near_b, far_a, far_b, gain, coef1, fields2, keep0, iterate, keep1, out, coef2, d1, b2, x2, y2, d2, xu, yu, x0, y0, d0
 ):
     rows = out.shape[0] // (2 * Z)
     even = (sub_of() & 1) == 0
@@ -590,7 +687,7 @@
     g0, g1, g2 = (gain[i] for i in range(3))
     for i in (0, 1):
         for at, take in ((HALO0 - EDGE, prev_of), (HALO0 + rows, next_of)):
-            whole = take(even_y, near_a.at[2:], edge_b, slice(0, EDGE_TILES))
+            whole = take(even_y, near_a, near_b, slice(2, 2 + EDGE_TILES))
             x0[i, 0, at : at + EDGE] = whole[i * EDGE : (i + 1) * EDGE]
             for j in range(EDGE):
                 x0[i, 1, at + j : at + j + 1] = roll_x(whole[2 * EDGE :], -(4 + 8 * (i * EDGE + j)))
@@ -613,13 +710,13 @@
             out[pl.ds(i * Z * rows + y, Z, stride=rows), :] = y0[i, 0, HALO0 + y]
 
 
-def call(kernel, out_shapes, scratch, *args, space=pltpu.VMEM):
+def call(kernel, out_shapes, scratch, *args, space=pltpu.VMEM, outs=None):
     out = [jax.ShapeDtypeStruct(shape, jnp.float32) for shape in out_shapes]
     return pl.pallas_call(
         kernel,
         out_shape=out,
         in_specs=[pl.BlockSpec(memory_space=space)] * len(args),
-        out_specs=[pl.BlockSpec(memory_space=pltpu.VMEM)] * len(out),
+        out_specs=[pl.BlockSpec(memory_space=m) for m in outs or [pltpu.VMEM] * len(out)],
         scratch_shapes=[pltpu.VMEM(s, jnp.float32) if isinstance(s, tuple) else s for s in scratch],
         compiler_params=pltpu.CompilerParams(vmem_limit_bytes=24 * 2**20),
     )(*args)
@@ -663,20 +760,18 @@
         space=pltpu.HBM,
     )
     y_packets = exchange(first, second, "gy")
-    (spread,) = call(spread_kernel, [(across * count, Z // 2, X)], [], main, coarse)
+    tiles = tiles_for(6 * rows + 2 * OWN + 1)
+    spread_shape = (across * count, Z // 2, X)
+    first, second, spread = call(
+        functools.partial(pack_own_kernel, rows),
+        [(tiles, Z, X), (tiles, Z, X), spread_shape],
+        [(PER * tiles, Z, X), spread_shape, pltpu.SemaphoreType.DMA],
+        main,
+        coarse,
+        outs=[pltpu.VMEM, pltpu.VMEM, pltpu.HBM],
+    )
+    own_x = exchange(first, second, "gx")
     spread = lax.all_to_all(spread, ("gx", "gy"), 0, 0, tiled=True)
-
-    tiles = tiles_for(6 * rows + 2 * OWN + 1)
-    own_x = exchange(
-        *call(
-            functools.partial(pack_own_kernel, rows),
-            [(tiles, Z, X), (tiles, Z, X)],
-            [(PER * tiles, Z, X)],
-            main,
-            coarse,
-        ),
-        "gx",
-    )
     tiles = tiles_for(2 * PACKET)
     corner_x = exchange(
         *call(pack_corner_kernel, [(tiles, Z, X), (tiles, Z, X)], [(PER * tiles, Z, X)], *y_packets), "gx"
@@ -684,33 +779,56 @@
 
     strip, edge = (2 * OWN, Z, X), (EDGE_TILES, Z, X)
     pair0 = (2, 2, total0, Z, X)
-    keep0, powers, sources = call(
-        functools.partial(level0_kernel, rows),
-        [(6, 2, total0, Z, X), (2, *pair0), (4, 2, OWN, Z, X)],
-        [(6, 2, total0, Z, X), pair0, pair0],
+    work = [(6, 2, total0, Z, X), (6, 2, total0, Z, X), pair0, pair0, pair0, pair0]
+    four = (4, 2, OWN, Z, X)
+    inside = call(
+        functools.partial(level0_inner_kernel, rows),
+        [
+            (6, 2, rows - 2, Z, X),
+            (2, 2, 4, Z, X),
+            (2, 2, rows - 4, Z, X),
+            (2, 2, rows - 6, Z, X),
+            (2, 2, 6, Z, X),
+            four,
+        ],
+        work,
+        main,
+        *own_x,
+    )
+    keep_in, _, y1_in, y2_in, _, _ = inside
+    keep_out, y1_out, y2_out, sources, edges = call(
+        functools.partial(level0_outer_kernel, rows),
+        [(6, 2, 8, Z, X), (2, 2, 4, Z, X), (2, 2, 6, Z, X), four, (3, 2, *edge)],
+        work,
         main,
         *y_packets,
         *own_x,
         *corner_x,
-    )
-    own, first, second, gain = call(
+        *inside,
+    )
+    own, first, second, edge_a, edge_b, gain = call(
         combine_kernel,
-        [(2, OWN, Z, X), strip, strip, (POWERS + 3, Z, X)],
+        [(2, OWN, Z, X), strip, strip, edge, edge, (POWERS + 3, Z, X)],
         [],
         sources,
+        edges,
         spread,
     )
-    coef1, iterate, edge_a, edge_b = call(
+    coef1, keep0, iterate = call(
         functools.partial(coarse1_kernel, rows),
-        [(3, 2, SIZE1, Z, X), (2, 2, rows, Z, X), edge, edge],
+        [(3, 2, SIZE1, Z, X), (6, 2, total0, Z, X), (2, 2, rows, Z, X)],
         [(2, 2 * GROUPS1, Z, X)],
         coarse,
         *y_packets,
         *own_x,
         *corner_x,
         gain,
-        keep0,
-        powers,
+        keep_in,
+        y1_in,
+        y2_in,
+        keep_out,
+        y1_out,
+        y2_out,
     )
     (fields2,) = call(
         functools.partial(fields2_kernel, rows), [(2, 3, Z, X)], [], coarse, *y_packets, *own_x, *corner_x
@@ -718,21 +836,21 @@
     b_packets = exchange(first, second, "gy")
 
     one, two, up = (2, SIZE1, Z, X), (2, SIZE2, Z, X), (2, SIZE_UP, Z, X)
-    edge_in = swap(edge_b, "gy", 1)
-    packet, first, to_far, to_far2, edge_out, keep1 = call(
+    near = (2 + EDGE_TILES, Z, X)
+    packet, first, second, to_far, keep1 = call(
         level1_kernel,
-        [(2, Z, X), (2 + EDGE_TILES, Z, X), (4, Z, X), (5, Z, X), edge, (2, *one)],
+        [(2, Z, X), near, near, (4, Z, X), (2, *one)],
         [one, one],
         own,
         *b_packets,
         edge_a,
-        edge_in,
+        edge_b,
         fields2,
         coef1,
         gain,
     )
-    near = (swap(first, "gy", -1), swap(packet, "gy", 1))
-    far = (swap_far(to_far, "gy", 1), swap_far(to_far2, "gy", -1))
+    far = (swap_far(to_far, "gy", 1), swap_far(to_far, "gy", -1))
+    near = exchange(first, second, "gy")
 
     (out,) = call(
         rest_kernel,
@@ -741,7 +859,6 @@
         packet,
         *near,
         *far,
-        edge_out,
         gain,
         coef1,
         fields2,

time: 39.5 us -> 38.7 us (0.980)
  starting transfers between devices: 23.1 us -> 20.4 us
  waiting for transfers between devices: 8.61 us -> 10.3 us
    ppermute x11 -> x10, starting transfers between devices: 19.5 us -> 15.3 us  [swap(): return lax.ppermute(value, axis, pairs + [(j, i) for i, j in pairs])]
    ppermute x2, waiting for transfers between devices: 0.93 us -> 2.93 us  [swap_far(): return lax.ppermute(value, axis, pairs + [(j, i) for i, j in pairs])]
    ppermute x2, starting transfers between devices: 0.99 us -> 2.61 us  [swap_far(): return lax.ppermute(value, axis, pairs + [(j, i) for i, j in pairs])]
    ppermute x11 -> x10, waiting for transfers between devices: 7.56 us -> 6.9 us  [swap(): return lax.ppermute(value, axis, pairs + [(j, i) for i, j in pairs])]
  transfers between devices with their start and end apart: 14 -> 13, of which waited for: 6 -> 7; matrix products, arithmetic and copies ran while one was open for 0% -> 0% of each run, Pallas kernels for 7% -> 8%
where the time goes in v7:
time: 38.7 us; the launch traced here: 38.5 us
  starting transfers between devices  20.4 us (53%)
  waiting for transfers between devices  10.3 us (27%)
  Pallas kernels  7.66 us (20%)
    ppermute x10, starting transfers between devices, swap(): return lax.ppermute(value, axis, pairs + [(j, i) for i, j in pairs])  15.3 us
    pallas_call x10, Pallas kernels, call(): pl.pallas_call(kernel, out_shape=out, in_specs=[pl.BlockSpec(memory_space...  7.66 us
    ppermute x10, waiting for transfers between devices, swap(): return lax.ppermute(value, axis, pairs + [(j, i) for i, j in pairs])  6.9 us
    ppermute x2, waiting for transfers between devices, swap_far(): return lax.ppermute(value, axis, pairs + [(j, i) for i, j in pairs])  2.93 us
    ppermute x2, starting transfers between devices, swap_far(): return lax.ppermute(value, axis, pairs + [(j, i) for i, j in pairs])  2.61 us
    all_to_all x1, starting transfers between devices, body(): spread = lax.all_to_all(spread, ('gx', 'gy'), 0, 0, tiled=True)  2.57 us
  transfers between devices with their start and end apart: 13, of which 7 were waited for; matrix products, arithmetic and copies ran while one was open for 0% of the time, Pallas kernels for 8%

profile of v7, /device:TPU:0, one launch (start us, length us, event | category | flops | bytes accessed | tf_op | source)
XLA Modules:
  0.0 38.5 jit_solution(12148014254044433919)
XLA Ops:
  0.0 1.4 %shard_map.46 = (f32[29,8,128]{2,1,0:T(8,128)S(1)}, f32[29,8,128]{2,1,0:T(8,128)S(1)}, f32[6,16,8,128]{3,2,1,0:T(8,128)S(1)}, f32[9,8,128]{2,1,0:T(8,128)S(1)}) custom-call(f32[256,128]{1,0:T(8,128)} %bitcast.5, f32[256,128]{1,0:T(8,128)} %bitcast.6, f32[128,128]{1,0:T(8,128)} %bitcast.7, f32[128,128]{1,0:T(8,128)} %bitcast.8), custom_call_target="tpu_custom_call" | custom-call | tf_op jit(solution)/shard_map/pallas_call | solution.py:715
  1.4 6.1 %collective-permute-start = (f32[29,8,128]{2,1,0:T(8,128)S(1)}, f32[29,8,128]{2,1,0:T(8,128)S(1)}, u32[]{:S(2)}, u32[]{:S(2)}) collective-permute-start(f32[29,8,128]{2,1,0:T(8,128)S(1)} %get-tuple-element.40), channel_id=1, source_target_pairs={{0,7},{2,1},{4,3},{6,5},{7,0},{1,2},{3,4},{5,6},{8,15},{10,9},{12,... | collective-permute-start | bytes 356360 | tf_op jit(solution)/shard_map/ppermute | solution.py:729
  7.5 0.8 %shard_map.47 = (f32[35,8,128]{2,1,0:T(8,128)S(1)}, f32[35,8,128]{2,1,0:T(8,128)S(1)}, f32[32,4,128]{2,1,0:T(4,128)}) custom-call(f32[6,16,8,128]{3,2,1,0:T(8,128)S(1)} %get-tuple-element.39.main, f32[9,8,128]{2,1,0:T(8,128)S(1)} %get-tuple-element.42.coarse), custom_call_target="tpu_custom_call" | custom-call | tf_op jit(solution)/shard_map/pallas_call | solution.py:715
  8.3 0.7 %collective-permute-start.2 = (f32[35,8,128]{2,1,0:T(8,128)S(1)}, f32[35,8,128]{2,1,0:T(8,128)S(1)}, u32[]{:S(2)}, u32[]{:S(2)}) collective-permute-start(f32[35,8,128]{2,1,0:T(8,128)S(1)} %get-tuple-element.43), channel_id=1, source_target_pairs={{0,24},{16,8},{24,0},{8,16},{1,25},{17,9},{25,1},{9,17},{2,26},{18... | collective-permute-start | bytes 430088 | tf_op jit(solution)/shard_map/ppermute | solution.py:729
  9.0 1.0 %collective-permute-start.3 = (f32[35,8,128]{2,1,0:T(8,128)S(1)}, f32[35,8,128]{2,1,0:T(8,128)S(1)}, u32[]{:S(2)}, u32[]{:S(2)}) collective-permute-start(f32[35,8,128]{2,1,0:T(8,128)S(1)} %get-tuple-element.44), channel_id=1, source_target_pairs={{0,8},{16,24},{8,0},{24,16},{1,9},{17,25},{9,1},{25,17},{2,10},{18... | collective-permute-start | bytes 430088 | tf_op jit(solution)/shard_map/ppermute | solution.py:729
  9.9 2.6 %all-to-all-start = ((f32[32,4,128]{2,1,0:T(4,128)}), f32[32,4,128]{2,1,0:T(4,128)S(1)}, u32[]{:S(2)}, u32[]{:S(2)}) async-start(f32[32,4,128]{2,1,0:T(4,128)} %get-tuple-element.55), calls=%async_computation | async-start | bytes 131072 | tf_op jit(solution)/shard_map/all_to_all | solution.py:774
  12.5 0.7 %collective-permute-done.1.y_second = f32[29,8,128]{2,1,0:T(8,128)S(1)} collective-permute-done((f32[29,8,128]{2,1,0:T(8,128)S(1)}, f32[29,8,128]{2,1,0:T(8,128)S(1)}, u32[]{:S(2)}, u32[]{:S(2)}) %collective-permute-start.1) | collective-permute-done | bytes 118816 | tf_op jit(solution)/shard_map/ppermute | solution.py:729
  13.2 0.2 shard_map.48
  13.4 0.9 %collective-permute-start.4 = (f32[20,8,128]{2,1,0:T(8,128)S(1)}, f32[20,8,128]{2,1,0:T(8,128)S(1)}, u32[]{:S(2)}, u32[]{:S(2)}) collective-permute-start(f32[20,8,128]{2,1,0:T(8,128)S(1)} %get-tuple-element.45), channel_id=1, source_target_pairs={{0,24},{16,8},{24,0},{8,16},{1,25},{17,9},{25,1},{9,17},{2,26},{18... | collective-permute-start | bytes 245768 | tf_op jit(solution)/shard_map/ppermute | solution.py:729
  14.4 0.7 %collective-permute-start.5 = (f32[20,8,128]{2,1,0:T(8,128)S(1)}, f32[20,8,128]{2,1,0:T(8,128)S(1)}, u32[]{:S(2)}, u32[]{:S(2)}) collective-permute-start(f32[20,8,128]{2,1,0:T(8,128)S(1)} %get-tuple-element.46), channel_id=1, source_target_pairs={{0,8},{16,24},{8,0},{24,16},{1,9},{17,25},{9,1},{25,17},{2,10},{18... | collective-permute-start | bytes 245768 | tf_op jit(solution)/shard_map/ppermute | solution.py:729
  15.1 0.9 %shard_map.49 = (f32[6,2,14,8,128]{4,3,2,1,0:T(8,128)S(1)}, f32[2,2,4,8,128]{4,3,2,1,0:T(8,128)S(1)}, f32[2,2,12,8,128]{4,3,2,1,0:T(8,128)S(1)}, f32[2,2,10,8,12...) custom-call(f32[6,16,8,128]{3,2,1,0:T(8,128)S(1)} %get-tuple-element.39.main, ...), custom_call_target="tpu_custom_call" | custom-call | tf_op jit(solution)/shard_map/pallas_call | solution.py:715
  16.0 2.5 %collective-permute-done.4.corner_a = f32[20,8,128]{2,1,0:T(8,128)S(1)} collective-permute-done((f32[20,8,128]{2,1,0:T(8,128)S(1)}, f32[20,8,128]{2,1,0:T(8,128)S(1)}, u32[]{:S(2)}, u32[]{:S(2)}) %collective-permute-start.4) | collective-permute-done | bytes 81952 | tf_op jit(solution)/shard_map/ppermute | solution.py:729
  18.5 0.8 %shard_map.50 = (f32[6,2,8,8,128]{4,3,2,1,0:T(8,128)S(1)}, f32[2,2,4,8,128]{4,3,2,1,0:T(8,128)S(1)}, f32[2,2,6,8,128]{4,3,2,1,0:T(8,128)S(1)}, f32[4,2,4,8,128]{4,3,2,1,0:T(8,128)S(1)}, f32[3,2,7,8,128]{4,3,2,1,0:T(8,128)S(1)}) custom-call(f32[6,16,8,128]{3,2,1,0:T(8,128)S(1)} %get-tuple-element.39.main, f32[29,8,128]{2,1,0:T(8,128)S(1)} %collective-permute-done.y_first, ...), custom_call_target="tpu_custom_call" | custom-call | tf_op jit(solution)/shard_map/pallas_call | solution.py:715
  19.3 0.5 %all-to-all-done.spread = f32[32,4,128]{2,1,0:T(4,128)S(1)} async-done(((f32[32,4,128]{2,1,0:T(4,128)}), f32[32,4,128]{2,1,0:T(4,128)S(1)}, u32[]{:S(2)}, u32[]{:S(2)}) %all-to-all-start) | async-done | bytes 65568 | tf_op jit(solution)/shard_map/all_to_all | solution.py:774
  19.9 3.1 %collective-permute-start.6 = (f32[8,8,128]{2,1,0:T(8,128)S(1)}, f32[8,8,128]{2,1,0:T(8,128)S(1)}, u32[]{:S(2)}, u32[]{:S(2)}) collective-permute-start(f32[8,8,128]{2,1,0:T(8,128)S(1)} %get-tuple-element.57), channel_id=1, source_target_pairs={{0,7},{2,1},{4,3},{6,5},{7,0},{1,2},{3,4},{5,6},{8,15},{10,9},{12,... | collective-permute-start | bytes 98312 | tf_op jit(solution)/shard_map/ppermute | solution.py:729
  23.1 0.2 shard_map.53
  23.3 3.3 %collective-permute-done.6.first = f32[8,8,128]{2,1,0:T(8,128)S(1)} collective-permute-done((f32[8,8,128]{2,1,0:T(8,128)S(1)}, f32[8,8,128]{2,1,0:T(8,128)S(1)}, u32[]{:S(2)}, u32[]{:S(2)}) %collective-permute-start.6) | collective-permute-done | bytes 32800 | tf_op jit(solution)/shard_map/ppermute | solution.py:729
  26.6 0.4 collective-permute-done.7.second
  26.9 0.6 %shard_map.54 = (f32[2,8,128]{2,1,0:T(8,128)S(1)}, f32[9,8,128]{2,1,0:T(8,128)S(1)}, f32[9,8,128]{2,1,0:T(8,128)S(1)}, f32[4,8,128]{2,1,0:T(8,128)S(1)}, f32[2,2,14,8,128]{4,3,2,1,0:T(8,128)S(1)}) custom-call(f32[2,4,8,128]{3,2,1,0:T(8,128)S(1)} %get-tuple-element.56.own, f32[8,8,128]{2,1,0:T(8,128)S(1)} %collective-permute-done.6.first, ...), custom_call_target="tpu_custom_call" | custom-call | tf_op jit(solution)/shard_map/pallas_call | solution.py:715
  27.5 2.7 %collective-permute-start.8 = (f32[9,8,128]{2,1,0:T(8,128)S(1)}, f32[9,8,128]{2,1,0:T(8,128)S(1)}, u32[]{:S(2)}, u32[]{:S(2)}) collective-permute-start(f32[9,8,128]{2,1,0:T(8,128)S(1)} %get-tuple-element.67), channel_id=1, source_target_pairs={{0,7},{2,1},{4,3},{6,5},{7,0},{1,2},{3,4},{5,6},{8,15},{10,9},{12,... | collective-permute-start | bytes 110600 | tf_op jit(solution)/shard_map/ppermute | solution.py:729
  30.3 2.6 %collective-permute-start.11 = (f32[4,8,128]{2,1,0:T(8,128)S(1)}, f32[4,8,128]{2,1,0:T(8,128)S(1)}, u32[]{:S(2)}, u32[]{:S(2)}) collective-permute-start(f32[4,8,128]{2,1,0:T(8,128)S(1)} %get-tuple-element.69), channel_id=1, source_target_pairs={{0,6},{1,7},{4,2},{5,3},{6,0},{7,1},{2,4},{3,5},{8,14},{9,15},{12,... | collective-permute-start | bytes 49160 | tf_op jit(solution)/shard_map/ppermute | solution.py:736
  32.9 1.1 %collective-permute-done.10.far_a = f32[4,8,128]{2,1,0:T(8,128)S(1)} collective-permute-done((f32[4,8,128]{2,1,0:T(8,128)S(1)}, f32[4,8,128]{2,1,0:T(8,128)S(1)}, u32[]{:S(2)}, u32[]{:S(2)}) %collective-permute-start.10) | collective-permute-done | bytes 16416 | tf_op jit(solution)/shard_map/ppermute | solution.py:736
  34.0 1.8 %collective-permute-done.11.far_b = f32[4,8,128]{2,1,0:T(8,128)S(1)} collective-permute-done((f32[4,8,128]{2,1,0:T(8,128)S(1)}, f32[4,8,128]{2,1,0:T(8,128)S(1)}, u32[]{:S(2)}, u32[]{:S(2)}) %collective-permute-start.11) | collective-permute-done | bytes 16416 | tf_op jit(solution)/shard_map/ppermute | solution.py:736
  35.8 2.7 %shard_map.55 = f32[256,128]{1,0:T(8,128)} custom-call(f32[2,8,128]{2,1,0:T(8,128)S(1)} %get-tuple-element.66.own2, f32[9,8,128]{2,1,0:T(8,128)S(1)} %collective-permute-done.8.near_a, f32[9,8,128]{2,1,0:T(8,128)S(1)} %collective-permute-done.9.near_b, f32[4,8,128]{2,1,0:T(8,128)S(1)} %collective-permute-done.10.far_a, ...), custom_call_target="tpu_custom_call" | custom-call | tf_op jit(solution)/shard_map/pallas_call | solution.py:715
  (12 shorter events, 0.2 us)
Async XLA Ops:
  1.4 11.1 %collective-permute-start = (f32[29,8,128]{2,1,0:T(8,128)S(1)}, f32[29,8,128]{2,1,0:T(8,128)S(1)}, u32[]{:S(2)}, u32[]{:S(2)}) collective-permute-start(f32[29,8,128]{2,1,0:T(8,128)S(1)} %get-tuple-element.40), channel_id=1, source_target_pairs={{0,7},{2,1},{4,3},{6,5},{7,0},{1,2},{3,4},{5,6},{8,15},{10,9},{12,... | collective-permute-start | bytes 356360 | tf_op jit(solution)/shard_map/ppermute | solution.py:729
  7.5 5.8 %collective-permute-start.1 = (f32[29,8,128]{2,1,0:T(8,128)S(1)}, f32[29,8,128]{2,1,0:T(8,128)S(1)}, u32[]{:S(2)}, u32[]{:S(2)}) collective-permute-start(f32[29,8,128]{2,1,0:T(8,128)S(1)} %get-tuple-element.41), channel_id=1, source_target_pairs={{0,1},{2,3},{4,5},{6,7},{1,0},{3,2},{5,4},{7,6},{8,9},{10,11},{12,... | collective-permute-start | bytes 356360 | tf_op jit(solution)/shard_map/ppermute | solution.py:729
  8.3 6.8 %collective-permute-start.2 = (f32[35,8,128]{2,1,0:T(8,128)S(1)}, f32[35,8,128]{2,1,0:T(8,128)S(1)}, u32[]{:S(2)}, u32[]{:S(2)}) collective-permute-start(f32[35,8,128]{2,1,0:T(8,128)S(1)} %get-tuple-element.43), channel_id=1, source_target_pairs={{0,24},{16,8},{24,0},{8,16},{1,25},{17,9},{25,1},{9,17},{2,26},{18... | collective-permute-start | bytes 430088 | tf_op jit(solution)/shard_map/ppermute | solution.py:729
  9.0 6.1 %collective-permute-start.3 = (f32[35,8,128]{2,1,0:T(8,128)S(1)}, f32[35,8,128]{2,1,0:T(8,128)S(1)}, u32[]{:S(2)}, u32[]{:S(2)}) collective-permute-start(f32[35,8,128]{2,1,0:T(8,128)S(1)} %get-tuple-element.44), channel_id=1, source_target_pairs={{0,8},{16,24},{8,0},{24,16},{1,9},{17,25},{9,1},{25,17},{2,10},{18... | collective-permute-start | bytes 430088 | tf_op jit(solution)/shard_map/ppermute | solution.py:729
  9.9 9.9 %all-to-all-start = ((f32[32,4,128]{2,1,0:T(4,128)}), f32[32,4,128]{2,1,0:T(4,128)S(1)}, u32[]{:S(2)}, u32[]{:S(2)}) async-start(f32[32,4,128]{2,1,0:T(4,128)} %get-tuple-element.55), calls=%async_computation | async-start | bytes 131072 | tf_op jit(solution)/shard_map/all_to_all | solution.py:774
  13.4 5.1 %collective-permute-start.4 = (f32[20,8,128]{2,1,0:T(8,128)S(1)}, f32[20,8,128]{2,1,0:T(8,128)S(1)}, u32[]{:S(2)}, u32[]{:S(2)}) collective-permute-start(f32[20,8,128]{2,1,0:T(8,128)S(1)} %get-tuple-element.45), channel_id=1, source_target_pairs={{0,24},{16,8},{24,0},{8,16},{1,25},{17,9},{25,1},{9,17},{2,26},{18... | collective-permute-start | bytes 245768 | tf_op jit(solution)/shard_map/ppermute | solution.py:729
  14.4 4.2 %collective-permute-start.5 = (f32[20,8,128]{2,1,0:T(8,128)S(1)}, f32[20,8,128]{2,1,0:T(8,128)S(1)}, u32[]{:S(2)}, u32[]{:S(2)}) collective-permute-start(f32[20,8,128]{2,1,0:T(8,128)S(1)} %get-tuple-element.46), channel_id=1, source_target_pairs={{0,8},{16,24},{8,0},{24,16},{1,9},{17,25},{9,1},{25,17},{2,10},{18... | collective-permute-start | bytes 245768 | tf_op jit(solution)/shard_map/ppermute | solution.py:729
  19.9 6.7 %collective-permute-start.6 = (f32[8,8,128]{2,1,0:T(8,128)S(1)}, f32[8,8,128]{2,1,0:T(8,128)S(1)}, u32[]{:S(2)}, u32[]{:S(2)}) collective-permute-start(f32[8,8,128]{2,1,0:T(8,128)S(1)} %get-tuple-element.57), channel_id=1, source_target_pairs={{0,7},{2,1},{4,3},{6,5},{7,0},{1,2},{3,4},{5,6},{8,15},{10,9},{12,... | collective-permute-start | bytes 98312 | tf_op jit(solution)/shard_map/ppermute | solution.py:729
  23.0 3.9 %collective-permute-start.7 = (f32[8,8,128]{2,1,0:T(8,128)S(1)}, f32[8,8,128]{2,1,0:T(8,128)S(1)}, u32[]{:S(2)}, u32[]{:S(2)}) collective-permute-start(f32[8,8,128]{2,1,0:T(8,128)S(1)} %get-tuple-element.58), channel_id=1, source_target_pairs={{0,1},{2,3},{4,5},{6,7},{1,0},{3,2},{5,4},{7,6},{8,9},{10,11},{12,... | collective-permute-start | bytes 98312 | tf_op jit(solution)/shard_map/ppermute | solution.py:729
  27.5 8.3 %collective-permute-start.8 = (f32[9,8,128]{2,1,0:T(8,128)S(1)}, f32[9,8,128]{2,1,0:T(8,128)S(1)}, u32[]{:S(2)}, u32[]{:S(2)}) collective-permute-start(f32[9,8,128]{2,1,0:T(8,128)S(1)} %get-tuple-element.67), channel_id=1, source_target_pairs={{0,7},{2,1},{4,3},{6,5},{7,0},{1,2},{3,4},{5,6},{8,15},{10,9},{12,... | collective-permute-start | bytes 110600 | tf_op jit(solution)/shard_map/ppermute | solution.py:729
  30.3 5.5 %collective-permute-start.9 = (f32[9,8,128]{2,1,0:T(8,128)S(1)}, f32[9,8,128]{2,1,0:T(8,128)S(1)}, u32[]{:S(2)}, u32[]{:S(2)}) collective-permute-start(f32[9,8,128]{2,1,0:T(8,128)S(1)} %get-tuple-element.68), channel_id=1, source_target_pairs={{0,1},{2,3},{4,5},{6,7},{1,0},{3,2},{5,4},{7,6},{8,9},{10,11},{12,... | collective-permute-start | bytes 110600 | tf_op jit(solution)/shard_map/ppermute | solution.py:729
  30.3 3.7 %collective-permute-start.10 = (f32[4,8,128]{2,1,0:T(8,128)S(1)}, f32[4,8,128]{2,1,0:T(8,128)S(1)}, u32[]{:S(2)}, u32[]{:S(2)}) collective-permute-start(f32[4,8,128]{2,1,0:T(8,128)S(1)} %get-tuple-element.69), channel_id=1, source_target_pairs={{0,2},{1,3},{4,6},{5,7},{2,0},{3,1},{6,4},{7,5},{8,10},{9,11},{12,... | collective-permute-start | bytes 49160 | tf_op jit(solution)/shard_map/ppermute | solution.py:736
  30.3 5.5 %collective-permute-start.11 = (f32[4,8,128]{2,1,0:T(8,128)S(1)}, f32[4,8,128]{2,1,0:T(8,128)S(1)}, u32[]{:S(2)}, u32[]{:S(2)}) collective-permute-start(f32[4,8,128]{2,1,0:T(8,128)S(1)} %get-tuple-element.69), channel_id=1, source_target_pairs={{0,6},{1,7},{4,2},{5,3},{6,0},{7,1},{2,4},{3,5},{8,14},{9,15},{12,... | collective-permute-start | bytes 49160 | tf_op jit(solution)/shard_map/ppermute | solution.py:736

commit v8 on v7

--- a/solution.py
+++ b/solution.py
@@ -21,9 +21,8 @@
 Z = 8
 X = 128
 HALO0 = 4
-HALOS = (4, 4, 3, 3, 3, 3)
-STARTS = tuple(sum(HALOS[:i]) for i in range(6))
-FIELDS1 = sum(HALOS)
+SENT = 3
+FIELDS1 = 6 * SENT
 FIELDS2 = FIELDS1 + 8
 PACKET = FIELDS2 + 1
 WIDE = 42
@@ -72,14 +71,14 @@
         body(hi - rest, rest)
 
 
-def neighbour_sums(read, r, n, k):
+def neighbour_sums(read, r, n, k, tiles=(0, 1)):
     lane = lane_of()
     low, high = lane < k, lane >= X - k
     centre = [read(t, r, n) for t in (0, 1)]
     right = [roll_x(c, k) for c in centre]
     left = [roll_x(c, -k) for c in centre]
     sums = []
-    for t in (0, 1):
+    for t in tiles:
         c = centre[t]
         along_x = jnp.where(low, right[1 - t], right[t]) + jnp.where(high, left[1 - t], left[t])
         along_y = read(t, r - 1, n) + read(t, r + 1, n)
@@ -97,13 +96,14 @@
     return 2.0 * product, squared, 1.0 / first, 1.0 / second, first, second
 
 
-def cheb_step(level, keep, source, target, d, r, n, carry, gain):
+def cheb_step(level, keep, source, target, d, r, n, carry, gain, tiles=(0, 1)):
     scale = 0.25**level
     k = 1 << level
-    u, nb_u = neighbour_sums(lambda t, a, m: source[0, t, pl.ds(a, m)], r, n, k)
-    v, nb_v = neighbour_sums(lambda t, a, m: source[1, t, pl.ds(a, m)], r, n, k)
+    u, nb_u = neighbour_sums(lambda t, a, m: source[0, t, pl.ds(a, m)], r, n, k, tiles)
+    v, nb_v = neighbour_sums(lambda t, a, m: source[1, t, pl.ds(a, m)], r, n, k, tiles)
     rows = pl.ds(r, n)
-    for t in (0, 1):
+    out = []
+    for t in tiles:
         cross, squared, inv_u, inv_v = (keep[i, t, rows] for i in range(4))
         res_u = inv_u * (keep[4, t, rows] - cross * v[t] + DIFF[0] * scale * nb_u[t]) - u[t]
         res_v = inv_v * (keep[5, t, rows] + squared * u[t] + DIFF[1] * scale * nb_v[t]) - v[t]
@@ -111,10 +111,13 @@
         if carry is not None:
             du = du + carry * d[0, t, rows]
             dv = dv + carry * d[1, t, rows]
-        d[0, t, rows] = du
-        d[1, t, rows] = dv
-        target[0, t, rows] = u[t] + du
-        target[1, t, rows] = v[t] + dv
+        if target is not None:
+            d[0, t, rows] = du
+            d[1, t, rows] = dv
+            target[0, t, rows] = u[t] + du
+            target[1, t, rows] = v[t] + dv
+        out.append((u[t] + du, v[t] + dv))
+    return out
 
 
 def next_power(keep, source, r, n):
@@ -264,38 +267,46 @@
     return jnp.where(even, second[at], first[at])
 
 
-def first_kernel(rows, state, previous, feed, kill, first, second, main, coarse, *scratch):
-    sources, sems = scratch[:4], scratch[4]
+SOURCES = ((0, 0), (0, 1), (1, 0), (1, 1), (2, 0), (3, 0))
+
+
+def first_kernel(rows, state, previous, feed, kill, first, second, coarse, *rest):
+    held, sems = rest[:4], rest[4]
     copies = [
-        pltpu.make_async_copy(ref, held, sems.at[i])
-        for i, (ref, held) in enumerate(zip((state, previous, feed, kill), sources))
+        pltpu.make_async_copy(ref, to, sems.at[i]) for i, (ref, to) in enumerate(zip((state, previous, feed, kill), held))
     ]
     for copy in copies:
         copy.start()
     for copy in copies:
         copy.wait()
     even = is_even("gy")
-    state, previous, feed, kill = sources
-    fields = [(state, 0), (state, 1), (previous, 0), (previous, 1), (feed, 0), (kill, 0)]
-    for i, (ref, f) in enumerate(fields):
-        for y in range(rows):
-            main[i, y] = plane(ref, f, y, rows)
-        top, bottom = main[i, 0 : HALOS[i]], main[i, rows - HALOS[i] : rows]
-        at = slice(STARTS[i], STARTS[i] + HALOS[i])
-        first[at] = jnp.where(even, top, bottom)
-        second[at] = jnp.where(even, bottom, top)
-    u, v, f, k = (main[i] for i in (0, 1, 4, 5))
-    sums = [pair_rows(value) for value in (u, v, f, k)]
+    values = []
+    for i, (j, f) in enumerate(SOURCES):
+        wanted = range(rows) if i not in (2, 3) else [*range(SENT), *range(rows - SENT, rows)]
+        values.append({y: plane(held[j], f, y, rows)[None] for y in wanted})
+    for i in (2, 3):
+        weight = DIFF[i - 2] / INV_STEP
+        values[i][SENT - 1] = values[i][SENT - 1] + weight * values[i - 2][SENT]
+        values[i][rows - SENT] = values[i][rows - SENT] + weight * values[i - 2][rows - SENT - 1]
+    for i in range(6):
+        for y in range(SENT):
+            top, bottom = values[i][y], values[i][rows - SENT + y]
+            at = slice(i * SENT + y, i * SENT + y + 1)
+            first[at] = jnp.where(even, top, bottom)
+            second[at] = jnp.where(even, bottom, top)
     pairs = []
-    for p in (0, 1):
-        values = [
-            restrict_01(sums[2 * p][2 * g : 2 * g + 2], sums[2 * p + 1][2 * g : 2 * g + 2]) for g in range(OWN)
-        ]
-        pairs.append(jnp.concatenate(values, axis=0))
+    for p, (i, j) in enumerate(((0, 1), (4, 5))):
+        parts = []
+        for g in range(OWN):
+            sums = [
+                jnp.concatenate([value[4 * g + 2 * q] + value[4 * g + 2 * q + 1] for q in (0, 1)], axis=0)
+                for value in (values[i], values[j])
+            ]
+            parts.append(restrict_01(*sums))
+        pairs.append(jnp.concatenate(parts, axis=0))
         coarse[p * OWN : (p + 1) * OWN] = pairs[p]
         for ref in (first, second):
             ref[FIELDS1 + p * OWN : FIELDS1 + (p + 1) * OWN] = pairs[p]
-
     uv, fk = (restrict_12([pair[j : j + 1] for j in range(OWN)]) for pair in pairs)
     both = jnp.where((sub_of() & 2) == 0, uv, fk)
     coarse[2 * OWN : 2 * OWN + 1] = both
@@ -358,7 +369,13 @@
     return out
 
 
-def pack_own_kernel(rows, main, coarse, first, second, spread, held, copies, sem):
+def pack_own_kernel(
+    rows, state, previous, feed, kill, coarse, first, second, spread, main, held, copies, sem
+):
+    inputs = (state, previous, feed, kill)
+    for i, (j, f) in enumerate(SOURCES):
+        for y in range(rows):
+            main[i, y] = plane(inputs[j], f, y, rows)
     write_spread(main, coarse, copies)
     copy = pltpu.make_async_copy(copies, spread, sem)
     copy.start()
@@ -489,22 +506,25 @@
     fields, keep, diag, y0, y1, y2 = scratch
     even, even_x = is_even("gy"), is_even("gx")
     total = rows + 2 * HALO0
-    near = HALO0 + 2
-    for i, halo in enumerate(HALOS):
-        strip = slice(STARTS[i], STARTS[i] + halo)
-        skip = HALO0 - halo
+    near, skip = HALO0 + 2, HALO0 - SENT
+    for i in range(6):
+        strip = slice(i * SENT, (i + 1) * SENT)
         fields[i, 0, skip:HALO0] = prev_of(even, y_first, y_second, strip)
         fields[i, 0, HALO0:near] = main[i, 0:2]
         fields[i, 0, total - near : total - HALO0] = main[i, rows - 2 : rows]
         fields[i, 0, HALO0 + rows : total - skip] = next_of(even, y_first, y_second, strip)
         for packets, lo, n, at in (
-            ((corner_a, corner_b), STARTS[i], halo, skip),
+            ((corner_a, corner_b), i * SENT, SENT, skip),
             ((own_a, own_b), i * rows, 2, HALO0),
             ((own_a, own_b), (i + 1) * rows - 2, 2, total - near),
-            ((corner_a, corner_b), PACKET + STARTS[i], halo, HALO0 + rows),
+            ((corner_a, corner_b), PACKET + i * SENT, SENT, HALO0 + rows),
         ):
             for a, b, value in halo_tiles(even_x, packets, lo, lo + n):
                 fields[i, 1, at + a : at + b] = value
+    for i in (0, 1):
+        for t in (0, 1):
+            for at in (0, total - 1):
+                fields[i, t, at] = jnp.zeros((Z, X), jnp.float32)
     for at, part in zip(ends(rows, 5, 8), (slice(0, 3), slice(rows - 5, rows - 2))):
         for i in range(6):
             for t in (0, 1):
@@ -627,14 +647,16 @@
     packed_step(1, coef1, 0, b1, x1, y1, d1, 1, n, CARRY1, g1)
     packed_step(1, coef1, 0, b1, y1, x1, d1, 1, n, CARRY2, g2)
     here = pl.ds(1 + OWN, OWN)
+    values = []
     for t, (c, other, spread) in enumerate(packed_terms(x1, 1 + OWN, OWN, 1)):
         res = b1[t, here] - coef1[2, t, here] * c + coef1[1, t, here] * other + spread
-        value = restrict_12([res[j : j + 1] for j in range(OWN)])
-        for ref in (packet, to_first, to_second, to_far):
-            ref[t : t + 1] = value
-        to_far[2 + t : 3 + t] = fields2[t, 1:2]
-    to_first[2:] = edge_a[...]
-    to_second[2:] = edge_b[...]
+        values.append(restrict_12([res[j : j + 1] for j in range(OWN)]))
+        to_far[1 + t : 2 + t] = fields2[t, 1:2]
+    value = jnp.where((sub_of() & 2) == 0, values[0], values[1])
+    for ref in (packet, to_first, to_second, to_far):
+        ref[0:1] = value
+    to_first[1:] = edge_a[...]
+    to_second[1:] = edge_b[...]
 
 
 def rest_kernel(
@@ -645,17 +667,17 @@
     b1, x1 = keep1.at[0], keep1.at[1]
 
     even_y, low = is_even("gy"), lax.rem(lax.axis_index("gy"), 4) < 2
-    for t in (0, 1):
-        at = slice(t, t + 1)
-        parts = [
-            next_of(low, far_a, far_b, at),
-            prev_of(even_y, near_a, near_b, at),
-            own2[at],
-            next_of(even_y, near_a, near_b, at),
-            prev_of(low, far_a, far_b, at),
-        ]
-        b2[t, 1 : SIZE2 - 1] = jnp.concatenate(parts, axis=0)
-        at = slice(2 + t, 3 + t)
+    at = slice(0, 1)
+    parts = [
+        next_of(low, far_a, far_b, at),
+        prev_of(even_y, near_a, near_b, at),
+        own2[at],
+        next_of(even_y, near_a, near_b, at),
+        prev_of(low, far_a, far_b, at),
+    ]
+    for t, values in enumerate(split_fields2(jnp.concatenate(parts, axis=0))):
+        b2[t, 1 : SIZE2 - 1] = values
+        at = slice(1 + t, 2 + t)
         parts = [next_of(low, far_a, far_b, at), fields2[t], prev_of(low, far_a, far_b, at)]
         inverse, other, _ = packed_jacobian(*split_fields2(jnp.concatenate(parts, axis=0)), 2)
         coef2[0, t, 1 : SIZE2 - 1] = inverse
@@ -687,7 +709,7 @@
     g0, g1, g2 = (gain[i] for i in range(3))
     for i in (0, 1):
         for at, take in ((HALO0 - EDGE, prev_of), (HALO0 + rows, next_of)):
-            whole = take(even_y, near_a, near_b, slice(2, 2 + EDGE_TILES))
+            whole = take(even_y, near_a, near_b, slice(1, 1 + EDGE_TILES))
             x0[i, 0, at : at + EDGE] = whole[i * EDGE : (i + 1) * EDGE]
             for j in range(EDGE):
                 x0[i, 1, at + j : at + j + 1] = roll_x(whole[2 * EDGE :], -(4 + 8 * (i * EDGE + j)))
@@ -704,10 +726,10 @@
     total = rows + 2 * HALO0
     rows_loop(2, total - 2, lambda r, n: cheb_step(0, keep0, x0, y0, d0, r, n, None, g0))
     rows_loop(3, total - 3, lambda r, n: cheb_step(0, keep0, y0, x0, d0, r, n, CARRY1, g1))
-    rows_loop(4, total - 4, lambda r, n: cheb_step(0, keep0, x0, y0, d0, r, n, CARRY2, g2))
+    last = cheb_step(0, keep0, x0, None, d0, HALO0, rows, CARRY2, g2, (0,))[0]
     for i in (0, 1):
         for y in range(rows):
-            out[pl.ds(i * Z * rows + y, Z, stride=rows), :] = y0[i, 0, HALO0 + y]
+            out[pl.ds(i * Z * rows + y, Z, stride=rows), :] = last[i][y]
 
 
 def call(kernel, out_shapes, scratch, *args, space=pltpu.VMEM, outs=None):
@@ -751,24 +773,25 @@
     kill = kill.reshape(Z * rows, X)
     inputs = (state, previous, feed, kill)
 
-    strip = (FIELDS2 + 1, Z, X)
-    first, second, main, coarse = call(
+    strip = (PACKET, Z, X)
+    first, second, coarse, *inputs = call(
         functools.partial(first_kernel, rows),
-        [strip, strip, (6, rows, Z, X), (2 * OWN + 1, Z, X)],
-        [*(a.shape for a in inputs), pltpu.SemaphoreType.DMA((4,))],
+        [strip, strip, (2 * OWN + 1, Z, X), *(a.shape for a in inputs)],
+        [pltpu.SemaphoreType.DMA((4,))],
         *(pltpu.with_memory_space_constraint(a, pltpu.HBM) for a in inputs),
         space=pltpu.HBM,
     )
     y_packets = exchange(first, second, "gy")
+
     tiles = tiles_for(6 * rows + 2 * OWN + 1)
     spread_shape = (across * count, Z // 2, X)
-    first, second, spread = call(
+    first, second, spread, main = call(
         functools.partial(pack_own_kernel, rows),
-        [(tiles, Z, X), (tiles, Z, X), spread_shape],
+        [(tiles, Z, X), (tiles, Z, X), spread_shape, (6, rows, Z, X)],
         [(PER * tiles, Z, X), spread_shape, pltpu.SemaphoreType.DMA],
-        main,
+        *inputs,
         coarse,
-        outs=[pltpu.VMEM, pltpu.VMEM, pltpu.HBM],
+        outs=[pltpu.VMEM, pltpu.VMEM, pltpu.HBM, pltpu.VMEM],
     )
     own_x = exchange(first, second, "gx")
     spread = lax.all_to_all(spread, ("gx", "gy"), 0, 0, tiled=True)
@@ -836,10 +859,10 @@
     b_packets = exchange(first, second, "gy")
 
     one, two, up = (2, SIZE1, Z, X), (2, SIZE2, Z, X), (2, SIZE_UP, Z, X)
-    near = (2 + EDGE_TILES, Z, X)
+    near = (1 + EDGE_TILES, Z, X)
     packet, first, second, to_far, keep1 = call(
         level1_kernel,
-        [(2, Z, X), near, near, (4, Z, X), (2, *one)],
+        [(1, Z, X), near, near, (3, Z, X), (2, *one)],
         [one, one],
         own,
         *b_packets,

time: 38.7 us -> 38.6 us (level)
    all_to_all x1, waiting for transfers between devices: 0.5 us -> 1.25 us  [body(): spread = lax.all_to_all(spread, ('gx', 'gy'), 0, 0, tiled=True)]
    ppermute x10, waiting for transfers between devices: 6.9 us -> 6.32 us  [swap(): return lax.ppermute(value, axis, pairs + [(j, i) for i, j in pairs])]
where the time goes in v8:
time: 38.6 us; the launch traced here: 38.4 us
  starting transfers between devices  20.3 us (53%)
  waiting for transfers between devices  10.3 us (27%)
  Pallas kernels  7.75 us (20%)
    ppermute x10, starting transfers between devices, swap(): return lax.ppermute(value, axis, pairs + [(j, i) for i, j in pairs])  14.9 us
    pallas_call x10, Pallas kernels, call(): pl.pallas_call(kernel, out_shape=out, in_specs=[pl.BlockSpec(memory_space...  7.75 us
    ppermute x10, waiting for transfers between devices, swap(): return lax.ppermute(value, axis, pairs + [(j, i) for i, j in pairs])  6.32 us
    ppermute x2, starting transfers between devices, swap_far(): return lax.ppermute(value, axis, pairs + [(j, i) for i, j in pairs])  2.77 us
    ppermute x2, waiting for transfers between devices, swap_far(): return lax.ppermute(value, axis, pairs + [(j, i) for i, j in pairs])  2.72 us
    all_to_all x1, starting transfers between devices, body(): spread = lax.all_to_all(spread, ('gx', 'gy'), 0, 0, tiled=True)  2.57 us
    all_to_all x1, waiting for transfers between devices, body(): spread = lax.all_to_all(spread, ('gx', 'gy'), 0, 0, tiled=True)  1.25 us
  transfers between devices with their start and end apart: 13, of which 7 were waited for; matrix products, arithmetic and copies ran while one was open for 0% of the time, Pallas kernels for 8%

profile of v8, /device:TPU:0, one launch (start us, length us, event | category | flops | bytes accessed | tf_op | source)
XLA Modules:
  0.0 38.4 jit_solution(9101488032585056284)
XLA Ops:
  0.0 1.3 %shard_map.46 = (f32[27,8,128]{2,1,0:T(8,128)S(1)}, f32[27,8,128]{2,1,0:T(8,128)S(1)}, f32[9,8,128]{2,1,0:T(8,128)S(1)}, f32[256,128]{1,0:T(8,128)S(1)}, f32[256...) custom-call(f32[256,128]{1,0:T(8,128)} %bitcast.5, f32[256,128]{1,0:T(8,128)} %bitcast.6, ...), custom_call_target="tpu_custom_call" | custom-call | tf_op jit(solution)/shard_map/pallas_call | solution.py:737
  1.3 6.1 %collective-permute-start = (f32[27,8,128]{2,1,0:T(8,128)S(1)}, f32[27,8,128]{2,1,0:T(8,128)S(1)}, u32[]{:S(2)}, u32[]{:S(2)}) collective-permute-start(f32[27,8,128]{2,1,0:T(8,128)S(1)} %get-tuple-element.49), channel_id=1, source_target_pairs={{0,7},{2,1},{4,3},{6,5},{7,0},{1,2},{3,4},{5,6},{8,15},{10,9},{12,... | collective-permute-start | bytes 331784 | tf_op jit(solution)/shard_map/ppermute | solution.py:751
  7.4 0.9 %shard_map.47 = (f32[35,8,128]{2,1,0:T(8,128)S(1)}, f32[35,8,128]{2,1,0:T(8,128)S(1)}, f32[32,4,128]{2,1,0:T(4,128)}, f32[6,16,8,128]{3,2,1,0:T(8,128)S(1)}) custom-call(f32[256,128]{1,0:T(8,128)S(1)} %get-tuple-element.43.state, f32[256,128]{1,0:T(8,128)S(1)} %get-tuple-element.44.previous, f32[128,128]{1,0:T(8,128)S(1)} %get-tuple-element.45.feed, ...), custom_call_target="tpu_custom_call" | custom-call | tf_op jit(solution)/shard_map/pallas_call | solution.py:737
  8.3 0.7 %collective-permute-start.2 = (f32[35,8,128]{2,1,0:T(8,128)S(1)}, f32[35,8,128]{2,1,0:T(8,128)S(1)}, u32[]{:S(2)}, u32[]{:S(2)}) collective-permute-start(f32[35,8,128]{2,1,0:T(8,128)S(1)} %get-tuple-element.51), channel_id=1, source_target_pairs={{0,24},{16,8},{24,0},{8,16},{1,25},{17,9},{25,1},{9,17},{2,26},{18... | collective-permute-start | bytes 430088 | tf_op jit(solution)/shard_map/ppermute | solution.py:751
  9.1 1.0 %collective-permute-start.3 = (f32[35,8,128]{2,1,0:T(8,128)S(1)}, f32[35,8,128]{2,1,0:T(8,128)S(1)}, u32[]{:S(2)}, u32[]{:S(2)}) collective-permute-start(f32[35,8,128]{2,1,0:T(8,128)S(1)} %get-tuple-element.52), channel_id=1, source_target_pairs={{0,8},{16,24},{8,0},{24,16},{1,9},{17,25},{9,1},{25,17},{2,10},{18... | collective-permute-start | bytes 430088 | tf_op jit(solution)/shard_map/ppermute | solution.py:751
  10.0 2.6 %all-to-all-start = ((f32[32,4,128]{2,1,0:T(4,128)}), f32[32,4,128]{2,1,0:T(4,128)S(1)}, u32[]{:S(2)}, u32[]{:S(2)}) async-start(f32[32,4,128]{2,1,0:T(4,128)} %get-tuple-element.63), calls=%async_computation | async-start | bytes 131072 | tf_op jit(solution)/shard_map/all_to_all | solution.py:797
  12.6 0.2 collective-permute-done.1.y_second
  12.8 0.2 shard_map.48
  13.0 1.2 %collective-permute-start.4 = (f32[18,8,128]{2,1,0:T(8,128)S(1)}, f32[18,8,128]{2,1,0:T(8,128)S(1)}, u32[]{:S(2)}, u32[]{:S(2)}) collective-permute-start(f32[18,8,128]{2,1,0:T(8,128)S(1)} %get-tuple-element.53), channel_id=1, source_target_pairs={{0,24},{16,8},{24,0},{8,16},{1,25},{17,9},{25,1},{9,17},{2,26},{18... | collective-permute-start | bytes 221192 | tf_op jit(solution)/shard_map/ppermute | solution.py:751
  14.3 0.4 %collective-permute-start.5 = (f32[18,8,128]{2,1,0:T(8,128)S(1)}, f32[18,8,128]{2,1,0:T(8,128)S(1)}, u32[]{:S(2)}, u32[]{:S(2)}) collective-permute-start(f32[18,8,128]{2,1,0:T(8,128)S(1)} %get-tuple-element.54), channel_id=1, source_target_pairs={{0,8},{16,24},{8,0},{24,16},{1,9},{17,25},{9,1},{25,17},{2,10},{18... | collective-permute-start | bytes 221192 | tf_op jit(solution)/shard_map/ppermute | solution.py:751
  14.7 0.9 %shard_map.49 = (f32[6,2,14,8,128]{4,3,2,1,0:T(8,128)S(1)}, f32[2,2,4,8,128]{4,3,2,1,0:T(8,128)S(1)}, f32[2,2,12,8,128]{4,3,2,1,0:T(8,128)S(1)}, f32[2,2,10,8,12...) custom-call(f32[6,16,8,128]{3,2,1,0:T(8,128)S(1)} %get-tuple-element.48.main, ...), custom_call_target="tpu_custom_call" | custom-call | tf_op jit(solution)/shard_map/pallas_call | solution.py:737
  15.6 2.3 %collective-permute-done.4.corner_a = f32[18,8,128]{2,1,0:T(8,128)S(1)} collective-permute-done((f32[18,8,128]{2,1,0:T(8,128)S(1)}, f32[18,8,128]{2,1,0:T(8,128)S(1)}, u32[]{:S(2)}, u32[]{:S(2)}) %collective-permute-start.4) | collective-permute-done | bytes 73760 | tf_op jit(solution)/shard_map/ppermute | solution.py:751
  17.9 0.8 %shard_map.50 = (f32[6,2,8,8,128]{4,3,2,1,0:T(8,128)S(1)}, f32[2,2,4,8,128]{4,3,2,1,0:T(8,128)S(1)}, f32[2,2,6,8,128]{4,3,2,1,0:T(8,128)S(1)}, f32[4,2,4,8,128]{4,3,2,1,0:T(8,128)S(1)}, f32[3,2,7,8,128]{4,3,2,1,0:T(8,128)S(1)}) custom-call(f32[6,16,8,128]{3,2,1,0:T(8,128)S(1)} %get-tuple-element.48.main, f32[27,8,128]{2,1,0:T(8,128)S(1)} %collective-permute-done.y_first, ...), custom_call_target="tpu_custom_call" | custom-call | tf_op jit(solution)/shard_map/pallas_call | solution.py:737
  18.6 1.2 %all-to-all-done.spread = f32[32,4,128]{2,1,0:T(4,128)S(1)} async-done(((f32[32,4,128]{2,1,0:T(4,128)}), f32[32,4,128]{2,1,0:T(4,128)S(1)}, u32[]{:S(2)}, u32[]{:S(2)}) %all-to-all-start) | async-done | bytes 65568 | tf_op jit(solution)/shard_map/all_to_all | solution.py:797
  20.0 2.9 %collective-permute-start.6 = (f32[8,8,128]{2,1,0:T(8,128)S(1)}, f32[8,8,128]{2,1,0:T(8,128)S(1)}, u32[]{:S(2)}, u32[]{:S(2)}) collective-permute-start(f32[8,8,128]{2,1,0:T(8,128)S(1)} %get-tuple-element.65), channel_id=1, source_target_pairs={{0,7},{2,1},{4,3},{6,5},{7,0},{1,2},{3,4},{5,6},{8,15},{10,9},{12,... | collective-permute-start | bytes 98312 | tf_op jit(solution)/shard_map/ppermute | solution.py:751
  23.0 0.2 shard_map.53
  23.2 3.4 %collective-permute-done.6.first = f32[8,8,128]{2,1,0:T(8,128)S(1)} collective-permute-done((f32[8,8,128]{2,1,0:T(8,128)S(1)}, f32[8,8,128]{2,1,0:T(8,128)S(1)}, u32[]{:S(2)}, u32[]{:S(2)}) %collective-permute-start.6) | collective-permute-done | bytes 32800 | tf_op jit(solution)/shard_map/ppermute | solution.py:751
  26.7 0.3 collective-permute-done.7.second
  27.0 0.6 %shard_map.54 = (f32[1,8,128]{2,1,0:T(8,128)S(1)}, f32[8,8,128]{2,1,0:T(8,128)S(1)}, f32[8,8,128]{2,1,0:T(8,128)S(1)}, f32[3,8,128]{2,1,0:T(8,128)S(1)}, f32[2,2,14,8,128]{4,3,2,1,0:T(8,128)S(1)}) custom-call(f32[2,4,8,128]{3,2,1,0:T(8,128)S(1)} %get-tuple-element.64.own, f32[8,8,128]{2,1,0:T(8,128)S(1)} %collective-permute-done.6.first, ...), custom_call_target="tpu_custom_call" | custom-call | tf_op jit(solution)/shard_map/pallas_call | solution.py:737
  27.6 2.6 %collective-permute-start.8 = (f32[8,8,128]{2,1,0:T(8,128)S(1)}, f32[8,8,128]{2,1,0:T(8,128)S(1)}, u32[]{:S(2)}, u32[]{:S(2)}) collective-permute-start(f32[8,8,128]{2,1,0:T(8,128)S(1)} %get-tuple-element.75), channel_id=1, source_target_pairs={{0,7},{2,1},{4,3},{6,5},{7,0},{1,2},{3,4},{5,6},{8,15},{10,9},{12,... | collective-permute-start | bytes 98312 | tf_op jit(solution)/shard_map/ppermute | solution.py:751
  30.2 2.8 %collective-permute-start.11 = (f32[3,8,128]{2,1,0:T(8,128)S(1)}, f32[3,8,128]{2,1,0:T(8,128)S(1)}, u32[]{:S(2)}, u32[]{:S(2)}) collective-permute-start(f32[3,8,128]{2,1,0:T(8,128)S(1)} %get-tuple-element.77), channel_id=1, source_target_pairs={{0,6},{1,7},{4,2},{5,3},{6,0},{7,1},{2,4},{3,5},{8,14},{9,15},{12,... | collective-permute-start | bytes 36872 | tf_op jit(solution)/shard_map/ppermute | solution.py:758
  33.0 0.9 %collective-permute-done.10.far_a = f32[3,8,128]{2,1,0:T(8,128)S(1)} collective-permute-done((f32[3,8,128]{2,1,0:T(8,128)S(1)}, f32[3,8,128]{2,1,0:T(8,128)S(1)}, u32[]{:S(2)}, u32[]{:S(2)}) %collective-permute-start.10) | collective-permute-done | bytes 12320 | tf_op jit(solution)/shard_map/ppermute | solution.py:758
  33.9 1.8 %collective-permute-done.11.far_b = f32[3,8,128]{2,1,0:T(8,128)S(1)} collective-permute-done((f32[3,8,128]{2,1,0:T(8,128)S(1)}, f32[3,8,128]{2,1,0:T(8,128)S(1)}, u32[]{:S(2)}, u32[]{:S(2)}) %collective-permute-start.11) | collective-permute-done | bytes 12320 | tf_op jit(solution)/shard_map/ppermute | solution.py:758
  35.7 2.7 %shard_map.55 = f32[256,128]{1,0:T(8,128)} custom-call(f32[1,8,128]{2,1,0:T(8,128)S(1)} %get-tuple-element.74.own2, f32[8,8,128]{2,1,0:T(8,128)S(1)} %collective-permute-done.8.near_a, f32[8,8,128]{2,1,0:T(8,128)S(1)} %collective-permute-done.9.near_b, f32[3,8,128]{2,1,0:T(8,128)S(1)} %collective-permute-done.10.far_a, ...), custom_call_target="tpu_custom_call" | custom-call | tf_op jit(solution)/shard_map/pallas_call | solution.py:737
  (12 shorter events, 0.2 us)
Async XLA Ops:
  1.3 11.3 %collective-permute-start = (f32[27,8,128]{2,1,0:T(8,128)S(1)}, f32[27,8,128]{2,1,0:T(8,128)S(1)}, u32[]{:S(2)}, u32[]{:S(2)}) collective-permute-start(f32[27,8,128]{2,1,0:T(8,128)S(1)} %get-tuple-element.49), channel_id=1, source_target_pairs={{0,7},{2,1},{4,3},{6,5},{7,0},{1,2},{3,4},{5,6},{8,15},{10,9},{12,... | collective-permute-start | bytes 331784 | tf_op jit(solution)/shard_map/ppermute | solution.py:751
  7.4 5.4 %collective-permute-start.1 = (f32[27,8,128]{2,1,0:T(8,128)S(1)}, f32[27,8,128]{2,1,0:T(8,128)S(1)}, u32[]{:S(2)}, u32[]{:S(2)}) collective-permute-start(f32[27,8,128]{2,1,0:T(8,128)S(1)} %get-tuple-element.50), channel_id=1, source_target_pairs={{0,1},{2,3},{4,5},{6,7},{1,0},{3,2},{5,4},{7,6},{8,9},{10,11},{12,... | collective-permute-start | bytes 331784 | tf_op jit(solution)/shard_map/ppermute | solution.py:751
  8.3 6.4 %collective-permute-start.2 = (f32[35,8,128]{2,1,0:T(8,128)S(1)}, f32[35,8,128]{2,1,0:T(8,128)S(1)}, u32[]{:S(2)}, u32[]{:S(2)}) collective-permute-start(f32[35,8,128]{2,1,0:T(8,128)S(1)} %get-tuple-element.51), channel_id=1, source_target_pairs={{0,24},{16,8},{24,0},{8,16},{1,25},{17,9},{25,1},{9,17},{2,26},{18... | collective-permute-start | bytes 430088 | tf_op jit(solution)/shard_map/ppermute | solution.py:751
  9.1 5.6 %collective-permute-start.3 = (f32[35,8,128]{2,1,0:T(8,128)S(1)}, f32[35,8,128]{2,1,0:T(8,128)S(1)}, u32[]{:S(2)}, u32[]{:S(2)}) collective-permute-start(f32[35,8,128]{2,1,0:T(8,128)S(1)} %get-tuple-element.52), channel_id=1, source_target_pairs={{0,8},{16,24},{8,0},{24,16},{1,9},{17,25},{9,1},{25,17},{2,10},{18... | collective-permute-start | bytes 430088 | tf_op jit(solution)/shard_map/ppermute | solution.py:751
  10.0 9.9 %all-to-all-start = ((f32[32,4,128]{2,1,0:T(4,128)}), f32[32,4,128]{2,1,0:T(4,128)S(1)}, u32[]{:S(2)}, u32[]{:S(2)}) async-start(f32[32,4,128]{2,1,0:T(4,128)} %get-tuple-element.63), calls=%async_computation | async-start | bytes 131072 | tf_op jit(solution)/shard_map/all_to_all | solution.py:797
  13.0 4.8 %collective-permute-start.4 = (f32[18,8,128]{2,1,0:T(8,128)S(1)}, f32[18,8,128]{2,1,0:T(8,128)S(1)}, u32[]{:S(2)}, u32[]{:S(2)}) collective-permute-start(f32[18,8,128]{2,1,0:T(8,128)S(1)} %get-tuple-element.53), channel_id=1, source_target_pairs={{0,24},{16,8},{24,0},{8,16},{1,25},{17,9},{25,1},{9,17},{2,26},{18... | collective-permute-start | bytes 221192 | tf_op jit(solution)/shard_map/ppermute | solution.py:751
  14.3 3.6 %collective-permute-start.5 = (f32[18,8,128]{2,1,0:T(8,128)S(1)}, f32[18,8,128]{2,1,0:T(8,128)S(1)}, u32[]{:S(2)}, u32[]{:S(2)}) collective-permute-start(f32[18,8,128]{2,1,0:T(8,128)S(1)} %get-tuple-element.54), channel_id=1, source_target_pairs={{0,8},{16,24},{8,0},{24,16},{1,9},{17,25},{9,1},{25,17},{2,10},{18... | collective-permute-start | bytes 221192 | tf_op jit(solution)/shard_map/ppermute | solution.py:751
  20.0 6.7 %collective-permute-start.6 = (f32[8,8,128]{2,1,0:T(8,128)S(1)}, f32[8,8,128]{2,1,0:T(8,128)S(1)}, u32[]{:S(2)}, u32[]{:S(2)}) collective-permute-start(f32[8,8,128]{2,1,0:T(8,128)S(1)} %get-tuple-element.65), channel_id=1, source_target_pairs={{0,7},{2,1},{4,3},{6,5},{7,0},{1,2},{3,4},{5,6},{8,15},{10,9},{12,... | collective-permute-start | bytes 98312 | tf_op jit(solution)/shard_map/ppermute | solution.py:751
  22.9 4.1 %collective-permute-start.7 = (f32[8,8,128]{2,1,0:T(8,128)S(1)}, f32[8,8,128]{2,1,0:T(8,128)S(1)}, u32[]{:S(2)}, u32[]{:S(2)}) collective-permute-start(f32[8,8,128]{2,1,0:T(8,128)S(1)} %get-tuple-element.66), channel_id=1, source_target_pairs={{0,1},{2,3},{4,5},{6,7},{1,0},{3,2},{5,4},{7,6},{8,9},{10,11},{12,... | collective-permute-start | bytes 98312 | tf_op jit(solution)/shard_map/ppermute | solution.py:751
  27.6 8.1 %collective-permute-start.8 = (f32[8,8,128]{2,1,0:T(8,128)S(1)}, f32[8,8,128]{2,1,0:T(8,128)S(1)}, u32[]{:S(2)}, u32[]{:S(2)}) collective-permute-start(f32[8,8,128]{2,1,0:T(8,128)S(1)} %get-tuple-element.75), channel_id=1, source_target_pairs={{0,7},{2,1},{4,3},{6,5},{7,0},{1,2},{3,4},{5,6},{8,15},{10,9},{12,... | collective-permute-start | bytes 98312 | tf_op jit(solution)/shard_map/ppermute | solution.py:751
  30.2 5.5 %collective-permute-start.9 = (f32[8,8,128]{2,1,0:T(8,128)S(1)}, f32[8,8,128]{2,1,0:T(8,128)S(1)}, u32[]{:S(2)}, u32[]{:S(2)}) collective-permute-start(f32[8,8,128]{2,1,0:T(8,128)S(1)} %get-tuple-element.76), channel_id=1, source_target_pairs={{0,1},{2,3},{4,5},{6,7},{1,0},{3,2},{5,4},{7,6},{8,9},{10,11},{12,... | collective-permute-start | bytes 98312 | tf_op jit(solution)/shard_map/ppermute | solution.py:751
  30.2 3.7 %collective-permute-start.10 = (f32[3,8,128]{2,1,0:T(8,128)S(1)}, f32[3,8,128]{2,1,0:T(8,128)S(1)}, u32[]{:S(2)}, u32[]{:S(2)}) collective-permute-start(f32[3,8,128]{2,1,0:T(8,128)S(1)} %get-tuple-element.77), channel_id=1, source_target_pairs={{0,2},{1,3},{4,6},{5,7},{2,0},{3,1},{6,4},{7,5},{8,10},{9,11},{12,... | collective-permute-start | bytes 36872 | tf_op jit(solution)/shard_map/ppermute | solution.py:758
  30.2 5.5 %collective-permute-start.11 = (f32[3,8,128]{2,1,0:T(8,128)S(1)}, f32[3,8,128]{2,1,0:T(8,128)S(1)}, u32[]{:S(2)}, u32[]{:S(2)}) collective-permute-start(f32[3,8,128]{2,1,0:T(8,128)S(1)} %get-tuple-element.77), channel_id=1, source_target_pairs={{0,6},{1,7},{4,2},{5,3},{6,0},{7,1},{2,4},{3,5},{8,14},{9,15},{12,... | collective-permute-start | bytes 36872 | tf_op jit(solution)/shard_map/ppermute | solution.py:758

commit v9 on v8

--- a/solution.py
+++ b/solution.py
@@ -794,7 +794,8 @@
         outs=[pltpu.VMEM, pltpu.VMEM, pltpu.HBM, pltpu.VMEM],
     )
     own_x = exchange(first, second, "gx")
-    spread = lax.all_to_all(spread, ("gx", "gy"), 0, 0, tiled=True)
+    ranks = [(i + across // 2 * count + count // 2) % (across * count) for i in range(across * count)]
+    spread = lax.all_to_all(spread, ("gx", "gy"), 0, 0, axis_index_groups=[ranks], tiled=True)
     tiles = tiles_for(2 * PACKET)
     corner_x = exchange(
         *call(pack_corner_kernel, [(tiles, Z, X), (tiles, Z, X)], [(PER * tiles, Z, X)], *y_packets), "gx"

time: 38.6 us -> 38.6 us (level)
  no operation moved by 1% of the time
where the time goes in v9:
time: 38.6 us; the launch traced here: 38.4 us
  starting transfers between devices  20.3 us (53%)
  waiting for transfers between devices  10.3 us (27%)
  Pallas kernels  7.75 us (20%)
    ppermute x10, starting transfers between devices, swap(): return lax.ppermute(value, axis, pairs + [(j, i) for i, j in pairs])  14.9 us
    pallas_call x10, Pallas kernels, call(): pl.pallas_call(kernel, out_shape=out, in_specs=[pl.BlockSpec(memory_space...  7.75 us
    ppermute x10, waiting for transfers between devices, swap(): return lax.ppermute(value, axis, pairs + [(j, i) for i, j in pairs])  6.32 us
    ppermute x2, starting transfers between devices, swap_far(): return lax.ppermute(value, axis, pairs + [(j, i) for i, j in pairs])  2.77 us
    ppermute x2, waiting for transfers between devices, swap_far(): return lax.ppermute(value, axis, pairs + [(j, i) for i, j in pairs])  2.72 us
    all_to_all x1, starting transfers between devices, body(): lax.all_to_all(spread, ('gx', 'gy'), 0, 0, axis_index_groups=[ranks], til...  2.57 us
    all_to_all x1, waiting for transfers between devices, body(): lax.all_to_all(spread, ('gx', 'gy'), 0, 0, axis_index_groups=[ranks], til...  1.25 us
  transfers between devices with their start and end apart: 13, of which 7 were waited for; matrix products, arithmetic and copies ran while one was open for 0% of the time, Pallas kernels for 8%

profile of v9, /device:TPU:0, one launch (start us, length us, event | category | flops | bytes accessed | tf_op | source)
XLA Modules:
  0.0 38.4 jit_solution(9129115139924458878)
XLA Ops:
  0.0 1.3 %shard_map.46 = (f32[27,8,128]{2,1,0:T(8,128)S(1)}, f32[27,8,128]{2,1,0:T(8,128)S(1)}, f32[9,8,128]{2,1,0:T(8,128)S(1)}, f32[256,128]{1,0:T(8,128)S(1)}, f32[256...) custom-call(f32[256,128]{1,0:T(8,128)} %bitcast.5, f32[256,128]{1,0:T(8,128)} %bitcast.6, ...), custom_call_target="tpu_custom_call" | custom-call | tf_op jit(solution)/shard_map/pallas_call | solution.py:737
  1.3 6.1 %collective-permute-start = (f32[27,8,128]{2,1,0:T(8,128)S(1)}, f32[27,8,128]{2,1,0:T(8,128)S(1)}, u32[]{:S(2)}, u32[]{:S(2)}) collective-permute-start(f32[27,8,128]{2,1,0:T(8,128)S(1)} %get-tuple-element.49), channel_id=1, source_target_pairs={{0,7},{2,1},{4,3},{6,5},{7,0},{1,2},{3,4},{5,6},{8,15},{10,9},{12,... | collective-permute-start | bytes 331784 | tf_op jit(solution)/shard_map/ppermute | solution.py:751
  7.4 0.9 %shard_map.47 = (f32[35,8,128]{2,1,0:T(8,128)S(1)}, f32[35,8,128]{2,1,0:T(8,128)S(1)}, f32[32,4,128]{2,1,0:T(4,128)}, f32[6,16,8,128]{3,2,1,0:T(8,128)S(1)}) custom-call(f32[256,128]{1,0:T(8,128)S(1)} %get-tuple-element.43.state, f32[256,128]{1,0:T(8,128)S(1)} %get-tuple-element.44.previous, f32[128,128]{1,0:T(8,128)S(1)} %get-tuple-element.45.feed, ...), custom_call_target="tpu_custom_call" | custom-call | tf_op jit(solution)/shard_map/pallas_call | solution.py:737
  8.3 0.7 %collective-permute-start.2 = (f32[35,8,128]{2,1,0:T(8,128)S(1)}, f32[35,8,128]{2,1,0:T(8,128)S(1)}, u32[]{:S(2)}, u32[]{:S(2)}) collective-permute-start(f32[35,8,128]{2,1,0:T(8,128)S(1)} %get-tuple-element.51), channel_id=1, source_target_pairs={{0,24},{16,8},{24,0},{8,16},{1,25},{17,9},{25,1},{9,17},{2,26},{18... | collective-permute-start | bytes 430088 | tf_op jit(solution)/shard_map/ppermute | solution.py:751
  9.1 1.0 %collective-permute-start.3 = (f32[35,8,128]{2,1,0:T(8,128)S(1)}, f32[35,8,128]{2,1,0:T(8,128)S(1)}, u32[]{:S(2)}, u32[]{:S(2)}) collective-permute-start(f32[35,8,128]{2,1,0:T(8,128)S(1)} %get-tuple-element.52), channel_id=1, source_target_pairs={{0,8},{16,24},{8,0},{24,16},{1,9},{17,25},{9,1},{25,17},{2,10},{18... | collective-permute-start | bytes 430088 | tf_op jit(solution)/shard_map/ppermute | solution.py:751
  10.0 2.6 %all-to-all-start = ((f32[32,4,128]{2,1,0:T(4,128)}), f32[32,4,128]{2,1,0:T(4,128)S(1)}, u32[]{:S(2)}, u32[]{:S(2)}) async-start(f32[32,4,128]{2,1,0:T(4,128)} %get-tuple-element.63), calls=%async_computation | async-start | bytes 131072 | tf_op jit(solution)/shard_map/all_to_all | solution.py:798
  12.6 0.2 collective-permute-done.1.y_second
  12.8 0.2 shard_map.48
  13.0 1.2 %collective-permute-start.4 = (f32[18,8,128]{2,1,0:T(8,128)S(1)}, f32[18,8,128]{2,1,0:T(8,128)S(1)}, u32[]{:S(2)}, u32[]{:S(2)}) collective-permute-start(f32[18,8,128]{2,1,0:T(8,128)S(1)} %get-tuple-element.53), channel_id=1, source_target_pairs={{0,24},{16,8},{24,0},{8,16},{1,25},{17,9},{25,1},{9,17},{2,26},{18... | collective-permute-start | bytes 221192 | tf_op jit(solution)/shard_map/ppermute | solution.py:751
  14.3 0.4 %collective-permute-start.5 = (f32[18,8,128]{2,1,0:T(8,128)S(1)}, f32[18,8,128]{2,1,0:T(8,128)S(1)}, u32[]{:S(2)}, u32[]{:S(2)}) collective-permute-start(f32[18,8,128]{2,1,0:T(8,128)S(1)} %get-tuple-element.54), channel_id=1, source_target_pairs={{0,8},{16,24},{8,0},{24,16},{1,9},{17,25},{9,1},{25,17},{2,10},{18... | collective-permute-start | bytes 221192 | tf_op jit(solution)/shard_map/ppermute | solution.py:751
  14.7 0.9 %shard_map.49 = (f32[6,2,14,8,128]{4,3,2,1,0:T(8,128)S(1)}, f32[2,2,4,8,128]{4,3,2,1,0:T(8,128)S(1)}, f32[2,2,12,8,128]{4,3,2,1,0:T(8,128)S(1)}, f32[2,2,10,8,12...) custom-call(f32[6,16,8,128]{3,2,1,0:T(8,128)S(1)} %get-tuple-element.48.main, ...), custom_call_target="tpu_custom_call" | custom-call | tf_op jit(solution)/shard_map/pallas_call | solution.py:737
  15.6 2.3 %collective-permute-done.4.corner_a = f32[18,8,128]{2,1,0:T(8,128)S(1)} collective-permute-done((f32[18,8,128]{2,1,0:T(8,128)S(1)}, f32[18,8,128]{2,1,0:T(8,128)S(1)}, u32[]{:S(2)}, u32[]{:S(2)}) %collective-permute-start.4) | collective-permute-done | bytes 73760 | tf_op jit(solution)/shard_map/ppermute | solution.py:751
  17.9 0.8 %shard_map.50 = (f32[6,2,8,8,128]{4,3,2,1,0:T(8,128)S(1)}, f32[2,2,4,8,128]{4,3,2,1,0:T(8,128)S(1)}, f32[2,2,6,8,128]{4,3,2,1,0:T(8,128)S(1)}, f32[4,2,4,8,128]{4,3,2,1,0:T(8,128)S(1)}, f32[3,2,7,8,128]{4,3,2,1,0:T(8,128)S(1)}) custom-call(f32[6,16,8,128]{3,2,1,0:T(8,128)S(1)} %get-tuple-element.48.main, f32[27,8,128]{2,1,0:T(8,128)S(1)} %collective-permute-done.y_first, ...), custom_call_target="tpu_custom_call" | custom-call | tf_op jit(solution)/shard_map/pallas_call | solution.py:737
  18.6 1.2 %all-to-all-done.spread = f32[32,4,128]{2,1,0:T(4,128)S(1)} async-done(((f32[32,4,128]{2,1,0:T(4,128)}), f32[32,4,128]{2,1,0:T(4,128)S(1)}, u32[]{:S(2)}, u32[]{:S(2)}) %all-to-all-start) | async-done | bytes 65568 | tf_op jit(solution)/shard_map/all_to_all | solution.py:798
  20.0 2.9 %collective-permute-start.6 = (f32[8,8,128]{2,1,0:T(8,128)S(1)}, f32[8,8,128]{2,1,0:T(8,128)S(1)}, u32[]{:S(2)}, u32[]{:S(2)}) collective-permute-start(f32[8,8,128]{2,1,0:T(8,128)S(1)} %get-tuple-element.65), channel_id=1, source_target_pairs={{0,7},{2,1},{4,3},{6,5},{7,0},{1,2},{3,4},{5,6},{8,15},{10,9},{12,... | collective-permute-start | bytes 98312 | tf_op jit(solution)/shard_map/ppermute | solution.py:751
  23.0 0.2 shard_map.53
  23.2 3.4 %collective-permute-done.6.first = f32[8,8,128]{2,1,0:T(8,128)S(1)} collective-permute-done((f32[8,8,128]{2,1,0:T(8,128)S(1)}, f32[8,8,128]{2,1,0:T(8,128)S(1)}, u32[]{:S(2)}, u32[]{:S(2)}) %collective-permute-start.6) | collective-permute-done | bytes 32800 | tf_op jit(solution)/shard_map/ppermute | solution.py:751
  26.7 0.3 collective-permute-done.7.second
  27.0 0.6 %shard_map.54 = (f32[1,8,128]{2,1,0:T(8,128)S(1)}, f32[8,8,128]{2,1,0:T(8,128)S(1)}, f32[8,8,128]{2,1,0:T(8,128)S(1)}, f32[3,8,128]{2,1,0:T(8,128)S(1)}, f32[2,2,14,8,128]{4,3,2,1,0:T(8,128)S(1)}) custom-call(f32[2,4,8,128]{3,2,1,0:T(8,128)S(1)} %get-tuple-element.64.own, f32[8,8,128]{2,1,0:T(8,128)S(1)} %collective-permute-done.6.first, ...), custom_call_target="tpu_custom_call" | custom-call | tf_op jit(solution)/shard_map/pallas_call | solution.py:737
  27.6 2.6 %collective-permute-start.8 = (f32[8,8,128]{2,1,0:T(8,128)S(1)}, f32[8,8,128]{2,1,0:T(8,128)S(1)}, u32[]{:S(2)}, u32[]{:S(2)}) collective-permute-start(f32[8,8,128]{2,1,0:T(8,128)S(1)} %get-tuple-element.75), channel_id=1, source_target_pairs={{0,7},{2,1},{4,3},{6,5},{7,0},{1,2},{3,4},{5,6},{8,15},{10,9},{12,... | collective-permute-start | bytes 98312 | tf_op jit(solution)/shard_map/ppermute | solution.py:751
  30.2 2.8 %collective-permute-start.11 = (f32[3,8,128]{2,1,0:T(8,128)S(1)}, f32[3,8,128]{2,1,0:T(8,128)S(1)}, u32[]{:S(2)}, u32[]{:S(2)}) collective-permute-start(f32[3,8,128]{2,1,0:T(8,128)S(1)} %get-tuple-element.77), channel_id=1, source_target_pairs={{0,6},{1,7},{4,2},{5,3},{6,0},{7,1},{2,4},{3,5},{8,14},{9,15},{12,... | collective-permute-start | bytes 36872 | tf_op jit(solution)/shard_map/ppermute | solution.py:758
  33.0 0.9 %collective-permute-done.10.far_a = f32[3,8,128]{2,1,0:T(8,128)S(1)} collective-permute-done((f32[3,8,128]{2,1,0:T(8,128)S(1)}, f32[3,8,128]{2,1,0:T(8,128)S(1)}, u32[]{:S(2)}, u32[]{:S(2)}) %collective-permute-start.10) | collective-permute-done | bytes 12320 | tf_op jit(solution)/shard_map/ppermute | solution.py:758
  33.9 1.8 %collective-permute-done.11.far_b = f32[3,8,128]{2,1,0:T(8,128)S(1)} collective-permute-done((f32[3,8,128]{2,1,0:T(8,128)S(1)}, f32[3,8,128]{2,1,0:T(8,128)S(1)}, u32[]{:S(2)}, u32[]{:S(2)}) %collective-permute-start.11) | collective-permute-done | bytes 12320 | tf_op jit(solution)/shard_map/ppermute | solution.py:758
  35.7 2.7 %shard_map.55 = f32[256,128]{1,0:T(8,128)} custom-call(f32[1,8,128]{2,1,0:T(8,128)S(1)} %get-tuple-element.74.own2, f32[8,8,128]{2,1,0:T(8,128)S(1)} %collective-permute-done.8.near_a, f32[8,8,128]{2,1,0:T(8,128)S(1)} %collective-permute-done.9.near_b, f32[3,8,128]{2,1,0:T(8,128)S(1)} %collective-permute-done.10.far_a, ...), custom_call_target="tpu_custom_call" | custom-call | tf_op jit(solution)/shard_map/pallas_call | solution.py:737
  (12 shorter events, 0.2 us)
Async XLA Ops:
  1.3 11.3 %collective-permute-start = (f32[27,8,128]{2,1,0:T(8,128)S(1)}, f32[27,8,128]{2,1,0:T(8,128)S(1)}, u32[]{:S(2)}, u32[]{:S(2)}) collective-permute-start(f32[27,8,128]{2,1,0:T(8,128)S(1)} %get-tuple-element.49), channel_id=1, source_target_pairs={{0,7},{2,1},{4,3},{6,5},{7,0},{1,2},{3,4},{5,6},{8,15},{10,9},{12,... | collective-permute-start | bytes 331784 | tf_op jit(solution)/shard_map/ppermute | solution.py:751
  7.4 5.4 %collective-permute-start.1 = (f32[27,8,128]{2,1,0:T(8,128)S(1)}, f32[27,8,128]{2,1,0:T(8,128)S(1)}, u32[]{:S(2)}, u32[]{:S(2)}) collective-permute-start(f32[27,8,128]{2,1,0:T(8,128)S(1)} %get-tuple-element.50), channel_id=1, source_target_pairs={{0,1},{2,3},{4,5},{6,7},{1,0},{3,2},{5,4},{7,6},{8,9},{10,11},{12,... | collective-permute-start | bytes 331784 | tf_op jit(solution)/shard_map/ppermute | solution.py:751
  8.3 6.4 %collective-permute-start.2 = (f32[35,8,128]{2,1,0:T(8,128)S(1)}, f32[35,8,128]{2,1,0:T(8,128)S(1)}, u32[]{:S(2)}, u32[]{:S(2)}) collective-permute-start(f32[35,8,128]{2,1,0:T(8,128)S(1)} %get-tuple-element.51), channel_id=1, source_target_pairs={{0,24},{16,8},{24,0},{8,16},{1,25},{17,9},{25,1},{9,17},{2,26},{18... | collective-permute-start | bytes 430088 | tf_op jit(solution)/shard_map/ppermute | solution.py:751
  9.1 5.6 %collective-permute-start.3 = (f32[35,8,128]{2,1,0:T(8,128)S(1)}, f32[35,8,128]{2,1,0:T(8,128)S(1)}, u32[]{:S(2)}, u32[]{:S(2)}) collective-permute-start(f32[35,8,128]{2,1,0:T(8,128)S(1)} %get-tuple-element.52), channel_id=1, source_target_pairs={{0,8},{16,24},{8,0},{24,16},{1,9},{17,25},{9,1},{25,17},{2,10},{18... | collective-permute-start | bytes 430088 | tf_op jit(solution)/shard_map/ppermute | solution.py:751
  10.0 9.9 %all-to-all-start = ((f32[32,4,128]{2,1,0:T(4,128)}), f32[32,4,128]{2,1,0:T(4,128)S(1)}, u32[]{:S(2)}, u32[]{:S(2)}) async-start(f32[32,4,128]{2,1,0:T(4,128)} %get-tuple-element.63), calls=%async_computation | async-start | bytes 131072 | tf_op jit(solution)/shard_map/all_to_all | solution.py:798
  13.0 4.8 %collective-permute-start.4 = (f32[18,8,128]{2,1,0:T(8,128)S(1)}, f32[18,8,128]{2,1,0:T(8,128)S(1)}, u32[]{:S(2)}, u32[]{:S(2)}) collective-permute-start(f32[18,8,128]{2,1,0:T(8,128)S(1)} %get-tuple-element.53), channel_id=1, source_target_pairs={{0,24},{16,8},{24,0},{8,16},{1,25},{17,9},{25,1},{9,17},{2,26},{18... | collective-permute-start | bytes 221192 | tf_op jit(solution)/shard_map/ppermute | solution.py:751
  14.3 3.6 %collective-permute-start.5 = (f32[18,8,128]{2,1,0:T(8,128)S(1)}, f32[18,8,128]{2,1,0:T(8,128)S(1)}, u32[]{:S(2)}, u32[]{:S(2)}) collective-permute-start(f32[18,8,128]{2,1,0:T(8,128)S(1)} %get-tuple-element.54), channel_id=1, source_target_pairs={{0,8},{16,24},{8,0},{24,16},{1,9},{17,25},{9,1},{25,17},{2,10},{18... | collective-permute-start | bytes 221192 | tf_op jit(solution)/shard_map/ppermute | solution.py:751
  20.0 6.7 %collective-permute-start.6 = (f32[8,8,128]{2,1,0:T(8,128)S(1)}, f32[8,8,128]{2,1,0:T(8,128)S(1)}, u32[]{:S(2)}, u32[]{:S(2)}) collective-permute-start(f32[8,8,128]{2,1,0:T(8,128)S(1)} %get-tuple-element.65), channel_id=1, source_target_pairs={{0,7},{2,1},{4,3},{6,5},{7,0},{1,2},{3,4},{5,6},{8,15},{10,9},{12,... | collective-permute-start | bytes 98312 | tf_op jit(solution)/shard_map/ppermute | solution.py:751
  22.9 4.1 %collective-permute-start.7 = (f32[8,8,128]{2,1,0:T(8,128)S(1)}, f32[8,8,128]{2,1,0:T(8,128)S(1)}, u32[]{:S(2)}, u32[]{:S(2)}) collective-permute-start(f32[8,8,128]{2,1,0:T(8,128)S(1)} %get-tuple-element.66), channel_id=1, source_target_pairs={{0,1},{2,3},{4,5},{6,7},{1,0},{3,2},{5,4},{7,6},{8,9},{10,11},{12,... | collective-permute-start | bytes 98312 | tf_op jit(solution)/shard_map/ppermute | solution.py:751
  27.6 8.1 %collective-permute-start.8 = (f32[8,8,128]{2,1,0:T(8,128)S(1)}, f32[8,8,128]{2,1,0:T(8,128)S(1)}, u32[]{:S(2)}, u32[]{:S(2)}) collective-permute-start(f32[8,8,128]{2,1,0:T(8,128)S(1)} %get-tuple-element.75), channel_id=1, source_target_pairs={{0,7},{2,1},{4,3},{6,5},{7,0},{1,2},{3,4},{5,6},{8,15},{10,9},{12,... | collective-permute-start | bytes 98312 | tf_op jit(solution)/shard_map/ppermute | solution.py:751
  30.2 5.5 %collective-permute-start.9 = (f32[8,8,128]{2,1,0:T(8,128)S(1)}, f32[8,8,128]{2,1,0:T(8,128)S(1)}, u32[]{:S(2)}, u32[]{:S(2)}) collective-permute-start(f32[8,8,128]{2,1,0:T(8,128)S(1)} %get-tuple-element.76), channel_id=1, source_target_pairs={{0,1},{2,3},{4,5},{6,7},{1,0},{3,2},{5,4},{7,6},{8,9},{10,11},{12,... | collective-permute-start | bytes 98312 | tf_op jit(solution)/shard_map/ppermute | solution.py:751
  30.2 3.7 %collective-permute-start.10 = (f32[3,8,128]{2,1,0:T(8,128)S(1)}, f32[3,8,128]{2,1,0:T(8,128)S(1)}, u32[]{:S(2)}, u32[]{:S(2)}) collective-permute-start(f32[3,8,128]{2,1,0:T(8,128)S(1)} %get-tuple-element.77), channel_id=1, source_target_pairs={{0,2},{1,3},{4,6},{5,7},{2,0},{3,1},{6,4},{7,5},{8,10},{9,11},{12,... | collective-permute-start | bytes 36872 | tf_op jit(solution)/shard_map/ppermute | solution.py:758
  30.2 5.5 %collective-permute-start.11 = (f32[3,8,128]{2,1,0:T(8,128)S(1)}, f32[3,8,128]{2,1,0:T(8,128)S(1)}, u32[]{:S(2)}, u32[]{:S(2)}) collective-permute-start(f32[3,8,128]{2,1,0:T(8,128)S(1)} %get-tuple-element.77), channel_id=1, source_target_pairs={{0,6},{1,7},{4,2},{5,3},{6,0},{7,1},{2,4},{3,5},{8,14},{9,15},{12,... | collective-permute-start | bytes 36872 | tf_op jit(solution)/shard_map/ppermute | solution.py:758

commit v10 on v8

--- a/solution.py
+++ b/solution.py
@@ -567,6 +567,19 @@
     return jnp.concatenate([x[i, 0, start : start + EDGE] for i in (0, 1)] + [halo], axis=0)
 
 
+def squeeze(halo):
+    lane = lane_of()
+    last = halo[OWN - 1 : OWN]
+    ahead = (lane >= WIDE) & (lane < 2 * WIDE)
+    parts = [jnp.where(ahead, roll_x(last, WIDE), halo[0:1]), jnp.where(ahead, roll_x(last, 2 * WIDE - X), halo[1:2])]
+    return jnp.concatenate(parts + [halo[2 : OWN - 1]], axis=0)
+
+
+def unsqueeze(tiles):
+    last = jnp.where(lane_of() < X // 2, roll_x(tiles[0:1], -WIDE), roll_x(tiles[1:2], X - 2 * WIDE))
+    return jnp.concatenate([tiles, last], axis=0)
+
+
 def combine_kernel(sources, edges, spread, own, first, second, edge_first, edge_second, gain):
     write_gains(jnp.max(spread[...], axis=0)[0:1], gain)
     p0, p1, p2 = (gain[POWERS + i] for i in range(3))
@@ -574,7 +587,10 @@
         value = sources[0, t] - p0 * sources[1, t] + p1 * sources[2, t] - p2 * sources[3, t]
         own[t] = value
         for ref in (first, second):
-            ref[t * OWN : (t + 1) * OWN] = value
+            if t == 0:
+                ref[0:OWN] = value
+            else:
+                ref[OWN:] = squeeze(value)
     even = is_even("gy")
     top, bottom = (p0 * edges[0, side] - p1 * edges[1, side] + p2 * edges[2, side] for side in (0, 1))
     edge_first[...] = jnp.where(even, top, bottom)
@@ -638,14 +654,16 @@
     even = is_even("gy")
     for t in (0, 1):
         b1[t, 1 + OWN : 1 + 2 * OWN] = own[t]
-        strip = slice(t * OWN, (t + 1) * OWN)
-        b1[t, 1 : 1 + OWN] = prev_of(even, first, second, strip)
-        b1[t, 1 + 2 * OWN : 1 + 3 * OWN] = next_of(even, first, second, strip)
+        for at, take in ((1, prev_of), (1 + 2 * OWN, next_of)):
+            if t == 0:
+                b1[t, at : at + OWN] = take(even, first, second, slice(0, OWN))
+            else:
+                b1[t, at : at + OWN] = unsqueeze(take(even, first, second, slice(OWN, 2 * OWN - 1)))
     g0, g1, g2 = (gain[3 + i] for i in range(3))
     n = GROUPS1
     packed_first(coef1, 0, b1, x1, d1, 1, n, g0)
-    packed_step(1, coef1, 0, b1, x1, y1, d1, 1, n, CARRY1, g1)
-    packed_step(1, coef1, 0, b1, y1, x1, d1, 1, n, CARRY2, g2)
+    packed_step(1, coef1, 0, b1, x1, y1, d1, 2, n - 2, CARRY1, g1)
+    packed_step(1, coef1, 0, b1, y1, x1, d1, 2, n - 2, CARRY2, g2)
     here = pl.ds(1 + OWN, OWN)
     values = []
     for t, (c, other, spread) in enumerate(packed_terms(x1, 1 + OWN, OWN, 1)):
@@ -689,8 +707,8 @@
     packed_step(2, coef2, 0, b2, x2, y2, d2, 1, n, CARRY1, g1)
     packed_step(2, coef2, 0, b2, y2, x2, d2, 1, n, CARRY2, g2)
     packed_step(2, coef2, 0, b2, x2, y2, d2, 1, n, None, g0)
-    packed_step(2, coef2, 0, b2, y2, x2, d2, 1, n, CARRY1, g1)
-    packed_step(2, coef2, 0, b2, x2, y2, d2, 1, n, CARRY2, g2)
+    packed_step(2, coef2, 0, b2, y2, x2, d2, 2, n - 2, CARRY1, g1)
+    packed_step(2, coef2, 0, b2, x2, y2, d2, 2, n - 2, CARRY2, g2)
 
     g0, g1, g2 = (gain[3 + i] for i in range(3))
     shift = LO_UP - LO1
@@ -702,9 +720,9 @@
             at = g - LO_UP + 1
             xu[t, at : at + 1] = x1[t, at + shift : at + shift + 1] + value
     n = HI_UP - LO_UP
-    packed_step(1, coef1, shift, b1, xu, yu, d1, 1, n, None, g0)
-    packed_step(1, coef1, shift, b1, yu, xu, d1, 1, n, CARRY1, g1)
-    packed_step(1, coef1, shift, b1, xu, yu, d1, 1, n, CARRY2, g2)
+    packed_step(1, coef1, shift, b1, xu, yu, d1, 2, n - 2, None, g0)
+    packed_step(1, coef1, shift, b1, yu, xu, d1, 2, n - 2, CARRY1, g1)
+    packed_step(1, coef1, shift, b1, xu, yu, d1, 3, n - 4, CARRY2, g2)
 
     g0, g1, g2 = (gain[i] for i in range(3))
     for i in (0, 1):
@@ -800,7 +818,7 @@
         *call(pack_corner_kernel, [(tiles, Z, X), (tiles, Z, X)], [(PER * tiles, Z, X)], *y_packets), "gx"
     )
 
-    strip, edge = (2 * OWN, Z, X), (EDGE_TILES, Z, X)
+    strip, edge = (2 * OWN - 1, Z, X), (EDGE_TILES, Z, X)
     pair0 = (2, 2, total0, Z, X)
     work = [(6, 2, total0, Z, X), (6, 2, total0, Z, X), pair0, pair0, pair0, pair0]
     four = (4, 2, OWN, Z, X)

time: 38.6 us -> 38.4 us (level)
  no operation moved by 1% of the time
where the time goes in v10:
time: 38.4 us; the launch traced here: 38.2 us
  starting transfers between devices  20.2 us (53%)
  waiting for transfers between devices  10.3 us (27%)
  Pallas kernels  7.7 us (20%)
    ppermute x10, starting transfers between devices, swap(): return lax.ppermute(value, axis, pairs + [(j, i) for i, j in pairs])  14.9 us
    pallas_call x10, Pallas kernels, call(): pl.pallas_call(kernel, out_shape=out, in_specs=[pl.BlockSpec(memory_space...  7.7 us
    ppermute x10, waiting for transfers between devices, swap(): return lax.ppermute(value, axis, pairs + [(j, i) for i, j in pairs])  6.24 us
    ppermute x2, waiting for transfers between devices, swap_far(): return lax.ppermute(value, axis, pairs + [(j, i) for i, j in pairs])  2.77 us
    ppermute x2, starting transfers between devices, swap_far(): return lax.ppermute(value, axis, pairs + [(j, i) for i, j in pairs])  2.73 us
    all_to_all x1, starting transfers between devices, body(): spread = lax.all_to_all(spread, ('gx', 'gy'), 0, 0, tiled=True)  2.57 us
    all_to_all x1, waiting for transfers between devices, body(): spread = lax.all_to_all(spread, ('gx', 'gy'), 0, 0, tiled=True)  1.25 us
  transfers between devices with their start and end apart: 13, of which 7 were waited for; matrix products, arithmetic and copies ran while one was open for 0% of the time, Pallas kernels for 8%

profile of v10, /device:TPU:0, one launch (start us, length us, event | category | flops | bytes accessed | tf_op | source)
XLA Modules:
  0.0 38.2 jit_solution(10457677347939074247)
XLA Ops:
  0.0 1.3 %shard_map.46 = (f32[27,8,128]{2,1,0:T(8,128)S(1)}, f32[27,8,128]{2,1,0:T(8,128)S(1)}, f32[9,8,128]{2,1,0:T(8,128)S(1)}, f32[256,128]{1,0:T(8,128)S(1)}, f32[256...) custom-call(f32[256,128]{1,0:T(8,128)} %bitcast.5, f32[256,128]{1,0:T(8,128)} %bitcast.6, ...), custom_call_target="tpu_custom_call" | custom-call | tf_op jit(solution)/shard_map/pallas_call | solution.py:755
  1.3 6.1 %collective-permute-start = (f32[27,8,128]{2,1,0:T(8,128)S(1)}, f32[27,8,128]{2,1,0:T(8,128)S(1)}, u32[]{:S(2)}, u32[]{:S(2)}) collective-permute-start(f32[27,8,128]{2,1,0:T(8,128)S(1)} %get-tuple-element.49), channel_id=1, source_target_pairs={{0,7},{2,1},{4,3},{6,5},{7,0},{1,2},{3,4},{5,6},{8,15},{10,9},{12,... | collective-permute-start | bytes 331784 | tf_op jit(solution)/shard_map/ppermute | solution.py:769
  7.4 0.9 %shard_map.47 = (f32[35,8,128]{2,1,0:T(8,128)S(1)}, f32[35,8,128]{2,1,0:T(8,128)S(1)}, f32[32,4,128]{2,1,0:T(4,128)}, f32[6,16,8,128]{3,2,1,0:T(8,128)S(1)}) custom-call(f32[256,128]{1,0:T(8,128)S(1)} %get-tuple-element.43.state, f32[256,128]{1,0:T(8,128)S(1)} %get-tuple-element.44.previous, f32[128,128]{1,0:T(8,128)S(1)} %get-tuple-element.45.feed, ...), custom_call_target="tpu_custom_call" | custom-call | tf_op jit(solution)/shard_map/pallas_call | solution.py:755
  8.3 0.7 %collective-permute-start.2 = (f32[35,8,128]{2,1,0:T(8,128)S(1)}, f32[35,8,128]{2,1,0:T(8,128)S(1)}, u32[]{:S(2)}, u32[]{:S(2)}) collective-permute-start(f32[35,8,128]{2,1,0:T(8,128)S(1)} %get-tuple-element.51), channel_id=1, source_target_pairs={{0,24},{16,8},{24,0},{8,16},{1,25},{17,9},{25,1},{9,17},{2,26},{18... | collective-permute-start | bytes 430088 | tf_op jit(solution)/shard_map/ppermute | solution.py:769
  9.1 1.0 %collective-permute-start.3 = (f32[35,8,128]{2,1,0:T(8,128)S(1)}, f32[35,8,128]{2,1,0:T(8,128)S(1)}, u32[]{:S(2)}, u32[]{:S(2)}) collective-permute-start(f32[35,8,128]{2,1,0:T(8,128)S(1)} %get-tuple-element.52), channel_id=1, source_target_pairs={{0,8},{16,24},{8,0},{24,16},{1,9},{17,25},{9,1},{25,17},{2,10},{18... | collective-permute-start | bytes 430088 | tf_op jit(solution)/shard_map/ppermute | solution.py:769
  10.0 2.6 %all-to-all-start = ((f32[32,4,128]{2,1,0:T(4,128)}), f32[32,4,128]{2,1,0:T(4,128)S(1)}, u32[]{:S(2)}, u32[]{:S(2)}) async-start(f32[32,4,128]{2,1,0:T(4,128)} %get-tuple-element.63), calls=%async_computation | async-start | bytes 131072 | tf_op jit(solution)/shard_map/all_to_all | solution.py:815
  12.6 0.2 collective-permute-done.1.y_second
  13.0 1.2 %collective-permute-start.4 = (f32[18,8,128]{2,1,0:T(8,128)S(1)}, f32[18,8,128]{2,1,0:T(8,128)S(1)}, u32[]{:S(2)}, u32[]{:S(2)}) collective-permute-start(f32[18,8,128]{2,1,0:T(8,128)S(1)} %get-tuple-element.53), channel_id=1, source_target_pairs={{0,24},{16,8},{24,0},{8,16},{1,25},{17,9},{25,1},{9,17},{2,26},{18... | collective-permute-start | bytes 221192 | tf_op jit(solution)/shard_map/ppermute | solution.py:769
  14.3 0.4 %collective-permute-start.5 = (f32[18,8,128]{2,1,0:T(8,128)S(1)}, f32[18,8,128]{2,1,0:T(8,128)S(1)}, u32[]{:S(2)}, u32[]{:S(2)}) collective-permute-start(f32[18,8,128]{2,1,0:T(8,128)S(1)} %get-tuple-element.54), channel_id=1, source_target_pairs={{0,8},{16,24},{8,0},{24,16},{1,9},{17,25},{9,1},{25,17},{2,10},{18... | collective-permute-start | bytes 221192 | tf_op jit(solution)/shard_map/ppermute | solution.py:769
  14.7 0.9 %shard_map.49 = (f32[6,2,14,8,128]{4,3,2,1,0:T(8,128)S(1)}, f32[2,2,4,8,128]{4,3,2,1,0:T(8,128)S(1)}, f32[2,2,12,8,128]{4,3,2,1,0:T(8,128)S(1)}, f32[2,2,10,8,12...) custom-call(f32[6,16,8,128]{3,2,1,0:T(8,128)S(1)} %get-tuple-element.48.main, ...), custom_call_target="tpu_custom_call" | custom-call | tf_op jit(solution)/shard_map/pallas_call | solution.py:755
  15.6 2.3 %collective-permute-done.4.corner_a = f32[18,8,128]{2,1,0:T(8,128)S(1)} collective-permute-done((f32[18,8,128]{2,1,0:T(8,128)S(1)}, f32[18,8,128]{2,1,0:T(8,128)S(1)}, u32[]{:S(2)}, u32[]{:S(2)}) %collective-permute-start.4) | collective-permute-done | bytes 73760 | tf_op jit(solution)/shard_map/ppermute | solution.py:769
  17.9 0.8 %shard_map.50 = (f32[6,2,8,8,128]{4,3,2,1,0:T(8,128)S(1)}, f32[2,2,4,8,128]{4,3,2,1,0:T(8,128)S(1)}, f32[2,2,6,8,128]{4,3,2,1,0:T(8,128)S(1)}, f32[4,2,4,8,128]{4,3,2,1,0:T(8,128)S(1)}, f32[3,2,7,8,128]{4,3,2,1,0:T(8,128)S(1)}) custom-call(f32[6,16,8,128]{3,2,1,0:T(8,128)S(1)} %get-tuple-element.48.main, f32[27,8,128]{2,1,0:T(8,128)S(1)} %collective-permute-done.y_first, ...), custom_call_target="tpu_custom_call" | custom-call | tf_op jit(solution)/shard_map/pallas_call | solution.py:755
  18.6 1.2 %all-to-all-done.spread = f32[32,4,128]{2,1,0:T(4,128)S(1)} async-done(((f32[32,4,128]{2,1,0:T(4,128)}), f32[32,4,128]{2,1,0:T(4,128)S(1)}, u32[]{:S(2)}, u32[]{:S(2)}) %all-to-all-start) | async-done | bytes 65568 | tf_op jit(solution)/shard_map/all_to_all | solution.py:815
  19.9 0.2 shard_map.51
  20.1 2.9 %collective-permute-start.6 = (f32[7,8,128]{2,1,0:T(8,128)S(1)}, f32[7,8,128]{2,1,0:T(8,128)S(1)}, u32[]{:S(2)}, u32[]{:S(2)}) collective-permute-start(f32[7,8,128]{2,1,0:T(8,128)S(1)} %get-tuple-element.65), channel_id=1, source_target_pairs={{0,7},{2,1},{4,3},{6,5},{7,0},{1,2},{3,4},{5,6},{8,15},{10,9},{12,... | collective-permute-start | bytes 86024 | tf_op jit(solution)/shard_map/ppermute | solution.py:769
  23.0 0.2 shard_map.53
  23.2 3.4 %collective-permute-done.6.first = f32[7,8,128]{2,1,0:T(8,128)S(1)} collective-permute-done((f32[7,8,128]{2,1,0:T(8,128)S(1)}, f32[7,8,128]{2,1,0:T(8,128)S(1)}, u32[]{:S(2)}, u32[]{:S(2)}) %collective-permute-start.6) | collective-permute-done | bytes 28704 | tf_op jit(solution)/shard_map/ppermute | solution.py:769
  26.6 0.3 collective-permute-done.7.second
  26.9 0.5 %shard_map.54 = (f32[1,8,128]{2,1,0:T(8,128)S(1)}, f32[8,8,128]{2,1,0:T(8,128)S(1)}, f32[8,8,128]{2,1,0:T(8,128)S(1)}, f32[3,8,128]{2,1,0:T(8,128)S(1)}, f32[2,2,14,8,128]{4,3,2,1,0:T(8,128)S(1)}) custom-call(f32[2,4,8,128]{3,2,1,0:T(8,128)S(1)} %get-tuple-element.64.own, f32[7,8,128]{2,1,0:T(8,128)S(1)} %collective-permute-done.6.first, ...), custom_call_target="tpu_custom_call" | custom-call | tf_op jit(solution)/shard_map/pallas_call | solution.py:755
  27.5 2.6 %collective-permute-start.8 = (f32[8,8,128]{2,1,0:T(8,128)S(1)}, f32[8,8,128]{2,1,0:T(8,128)S(1)}, u32[]{:S(2)}, u32[]{:S(2)}) collective-permute-start(f32[8,8,128]{2,1,0:T(8,128)S(1)} %get-tuple-element.75), channel_id=1, source_target_pairs={{0,7},{2,1},{4,3},{6,5},{7,0},{1,2},{3,4},{5,6},{8,15},{10,9},{12,... | collective-permute-start | bytes 98312 | tf_op jit(solution)/shard_map/ppermute | solution.py:769
  30.1 2.7 %collective-permute-start.11 = (f32[3,8,128]{2,1,0:T(8,128)S(1)}, f32[3,8,128]{2,1,0:T(8,128)S(1)}, u32[]{:S(2)}, u32[]{:S(2)}) collective-permute-start(f32[3,8,128]{2,1,0:T(8,128)S(1)} %get-tuple-element.77), channel_id=1, source_target_pairs={{0,6},{1,7},{4,2},{5,3},{6,0},{7,1},{2,4},{3,5},{8,14},{9,15},{12,... | collective-permute-start | bytes 36872 | tf_op jit(solution)/shard_map/ppermute | solution.py:776
  32.8 1.0 %collective-permute-done.10.far_a = f32[3,8,128]{2,1,0:T(8,128)S(1)} collective-permute-done((f32[3,8,128]{2,1,0:T(8,128)S(1)}, f32[3,8,128]{2,1,0:T(8,128)S(1)}, u32[]{:S(2)}, u32[]{:S(2)}) %collective-permute-start.10) | collective-permute-done | bytes 12320 | tf_op jit(solution)/shard_map/ppermute | solution.py:776
  33.8 1.8 %collective-permute-done.11.far_b = f32[3,8,128]{2,1,0:T(8,128)S(1)} collective-permute-done((f32[3,8,128]{2,1,0:T(8,128)S(1)}, f32[3,8,128]{2,1,0:T(8,128)S(1)}, u32[]{:S(2)}, u32[]{:S(2)}) %collective-permute-start.11) | collective-permute-done | bytes 12320 | tf_op jit(solution)/shard_map/ppermute | solution.py:776
  35.6 2.6 %shard_map.55 = f32[256,128]{1,0:T(8,128)} custom-call(f32[1,8,128]{2,1,0:T(8,128)S(1)} %get-tuple-element.74.own2, f32[8,8,128]{2,1,0:T(8,128)S(1)} %collective-permute-done.8.near_a, f32[8,8,128]{2,1,0:T(8,128)S(1)} %collective-permute-done.9.near_b, f32[3,8,128]{2,1,0:T(8,128)S(1)} %collective-permute-done.10.far_a, ...), custom_call_target="tpu_custom_call" | custom-call | tf_op jit(solution)/shard_map/pallas_call | solution.py:755
  (12 shorter events, 0.3 us)
Async XLA Ops:
  1.3 11.3 %collective-permute-start = (f32[27,8,128]{2,1,0:T(8,128)S(1)}, f32[27,8,128]{2,1,0:T(8,128)S(1)}, u32[]{:S(2)}, u32[]{:S(2)}) collective-permute-start(f32[27,8,128]{2,1,0:T(8,128)S(1)} %get-tuple-element.49), channel_id=1, source_target_pairs={{0,7},{2,1},{4,3},{6,5},{7,0},{1,2},{3,4},{5,6},{8,15},{10,9},{12,... | collective-permute-start | bytes 331784 | tf_op jit(solution)/shard_map/ppermute | solution.py:769
  7.4 5.4 %collective-permute-start.1 = (f32[27,8,128]{2,1,0:T(8,128)S(1)}, f32[27,8,128]{2,1,0:T(8,128)S(1)}, u32[]{:S(2)}, u32[]{:S(2)}) collective-permute-start(f32[27,8,128]{2,1,0:T(8,128)S(1)} %get-tuple-element.50), channel_id=1, source_target_pairs={{0,1},{2,3},{4,5},{6,7},{1,0},{3,2},{5,4},{7,6},{8,9},{10,11},{12,... | collective-permute-start | bytes 331784 | tf_op jit(solution)/shard_map/ppermute | solution.py:769
  8.3 6.4 %collective-permute-start.2 = (f32[35,8,128]{2,1,0:T(8,128)S(1)}, f32[35,8,128]{2,1,0:T(8,128)S(1)}, u32[]{:S(2)}, u32[]{:S(2)}) collective-permute-start(f32[35,8,128]{2,1,0:T(8,128)S(1)} %get-tuple-element.51), channel_id=1, source_target_pairs={{0,24},{16,8},{24,0},{8,16},{1,25},{17,9},{25,1},{9,17},{2,26},{18... | collective-permute-start | bytes 430088 | tf_op jit(solution)/shard_map/ppermute | solution.py:769
  9.1 5.6 %collective-permute-start.3 = (f32[35,8,128]{2,1,0:T(8,128)S(1)}, f32[35,8,128]{2,1,0:T(8,128)S(1)}, u32[]{:S(2)}, u32[]{:S(2)}) collective-permute-start(f32[35,8,128]{2,1,0:T(8,128)S(1)} %get-tuple-element.52), channel_id=1, source_target_pairs={{0,8},{16,24},{8,0},{24,16},{1,9},{17,25},{9,1},{25,17},{2,10},{18... | collective-permute-start | bytes 430088 | tf_op jit(solution)/shard_map/ppermute | solution.py:769
  10.0 9.9 %all-to-all-start = ((f32[32,4,128]{2,1,0:T(4,128)}), f32[32,4,128]{2,1,0:T(4,128)S(1)}, u32[]{:S(2)}, u32[]{:S(2)}) async-start(f32[32,4,128]{2,1,0:T(4,128)} %get-tuple-element.63), calls=%async_computation | async-start | bytes 131072 | tf_op jit(solution)/shard_map/all_to_all | solution.py:815
  13.0 4.8 %collective-permute-start.4 = (f32[18,8,128]{2,1,0:T(8,128)S(1)}, f32[18,8,128]{2,1,0:T(8,128)S(1)}, u32[]{:S(2)}, u32[]{:S(2)}) collective-permute-start(f32[18,8,128]{2,1,0:T(8,128)S(1)} %get-tuple-element.53), channel_id=1, source_target_pairs={{0,24},{16,8},{24,0},{8,16},{1,25},{17,9},{25,1},{9,17},{2,26},{18... | collective-permute-start | bytes 221192 | tf_op jit(solution)/shard_map/ppermute | solution.py:769
  14.3 3.6 %collective-permute-start.5 = (f32[18,8,128]{2,1,0:T(8,128)S(1)}, f32[18,8,128]{2,1,0:T(8,128)S(1)}, u32[]{:S(2)}, u32[]{:S(2)}) collective-permute-start(f32[18,8,128]{2,1,0:T(8,128)S(1)} %get-tuple-element.54), channel_id=1, source_target_pairs={{0,8},{16,24},{8,0},{24,16},{1,9},{17,25},{9,1},{25,17},{2,10},{18... | collective-permute-start | bytes 221192 | tf_op jit(solution)/shard_map/ppermute | solution.py:769
  20.1 6.6 %collective-permute-start.6 = (f32[7,8,128]{2,1,0:T(8,128)S(1)}, f32[7,8,128]{2,1,0:T(8,128)S(1)}, u32[]{:S(2)}, u32[]{:S(2)}) collective-permute-start(f32[7,8,128]{2,1,0:T(8,128)S(1)} %get-tuple-element.65), channel_id=1, source_target_pairs={{0,7},{2,1},{4,3},{6,5},{7,0},{1,2},{3,4},{5,6},{8,15},{10,9},{12,... | collective-permute-start | bytes 86024 | tf_op jit(solution)/shard_map/ppermute | solution.py:769
  22.9 4.0 %collective-permute-start.7 = (f32[7,8,128]{2,1,0:T(8,128)S(1)}, f32[7,8,128]{2,1,0:T(8,128)S(1)}, u32[]{:S(2)}, u32[]{:S(2)}) collective-permute-start(f32[7,8,128]{2,1,0:T(8,128)S(1)} %get-tuple-element.66), channel_id=1, source_target_pairs={{0,1},{2,3},{4,5},{6,7},{1,0},{3,2},{5,4},{7,6},{8,9},{10,11},{12,... | collective-permute-start | bytes 86024 | tf_op jit(solution)/shard_map/ppermute | solution.py:769
  27.5 8.1 %collective-permute-start.8 = (f32[8,8,128]{2,1,0:T(8,128)S(1)}, f32[8,8,128]{2,1,0:T(8,128)S(1)}, u32[]{:S(2)}, u32[]{:S(2)}) collective-permute-start(f32[8,8,128]{2,1,0:T(8,128)S(1)} %get-tuple-element.75), channel_id=1, source_target_pairs={{0,7},{2,1},{4,3},{6,5},{7,0},{1,2},{3,4},{5,6},{8,15},{10,9},{12,... | collective-permute-start | bytes 98312 | tf_op jit(solution)/shard_map/ppermute | solution.py:769
  30.1 5.5 %collective-permute-start.9 = (f32[8,8,128]{2,1,0:T(8,128)S(1)}, f32[8,8,128]{2,1,0:T(8,128)S(1)}, u32[]{:S(2)}, u32[]{:S(2)}) collective-permute-start(f32[8,8,128]{2,1,0:T(8,128)S(1)} %get-tuple-element.76), channel_id=1, source_target_pairs={{0,1},{2,3},{4,5},{6,7},{1,0},{3,2},{5,4},{7,6},{8,9},{10,11},{12,... | collective-permute-start | bytes 98312 | tf_op jit(solution)/shard_map/ppermute | solution.py:769
  30.1 3.7 %collective-permute-start.10 = (f32[3,8,128]{2,1,0:T(8,128)S(1)}, f32[3,8,128]{2,1,0:T(8,128)S(1)}, u32[]{:S(2)}, u32[]{:S(2)}) collective-permute-start(f32[3,8,128]{2,1,0:T(8,128)S(1)} %get-tuple-element.77), channel_id=1, source_target_pairs={{0,2},{1,3},{4,6},{5,7},{2,0},{3,1},{6,4},{7,5},{8,10},{9,11},{12,... | collective-permute-start | bytes 36872 | tf_op jit(solution)/shard_map/ppermute | solution.py:776
  30.1 5.5 %collective-permute-start.11 = (f32[3,8,128]{2,1,0:T(8,128)S(1)}, f32[3,8,128]{2,1,0:T(8,128)S(1)}, u32[]{:S(2)}, u32[]{:S(2)}) collective-permute-start(f32[3,8,128]{2,1,0:T(8,128)S(1)} %get-tuple-element.77), channel_id=1, source_target_pairs={{0,6},{1,7},{4,2},{5,3},{6,0},{7,1},{2,4},{3,5},{8,14},{9,15},{12,... | collective-permute-start | bytes 36872 | tf_op jit(solution)/shard_map/ppermute | solution.py:776

commit v11 on v10

--- a/solution.py
+++ b/solution.py
@@ -54,21 +54,8 @@
     return pltpu.roll(tile, shift, 1) if shift else tile
 
 
-def rows_loop(lo, hi, body, step=None):
-    step = step or hi - lo
-    full = (hi - lo) // step
-    if full == 1:
-        body(lo, step)
-    elif full > 1:
-
-        def trip(i, carry):
-            body(lo + i * step, step)
-            return carry
-
-        lax.fori_loop(0, full, trip, 0)
-    rest = hi - lo - full * step
-    if rest:
-        body(hi - rest, rest)
+def chunks(lo, hi, step=4):
+    return [(r, min(step, hi - r)) for r in range(lo, hi, step)]
 
 
 def neighbour_sums(read, r, n, k, tiles=(0, 1)):
@@ -742,12 +729,15 @@
                     if -EDGE <= y < rows + EDGE:
                         x0[i, t, y + HALO0 : y + HALO0 + 1] = x0[i, t, y + HALO0 : y + HALO0 + 1] + fine
     total = rows + 2 * HALO0
-    rows_loop(2, total - 2, lambda r, n: cheb_step(0, keep0, x0, y0, d0, r, n, None, g0))
-    rows_loop(3, total - 3, lambda r, n: cheb_step(0, keep0, y0, x0, d0, r, n, CARRY1, g1))
-    last = cheb_step(0, keep0, x0, None, d0, HALO0, rows, CARRY2, g2, (0,))[0]
-    for i in (0, 1):
-        for y in range(rows):
-            out[pl.ds(i * Z * rows + y, Z, stride=rows), :] = last[i][y]
+    for r, n in chunks(2, total - 2):
+        cheb_step(0, keep0, x0, y0, d0, r, n, None, g0)
+    for r, n in chunks(3, total - 3):
+        cheb_step(0, keep0, y0, x0, d0, r, n, CARRY1, g1)
+    for r, n in chunks(4, total - 4):
+        last = cheb_step(0, keep0, x0, None, d0, r, n, CARRY2, g2, (0,))[0]
+        for i in (0, 1):
+            for j in range(n):
+                out[pl.ds(i * Z * rows + r - HALO0 + j, Z, stride=rows), :] = last[i][j]
 
 
 def call(kernel, out_shapes, scratch, *args, space=pltpu.VMEM, outs=None):

time: 38.4 us -> 38.4 us (level)
  no operation moved by 1% of the time
where the time goes in v11:
time: 38.4 us; the launch traced here: 38.2 us
  starting transfers between devices  20.2 us (53%)
  waiting for transfers between devices  10.3 us (27%)
  Pallas kernels  7.66 us (20%)
    ppermute x10, starting transfers between devices, swap(): return lax.ppermute(value, axis, pairs + [(j, i) for i, j in pairs])  14.9 us
    pallas_call x10, Pallas kernels, call(): pl.pallas_call(kernel, out_shape=out, in_specs=[pl.BlockSpec(memory_space...  7.66 us
    ppermute x10, waiting for transfers between devices, swap(): return lax.ppermute(value, axis, pairs + [(j, i) for i, j in pairs])  6.24 us
    ppermute x2, waiting for transfers between devices, swap_far(): return lax.ppermute(value, axis, pairs + [(j, i) for i, j in pairs])  2.77 us
    ppermute x2, starting transfers between devices, swap_far(): return lax.ppermute(value, axis, pairs + [(j, i) for i, j in pairs])  2.73 us
    all_to_all x1, starting transfers between devices, body(): spread = lax.all_to_all(spread, ('gx', 'gy'), 0, 0, tiled=True)  2.57 us
    all_to_all x1, waiting for transfers between devices, body(): spread = lax.all_to_all(spread, ('gx', 'gy'), 0, 0, tiled=True)  1.25 us
  transfers between devices with their start and end apart: 13, of which 7 were waited for; matrix products, arithmetic and copies ran while one was open for 0% of the time, Pallas kernels for 8%

profile of v11, /device:TPU:0, one launch (start us, length us, event | category | flops | bytes accessed | tf_op | source)
XLA Modules:
  0.0 38.2 jit_solution(4641461256013687104)
XLA Ops:
  0.0 1.3 %shard_map.46 = (f32[27,8,128]{2,1,0:T(8,128)S(1)}, f32[27,8,128]{2,1,0:T(8,128)S(1)}, f32[9,8,128]{2,1,0:T(8,128)S(1)}, f32[256,128]{1,0:T(8,128)S(1)}, f32[256...) custom-call(f32[256,128]{1,0:T(8,128)} %bitcast.5, f32[256,128]{1,0:T(8,128)} %bitcast.6, ...), custom_call_target="tpu_custom_call" | custom-call | tf_op jit(solution)/shard_map/pallas_call | solution.py:745
  1.3 6.1 %collective-permute-start = (f32[27,8,128]{2,1,0:T(8,128)S(1)}, f32[27,8,128]{2,1,0:T(8,128)S(1)}, u32[]{:S(2)}, u32[]{:S(2)}) collective-permute-start(f32[27,8,128]{2,1,0:T(8,128)S(1)} %get-tuple-element.49), channel_id=1, source_target_pairs={{0,7},{2,1},{4,3},{6,5},{7,0},{1,2},{3,4},{5,6},{8,15},{10,9},{12,... | collective-permute-start | bytes 331784 | tf_op jit(solution)/shard_map/ppermute | solution.py:759
  7.4 0.9 %shard_map.47 = (f32[35,8,128]{2,1,0:T(8,128)S(1)}, f32[35,8,128]{2,1,0:T(8,128)S(1)}, f32[32,4,128]{2,1,0:T(4,128)}, f32[6,16,8,128]{3,2,1,0:T(8,128)S(1)}) custom-call(f32[256,128]{1,0:T(8,128)S(1)} %get-tuple-element.43.state, f32[256,128]{1,0:T(8,128)S(1)} %get-tuple-element.44.previous, f32[128,128]{1,0:T(8,128)S(1)} %get-tuple-element.45.feed, ...), custom_call_target="tpu_custom_call" | custom-call | tf_op jit(solution)/shard_map/pallas_call | solution.py:745
  8.3 0.7 %collective-permute-start.2 = (f32[35,8,128]{2,1,0:T(8,128)S(1)}, f32[35,8,128]{2,1,0:T(8,128)S(1)}, u32[]{:S(2)}, u32[]{:S(2)}) collective-permute-start(f32[35,8,128]{2,1,0:T(8,128)S(1)} %get-tuple-element.51), channel_id=1, source_target_pairs={{0,24},{16,8},{24,0},{8,16},{1,25},{17,9},{25,1},{9,17},{2,26},{18... | collective-permute-start | bytes 430088 | tf_op jit(solution)/shard_map/ppermute | solution.py:759
  9.1 1.0 %collective-permute-start.3 = (f32[35,8,128]{2,1,0:T(8,128)S(1)}, f32[35,8,128]{2,1,0:T(8,128)S(1)}, u32[]{:S(2)}, u32[]{:S(2)}) collective-permute-start(f32[35,8,128]{2,1,0:T(8,128)S(1)} %get-tuple-element.52), channel_id=1, source_target_pairs={{0,8},{16,24},{8,0},{24,16},{1,9},{17,25},{9,1},{25,17},{2,10},{18... | collective-permute-start | bytes 430088 | tf_op jit(solution)/shard_map/ppermute | solution.py:759
  10.0 2.6 %all-to-all-start = ((f32[32,4,128]{2,1,0:T(4,128)}), f32[32,4,128]{2,1,0:T(4,128)S(1)}, u32[]{:S(2)}, u32[]{:S(2)}) async-start(f32[32,4,128]{2,1,0:T(4,128)} %get-tuple-element.63), calls=%async_computation | async-start | bytes 131072 | tf_op jit(solution)/shard_map/all_to_all | solution.py:805
  12.6 0.2 collective-permute-done.1.y_second
  13.0 1.2 %collective-permute-start.4 = (f32[18,8,128]{2,1,0:T(8,128)S(1)}, f32[18,8,128]{2,1,0:T(8,128)S(1)}, u32[]{:S(2)}, u32[]{:S(2)}) collective-permute-start(f32[18,8,128]{2,1,0:T(8,128)S(1)} %get-tuple-element.53), channel_id=1, source_target_pairs={{0,24},{16,8},{24,0},{8,16},{1,25},{17,9},{25,1},{9,17},{2,26},{18... | collective-permute-start | bytes 221192 | tf_op jit(solution)/shard_map/ppermute | solution.py:759
  14.3 0.4 %collective-permute-start.5 = (f32[18,8,128]{2,1,0:T(8,128)S(1)}, f32[18,8,128]{2,1,0:T(8,128)S(1)}, u32[]{:S(2)}, u32[]{:S(2)}) collective-permute-start(f32[18,8,128]{2,1,0:T(8,128)S(1)} %get-tuple-element.54), channel_id=1, source_target_pairs={{0,8},{16,24},{8,0},{24,16},{1,9},{17,25},{9,1},{25,17},{2,10},{18... | collective-permute-start | bytes 221192 | tf_op jit(solution)/shard_map/ppermute | solution.py:759
  14.7 0.9 %shard_map.49 = (f32[6,2,14,8,128]{4,3,2,1,0:T(8,128)S(1)}, f32[2,2,4,8,128]{4,3,2,1,0:T(8,128)S(1)}, f32[2,2,12,8,128]{4,3,2,1,0:T(8,128)S(1)}, f32[2,2,10,8,12...) custom-call(f32[6,16,8,128]{3,2,1,0:T(8,128)S(1)} %get-tuple-element.48.main, ...), custom_call_target="tpu_custom_call" | custom-call | tf_op jit(solution)/shard_map/pallas_call | solution.py:745
  15.6 2.3 %collective-permute-done.4.corner_a = f32[18,8,128]{2,1,0:T(8,128)S(1)} collective-permute-done((f32[18,8,128]{2,1,0:T(8,128)S(1)}, f32[18,8,128]{2,1,0:T(8,128)S(1)}, u32[]{:S(2)}, u32[]{:S(2)}) %collective-permute-start.4) | collective-permute-done | bytes 73760 | tf_op jit(solution)/shard_map/ppermute | solution.py:759
  17.9 0.8 %shard_map.50 = (f32[6,2,8,8,128]{4,3,2,1,0:T(8,128)S(1)}, f32[2,2,4,8,128]{4,3,2,1,0:T(8,128)S(1)}, f32[2,2,6,8,128]{4,3,2,1,0:T(8,128)S(1)}, f32[4,2,4,8,128]{4,3,2,1,0:T(8,128)S(1)}, f32[3,2,7,8,128]{4,3,2,1,0:T(8,128)S(1)}) custom-call(f32[6,16,8,128]{3,2,1,0:T(8,128)S(1)} %get-tuple-element.48.main, f32[27,8,128]{2,1,0:T(8,128)S(1)} %collective-permute-done.y_first, ...), custom_call_target="tpu_custom_call" | custom-call | tf_op jit(solution)/shard_map/pallas_call | solution.py:745
  18.6 1.2 %all-to-all-done.spread = f32[32,4,128]{2,1,0:T(4,128)S(1)} async-done(((f32[32,4,128]{2,1,0:T(4,128)}), f32[32,4,128]{2,1,0:T(4,128)S(1)}, u32[]{:S(2)}, u32[]{:S(2)}) %all-to-all-start) | async-done | bytes 65568 | tf_op jit(solution)/shard_map/all_to_all | solution.py:805
  19.9 0.2 shard_map.51
  20.1 2.9 %collective-permute-start.6 = (f32[7,8,128]{2,1,0:T(8,128)S(1)}, f32[7,8,128]{2,1,0:T(8,128)S(1)}, u32[]{:S(2)}, u32[]{:S(2)}) collective-permute-start(f32[7,8,128]{2,1,0:T(8,128)S(1)} %get-tuple-element.65), channel_id=1, source_target_pairs={{0,7},{2,1},{4,3},{6,5},{7,0},{1,2},{3,4},{5,6},{8,15},{10,9},{12,... | collective-permute-start | bytes 86024 | tf_op jit(solution)/shard_map/ppermute | solution.py:759
  23.0 0.2 shard_map.53
  23.2 3.4 %collective-permute-done.6.first = f32[7,8,128]{2,1,0:T(8,128)S(1)} collective-permute-done((f32[7,8,128]{2,1,0:T(8,128)S(1)}, f32[7,8,128]{2,1,0:T(8,128)S(1)}, u32[]{:S(2)}, u32[]{:S(2)}) %collective-permute-start.6) | collective-permute-done | bytes 28704 | tf_op jit(solution)/shard_map/ppermute | solution.py:759
  26.6 0.3 collective-permute-done.7.second
  26.9 0.5 %shard_map.54 = (f32[1,8,128]{2,1,0:T(8,128)S(1)}, f32[8,8,128]{2,1,0:T(8,128)S(1)}, f32[8,8,128]{2,1,0:T(8,128)S(1)}, f32[3,8,128]{2,1,0:T(8,128)S(1)}, f32[2,2,14,8,128]{4,3,2,1,0:T(8,128)S(1)}) custom-call(f32[2,4,8,128]{3,2,1,0:T(8,128)S(1)} %get-tuple-element.64.own, f32[7,8,128]{2,1,0:T(8,128)S(1)} %collective-permute-done.6.first, ...), custom_call_target="tpu_custom_call" | custom-call | tf_op jit(solution)/shard_map/pallas_call | solution.py:745
  27.5 2.6 %collective-permute-start.8 = (f32[8,8,128]{2,1,0:T(8,128)S(1)}, f32[8,8,128]{2,1,0:T(8,128)S(1)}, u32[]{:S(2)}, u32[]{:S(2)}) collective-permute-start(f32[8,8,128]{2,1,0:T(8,128)S(1)} %get-tuple-element.75), channel_id=1, source_target_pairs={{0,7},{2,1},{4,3},{6,5},{7,0},{1,2},{3,4},{5,6},{8,15},{10,9},{12,... | collective-permute-start | bytes 98312 | tf_op jit(solution)/shard_map/ppermute | solution.py:759
  30.1 2.7 %collective-permute-start.11 = (f32[3,8,128]{2,1,0:T(8,128)S(1)}, f32[3,8,128]{2,1,0:T(8,128)S(1)}, u32[]{:S(2)}, u32[]{:S(2)}) collective-permute-start(f32[3,8,128]{2,1,0:T(8,128)S(1)} %get-tuple-element.77), channel_id=1, source_target_pairs={{0,6},{1,7},{4,2},{5,3},{6,0},{7,1},{2,4},{3,5},{8,14},{9,15},{12,... | collective-permute-start | bytes 36872 | tf_op jit(solution)/shard_map/ppermute | solution.py:766
  32.8 1.0 %collective-permute-done.10.far_a = f32[3,8,128]{2,1,0:T(8,128)S(1)} collective-permute-done((f32[3,8,128]{2,1,0:T(8,128)S(1)}, f32[3,8,128]{2,1,0:T(8,128)S(1)}, u32[]{:S(2)}, u32[]{:S(2)}) %collective-permute-start.10) | collective-permute-done | bytes 12320 | tf_op jit(solution)/shard_map/ppermute | solution.py:766
  33.8 1.8 %collective-permute-done.11.far_b = f32[3,8,128]{2,1,0:T(8,128)S(1)} collective-permute-done((f32[3,8,128]{2,1,0:T(8,128)S(1)}, f32[3,8,128]{2,1,0:T(8,128)S(1)}, u32[]{:S(2)}, u32[]{:S(2)}) %collective-permute-start.11) | collective-permute-done | bytes 12320 | tf_op jit(solution)/shard_map/ppermute | solution.py:766
  35.6 2.6 %shard_map.55 = f32[256,128]{1,0:T(8,128)} custom-call(f32[1,8,128]{2,1,0:T(8,128)S(1)} %get-tuple-element.74.own2, f32[8,8,128]{2,1,0:T(8,128)S(1)} %collective-permute-done.8.near_a, f32[8,8,128]{2,1,0:T(8,128)S(1)} %collective-permute-done.9.near_b, f32[3,8,128]{2,1,0:T(8,128)S(1)} %collective-permute-done.10.far_a, ...), custom_call_target="tpu_custom_call" | custom-call | tf_op jit(solution)/shard_map/pallas_call | solution.py:745
  (12 shorter events, 0.3 us)
Async XLA Ops:
  1.3 11.3 %collective-permute-start = (f32[27,8,128]{2,1,0:T(8,128)S(1)}, f32[27,8,128]{2,1,0:T(8,128)S(1)}, u32[]{:S(2)}, u32[]{:S(2)}) collective-permute-start(f32[27,8,128]{2,1,0:T(8,128)S(1)} %get-tuple-element.49), channel_id=1, source_target_pairs={{0,7},{2,1},{4,3},{6,5},{7,0},{1,2},{3,4},{5,6},{8,15},{10,9},{12,... | collective-permute-start | bytes 331784 | tf_op jit(solution)/shard_map/ppermute | solution.py:759
  7.4 5.4 %collective-permute-start.1 = (f32[27,8,128]{2,1,0:T(8,128)S(1)}, f32[27,8,128]{2,1,0:T(8,128)S(1)}, u32[]{:S(2)}, u32[]{:S(2)}) collective-permute-start(f32[27,8,128]{2,1,0:T(8,128)S(1)} %get-tuple-element.50), channel_id=1, source_target_pairs={{0,1},{2,3},{4,5},{6,7},{1,0},{3,2},{5,4},{7,6},{8,9},{10,11},{12,... | collective-permute-start | bytes 331784 | tf_op jit(solution)/shard_map/ppermute | solution.py:759
  8.3 6.4 %collective-permute-start.2 = (f32[35,8,128]{2,1,0:T(8,128)S(1)}, f32[35,8,128]{2,1,0:T(8,128)S(1)}, u32[]{:S(2)}, u32[]{:S(2)}) collective-permute-start(f32[35,8,128]{2,1,0:T(8,128)S(1)} %get-tuple-element.51), channel_id=1, source_target_pairs={{0,24},{16,8},{24,0},{8,16},{1,25},{17,9},{25,1},{9,17},{2,26},{18... | collective-permute-start | bytes 430088 | tf_op jit(solution)/shard_map/ppermute | solution.py:759
  9.1 5.6 %collective-permute-start.3 = (f32[35,8,128]{2,1,0:T(8,128)S(1)}, f32[35,8,128]{2,1,0:T(8,128)S(1)}, u32[]{:S(2)}, u32[]{:S(2)}) collective-permute-start(f32[35,8,128]{2,1,0:T(8,128)S(1)} %get-tuple-element.52), channel_id=1, source_target_pairs={{0,8},{16,24},{8,0},{24,16},{1,9},{17,25},{9,1},{25,17},{2,10},{18... | collective-permute-start | bytes 430088 | tf_op jit(solution)/shard_map/ppermute | solution.py:759
  10.0 9.9 %all-to-all-start = ((f32[32,4,128]{2,1,0:T(4,128)}), f32[32,4,128]{2,1,0:T(4,128)S(1)}, u32[]{:S(2)}, u32[]{:S(2)}) async-start(f32[32,4,128]{2,1,0:T(4,128)} %get-tuple-element.63), calls=%async_computation | async-start | bytes 131072 | tf_op jit(solution)/shard_map/all_to_all | solution.py:805
  13.0 4.8 %collective-permute-start.4 = (f32[18,8,128]{2,1,0:T(8,128)S(1)}, f32[18,8,128]{2,1,0:T(8,128)S(1)}, u32[]{:S(2)}, u32[]{:S(2)}) collective-permute-start(f32[18,8,128]{2,1,0:T(8,128)S(1)} %get-tuple-element.53), channel_id=1, source_target_pairs={{0,24},{16,8},{24,0},{8,16},{1,25},{17,9},{25,1},{9,17},{2,26},{18... | collective-permute-start | bytes 221192 | tf_op jit(solution)/shard_map/ppermute | solution.py:759
  14.3 3.6 %collective-permute-start.5 = (f32[18,8,128]{2,1,0:T(8,128)S(1)}, f32[18,8,128]{2,1,0:T(8,128)S(1)}, u32[]{:S(2)}, u32[]{:S(2)}) collective-permute-start(f32[18,8,128]{2,1,0:T(8,128)S(1)} %get-tuple-element.54), channel_id=1, source_target_pairs={{0,8},{16,24},{8,0},{24,16},{1,9},{17,25},{9,1},{25,17},{2,10},{18... | collective-permute-start | bytes 221192 | tf_op jit(solution)/shard_map/ppermute | solution.py:759
  20.1 6.6 %collective-permute-start.6 = (f32[7,8,128]{2,1,0:T(8,128)S(1)}, f32[7,8,128]{2,1,0:T(8,128)S(1)}, u32[]{:S(2)}, u32[]{:S(2)}) collective-permute-start(f32[7,8,128]{2,1,0:T(8,128)S(1)} %get-tuple-element.65), channel_id=1, source_target_pairs={{0,7},{2,1},{4,3},{6,5},{7,0},{1,2},{3,4},{5,6},{8,15},{10,9},{12,... | collective-permute-start | bytes 86024 | tf_op jit(solution)/shard_map/ppermute | solution.py:759
  22.9 4.0 %collective-permute-start.7 = (f32[7,8,128]{2,1,0:T(8,128)S(1)}, f32[7,8,128]{2,1,0:T(8,128)S(1)}, u32[]{:S(2)}, u32[]{:S(2)}) collective-permute-start(f32[7,8,128]{2,1,0:T(8,128)S(1)} %get-tuple-element.66), channel_id=1, source_target_pairs={{0,1},{2,3},{4,5},{6,7},{1,0},{3,2},{5,4},{7,6},{8,9},{10,11},{12,... | collective-permute-start | bytes 86024 | tf_op jit(solution)/shard_map/ppermute | solution.py:759
  27.5 8.1 %collective-permute-start.8 = (f32[8,8,128]{2,1,0:T(8,128)S(1)}, f32[8,8,128]{2,1,0:T(8,128)S(1)}, u32[]{:S(2)}, u32[]{:S(2)}) collective-permute-start(f32[8,8,128]{2,1,0:T(8,128)S(1)} %get-tuple-element.75), channel_id=1, source_target_pairs={{0,7},{2,1},{4,3},{6,5},{7,0},{1,2},{3,4},{5,6},{8,15},{10,9},{12,... | collective-permute-start | bytes 98312 | tf_op jit(solution)/shard_map/ppermute | solution.py:759
  30.1 5.5 %collective-permute-start.9 = (f32[8,8,128]{2,1,0:T(8,128)S(1)}, f32[8,8,128]{2,1,0:T(8,128)S(1)}, u32[]{:S(2)}, u32[]{:S(2)}) collective-permute-start(f32[8,8,128]{2,1,0:T(8,128)S(1)} %get-tuple-element.76), channel_id=1, source_target_pairs={{0,1},{2,3},{4,5},{6,7},{1,0},{3,2},{5,4},{7,6},{8,9},{10,11},{12,... | collective-permute-start | bytes 98312 | tf_op jit(solution)/shard_map/ppermute | solution.py:759
  30.1 3.7 %collective-permute-start.10 = (f32[3,8,128]{2,1,0:T(8,128)S(1)}, f32[3,8,128]{2,1,0:T(8,128)S(1)}, u32[]{:S(2)}, u32[]{:S(2)}) collective-permute-start(f32[3,8,128]{2,1,0:T(8,128)S(1)} %get-tuple-element.77), channel_id=1, source_target_pairs={{0,2},{1,3},{4,6},{5,7},{2,0},{3,1},{6,4},{7,5},{8,10},{9,11},{12,... | collective-permute-start | bytes 36872 | tf_op jit(solution)/shard_map/ppermute | solution.py:766
  30.1 5.5 %collective-permute-start.11 = (f32[3,8,128]{2,1,0:T(8,128)S(1)}, f32[3,8,128]{2,1,0:T(8,128)S(1)}, u32[]{:S(2)}, u32[]{:S(2)}) collective-permute-start(f32[3,8,128]{2,1,0:T(8,128)S(1)} %get-tuple-element.77), channel_id=1, source_target_pairs={{0,6},{1,7},{4,2},{5,3},{6,0},{7,1},{2,4},{3,5},{8,14},{9,15},{12,... | collective-permute-start | bytes 36872 | tf_op jit(solution)/shard_map/ppermute | solution.py:766

commit v12 on v11

--- a/solution.py
+++ b/solution.py
@@ -767,7 +767,8 @@
 
 
 def exchange(first, second, axis):
-    return swap(first, axis, -1), swap(second, axis, 1)
+    other = swap(second, axis, 1)
+    return swap(first, axis, -1), other
 
 
 def body(state, previous, feed, kill):

time: 38.4 us -> 38.4 us (level)
  no operation moved by 1% of the time
where the time goes in v12:
time: 38.4 us; the launch traced here: 38.2 us
  starting transfers between devices  20.2 us (53%)
  waiting for transfers between devices  10.3 us (27%)
  Pallas kernels  7.66 us (20%)
    ppermute x10, starting transfers between devices, swap(): return lax.ppermute(value, axis, pairs + [(j, i) for i, j in pairs])  14.9 us
    pallas_call x10, Pallas kernels, call(): pl.pallas_call(kernel, out_shape=out, in_specs=[pl.BlockSpec(memory_space...  7.66 us
    ppermute x10, waiting for transfers between devices, swap(): return lax.ppermute(value, axis, pairs + [(j, i) for i, j in pairs])  6.24 us
    ppermute x2, waiting for transfers between devices, swap_far(): return lax.ppermute(value, axis, pairs + [(j, i) for i, j in pairs])  2.77 us
    ppermute x2, starting transfers between devices, swap_far(): return lax.ppermute(value, axis, pairs + [(j, i) for i, j in pairs])  2.73 us
    all_to_all x1, starting transfers between devices, body(): spread = lax.all_to_all(spread, ('gx', 'gy'), 0, 0, tiled=True)  2.57 us
    all_to_all x1, waiting for transfers between devices, body(): spread = lax.all_to_all(spread, ('gx', 'gy'), 0, 0, tiled=True)  1.25 us
  transfers between devices with their start and end apart: 13, of which 7 were waited for; matrix products, arithmetic and copies ran while one was open for 0% of the time, Pallas kernels for 8%

profile of v12, /device:TPU:0, one launch (start us, length us, event | category | flops | bytes accessed | tf_op | source)
XLA Modules:
  0.0 38.2 jit_solution(4641461256013687104)
XLA Ops:
  0.0 1.3 %shard_map.46 = (f32[27,8,128]{2,1,0:T(8,128)S(1)}, f32[27,8,128]{2,1,0:T(8,128)S(1)}, f32[9,8,128]{2,1,0:T(8,128)S(1)}, f32[256,128]{1,0:T(8,128)S(1)}, f32[256...) custom-call(f32[256,128]{1,0:T(8,128)} %bitcast.5, f32[256,128]{1,0:T(8,128)} %bitcast.6, ...), custom_call_target="tpu_custom_call" | custom-call | tf_op jit(solution)/shard_map/pallas_call | solution.py:745
  1.3 6.1 %collective-permute-start = (f32[27,8,128]{2,1,0:T(8,128)S(1)}, f32[27,8,128]{2,1,0:T(8,128)S(1)}, u32[]{:S(2)}, u32[]{:S(2)}) collective-permute-start(f32[27,8,128]{2,1,0:T(8,128)S(1)} %get-tuple-element.49), channel_id=1, source_target_pairs={{0,7},{2,1},{4,3},{6,5},{7,0},{1,2},{3,4},{5,6},{8,15},{10,9},{12,... | collective-permute-start | bytes 331784 | tf_op jit(solution)/shard_map/ppermute | solution.py:759
  7.4 0.9 %shard_map.47 = (f32[35,8,128]{2,1,0:T(8,128)S(1)}, f32[35,8,128]{2,1,0:T(8,128)S(1)}, f32[32,4,128]{2,1,0:T(4,128)}, f32[6,16,8,128]{3,2,1,0:T(8,128)S(1)}) custom-call(f32[256,128]{1,0:T(8,128)S(1)} %get-tuple-element.43.state, f32[256,128]{1,0:T(8,128)S(1)} %get-tuple-element.44.previous, f32[128,128]{1,0:T(8,128)S(1)} %get-tuple-element.45.feed, ...), custom_call_target="tpu_custom_call" | custom-call | tf_op jit(solution)/shard_map/pallas_call | solution.py:745
  8.3 0.7 %collective-permute-start.2 = (f32[35,8,128]{2,1,0:T(8,128)S(1)}, f32[35,8,128]{2,1,0:T(8,128)S(1)}, u32[]{:S(2)}, u32[]{:S(2)}) collective-permute-start(f32[35,8,128]{2,1,0:T(8,128)S(1)} %get-tuple-element.51), channel_id=1, source_target_pairs={{0,24},{16,8},{24,0},{8,16},{1,25},{17,9},{25,1},{9,17},{2,26},{18... | collective-permute-start | bytes 430088 | tf_op jit(solution)/shard_map/ppermute | solution.py:759
  9.1 1.0 %collective-permute-start.3 = (f32[35,8,128]{2,1,0:T(8,128)S(1)}, f32[35,8,128]{2,1,0:T(8,128)S(1)}, u32[]{:S(2)}, u32[]{:S(2)}) collective-permute-start(f32[35,8,128]{2,1,0:T(8,128)S(1)} %get-tuple-element.52), channel_id=1, source_target_pairs={{0,8},{16,24},{8,0},{24,16},{1,9},{17,25},{9,1},{25,17},{2,10},{18... | collective-permute-start | bytes 430088 | tf_op jit(solution)/shard_map/ppermute | solution.py:759
  10.0 2.6 %all-to-all-start = ((f32[32,4,128]{2,1,0:T(4,128)}), f32[32,4,128]{2,1,0:T(4,128)S(1)}, u32[]{:S(2)}, u32[]{:S(2)}) async-start(f32[32,4,128]{2,1,0:T(4,128)} %get-tuple-element.63), calls=%async_computation | async-start | bytes 131072 | tf_op jit(solution)/shard_map/all_to_all | solution.py:806
  12.6 0.2 collective-permute-done.1.y_second
  13.0 1.2 %collective-permute-start.4 = (f32[18,8,128]{2,1,0:T(8,128)S(1)}, f32[18,8,128]{2,1,0:T(8,128)S(1)}, u32[]{:S(2)}, u32[]{:S(2)}) collective-permute-start(f32[18,8,128]{2,1,0:T(8,128)S(1)} %get-tuple-element.53), channel_id=1, source_target_pairs={{0,24},{16,8},{24,0},{8,16},{1,25},{17,9},{25,1},{9,17},{2,26},{18... | collective-permute-start | bytes 221192 | tf_op jit(solution)/shard_map/ppermute | solution.py:759
  14.3 0.4 %collective-permute-start.5 = (f32[18,8,128]{2,1,0:T(8,128)S(1)}, f32[18,8,128]{2,1,0:T(8,128)S(1)}, u32[]{:S(2)}, u32[]{:S(2)}) collective-permute-start(f32[18,8,128]{2,1,0:T(8,128)S(1)} %get-tuple-element.54), channel_id=1, source_target_pairs={{0,8},{16,24},{8,0},{24,16},{1,9},{17,25},{9,1},{25,17},{2,10},{18... | collective-permute-start | bytes 221192 | tf_op jit(solution)/shard_map/ppermute | solution.py:759
  14.7 0.9 %shard_map.49 = (f32[6,2,14,8,128]{4,3,2,1,0:T(8,128)S(1)}, f32[2,2,4,8,128]{4,3,2,1,0:T(8,128)S(1)}, f32[2,2,12,8,128]{4,3,2,1,0:T(8,128)S(1)}, f32[2,2,10,8,12...) custom-call(f32[6,16,8,128]{3,2,1,0:T(8,128)S(1)} %get-tuple-element.48.main, ...), custom_call_target="tpu_custom_call" | custom-call | tf_op jit(solution)/shard_map/pallas_call | solution.py:745
  15.6 2.3 %collective-permute-done.4.corner_a = f32[18,8,128]{2,1,0:T(8,128)S(1)} collective-permute-done((f32[18,8,128]{2,1,0:T(8,128)S(1)}, f32[18,8,128]{2,1,0:T(8,128)S(1)}, u32[]{:S(2)}, u32[]{:S(2)}) %collective-permute-start.4) | collective-permute-done | bytes 73760 | tf_op jit(solution)/shard_map/ppermute | solution.py:759
  17.9 0.8 %shard_map.50 = (f32[6,2,8,8,128]{4,3,2,1,0:T(8,128)S(1)}, f32[2,2,4,8,128]{4,3,2,1,0:T(8,128)S(1)}, f32[2,2,6,8,128]{4,3,2,1,0:T(8,128)S(1)}, f32[4,2,4,8,128]{4,3,2,1,0:T(8,128)S(1)}, f32[3,2,7,8,128]{4,3,2,1,0:T(8,128)S(1)}) custom-call(f32[6,16,8,128]{3,2,1,0:T(8,128)S(1)} %get-tuple-element.48.main, f32[27,8,128]{2,1,0:T(8,128)S(1)} %collective-permute-done.y_first, ...), custom_call_target="tpu_custom_call" | custom-call | tf_op jit(solution)/shard_map/pallas_call | solution.py:745
  18.6 1.2 %all-to-all-done.spread = f32[32,4,128]{2,1,0:T(4,128)S(1)} async-done(((f32[32,4,128]{2,1,0:T(4,128)}), f32[32,4,128]{2,1,0:T(4,128)S(1)}, u32[]{:S(2)}, u32[]{:S(2)}) %all-to-all-start) | async-done | bytes 65568 | tf_op jit(solution)/shard_map/all_to_all | solution.py:806
  19.9 0.2 shard_map.51
  20.1 2.9 %collective-permute-start.6 = (f32[7,8,128]{2,1,0:T(8,128)S(1)}, f32[7,8,128]{2,1,0:T(8,128)S(1)}, u32[]{:S(2)}, u32[]{:S(2)}) collective-permute-start(f32[7,8,128]{2,1,0:T(8,128)S(1)} %get-tuple-element.65), channel_id=1, source_target_pairs={{0,7},{2,1},{4,3},{6,5},{7,0},{1,2},{3,4},{5,6},{8,15},{10,9},{12,... | collective-permute-start | bytes 86024 | tf_op jit(solution)/shard_map/ppermute | solution.py:759
  23.0 0.2 shard_map.53
  23.2 3.4 %collective-permute-done.6.first = f32[7,8,128]{2,1,0:T(8,128)S(1)} collective-permute-done((f32[7,8,128]{2,1,0:T(8,128)S(1)}, f32[7,8,128]{2,1,0:T(8,128)S(1)}, u32[]{:S(2)}, u32[]{:S(2)}) %collective-permute-start.6) | collective-permute-done | bytes 28704 | tf_op jit(solution)/shard_map/ppermute | solution.py:759
  26.6 0.3 collective-permute-done.7.second
  26.9 0.5 %shard_map.54 = (f32[1,8,128]{2,1,0:T(8,128)S(1)}, f32[8,8,128]{2,1,0:T(8,128)S(1)}, f32[8,8,128]{2,1,0:T(8,128)S(1)}, f32[3,8,128]{2,1,0:T(8,128)S(1)}, f32[2,2,14,8,128]{4,3,2,1,0:T(8,128)S(1)}) custom-call(f32[2,4,8,128]{3,2,1,0:T(8,128)S(1)} %get-tuple-element.64.own, f32[7,8,128]{2,1,0:T(8,128)S(1)} %collective-permute-done.6.first, ...), custom_call_target="tpu_custom_call" | custom-call | tf_op jit(solution)/shard_map/pallas_call | solution.py:745
  27.5 2.6 %collective-permute-start.8 = (f32[8,8,128]{2,1,0:T(8,128)S(1)}, f32[8,8,128]{2,1,0:T(8,128)S(1)}, u32[]{:S(2)}, u32[]{:S(2)}) collective-permute-start(f32[8,8,128]{2,1,0:T(8,128)S(1)} %get-tuple-element.75), channel_id=1, source_target_pairs={{0,7},{2,1},{4,3},{6,5},{7,0},{1,2},{3,4},{5,6},{8,15},{10,9},{12,... | collective-permute-start | bytes 98312 | tf_op jit(solution)/shard_map/ppermute | solution.py:759
  30.1 2.7 %collective-permute-start.11 = (f32[3,8,128]{2,1,0:T(8,128)S(1)}, f32[3,8,128]{2,1,0:T(8,128)S(1)}, u32[]{:S(2)}, u32[]{:S(2)}) collective-permute-start(f32[3,8,128]{2,1,0:T(8,128)S(1)} %get-tuple-element.77), channel_id=1, source_target_pairs={{0,6},{1,7},{4,2},{5,3},{6,0},{7,1},{2,4},{3,5},{8,14},{9,15},{12,... | collective-permute-start | bytes 36872 | tf_op jit(solution)/shard_map/ppermute | solution.py:766
  32.8 1.0 %collective-permute-done.10.far_a = f32[3,8,128]{2,1,0:T(8,128)S(1)} collective-permute-done((f32[3,8,128]{2,1,0:T(8,128)S(1)}, f32[3,8,128]{2,1,0:T(8,128)S(1)}, u32[]{:S(2)}, u32[]{:S(2)}) %collective-permute-start.10) | collective-permute-done | bytes 12320 | tf_op jit(solution)/shard_map/ppermute | solution.py:766
  33.8 1.8 %collective-permute-done.11.far_b = f32[3,8,128]{2,1,0:T(8,128)S(1)} collective-permute-done((f32[3,8,128]{2,1,0:T(8,128)S(1)}, f32[3,8,128]{2,1,0:T(8,128)S(1)}, u32[]{:S(2)}, u32[]{:S(2)}) %collective-permute-start.11) | collective-permute-done | bytes 12320 | tf_op jit(solution)/shard_map/ppermute | solution.py:766
  35.6 2.6 %shard_map.55 = f32[256,128]{1,0:T(8,128)} custom-call(f32[1,8,128]{2,1,0:T(8,128)S(1)} %get-tuple-element.74.own2, f32[8,8,128]{2,1,0:T(8,128)S(1)} %collective-permute-done.8.near_a, f32[8,8,128]{2,1,0:T(8,128)S(1)} %collective-permute-done.9.near_b, f32[3,8,128]{2,1,0:T(8,128)S(1)} %collective-permute-done.10.far_a, ...), custom_call_target="tpu_custom_call" | custom-call | tf_op jit(solution)/shard_map/pallas_call | solution.py:745
  (12 shorter events, 0.3 us)
Async XLA Ops:
  1.3 11.3 %collective-permute-start = (f32[27,8,128]{2,1,0:T(8,128)S(1)}, f32[27,8,128]{2,1,0:T(8,128)S(1)}, u32[]{:S(2)}, u32[]{:S(2)}) collective-permute-start(f32[27,8,128]{2,1,0:T(8,128)S(1)} %get-tuple-element.49), channel_id=1, source_target_pairs={{0,7},{2,1},{4,3},{6,5},{7,0},{1,2},{3,4},{5,6},{8,15},{10,9},{12,... | collective-permute-start | bytes 331784 | tf_op jit(solution)/shard_map/ppermute | solution.py:759
  7.4 5.4 %collective-permute-start.1 = (f32[27,8,128]{2,1,0:T(8,128)S(1)}, f32[27,8,128]{2,1,0:T(8,128)S(1)}, u32[]{:S(2)}, u32[]{:S(2)}) collective-permute-start(f32[27,8,128]{2,1,0:T(8,128)S(1)} %get-tuple-element.50), channel_id=1, source_target_pairs={{0,1},{2,3},{4,5},{6,7},{1,0},{3,2},{5,4},{7,6},{8,9},{10,11},{12,... | collective-permute-start | bytes 331784 | tf_op jit(solution)/shard_map/ppermute | solution.py:759
  8.3 6.4 %collective-permute-start.2 = (f32[35,8,128]{2,1,0:T(8,128)S(1)}, f32[35,8,128]{2,1,0:T(8,128)S(1)}, u32[]{:S(2)}, u32[]{:S(2)}) collective-permute-start(f32[35,8,128]{2,1,0:T(8,128)S(1)} %get-tuple-element.51), channel_id=1, source_target_pairs={{0,24},{16,8},{24,0},{8,16},{1,25},{17,9},{25,1},{9,17},{2,26},{18... | collective-permute-start | bytes 430088 | tf_op jit(solution)/shard_map/ppermute | solution.py:759
  9.1 5.6 %collective-permute-start.3 = (f32[35,8,128]{2,1,0:T(8,128)S(1)}, f32[35,8,128]{2,1,0:T(8,128)S(1)}, u32[]{:S(2)}, u32[]{:S(2)}) collective-permute-start(f32[35,8,128]{2,1,0:T(8,128)S(1)} %get-tuple-element.52), channel_id=1, source_target_pairs={{0,8},{16,24},{8,0},{24,16},{1,9},{17,25},{9,1},{25,17},{2,10},{18... | collective-permute-start | bytes 430088 | tf_op jit(solution)/shard_map/ppermute | solution.py:759
  10.0 9.9 %all-to-all-start = ((f32[32,4,128]{2,1,0:T(4,128)}), f32[32,4,128]{2,1,0:T(4,128)S(1)}, u32[]{:S(2)}, u32[]{:S(2)}) async-start(f32[32,4,128]{2,1,0:T(4,128)} %get-tuple-element.63), calls=%async_computation | async-start | bytes 131072 | tf_op jit(solution)/shard_map/all_to_all | solution.py:806
  13.0 4.8 %collective-permute-start.4 = (f32[18,8,128]{2,1,0:T(8,128)S(1)}, f32[18,8,128]{2,1,0:T(8,128)S(1)}, u32[]{:S(2)}, u32[]{:S(2)}) collective-permute-start(f32[18,8,128]{2,1,0:T(8,128)S(1)} %get-tuple-element.53), channel_id=1, source_target_pairs={{0,24},{16,8},{24,0},{8,16},{1,25},{17,9},{25,1},{9,17},{2,26},{18... | collective-permute-start | bytes 221192 | tf_op jit(solution)/shard_map/ppermute | solution.py:759
  14.3 3.6 %collective-permute-start.5 = (f32[18,8,128]{2,1,0:T(8,128)S(1)}, f32[18,8,128]{2,1,0:T(8,128)S(1)}, u32[]{:S(2)}, u32[]{:S(2)}) collective-permute-start(f32[18,8,128]{2,1,0:T(8,128)S(1)} %get-tuple-element.54), channel_id=1, source_target_pairs={{0,8},{16,24},{8,0},{24,16},{1,9},{17,25},{9,1},{25,17},{2,10},{18... | collective-permute-start | bytes 221192 | tf_op jit(solution)/shard_map/ppermute | solution.py:759
  20.1 6.6 %collective-permute-start.6 = (f32[7,8,128]{2,1,0:T(8,128)S(1)}, f32[7,8,128]{2,1,0:T(8,128)S(1)}, u32[]{:S(2)}, u32[]{:S(2)}) collective-permute-start(f32[7,8,128]{2,1,0:T(8,128)S(1)} %get-tuple-element.65), channel_id=1, source_target_pairs={{0,7},{2,1},{4,3},{6,5},{7,0},{1,2},{3,4},{5,6},{8,15},{10,9},{12,... | collective-permute-start | bytes 86024 | tf_op jit(solution)/shard_map/ppermute | solution.py:759
  22.9 4.0 %collective-permute-start.7 = (f32[7,8,128]{2,1,0:T(8,128)S(1)}, f32[7,8,128]{2,1,0:T(8,128)S(1)}, u32[]{:S(2)}, u32[]{:S(2)}) collective-permute-start(f32[7,8,128]{2,1,0:T(8,128)S(1)} %get-tuple-element.66), channel_id=1, source_target_pairs={{0,1},{2,3},{4,5},{6,7},{1,0},{3,2},{5,4},{7,6},{8,9},{10,11},{12,... | collective-permute-start | bytes 86024 | tf_op jit(solution)/shard_map/ppermute | solution.py:759
  27.5 8.1 %collective-permute-start.8 = (f32[8,8,128]{2,1,0:T(8,128)S(1)}, f32[8,8,128]{2,1,0:T(8,128)S(1)}, u32[]{:S(2)}, u32[]{:S(2)}) collective-permute-start(f32[8,8,128]{2,1,0:T(8,128)S(1)} %get-tuple-element.75), channel_id=1, source_target_pairs={{0,7},{2,1},{4,3},{6,5},{7,0},{1,2},{3,4},{5,6},{8,15},{10,9},{12,... | collective-permute-start | bytes 98312 | tf_op jit(solution)/shard_map/ppermute | solution.py:759
  30.1 5.5 %collective-permute-start.9 = (f32[8,8,128]{2,1,0:T(8,128)S(1)}, f32[8,8,128]{2,1,0:T(8,128)S(1)}, u32[]{:S(2)}, u32[]{:S(2)}) collective-permute-start(f32[8,8,128]{2,1,0:T(8,128)S(1)} %get-tuple-element.76), channel_id=1, source_target_pairs={{0,1},{2,3},{4,5},{6,7},{1,0},{3,2},{5,4},{7,6},{8,9},{10,11},{12,... | collective-permute-start | bytes 98312 | tf_op jit(solution)/shard_map/ppermute | solution.py:759
  30.1 3.7 %collective-permute-start.10 = (f32[3,8,128]{2,1,0:T(8,128)S(1)}, f32[3,8,128]{2,1,0:T(8,128)S(1)}, u32[]{:S(2)}, u32[]{:S(2)}) collective-permute-start(f32[3,8,128]{2,1,0:T(8,128)S(1)} %get-tuple-element.77), channel_id=1, source_target_pairs={{0,2},{1,3},{4,6},{5,7},{2,0},{3,1},{6,4},{7,5},{8,10},{9,11},{12,... | collective-permute-start | bytes 36872 | tf_op jit(solution)/shard_map/ppermute | solution.py:766
  30.1 5.5 %collective-permute-start.11 = (f32[3,8,128]{2,1,0:T(8,128)S(1)}, f32[3,8,128]{2,1,0:T(8,128)S(1)}, u32[]{:S(2)}, u32[]{:S(2)}) collective-permute-start(f32[3,8,128]{2,1,0:T(8,128)S(1)} %get-tuple-element.77), channel_id=1, source_target_pairs={{0,6},{1,7},{4,2},{5,3},{6,0},{7,1},{2,4},{3,5},{8,14},{9,15},{12,... | collective-permute-start | bytes 36872 | tf_op jit(solution)/shard_map/ppermute | solution.py:766

commit v13 on v11

--- a/solution.py
+++ b/solution.py
@@ -298,7 +298,7 @@
     both = jnp.where((sub_of() & 2) == 0, uv, fk)
     coarse[2 * OWN : 2 * OWN + 1] = both
     for ref in (first, second):
-        ref[FIELDS2 : FIELDS2 + 1] = both
+        ref[FIELDS2:] = jnp.broadcast_to(both, (ref.shape[0] - FIELDS2, Z, X))
 
 
 def split_fields2(both):
@@ -661,7 +661,8 @@
     for ref in (packet, to_first, to_second, to_far):
         ref[0:1] = value
     to_first[1:] = edge_a[...]
-    to_second[1:] = edge_b[...]
+    to_second[1 : 1 + EDGE_TILES] = edge_b[...]
+    to_second[1 + EDGE_TILES :] = value
 
 
 def rest_kernel(
@@ -766,6 +767,10 @@
     return lax.ppermute(value, axis, pairs + [(j, i) for i, j in pairs])
 
 
+def spare(shape):
+    return (shape[0] + 1, *shape[1:])
+
+
 def exchange(first, second, axis):
     return swap(first, axis, -1), swap(second, axis, 1)
 
@@ -784,7 +789,7 @@
     strip = (PACKET, Z, X)
     first, second, coarse, *inputs = call(
         functools.partial(first_kernel, rows),
-        [strip, strip, (2 * OWN + 1, Z, X), *(a.shape for a in inputs)],
+        [strip, spare(strip), (2 * OWN + 1, Z, X), *(a.shape for a in inputs)],
         [pltpu.SemaphoreType.DMA((4,))],
         *(pltpu.with_memory_space_constraint(a, pltpu.HBM) for a in inputs),
         space=pltpu.HBM,
@@ -870,7 +875,7 @@
     near = (1 + EDGE_TILES, Z, X)
     packet, first, second, to_far, keep1 = call(
         level1_kernel,
-        [(1, Z, X), near, near, (3, Z, X), (2, *one)],
+        [(1, Z, X), near, spare(near), (3, Z, X), (2, *one)],
         [one, one],
         own,
         *b_packets,

time: 38.4 us -> 39.8 us (1.036)
  waiting for transfers between devices: 10.3 us -> 12.6 us
  starting transfers between devices: 20.2 us -> 19.2 us
    ppermute x2, waiting for transfers between devices: 2.77 us -> 5.35 us  [swap_far(): return lax.ppermute(value, axis, pairs + [(j, i) for i, j in pairs])]
    ppermute x2, starting transfers between devices: 2.73 us -> 0.98 us  [swap_far(): return lax.ppermute(value, axis, pairs + [(j, i) for i, j in pairs])]
    ppermute x10, starting transfers between devices: 14.9 us -> 15.7 us  [swap(): return lax.ppermute(value, axis, pairs + [(j, i) for i, j in pairs])]
    ppermute x10, waiting for transfers between devices: 6.24 us -> 5.75 us  [swap(): return lax.ppermute(value, axis, pairs + [(j, i) for i, j in pairs])]
  transfers between devices with their start and end apart: 13 -> 13, of which waited for: 7 -> 6; matrix products, arithmetic and copies ran while one was open for 0% -> 0% of each run, Pallas kernels for 8% -> 8%
where the time goes in v13:
time: 39.8 us; the launch traced here: 39.6 us
  starting transfers between devices  19.2 us (48%)
  waiting for transfers between devices  12.6 us (32%)
  Pallas kernels  7.69 us (19%)
    ppermute x10, starting transfers between devices, swap(): return lax.ppermute(value, axis, pairs + [(j, i) for i, j in pairs])  15.7 us
    pallas_call x10, Pallas kernels, call(): pl.pallas_call(kernel, out_shape=out, in_specs=[pl.BlockSpec(memory_space...  7.69 us
    ppermute x10, waiting for transfers between devices, swap(): return lax.ppermute(value, axis, pairs + [(j, i) for i, j in pairs])  5.75 us
    ppermute x2, waiting for transfers between devices, swap_far(): return lax.ppermute(value, axis, pairs + [(j, i) for i, j in pairs])  5.35 us
    all_to_all x1, starting transfers between devices, body(): spread = lax.all_to_all(spread, ('gx', 'gy'), 0, 0, tiled=True)  2.57 us
    all_to_all x1, waiting for transfers between devices, body(): spread = lax.all_to_all(spread, ('gx', 'gy'), 0, 0, tiled=True)  1.54 us
    ppermute x2, starting transfers between devices, swap_far(): return lax.ppermute(value, axis, pairs + [(j, i) for i, j in pairs])  0.98 us
  transfers between devices with their start and end apart: 13, of which 6 were waited for; matrix products, arithmetic and copies ran while one was open for 0% of the time, Pallas kernels for 8%

profile of v13, /device:TPU:0, one launch (start us, length us, event | category | flops | bytes accessed | tf_op | source)
XLA Modules:
  0.0 39.6 jit_solution(14317242519414937634)
XLA Ops:
  0.0 1.3 %shard_map.46 = (f32[27,8,128]{2,1,0:T(8,128)S(1)}, f32[28,8,128]{2,1,0:T(8,128)S(1)}, f32[9,8,128]{2,1,0:T(8,128)S(1)}, f32[256,128]{1,0:T(8,128)S(1)}, f32[256...) custom-call(f32[256,128]{1,0:T(8,128)} %bitcast.5, f32[256,128]{1,0:T(8,128)} %bitcast.6, ...), custom_call_target="tpu_custom_call" | custom-call | tf_op jit(solution)/shard_map/pallas_call | solution.py:746
  1.3 3.0 %collective-permute-start.1 = (f32[28,8,128]{2,1,0:T(8,128)S(1)}, f32[28,8,128]{2,1,0:T(8,128)S(1)}, u32[]{:S(2)}, u32[]{:S(2)}) collective-permute-start(f32[28,8,128]{2,1,0:T(8,128)S(1)} %get-tuple-element.50), channel_id=1, source_target_pairs={{0,1},{2,3},{4,5},{6,7},{1,0},{3,2},{5,4},{7,6},{8,9},{10,11},{12,... | collective-permute-start | bytes 344072 | tf_op jit(solution)/shard_map/ppermute | solution.py:760
  4.4 3.5 %collective-permute-start = (f32[27,8,128]{2,1,0:T(8,128)S(1)}, f32[27,8,128]{2,1,0:T(8,128)S(1)}, u32[]{:S(2)}, u32[]{:S(2)}) collective-permute-start(f32[27,8,128]{2,1,0:T(8,128)S(1)} %get-tuple-element.49), channel_id=1, source_target_pairs={{0,7},{2,1},{4,3},{6,5},{7,0},{1,2},{3,4},{5,6},{8,15},{10,9},{12,... | collective-permute-start | bytes 331784 | tf_op jit(solution)/shard_map/ppermute | solution.py:760
  7.9 0.9 %shard_map.47 = (f32[35,8,128]{2,1,0:T(8,128)S(1)}, f32[35,8,128]{2,1,0:T(8,128)S(1)}, f32[32,4,128]{2,1,0:T(4,128)}, f32[6,16,8,128]{3,2,1,0:T(8,128)S(1)}) custom-call(f32[256,128]{1,0:T(8,128)S(1)} %get-tuple-element.43.state, f32[256,128]{1,0:T(8,128)S(1)} %get-tuple-element.44.previous, f32[128,128]{1,0:T(8,128)S(1)} %get-tuple-element.45.feed, ...), custom_call_target="tpu_custom_call" | custom-call | tf_op jit(solution)/shard_map/pallas_call | solution.py:746
  8.8 0.4 %collective-permute-start.2 = (f32[35,8,128]{2,1,0:T(8,128)S(1)}, f32[35,8,128]{2,1,0:T(8,128)S(1)}, u32[]{:S(2)}, u32[]{:S(2)}) collective-permute-start(f32[35,8,128]{2,1,0:T(8,128)S(1)} %get-tuple-element.51), channel_id=1, source_target_pairs={{0,24},{16,8},{24,0},{8,16},{1,25},{17,9},{25,1},{9,17},{2,26},{18... | collective-permute-start | bytes 430088 | tf_op jit(solution)/shard_map/ppermute | solution.py:760
  9.3 1.2 %collective-permute-start.3 = (f32[35,8,128]{2,1,0:T(8,128)S(1)}, f32[35,8,128]{2,1,0:T(8,128)S(1)}, u32[]{:S(2)}, u32[]{:S(2)}) collective-permute-start(f32[35,8,128]{2,1,0:T(8,128)S(1)} %get-tuple-element.52), channel_id=1, source_target_pairs={{0,8},{16,24},{8,0},{24,16},{1,9},{17,25},{9,1},{25,17},{2,10},{18... | collective-permute-start | bytes 430088 | tf_op jit(solution)/shard_map/ppermute | solution.py:760
  10.5 2.6 %all-to-all-start = ((f32[32,4,128]{2,1,0:T(4,128)}), f32[32,4,128]{2,1,0:T(4,128)S(1)}, u32[]{:S(2)}, u32[]{:S(2)}) async-start(f32[32,4,128]{2,1,0:T(4,128)} %get-tuple-element.63), calls=%async_computation | async-start | bytes 131072 | tf_op jit(solution)/shard_map/all_to_all | solution.py:810
  13.3 1.5 %collective-permute-start.4 = (f32[18,8,128]{2,1,0:T(8,128)S(1)}, f32[18,8,128]{2,1,0:T(8,128)S(1)}, u32[]{:S(2)}, u32[]{:S(2)}) collective-permute-start(f32[18,8,128]{2,1,0:T(8,128)S(1)} %get-tuple-element.53), channel_id=1, source_target_pairs={{0,24},{16,8},{24,0},{8,16},{1,25},{17,9},{25,1},{9,17},{2,26},{18... | collective-permute-start | bytes 221192 | tf_op jit(solution)/shard_map/ppermute | solution.py:760
  14.8 0.4 collective-permute-start.5
  15.1 0.9 %shard_map.49 = (f32[6,2,14,8,128]{4,3,2,1,0:T(8,128)S(1)}, f32[2,2,4,8,128]{4,3,2,1,0:T(8,128)S(1)}, f32[2,2,12,8,128]{4,3,2,1,0:T(8,128)S(1)}, f32[2,2,10,8,12...) custom-call(f32[6,16,8,128]{3,2,1,0:T(8,128)S(1)} %get-tuple-element.48.main, ...), custom_call_target="tpu_custom_call" | custom-call | tf_op jit(solution)/shard_map/pallas_call | solution.py:746
  16.0 2.0 %collective-permute-done.4.corner_a = f32[18,8,128]{2,1,0:T(8,128)S(1)} collective-permute-done((f32[18,8,128]{2,1,0:T(8,128)S(1)}, f32[18,8,128]{2,1,0:T(8,128)S(1)}, u32[]{:S(2)}, u32[]{:S(2)}) %collective-permute-start.4) | collective-permute-done | bytes 73760 | tf_op jit(solution)/shard_map/ppermute | solution.py:760
  18.1 0.8 %shard_map.50 = (f32[6,2,8,8,128]{4,3,2,1,0:T(8,128)S(1)}, f32[2,2,4,8,128]{4,3,2,1,0:T(8,128)S(1)}, f32[2,2,6,8,128]{4,3,2,1,0:T(8,128)S(1)}, f32[4,2,4,8,128]{4,3,2,1,0:T(8,128)S(1)}, f32[3,2,7,8,128]{4,3,2,1,0:T(8,128)S(1)}) custom-call(f32[6,16,8,128]{3,2,1,0:T(8,128)S(1)} %get-tuple-element.48.main, f32[27,8,128]{2,1,0:T(8,128)S(1)} %collective-permute-done.y_first, ...), custom_call_target="tpu_custom_call" | custom-call | tf_op jit(solution)/shard_map/pallas_call | solution.py:746
  18.8 1.5 %all-to-all-done.spread = f32[32,4,128]{2,1,0:T(4,128)S(1)} async-done(((f32[32,4,128]{2,1,0:T(4,128)}), f32[32,4,128]{2,1,0:T(4,128)S(1)}, u32[]{:S(2)}, u32[]{:S(2)}) %all-to-all-start) | async-done | bytes 65568 | tf_op jit(solution)/shard_map/all_to_all | solution.py:810
  20.4 0.2 shard_map.51
  20.6 2.9 %collective-permute-start.6 = (f32[7,8,128]{2,1,0:T(8,128)S(1)}, f32[7,8,128]{2,1,0:T(8,128)S(1)}, u32[]{:S(2)}, u32[]{:S(2)}) collective-permute-start(f32[7,8,128]{2,1,0:T(8,128)S(1)} %get-tuple-element.65), channel_id=1, source_target_pairs={{0,7},{2,1},{4,3},{6,5},{7,0},{1,2},{3,4},{5,6},{8,15},{10,9},{12,... | collective-permute-start | bytes 86024 | tf_op jit(solution)/shard_map/ppermute | solution.py:760
  23.5 0.2 shard_map.53
  23.8 3.4 %collective-permute-done.6.first = f32[7,8,128]{2,1,0:T(8,128)S(1)} collective-permute-done((f32[7,8,128]{2,1,0:T(8,128)S(1)}, f32[7,8,128]{2,1,0:T(8,128)S(1)}, u32[]{:S(2)}, u32[]{:S(2)}) %collective-permute-start.6) | collective-permute-done | bytes 28704 | tf_op jit(solution)/shard_map/ppermute | solution.py:760
  27.2 0.3 collective-permute-done.7.second
  27.5 0.5 %shard_map.54 = (f32[1,8,128]{2,1,0:T(8,128)S(1)}, f32[8,8,128]{2,1,0:T(8,128)S(1)}, f32[9,8,128]{2,1,0:T(8,128)S(1)}, f32[3,8,128]{2,1,0:T(8,128)S(1)}, f32[2,2,14,8,128]{4,3,2,1,0:T(8,128)S(1)}) custom-call(f32[2,4,8,128]{3,2,1,0:T(8,128)S(1)} %get-tuple-element.64.own, f32[7,8,128]{2,1,0:T(8,128)S(1)} %collective-permute-done.6.first, ...), custom_call_target="tpu_custom_call" | custom-call | tf_op jit(solution)/shard_map/pallas_call | solution.py:746
  28.1 2.6 %collective-permute-start.8 = (f32[8,8,128]{2,1,0:T(8,128)S(1)}, f32[8,8,128]{2,1,0:T(8,128)S(1)}, u32[]{:S(2)}, u32[]{:S(2)}) collective-permute-start(f32[8,8,128]{2,1,0:T(8,128)S(1)} %get-tuple-element.75), channel_id=1, source_target_pairs={{0,7},{2,1},{4,3},{6,5},{7,0},{1,2},{3,4},{5,6},{8,15},{10,9},{12,... | collective-permute-start | bytes 98312 | tf_op jit(solution)/shard_map/ppermute | solution.py:760
  30.7 0.8 %collective-permute-start.10 = (f32[3,8,128]{2,1,0:T(8,128)S(1)}, f32[3,8,128]{2,1,0:T(8,128)S(1)}, u32[]{:S(2)}, u32[]{:S(2)}) collective-permute-start(f32[3,8,128]{2,1,0:T(8,128)S(1)} %get-tuple-element.77), channel_id=1, source_target_pairs={{0,2},{1,3},{4,6},{5,7},{2,0},{3,1},{6,4},{7,5},{8,10},{9,11},{12,... | collective-permute-start | bytes 36872 | tf_op jit(solution)/shard_map/ppermute | solution.py:767
  31.7 2.8 %collective-permute-done.10.far_a = f32[3,8,128]{2,1,0:T(8,128)S(1)} collective-permute-done((f32[3,8,128]{2,1,0:T(8,128)S(1)}, f32[3,8,128]{2,1,0:T(8,128)S(1)}, u32[]{:S(2)}, u32[]{:S(2)}) %collective-permute-start.10) | collective-permute-done | bytes 12320 | tf_op jit(solution)/shard_map/ppermute | solution.py:767
  34.5 2.5 %collective-permute-done.11.far_b = f32[3,8,128]{2,1,0:T(8,128)S(1)} collective-permute-done((f32[3,8,128]{2,1,0:T(8,128)S(1)}, f32[3,8,128]{2,1,0:T(8,128)S(1)}, u32[]{:S(2)}, u32[]{:S(2)}) %collective-permute-start.11) | collective-permute-done | bytes 12320 | tf_op jit(solution)/shard_map/ppermute | solution.py:767
  37.0 2.6 %shard_map.55 = f32[256,128]{1,0:T(8,128)} custom-call(f32[1,8,128]{2,1,0:T(8,128)S(1)} %get-tuple-element.74.own2, f32[8,8,128]{2,1,0:T(8,128)S(1)} %collective-permute-done.8.near_a, f32[9,8,128]{2,1,0:T(8,128)S(1)} %collective-permute-done.9.near_b, f32[3,8,128]{2,1,0:T(8,128)S(1)} %collective-permute-done.10.far_a, ...), custom_call_target="tpu_custom_call" | custom-call | tf_op jit(solution)/shard_map/pallas_call | solution.py:746
  (12 shorter events, 0.5 us)
Async XLA Ops:
  1.3 11.8 %collective-permute-start.1 = (f32[28,8,128]{2,1,0:T(8,128)S(1)}, f32[28,8,128]{2,1,0:T(8,128)S(1)}, u32[]{:S(2)}, u32[]{:S(2)}) collective-permute-start(f32[28,8,128]{2,1,0:T(8,128)S(1)} %get-tuple-element.50), channel_id=1, source_target_pairs={{0,1},{2,3},{4,5},{6,7},{1,0},{3,2},{5,4},{7,6},{8,9},{10,11},{12,... | collective-permute-start | bytes 344072 | tf_op jit(solution)/shard_map/ppermute | solution.py:760
  4.4 8.7 %collective-permute-start = (f32[27,8,128]{2,1,0:T(8,128)S(1)}, f32[27,8,128]{2,1,0:T(8,128)S(1)}, u32[]{:S(2)}, u32[]{:S(2)}) collective-permute-start(f32[27,8,128]{2,1,0:T(8,128)S(1)} %get-tuple-element.49), channel_id=1, source_target_pairs={{0,7},{2,1},{4,3},{6,5},{7,0},{1,2},{3,4},{5,6},{8,15},{10,9},{12,... | collective-permute-start | bytes 331784 | tf_op jit(solution)/shard_map/ppermute | solution.py:760
  8.8 6.3 %collective-permute-start.2 = (f32[35,8,128]{2,1,0:T(8,128)S(1)}, f32[35,8,128]{2,1,0:T(8,128)S(1)}, u32[]{:S(2)}, u32[]{:S(2)}) collective-permute-start(f32[35,8,128]{2,1,0:T(8,128)S(1)} %get-tuple-element.51), channel_id=1, source_target_pairs={{0,24},{16,8},{24,0},{8,16},{1,25},{17,9},{25,1},{9,17},{2,26},{18... | collective-permute-start | bytes 430088 | tf_op jit(solution)/shard_map/ppermute | solution.py:760
  9.3 5.8 %collective-permute-start.3 = (f32[35,8,128]{2,1,0:T(8,128)S(1)}, f32[35,8,128]{2,1,0:T(8,128)S(1)}, u32[]{:S(2)}, u32[]{:S(2)}) collective-permute-start(f32[35,8,128]{2,1,0:T(8,128)S(1)} %get-tuple-element.52), channel_id=1, source_target_pairs={{0,8},{16,24},{8,0},{24,16},{1,9},{17,25},{9,1},{25,17},{2,10},{18... | collective-permute-start | bytes 430088 | tf_op jit(solution)/shard_map/ppermute | solution.py:760
  10.5 9.9 %all-to-all-start = ((f32[32,4,128]{2,1,0:T(4,128)}), f32[32,4,128]{2,1,0:T(4,128)S(1)}, u32[]{:S(2)}, u32[]{:S(2)}) async-start(f32[32,4,128]{2,1,0:T(4,128)} %get-tuple-element.63), calls=%async_computation | async-start | bytes 131072 | tf_op jit(solution)/shard_map/all_to_all | solution.py:810
  13.3 4.8 %collective-permute-start.4 = (f32[18,8,128]{2,1,0:T(8,128)S(1)}, f32[18,8,128]{2,1,0:T(8,128)S(1)}, u32[]{:S(2)}, u32[]{:S(2)}) collective-permute-start(f32[18,8,128]{2,1,0:T(8,128)S(1)} %get-tuple-element.53), channel_id=1, source_target_pairs={{0,24},{16,8},{24,0},{8,16},{1,25},{17,9},{25,1},{9,17},{2,26},{18... | collective-permute-start | bytes 221192 | tf_op jit(solution)/shard_map/ppermute | solution.py:760
  14.8 3.3 %collective-permute-start.5 = (f32[18,8,128]{2,1,0:T(8,128)S(1)}, f32[18,8,128]{2,1,0:T(8,128)S(1)}, u32[]{:S(2)}, u32[]{:S(2)}) collective-permute-start(f32[18,8,128]{2,1,0:T(8,128)S(1)} %get-tuple-element.54), channel_id=1, source_target_pairs={{0,8},{16,24},{8,0},{24,16},{1,9},{17,25},{9,1},{25,17},{2,10},{18... | collective-permute-start | bytes 221192 | tf_op jit(solution)/shard_map/ppermute | solution.py:760
  20.6 6.6 %collective-permute-start.6 = (f32[7,8,128]{2,1,0:T(8,128)S(1)}, f32[7,8,128]{2,1,0:T(8,128)S(1)}, u32[]{:S(2)}, u32[]{:S(2)}) collective-permute-start(f32[7,8,128]{2,1,0:T(8,128)S(1)} %get-tuple-element.65), channel_id=1, source_target_pairs={{0,7},{2,1},{4,3},{6,5},{7,0},{1,2},{3,4},{5,6},{8,15},{10,9},{12,... | collective-permute-start | bytes 86024 | tf_op jit(solution)/shard_map/ppermute | solution.py:760
  23.4 4.0 %collective-permute-start.7 = (f32[7,8,128]{2,1,0:T(8,128)S(1)}, f32[7,8,128]{2,1,0:T(8,128)S(1)}, u32[]{:S(2)}, u32[]{:S(2)}) collective-permute-start(f32[7,8,128]{2,1,0:T(8,128)S(1)} %get-tuple-element.66), channel_id=1, source_target_pairs={{0,1},{2,3},{4,5},{6,7},{1,0},{3,2},{5,4},{7,6},{8,9},{10,11},{12,... | collective-permute-start | bytes 86024 | tf_op jit(solution)/shard_map/ppermute | solution.py:760
  28.0 9.1 %collective-permute-start.9 = (f32[9,8,128]{2,1,0:T(8,128)S(1)}, f32[9,8,128]{2,1,0:T(8,128)S(1)}, u32[]{:S(2)}, u32[]{:S(2)}) collective-permute-start(f32[9,8,128]{2,1,0:T(8,128)S(1)} %get-tuple-element.76), channel_id=1, source_target_pairs={{0,1},{2,3},{4,5},{6,7},{1,0},{3,2},{5,4},{7,6},{8,9},{10,11},{12,... | collective-permute-start | bytes 110600 | tf_op jit(solution)/shard_map/ppermute | solution.py:760
  28.1 9.0 %collective-permute-start.8 = (f32[8,8,128]{2,1,0:T(8,128)S(1)}, f32[8,8,128]{2,1,0:T(8,128)S(1)}, u32[]{:S(2)}, u32[]{:S(2)}) collective-permute-start(f32[8,8,128]{2,1,0:T(8,128)S(1)} %get-tuple-element.75), channel_id=1, source_target_pairs={{0,7},{2,1},{4,3},{6,5},{7,0},{1,2},{3,4},{5,6},{8,15},{10,9},{12,... | collective-permute-start | bytes 98312 | tf_op jit(solution)/shard_map/ppermute | solution.py:760
  30.7 3.8 %collective-permute-start.10 = (f32[3,8,128]{2,1,0:T(8,128)S(1)}, f32[3,8,128]{2,1,0:T(8,128)S(1)}, u32[]{:S(2)}, u32[]{:S(2)}) collective-permute-start(f32[3,8,128]{2,1,0:T(8,128)S(1)} %get-tuple-element.77), channel_id=1, source_target_pairs={{0,2},{1,3},{4,6},{5,7},{2,0},{3,1},{6,4},{7,5},{8,10},{9,11},{12,... | collective-permute-start | bytes 36872 | tf_op jit(solution)/shard_map/ppermute | solution.py:767
  31.6 5.5 %collective-permute-start.11 = (f32[3,8,128]{2,1,0:T(8,128)S(1)}, f32[3,8,128]{2,1,0:T(8,128)S(1)}, u32[]{:S(2)}, u32[]{:S(2)}) collective-permute-start(f32[3,8,128]{2,1,0:T(8,128)S(1)} %get-tuple-element.77), channel_id=1, source_target_pairs={{0,6},{1,7},{4,2},{5,3},{6,0},{7,1},{2,4},{3,5},{8,14},{9,15},{12,... | collective-permute-start | bytes 36872 | tf_op jit(solution)/shard_map/ppermute | solution.py:767

commit v14 on v11

--- a/solution.py
+++ b/solution.py
@@ -257,8 +257,8 @@
 SOURCES = ((0, 0), (0, 1), (1, 0), (1, 1), (2, 0), (3, 0))
 
 
-def first_kernel(rows, state, previous, feed, kill, first, second, coarse, *rest):
-    held, sems = rest[:4], rest[4]
+def first_kernel(rows, state, previous, feed, kill, first, second, coarse, spread, *rest):
+    held, (sems, spread_held, spread_sem) = rest[:4], rest[4:]
     copies = [
         pltpu.make_async_copy(ref, to, sems.at[i]) for i, (ref, to) in enumerate(zip((state, previous, feed, kill), held))
     ]
@@ -271,6 +271,21 @@
     for i, (j, f) in enumerate(SOURCES):
         wanted = range(rows) if i not in (2, 3) else [*range(SENT), *range(rows - SENT, rows)]
         values.append({y: plane(held[j], f, y, rows)[None] for y in wanted})
+    pairs = []
+    for p, (i, j) in enumerate(((0, 1), (4, 5))):
+        parts = []
+        for g in range(OWN):
+            sums = [
+                jnp.concatenate([value[4 * g + 2 * q] + value[4 * g + 2 * q + 1] for q in (0, 1)], axis=0)
+                for value in (values[i], values[j])
+            ]
+            parts.append(restrict_01(*sums))
+        pairs.append(jnp.concatenate(parts, axis=0))
+    uv, fk = (restrict_12([pair[j : j + 1] for j in range(OWN)]) for pair in pairs)
+    fields = [jnp.concatenate([values[i][y] for y in range(rows)], axis=0) for i in (0, 1, 4, 5)]
+    write_spread(fields, pairs, (uv, fk), spread_held)
+    copy = pltpu.make_async_copy(spread_held, spread, spread_sem)
+    copy.start()
     for i in (2, 3):
         weight = DIFF[i - 2] / INV_STEP
         values[i][SENT - 1] = values[i][SENT - 1] + weight * values[i - 2][SENT]
@@ -281,24 +296,15 @@
             at = slice(i * SENT + y, i * SENT + y + 1)
             first[at] = jnp.where(even, top, bottom)
             second[at] = jnp.where(even, bottom, top)
-    pairs = []
-    for p, (i, j) in enumerate(((0, 1), (4, 5))):
-        parts = []
-        for g in range(OWN):
-            sums = [
-                jnp.concatenate([value[4 * g + 2 * q] + value[4 * g + 2 * q + 1] for q in (0, 1)], axis=0)
-                for value in (values[i], values[j])
-            ]
-            parts.append(restrict_01(*sums))
-        pairs.append(jnp.concatenate(parts, axis=0))
+    for p in (0, 1):
         coarse[p * OWN : (p + 1) * OWN] = pairs[p]
         for ref in (first, second):
             ref[FIELDS1 + p * OWN : FIELDS1 + (p + 1) * OWN] = pairs[p]
-    uv, fk = (restrict_12([pair[j : j + 1] for j in range(OWN)]) for pair in pairs)
     both = jnp.where((sub_of() & 2) == 0, uv, fk)
     coarse[2 * OWN : 2 * OWN + 1] = both
     for ref in (first, second):
         ref[FIELDS2 : FIELDS2 + 1] = both
+    copy.wait()
 
 
 def split_fields2(both):
@@ -306,13 +312,12 @@
     return jnp.where(low, both, roll_z(both, 2)), jnp.where(low, roll_z(both, -2), both)
 
 
-def write_spread(main, coarse, out):
+def write_spread(fields, pairs, quads, out):
     lane = lax.broadcasted_iota(jnp.int32, (1, X), 1)
-    u, v, f, k = (main[i] for i in (0, 1, 4, 5))
-    cross, squared, inv_u, inv_v, _, _ = jacobian(u, v, f, k, 0)
+    cross, squared, inv_u, inv_v, _, _ = jacobian(*fields, 0)
     tops = [jnp.max(jnp.maximum((6.0 * DIFF[0] + cross) * inv_u, (6.0 * DIFF[1] + squared) * inv_v), axis=0)]
-    tops.append(jnp.max(packed_spread(coarse[0:OWN], coarse[OWN : 2 * OWN], 1), axis=0))
-    tops.append(packed_spread(*split_fields2(coarse[2 * OWN : 2 * OWN + 1]), 2)[0])
+    tops.append(jnp.max(packed_spread(*pairs, 1), axis=0))
+    tops.append(packed_spread(*quads, 2)[0])
     result = jnp.zeros((1, X), jnp.float32)
     for level, top in enumerate(tops):
         top = jnp.max(jnp.max(top, axis=0, keepdims=True), axis=1, keepdims=True)
@@ -356,21 +361,15 @@
     return out
 
 
-def pack_own_kernel(
-    rows, state, previous, feed, kill, coarse, first, second, spread, main, held, copies, sem
-):
+def pack_own_kernel(rows, state, previous, feed, kill, coarse, first, second, main, held):
     inputs = (state, previous, feed, kill)
     for i, (j, f) in enumerate(SOURCES):
         for y in range(rows):
-            main[i, y] = plane(inputs[j], f, y, rows)
-    write_spread(main, coarse, copies)
-    copy = pltpu.make_async_copy(copies, spread, sem)
-    copy.start()
-    for i in range(6):
-        held[i * rows : (i + 1) * rows] = main[i]
+            value = plane(inputs[j], f, y, rows)
+            main[i, y] = value
+            held[i * rows + y] = value
     held[6 * rows : 6 * rows + 2 * OWN + 1] = coarse[...]
     pack_edges(held, is_even("gx"), first, second)
-    copy.wait()
 
 
 def pack_corner_kernel(y_first, y_second, first, second, held):
@@ -782,24 +781,24 @@
     inputs = (state, previous, feed, kill)
 
     strip = (PACKET, Z, X)
-    first, second, coarse, *inputs = call(
+    spread_shape = (across * count, Z // 2, X)
+    first, second, coarse, spread, *inputs = call(
         functools.partial(first_kernel, rows),
-        [strip, strip, (2 * OWN + 1, Z, X), *(a.shape for a in inputs)],
-        [pltpu.SemaphoreType.DMA((4,))],
+        [strip, strip, (2 * OWN + 1, Z, X), spread_shape, *(a.shape for a in inputs)],
+        [pltpu.SemaphoreType.DMA((4,)), spread_shape, pltpu.SemaphoreType.DMA],
         *(pltpu.with_memory_space_constraint(a, pltpu.HBM) for a in inputs),
         space=pltpu.HBM,
+        outs=[pltpu.VMEM] * 3 + [pltpu.HBM] + [pltpu.VMEM] * 4,
     )
     y_packets = exchange(first, second, "gy")
 
     tiles = tiles_for(6 * rows + 2 * OWN + 1)
-    spread_shape = (across * count, Z // 2, X)
-    first, second, spread, main = call(
+    first, second, main = call(
         functools.partial(pack_own_kernel, rows),
-        [(tiles, Z, X), (tiles, Z, X), spread_shape, (6, rows, Z, X)],
-        [(PER * tiles, Z, X), spread_shape, pltpu.SemaphoreType.DMA],
+        [(tiles, Z, X), (tiles, Z, X), (6, rows, Z, X)],
+        [(PER * tiles, Z, X)],
         *inputs,
         coarse,
-        outs=[pltpu.VMEM, pltpu.VMEM, pltpu.HBM, pltpu.VMEM],
     )
     own_x = exchange(first, second, "gx")
     spread = lax.all_to_all(spread, ("gx", "gy"), 0, 0, tiled=True)

time: 38.4 us -> 38.5 us (level)
    ppermute x10, waiting for transfers between devices: 6.24 us -> 6.96 us  [swap(): return lax.ppermute(value, axis, pairs + [(j, i) for i, j in pairs])]
    all_to_all x1, waiting for transfers between devices: 1.25 us -> 0.52 us  [body(): spread = lax.all_to_all(spread, ('gx', 'gy'), 0, 0, tiled=True)]
  transfers between devices with their start and end apart: 13 -> 13, of which waited for: 7 -> 7; matrix products, arithmetic and copies ran while one was open for 0% -> 0% of each run, Pallas kernels for 8% -> 6%
where the time goes in v14:
time: 38.5 us; the launch traced here: 38.3 us
  starting transfers between devices  20.2 us (52%)
  waiting for transfers between devices  10.3 us (27%)
  Pallas kernels  7.77 us (20%)
    ppermute x10, starting transfers between devices, swap(): return lax.ppermute(value, axis, pairs + [(j, i) for i, j in pairs])  14.9 us
    pallas_call x10, Pallas kernels, call(): pl.pallas_call(kernel, out_shape=out, in_specs=[pl.BlockSpec(memory_space...  7.77 us
    ppermute x10, waiting for transfers between devices, swap(): return lax.ppermute(value, axis, pairs + [(j, i) for i, j in pairs])  6.96 us
    ppermute x2, waiting for transfers between devices, swap_far(): return lax.ppermute(value, axis, pairs + [(j, i) for i, j in pairs])  2.77 us
    ppermute x2, starting transfers between devices, swap_far(): return lax.ppermute(value, axis, pairs + [(j, i) for i, j in pairs])  2.73 us
    all_to_all x1, starting transfers between devices, body(): spread = lax.all_to_all(spread, ('gx', 'gy'), 0, 0, tiled=True)  2.57 us
  transfers between devices with their start and end apart: 13, of which 7 were waited for; matrix products, arithmetic and copies ran while one was open for 0% of the time, Pallas kernels for 6%

profile of v14, /device:TPU:0, one launch (start us, length us, event | category | flops | bytes accessed | tf_op | source)
XLA Modules:
  0.0 38.3 jit_solution(12030219946818312213)
XLA Ops:
  0.0 2.1 %shard_map.46 = (f32[27,8,128]{2,1,0:T(8,128)S(1)}, f32[27,8,128]{2,1,0:T(8,128)S(1)}, f32[9,8,128]{2,1,0:T(8,128)S(1)}, f32[32,4,128]{2,1,0:T(4,128)}, f32[256,...) custom-call(f32[256,128]{1,0:T(8,128)} %bitcast.5, ...), custom_call_target="tpu_custom_call" | custom-call | tf_op jit(solution)/shard_map/pallas_call | solution.py:744
  2.1 6.1 %collective-permute-start = (f32[27,8,128]{2,1,0:T(8,128)S(1)}, f32[27,8,128]{2,1,0:T(8,128)S(1)}, u32[]{:S(2)}, u32[]{:S(2)}) collective-permute-start(f32[27,8,128]{2,1,0:T(8,128)S(1)} %get-tuple-element.49), channel_id=1, source_target_pairs={{0,7},{2,1},{4,3},{6,5},{7,0},{1,2},{3,4},{5,6},{8,15},{10,9},{12,... | collective-permute-start | bytes 331784 | tf_op jit(solution)/shard_map/ppermute | solution.py:758
  8.2 0.3 shard_map.47
  8.4 0.7 %collective-permute-start.2 = (f32[35,8,128]{2,1,0:T(8,128)S(1)}, f32[35,8,128]{2,1,0:T(8,128)S(1)}, u32[]{:S(2)}, u32[]{:S(2)}) collective-permute-start(f32[35,8,128]{2,1,0:T(8,128)S(1)} %get-tuple-element.51), channel_id=1, source_target_pairs={{0,24},{16,8},{24,0},{8,16},{1,25},{17,9},{25,1},{9,17},{2,26},{18... | collective-permute-start | bytes 430088 | tf_op jit(solution)/shard_map/ppermute | solution.py:758
  9.2 1.0 %collective-permute-start.3 = (f32[35,8,128]{2,1,0:T(8,128)S(1)}, f32[35,8,128]{2,1,0:T(8,128)S(1)}, u32[]{:S(2)}, u32[]{:S(2)}) collective-permute-start(f32[35,8,128]{2,1,0:T(8,128)S(1)} %get-tuple-element.52), channel_id=1, source_target_pairs={{0,8},{16,24},{8,0},{24,16},{1,9},{17,25},{9,1},{25,17},{2,10},{18... | collective-permute-start | bytes 430088 | tf_op jit(solution)/shard_map/ppermute | solution.py:758
  10.1 2.6 %all-to-all-start = ((f32[32,4,128]{2,1,0:T(4,128)}), f32[32,4,128]{2,1,0:T(4,128)S(1)}, u32[]{:S(2)}, u32[]{:S(2)}) async-start(f32[32,4,128]{2,1,0:T(4,128)} %get-tuple-element.63), calls=%async_computation | async-start | bytes 131072 | tf_op jit(solution)/shard_map/all_to_all | solution.py:804
  12.7 0.9 %collective-permute-done.1.y_second = f32[27,8,128]{2,1,0:T(8,128)S(1)} collective-permute-done((f32[27,8,128]{2,1,0:T(8,128)S(1)}, f32[27,8,128]{2,1,0:T(8,128)S(1)}, u32[]{:S(2)}, u32[]{:S(2)}) %collective-permute-start.1) | collective-permute-done | bytes 110624 | tf_op jit(solution)/shard_map/ppermute | solution.py:758
  13.8 0.7 %collective-permute-start.4 = (f32[18,8,128]{2,1,0:T(8,128)S(1)}, f32[18,8,128]{2,1,0:T(8,128)S(1)}, u32[]{:S(2)}, u32[]{:S(2)}) collective-permute-start(f32[18,8,128]{2,1,0:T(8,128)S(1)} %get-tuple-element.53), channel_id=1, source_target_pairs={{0,24},{16,8},{24,0},{8,16},{1,25},{17,9},{25,1},{9,17},{2,26},{18... | collective-permute-start | bytes 221192 | tf_op jit(solution)/shard_map/ppermute | solution.py:758
  14.5 1.0 %collective-permute-start.5 = (f32[18,8,128]{2,1,0:T(8,128)S(1)}, f32[18,8,128]{2,1,0:T(8,128)S(1)}, u32[]{:S(2)}, u32[]{:S(2)}) collective-permute-start(f32[18,8,128]{2,1,0:T(8,128)S(1)} %get-tuple-element.54), channel_id=1, source_target_pairs={{0,8},{16,24},{8,0},{24,16},{1,9},{17,25},{9,1},{25,17},{2,10},{18... | collective-permute-start | bytes 221192 | tf_op jit(solution)/shard_map/ppermute | solution.py:758
  15.5 0.9 %shard_map.49 = (f32[6,2,14,8,128]{4,3,2,1,0:T(8,128)S(1)}, f32[2,2,4,8,128]{4,3,2,1,0:T(8,128)S(1)}, f32[2,2,12,8,128]{4,3,2,1,0:T(8,128)S(1)}, f32[2,2,10,8,12...) custom-call(f32[6,16,8,128]{3,2,1,0:T(8,128)S(1)} %get-tuple-element.48.main, ...), custom_call_target="tpu_custom_call" | custom-call | tf_op jit(solution)/shard_map/pallas_call | solution.py:744
  16.3 2.4 %collective-permute-done.4.corner_a = f32[18,8,128]{2,1,0:T(8,128)S(1)} collective-permute-done((f32[18,8,128]{2,1,0:T(8,128)S(1)}, f32[18,8,128]{2,1,0:T(8,128)S(1)}, u32[]{:S(2)}, u32[]{:S(2)}) %collective-permute-start.4) | collective-permute-done | bytes 73760 | tf_op jit(solution)/shard_map/ppermute | solution.py:758
  18.7 0.8 %shard_map.50 = (f32[6,2,8,8,128]{4,3,2,1,0:T(8,128)S(1)}, f32[2,2,4,8,128]{4,3,2,1,0:T(8,128)S(1)}, f32[2,2,6,8,128]{4,3,2,1,0:T(8,128)S(1)}, f32[4,2,4,8,128]{4,3,2,1,0:T(8,128)S(1)}, f32[3,2,7,8,128]{4,3,2,1,0:T(8,128)S(1)}) custom-call(f32[6,16,8,128]{3,2,1,0:T(8,128)S(1)} %get-tuple-element.48.main, f32[27,8,128]{2,1,0:T(8,128)S(1)} %collective-permute-done.y_first, ...), custom_call_target="tpu_custom_call" | custom-call | tf_op jit(solution)/shard_map/pallas_call | solution.py:744
  19.5 0.5 %all-to-all-done.spread = f32[32,4,128]{2,1,0:T(4,128)S(1)} async-done(((f32[32,4,128]{2,1,0:T(4,128)}), f32[32,4,128]{2,1,0:T(4,128)S(1)}, u32[]{:S(2)}, u32[]{:S(2)}) %all-to-all-start) | async-done | bytes 65568 | tf_op jit(solution)/shard_map/all_to_all | solution.py:804
  20.0 0.2 shard_map.51
  20.2 2.9 %collective-permute-start.6 = (f32[7,8,128]{2,1,0:T(8,128)S(1)}, f32[7,8,128]{2,1,0:T(8,128)S(1)}, u32[]{:S(2)}, u32[]{:S(2)}) collective-permute-start(f32[7,8,128]{2,1,0:T(8,128)S(1)} %get-tuple-element.65), channel_id=1, source_target_pairs={{0,7},{2,1},{4,3},{6,5},{7,0},{1,2},{3,4},{5,6},{8,15},{10,9},{12,... | collective-permute-start | bytes 86024 | tf_op jit(solution)/shard_map/ppermute | solution.py:758
  23.1 0.2 shard_map.53
  23.4 3.4 %collective-permute-done.6.first = f32[7,8,128]{2,1,0:T(8,128)S(1)} collective-permute-done((f32[7,8,128]{2,1,0:T(8,128)S(1)}, f32[7,8,128]{2,1,0:T(8,128)S(1)}, u32[]{:S(2)}, u32[]{:S(2)}) %collective-permute-start.6) | collective-permute-done | bytes 28704 | tf_op jit(solution)/shard_map/ppermute | solution.py:758
  26.8 0.3 collective-permute-done.7.second
  27.1 0.5 %shard_map.54 = (f32[1,8,128]{2,1,0:T(8,128)S(1)}, f32[8,8,128]{2,1,0:T(8,128)S(1)}, f32[8,8,128]{2,1,0:T(8,128)S(1)}, f32[3,8,128]{2,1,0:T(8,128)S(1)}, f32[2,2,14,8,128]{4,3,2,1,0:T(8,128)S(1)}) custom-call(f32[2,4,8,128]{3,2,1,0:T(8,128)S(1)} %get-tuple-element.64.own, f32[7,8,128]{2,1,0:T(8,128)S(1)} %collective-permute-done.6.first, ...), custom_call_target="tpu_custom_call" | custom-call | tf_op jit(solution)/shard_map/pallas_call | solution.py:744
  27.6 2.6 %collective-permute-start.8 = (f32[8,8,128]{2,1,0:T(8,128)S(1)}, f32[8,8,128]{2,1,0:T(8,128)S(1)}, u32[]{:S(2)}, u32[]{:S(2)}) collective-permute-start(f32[8,8,128]{2,1,0:T(8,128)S(1)} %get-tuple-element.75), channel_id=1, source_target_pairs={{0,7},{2,1},{4,3},{6,5},{7,0},{1,2},{3,4},{5,6},{8,15},{10,9},{12,... | collective-permute-start | bytes 98312 | tf_op jit(solution)/shard_map/ppermute | solution.py:758
  30.2 2.7 %collective-permute-start.11 = (f32[3,8,128]{2,1,0:T(8,128)S(1)}, f32[3,8,128]{2,1,0:T(8,128)S(1)}, u32[]{:S(2)}, u32[]{:S(2)}) collective-permute-start(f32[3,8,128]{2,1,0:T(8,128)S(1)} %get-tuple-element.77), channel_id=1, source_target_pairs={{0,6},{1,7},{4,2},{5,3},{6,0},{7,1},{2,4},{3,5},{8,14},{9,15},{12,... | collective-permute-start | bytes 36872 | tf_op jit(solution)/shard_map/ppermute | solution.py:765
  32.9 1.0 %collective-permute-done.10.far_a = f32[3,8,128]{2,1,0:T(8,128)S(1)} collective-permute-done((f32[3,8,128]{2,1,0:T(8,128)S(1)}, f32[3,8,128]{2,1,0:T(8,128)S(1)}, u32[]{:S(2)}, u32[]{:S(2)}) %collective-permute-start.10) | collective-permute-done | bytes 12320 | tf_op jit(solution)/shard_map/ppermute | solution.py:765
  33.9 1.8 %collective-permute-done.11.far_b = f32[3,8,128]{2,1,0:T(8,128)S(1)} collective-permute-done((f32[3,8,128]{2,1,0:T(8,128)S(1)}, f32[3,8,128]{2,1,0:T(8,128)S(1)}, u32[]{:S(2)}, u32[]{:S(2)}) %collective-permute-start.11) | collective-permute-done | bytes 12320 | tf_op jit(solution)/shard_map/ppermute | solution.py:765
  35.7 2.6 %shard_map.55 = f32[256,128]{1,0:T(8,128)} custom-call(f32[1,8,128]{2,1,0:T(8,128)S(1)} %get-tuple-element.74.own2, f32[8,8,128]{2,1,0:T(8,128)S(1)} %collective-permute-done.8.near_a, f32[8,8,128]{2,1,0:T(8,128)S(1)} %collective-permute-done.9.near_b, f32[3,8,128]{2,1,0:T(8,128)S(1)} %collective-permute-done.10.far_a, ...), custom_call_target="tpu_custom_call" | custom-call | tf_op jit(solution)/shard_map/pallas_call | solution.py:744
  (12 shorter events, 0.3 us)
Async XLA Ops:
  2.1 10.6 %collective-permute-start = (f32[27,8,128]{2,1,0:T(8,128)S(1)}, f32[27,8,128]{2,1,0:T(8,128)S(1)}, u32[]{:S(2)}, u32[]{:S(2)}) collective-permute-start(f32[27,8,128]{2,1,0:T(8,128)S(1)} %get-tuple-element.49), channel_id=1, source_target_pairs={{0,7},{2,1},{4,3},{6,5},{7,0},{1,2},{3,4},{5,6},{8,15},{10,9},{12,... | collective-permute-start | bytes 331784 | tf_op jit(solution)/shard_map/ppermute | solution.py:758
  8.2 5.4 %collective-permute-start.1 = (f32[27,8,128]{2,1,0:T(8,128)S(1)}, f32[27,8,128]{2,1,0:T(8,128)S(1)}, u32[]{:S(2)}, u32[]{:S(2)}) collective-permute-start(f32[27,8,128]{2,1,0:T(8,128)S(1)} %get-tuple-element.50), channel_id=1, source_target_pairs={{0,1},{2,3},{4,5},{6,7},{1,0},{3,2},{5,4},{7,6},{8,9},{10,11},{12,... | collective-permute-start | bytes 331784 | tf_op jit(solution)/shard_map/ppermute | solution.py:758
  8.4 7.0 %collective-permute-start.2 = (f32[35,8,128]{2,1,0:T(8,128)S(1)}, f32[35,8,128]{2,1,0:T(8,128)S(1)}, u32[]{:S(2)}, u32[]{:S(2)}) collective-permute-start(f32[35,8,128]{2,1,0:T(8,128)S(1)} %get-tuple-element.51), channel_id=1, source_target_pairs={{0,24},{16,8},{24,0},{8,16},{1,25},{17,9},{25,1},{9,17},{2,26},{18... | collective-permute-start | bytes 430088 | tf_op jit(solution)/shard_map/ppermute | solution.py:758
  9.2 6.3 %collective-permute-start.3 = (f32[35,8,128]{2,1,0:T(8,128)S(1)}, f32[35,8,128]{2,1,0:T(8,128)S(1)}, u32[]{:S(2)}, u32[]{:S(2)}) collective-permute-start(f32[35,8,128]{2,1,0:T(8,128)S(1)} %get-tuple-element.52), channel_id=1, source_target_pairs={{0,8},{16,24},{8,0},{24,16},{1,9},{17,25},{9,1},{25,17},{2,10},{18... | collective-permute-start | bytes 430088 | tf_op jit(solution)/shard_map/ppermute | solution.py:758
  10.1 9.9 %all-to-all-start = ((f32[32,4,128]{2,1,0:T(4,128)}), f32[32,4,128]{2,1,0:T(4,128)S(1)}, u32[]{:S(2)}, u32[]{:S(2)}) async-start(f32[32,4,128]{2,1,0:T(4,128)} %get-tuple-element.63), calls=%async_computation | async-start | bytes 131072 | tf_op jit(solution)/shard_map/all_to_all | solution.py:804
  13.8 4.9 %collective-permute-start.4 = (f32[18,8,128]{2,1,0:T(8,128)S(1)}, f32[18,8,128]{2,1,0:T(8,128)S(1)}, u32[]{:S(2)}, u32[]{:S(2)}) collective-permute-start(f32[18,8,128]{2,1,0:T(8,128)S(1)} %get-tuple-element.53), channel_id=1, source_target_pairs={{0,24},{16,8},{24,0},{8,16},{1,25},{17,9},{25,1},{9,17},{2,26},{18... | collective-permute-start | bytes 221192 | tf_op jit(solution)/shard_map/ppermute | solution.py:758
  14.5 4.2 %collective-permute-start.5 = (f32[18,8,128]{2,1,0:T(8,128)S(1)}, f32[18,8,128]{2,1,0:T(8,128)S(1)}, u32[]{:S(2)}, u32[]{:S(2)}) collective-permute-start(f32[18,8,128]{2,1,0:T(8,128)S(1)} %get-tuple-element.54), channel_id=1, source_target_pairs={{0,8},{16,24},{8,0},{24,16},{1,9},{17,25},{9,1},{25,17},{2,10},{18... | collective-permute-start | bytes 221192 | tf_op jit(solution)/shard_map/ppermute | solution.py:758
  20.2 6.6 %collective-permute-start.6 = (f32[7,8,128]{2,1,0:T(8,128)S(1)}, f32[7,8,128]{2,1,0:T(8,128)S(1)}, u32[]{:S(2)}, u32[]{:S(2)}) collective-permute-start(f32[7,8,128]{2,1,0:T(8,128)S(1)} %get-tuple-element.65), channel_id=1, source_target_pairs={{0,7},{2,1},{4,3},{6,5},{7,0},{1,2},{3,4},{5,6},{8,15},{10,9},{12,... | collective-permute-start | bytes 86024 | tf_op jit(solution)/shard_map/ppermute | solution.py:758
  23.0 4.0 %collective-permute-start.7 = (f32[7,8,128]{2,1,0:T(8,128)S(1)}, f32[7,8,128]{2,1,0:T(8,128)S(1)}, u32[]{:S(2)}, u32[]{:S(2)}) collective-permute-start(f32[7,8,128]{2,1,0:T(8,128)S(1)} %get-tuple-element.66), channel_id=1, source_target_pairs={{0,1},{2,3},{4,5},{6,7},{1,0},{3,2},{5,4},{7,6},{8,9},{10,11},{12,... | collective-permute-start | bytes 86024 | tf_op jit(solution)/shard_map/ppermute | solution.py:758
  27.6 8.1 %collective-permute-start.8 = (f32[8,8,128]{2,1,0:T(8,128)S(1)}, f32[8,8,128]{2,1,0:T(8,128)S(1)}, u32[]{:S(2)}, u32[]{:S(2)}) collective-permute-start(f32[8,8,128]{2,1,0:T(8,128)S(1)} %get-tuple-element.75), channel_id=1, source_target_pairs={{0,7},{2,1},{4,3},{6,5},{7,0},{1,2},{3,4},{5,6},{8,15},{10,9},{12,... | collective-permute-start | bytes 98312 | tf_op jit(solution)/shard_map/ppermute | solution.py:758
  30.2 5.5 %collective-permute-start.9 = (f32[8,8,128]{2,1,0:T(8,128)S(1)}, f32[8,8,128]{2,1,0:T(8,128)S(1)}, u32[]{:S(2)}, u32[]{:S(2)}) collective-permute-start(f32[8,8,128]{2,1,0:T(8,128)S(1)} %get-tuple-element.76), channel_id=1, source_target_pairs={{0,1},{2,3},{4,5},{6,7},{1,0},{3,2},{5,4},{7,6},{8,9},{10,11},{12,... | collective-permute-start | bytes 98312 | tf_op jit(solution)/shard_map/ppermute | solution.py:758
  30.2 3.7 %collective-permute-start.10 = (f32[3,8,128]{2,1,0:T(8,128)S(1)}, f32[3,8,128]{2,1,0:T(8,128)S(1)}, u32[]{:S(2)}, u32[]{:S(2)}) collective-permute-start(f32[3,8,128]{2,1,0:T(8,128)S(1)} %get-tuple-element.77), channel_id=1, source_target_pairs={{0,2},{1,3},{4,6},{5,7},{2,0},{3,1},{6,4},{7,5},{8,10},{9,11},{12,... | collective-permute-start | bytes 36872 | tf_op jit(solution)/shard_map/ppermute | solution.py:765
  30.2 5.5 %collective-permute-start.11 = (f32[3,8,128]{2,1,0:T(8,128)S(1)}, f32[3,8,128]{2,1,0:T(8,128)S(1)}, u32[]{:S(2)}, u32[]{:S(2)}) collective-permute-start(f32[3,8,128]{2,1,0:T(8,128)S(1)} %get-tuple-element.77), channel_id=1, source_target_pairs={{0,6},{1,7},{4,2},{5,3},{6,0},{7,1},{2,4},{3,5},{8,14},{9,15},{12,... | collective-permute-start | bytes 36872 | tf_op jit(solution)/shard_map/ppermute | solution.py:765

commit v15 on v11

--- a/solution.py
+++ b/solution.py
@@ -306,10 +306,9 @@
     return jnp.where(low, both, roll_z(both, 2)), jnp.where(low, roll_z(both, -2), both)
 
 
-def write_spread(main, coarse, out):
+def write_spread(fields, coarse, out):
     lane = lax.broadcasted_iota(jnp.int32, (1, X), 1)
-    u, v, f, k = (main[i] for i in (0, 1, 4, 5))
-    cross, squared, inv_u, inv_v, _, _ = jacobian(u, v, f, k, 0)
+    cross, squared, inv_u, inv_v, _, _ = jacobian(*fields, 0)
     tops = [jnp.max(jnp.maximum((6.0 * DIFF[0] + cross) * inv_u, (6.0 * DIFF[1] + squared) * inv_v), axis=0)]
     tops.append(jnp.max(packed_spread(coarse[0:OWN], coarse[OWN : 2 * OWN], 1), axis=0))
     tops.append(packed_spread(*split_fields2(coarse[2 * OWN : 2 * OWN + 1]), 2)[0])
@@ -360,14 +359,19 @@
     rows, state, previous, feed, kill, coarse, first, second, spread, main, held, copies, sem
 ):
     inputs = (state, previous, feed, kill)
-    for i, (j, f) in enumerate(SOURCES):
-        for y in range(rows):
-            main[i, y] = plane(inputs[j], f, y, rows)
-    write_spread(main, coarse, copies)
+
+    def field(i):
+        j, f = SOURCES[i]
+        return jnp.stack([plane(inputs[j], f, y, rows) for y in range(rows)])
+
+    fields = {i: field(i) for i in (0, 1, 4, 5)}
+    write_spread([fields[i] for i in (0, 1, 4, 5)], coarse, copies)
     copy = pltpu.make_async_copy(copies, spread, sem)
     copy.start()
     for i in range(6):
-        held[i * rows : (i + 1) * rows] = main[i]
+        value = fields[i] if i in fields else field(i)
+        main[i] = value
+        held[i * rows : (i + 1) * rows] = value
     held[6 * rows : 6 * rows + 2 * OWN + 1] = coarse[...]
     pack_edges(held, is_even("gx"), first, second)
     copy.wait()
@@ -712,14 +716,16 @@
     packed_step(1, coef1, shift, b1, xu, yu, d1, 3, n - 4, CARRY2, g2)
 
     g0, g1, g2 = (gain[i] for i in range(3))
-    for i in (0, 1):
-        for at, take in ((HALO0 - EDGE, prev_of), (HALO0 + rows, next_of)):
-            whole = take(even_y, near_a, near_b, slice(1, 1 + EDGE_TILES))
-            x0[i, 0, at : at + EDGE] = whole[i * EDGE : (i + 1) * EDGE]
-            for j in range(EDGE):
-                x0[i, 1, at + j : at + j + 1] = roll_x(whole[2 * EDGE :], -(4 + 8 * (i * EDGE + j)))
-        for t in (0, 1):
-            x0[i, t, HALO0 : HALO0 + rows] = iterate[i, t]
+    sides = [take(even_y, near_a, near_b, slice(1, 1 + EDGE_TILES)) for take in (prev_of, next_of)]
+
+    def before(i, t, y):
+        if 0 <= y < rows:
+            return iterate[i, t, y : y + 1]
+        side, j = (sides[0], y + EDGE) if y < 0 else (sides[1], y - rows)
+        if t == 0:
+            return side[i * EDGE + j : i * EDGE + j + 1]
+        return roll_x(side[2 * EDGE :], -(4 + 8 * (i * EDGE + j)))
+
     for t in (0, 1):
         for row in range(-2, rows // 2 + 2):
             at = row // 2 - LO_UP + 1
@@ -727,7 +733,7 @@
             for i, fine in enumerate((jnp.where(even, value, roll_z(value, 1)), jnp.where(even, roll_z(value, -1), value))):
                 for y in (2 * row, 2 * row + 1):
                     if -EDGE <= y < rows + EDGE:
-                        x0[i, t, y + HALO0 : y + HALO0 + 1] = x0[i, t, y + HALO0 : y + HALO0 + 1] + fine
+                        x0[i, t, y + HALO0 : y + HALO0 + 1] = before(i, t, y) + fine
     total = rows + 2 * HALO0
     for r, n in chunks(2, total - 2):
         cheb_step(0, keep0, x0, y0, d0, r, n, None, g0)

time: 38.4 us -> 38.4 us (level)
  no operation moved by 1% of the time
where the time goes in v15:
time: 38.4 us; the launch traced here: 38.2 us
  starting transfers between devices  20.2 us (53%)
  waiting for transfers between devices  10.3 us (27%)
  Pallas kernels  7.65 us (20%)
    ppermute x10, starting transfers between devices, swap(): return lax.ppermute(value, axis, pairs + [(j, i) for i, j in pairs])  14.9 us
    pallas_call x10, Pallas kernels, call(): pl.pallas_call(kernel, out_shape=out, in_specs=[pl.BlockSpec(memory_space...  7.65 us
    ppermute x10, waiting for transfers between devices, swap(): return lax.ppermute(value, axis, pairs + [(j, i) for i, j in pairs])  6.25 us
    ppermute x2, waiting for transfers between devices, swap_far(): return lax.ppermute(value, axis, pairs + [(j, i) for i, j in pairs])  2.77 us
    ppermute x2, starting transfers between devices, swap_far(): return lax.ppermute(value, axis, pairs + [(j, i) for i, j in pairs])  2.73 us
    all_to_all x1, starting transfers between devices, body(): spread = lax.all_to_all(spread, ('gx', 'gy'), 0, 0, tiled=True)  2.57 us
    all_to_all x1, waiting for transfers between devices, body(): spread = lax.all_to_all(spread, ('gx', 'gy'), 0, 0, tiled=True)  1.23 us
  transfers between devices with their start and end apart: 13, of which 7 were waited for; matrix products, arithmetic and copies ran while one was open for 0% of the time, Pallas kernels for 8%

profile of v15, /device:TPU:0, one launch (start us, length us, event | category | flops | bytes accessed | tf_op | source)
XLA Modules:
  0.0 38.2 jit_solution(6156112764535341307)
XLA Ops:
  0.0 1.3 %shard_map.46 = (f32[27,8,128]{2,1,0:T(8,128)S(1)}, f32[27,8,128]{2,1,0:T(8,128)S(1)}, f32[9,8,128]{2,1,0:T(8,128)S(1)}, f32[256,128]{1,0:T(8,128)S(1)}, f32[256...) custom-call(f32[256,128]{1,0:T(8,128)} %bitcast.5, f32[256,128]{1,0:T(8,128)} %bitcast.6, ...), custom_call_target="tpu_custom_call" | custom-call | tf_op jit(solution)/shard_map/pallas_call | solution.py:751
  1.3 6.1 %collective-permute-start = (f32[27,8,128]{2,1,0:T(8,128)S(1)}, f32[27,8,128]{2,1,0:T(8,128)S(1)}, u32[]{:S(2)}, u32[]{:S(2)}) collective-permute-start(f32[27,8,128]{2,1,0:T(8,128)S(1)} %get-tuple-element.49), channel_id=1, source_target_pairs={{0,7},{2,1},{4,3},{6,5},{7,0},{1,2},{3,4},{5,6},{8,15},{10,9},{12,... | collective-permute-start | bytes 331784 | tf_op jit(solution)/shard_map/ppermute | solution.py:765
  7.4 0.9 %shard_map.47 = (f32[35,8,128]{2,1,0:T(8,128)S(1)}, f32[35,8,128]{2,1,0:T(8,128)S(1)}, f32[32,4,128]{2,1,0:T(4,128)}, f32[6,16,8,128]{3,2,1,0:T(8,128)S(1)}) custom-call(f32[256,128]{1,0:T(8,128)S(1)} %get-tuple-element.43.state, f32[256,128]{1,0:T(8,128)S(1)} %get-tuple-element.44.previous, f32[128,128]{1,0:T(8,128)S(1)} %get-tuple-element.45.feed, ...), custom_call_target="tpu_custom_call" | custom-call | tf_op jit(solution)/shard_map/pallas_call | solution.py:751
  8.3 0.7 %collective-permute-start.2 = (f32[35,8,128]{2,1,0:T(8,128)S(1)}, f32[35,8,128]{2,1,0:T(8,128)S(1)}, u32[]{:S(2)}, u32[]{:S(2)}) collective-permute-start(f32[35,8,128]{2,1,0:T(8,128)S(1)} %get-tuple-element.51), channel_id=1, source_target_pairs={{0,24},{16,8},{24,0},{8,16},{1,25},{17,9},{25,1},{9,17},{2,26},{18... | collective-permute-start | bytes 430088 | tf_op jit(solution)/shard_map/ppermute | solution.py:765
  9.1 1.0 %collective-permute-start.3 = (f32[35,8,128]{2,1,0:T(8,128)S(1)}, f32[35,8,128]{2,1,0:T(8,128)S(1)}, u32[]{:S(2)}, u32[]{:S(2)}) collective-permute-start(f32[35,8,128]{2,1,0:T(8,128)S(1)} %get-tuple-element.52), channel_id=1, source_target_pairs={{0,8},{16,24},{8,0},{24,16},{1,9},{17,25},{9,1},{25,17},{2,10},{18... | collective-permute-start | bytes 430088 | tf_op jit(solution)/shard_map/ppermute | solution.py:765
  10.0 2.6 %all-to-all-start = ((f32[32,4,128]{2,1,0:T(4,128)}), f32[32,4,128]{2,1,0:T(4,128)S(1)}, u32[]{:S(2)}, u32[]{:S(2)}) async-start(f32[32,4,128]{2,1,0:T(4,128)} %get-tuple-element.63), calls=%async_computation | async-start | bytes 131072 | tf_op jit(solution)/shard_map/all_to_all | solution.py:811
  12.6 0.2 collective-permute-done.1.y_second
  13.0 1.2 %collective-permute-start.4 = (f32[18,8,128]{2,1,0:T(8,128)S(1)}, f32[18,8,128]{2,1,0:T(8,128)S(1)}, u32[]{:S(2)}, u32[]{:S(2)}) collective-permute-start(f32[18,8,128]{2,1,0:T(8,128)S(1)} %get-tuple-element.53), channel_id=1, source_target_pairs={{0,24},{16,8},{24,0},{8,16},{1,25},{17,9},{25,1},{9,17},{2,26},{18... | collective-permute-start | bytes 221192 | tf_op jit(solution)/shard_map/ppermute | solution.py:765
  14.2 0.4 %collective-permute-start.5 = (f32[18,8,128]{2,1,0:T(8,128)S(1)}, f32[18,8,128]{2,1,0:T(8,128)S(1)}, u32[]{:S(2)}, u32[]{:S(2)}) collective-permute-start(f32[18,8,128]{2,1,0:T(8,128)S(1)} %get-tuple-element.54), channel_id=1, source_target_pairs={{0,8},{16,24},{8,0},{24,16},{1,9},{17,25},{9,1},{25,17},{2,10},{18... | collective-permute-start | bytes 221192 | tf_op jit(solution)/shard_map/ppermute | solution.py:765
  14.7 0.9 %shard_map.49 = (f32[6,2,14,8,128]{4,3,2,1,0:T(8,128)S(1)}, f32[2,2,4,8,128]{4,3,2,1,0:T(8,128)S(1)}, f32[2,2,12,8,128]{4,3,2,1,0:T(8,128)S(1)}, f32[2,2,10,8,12...) custom-call(f32[6,16,8,128]{3,2,1,0:T(8,128)S(1)} %get-tuple-element.48.main, ...), custom_call_target="tpu_custom_call" | custom-call | tf_op jit(solution)/shard_map/pallas_call | solution.py:751
  15.6 2.3 %collective-permute-done.4.corner_a = f32[18,8,128]{2,1,0:T(8,128)S(1)} collective-permute-done((f32[18,8,128]{2,1,0:T(8,128)S(1)}, f32[18,8,128]{2,1,0:T(8,128)S(1)}, u32[]{:S(2)}, u32[]{:S(2)}) %collective-permute-start.4) | collective-permute-done | bytes 73760 | tf_op jit(solution)/shard_map/ppermute | solution.py:765
  17.9 0.8 %shard_map.50 = (f32[6,2,8,8,128]{4,3,2,1,0:T(8,128)S(1)}, f32[2,2,4,8,128]{4,3,2,1,0:T(8,128)S(1)}, f32[2,2,6,8,128]{4,3,2,1,0:T(8,128)S(1)}, f32[4,2,4,8,128]{4,3,2,1,0:T(8,128)S(1)}, f32[3,2,7,8,128]{4,3,2,1,0:T(8,128)S(1)}) custom-call(f32[6,16,8,128]{3,2,1,0:T(8,128)S(1)} %get-tuple-element.48.main, f32[27,8,128]{2,1,0:T(8,128)S(1)} %collective-permute-done.y_first, ...), custom_call_target="tpu_custom_call" | custom-call | tf_op jit(solution)/shard_map/pallas_call | solution.py:751
  18.6 1.2 %all-to-all-done.spread = f32[32,4,128]{2,1,0:T(4,128)S(1)} async-done(((f32[32,4,128]{2,1,0:T(4,128)}), f32[32,4,128]{2,1,0:T(4,128)S(1)}, u32[]{:S(2)}, u32[]{:S(2)}) %all-to-all-start) | async-done | bytes 65568 | tf_op jit(solution)/shard_map/all_to_all | solution.py:811
  19.9 0.2 shard_map.51
  20.0 2.9 %collective-permute-start.6 = (f32[7,8,128]{2,1,0:T(8,128)S(1)}, f32[7,8,128]{2,1,0:T(8,128)S(1)}, u32[]{:S(2)}, u32[]{:S(2)}) collective-permute-start(f32[7,8,128]{2,1,0:T(8,128)S(1)} %get-tuple-element.65), channel_id=1, source_target_pairs={{0,7},{2,1},{4,3},{6,5},{7,0},{1,2},{3,4},{5,6},{8,15},{10,9},{12,... | collective-permute-start | bytes 86024 | tf_op jit(solution)/shard_map/ppermute | solution.py:765
  23.0 0.2 shard_map.53
  23.2 3.4 %collective-permute-done.6.first = f32[7,8,128]{2,1,0:T(8,128)S(1)} collective-permute-done((f32[7,8,128]{2,1,0:T(8,128)S(1)}, f32[7,8,128]{2,1,0:T(8,128)S(1)}, u32[]{:S(2)}, u32[]{:S(2)}) %collective-permute-start.6) | collective-permute-done | bytes 28704 | tf_op jit(solution)/shard_map/ppermute | solution.py:765
  26.6 0.3 collective-permute-done.7.second
  26.9 0.5 %shard_map.54 = (f32[1,8,128]{2,1,0:T(8,128)S(1)}, f32[8,8,128]{2,1,0:T(8,128)S(1)}, f32[8,8,128]{2,1,0:T(8,128)S(1)}, f32[3,8,128]{2,1,0:T(8,128)S(1)}, f32[2,2,14,8,128]{4,3,2,1,0:T(8,128)S(1)}) custom-call(f32[2,4,8,128]{3,2,1,0:T(8,128)S(1)} %get-tuple-element.64.own, f32[7,8,128]{2,1,0:T(8,128)S(1)} %collective-permute-done.6.first, ...), custom_call_target="tpu_custom_call" | custom-call | tf_op jit(solution)/shard_map/pallas_call | solution.py:751
  27.5 2.6 %collective-permute-start.8 = (f32[8,8,128]{2,1,0:T(8,128)S(1)}, f32[8,8,128]{2,1,0:T(8,128)S(1)}, u32[]{:S(2)}, u32[]{:S(2)}) collective-permute-start(f32[8,8,128]{2,1,0:T(8,128)S(1)} %get-tuple-element.75), channel_id=1, source_target_pairs={{0,7},{2,1},{4,3},{6,5},{7,0},{1,2},{3,4},{5,6},{8,15},{10,9},{12,... | collective-permute-start | bytes 98312 | tf_op jit(solution)/shard_map/ppermute | solution.py:765
  30.1 2.7 %collective-permute-start.11 = (f32[3,8,128]{2,1,0:T(8,128)S(1)}, f32[3,8,128]{2,1,0:T(8,128)S(1)}, u32[]{:S(2)}, u32[]{:S(2)}) collective-permute-start(f32[3,8,128]{2,1,0:T(8,128)S(1)} %get-tuple-element.77), channel_id=1, source_target_pairs={{0,6},{1,7},{4,2},{5,3},{6,0},{7,1},{2,4},{3,5},{8,14},{9,15},{12,... | collective-permute-start | bytes 36872 | tf_op jit(solution)/shard_map/ppermute | solution.py:772
  32.8 1.0 %collective-permute-done.10.far_a = f32[3,8,128]{2,1,0:T(8,128)S(1)} collective-permute-done((f32[3,8,128]{2,1,0:T(8,128)S(1)}, f32[3,8,128]{2,1,0:T(8,128)S(1)}, u32[]{:S(2)}, u32[]{:S(2)}) %collective-permute-start.10) | collective-permute-done | bytes 12320 | tf_op jit(solution)/shard_map/ppermute | solution.py:772
  33.8 1.8 %collective-permute-done.11.far_b = f32[3,8,128]{2,1,0:T(8,128)S(1)} collective-permute-done((f32[3,8,128]{2,1,0:T(8,128)S(1)}, f32[3,8,128]{2,1,0:T(8,128)S(1)}, u32[]{:S(2)}, u32[]{:S(2)}) %collective-permute-start.11) | collective-permute-done | bytes 12320 | tf_op jit(solution)/shard_map/ppermute | solution.py:772
  35.6 2.6 %shard_map.55 = f32[256,128]{1,0:T(8,128)} custom-call(f32[1,8,128]{2,1,0:T(8,128)S(1)} %get-tuple-element.74.own2, f32[8,8,128]{2,1,0:T(8,128)S(1)} %collective-permute-done.8.near_a, f32[8,8,128]{2,1,0:T(8,128)S(1)} %collective-permute-done.9.near_b, f32[3,8,128]{2,1,0:T(8,128)S(1)} %collective-permute-done.10.far_a, ...), custom_call_target="tpu_custom_call" | custom-call | tf_op jit(solution)/shard_map/pallas_call | solution.py:751
  (12 shorter events, 0.3 us)
Async XLA Ops:
  1.3 11.2 %collective-permute-start = (f32[27,8,128]{2,1,0:T(8,128)S(1)}, f32[27,8,128]{2,1,0:T(8,128)S(1)}, u32[]{:S(2)}, u32[]{:S(2)}) collective-permute-start(f32[27,8,128]{2,1,0:T(8,128)S(1)} %get-tuple-element.49), channel_id=1, source_target_pairs={{0,7},{2,1},{4,3},{6,5},{7,0},{1,2},{3,4},{5,6},{8,15},{10,9},{12,... | collective-permute-start | bytes 331784 | tf_op jit(solution)/shard_map/ppermute | solution.py:765
  7.4 5.4 %collective-permute-start.1 = (f32[27,8,128]{2,1,0:T(8,128)S(1)}, f32[27,8,128]{2,1,0:T(8,128)S(1)}, u32[]{:S(2)}, u32[]{:S(2)}) collective-permute-start(f32[27,8,128]{2,1,0:T(8,128)S(1)} %get-tuple-element.50), channel_id=1, source_target_pairs={{0,1},{2,3},{4,5},{6,7},{1,0},{3,2},{5,4},{7,6},{8,9},{10,11},{12,... | collective-permute-start | bytes 331784 | tf_op jit(solution)/shard_map/ppermute | solution.py:765
  8.3 6.4 %collective-permute-start.2 = (f32[35,8,128]{2,1,0:T(8,128)S(1)}, f32[35,8,128]{2,1,0:T(8,128)S(1)}, u32[]{:S(2)}, u32[]{:S(2)}) collective-permute-start(f32[35,8,128]{2,1,0:T(8,128)S(1)} %get-tuple-element.51), channel_id=1, source_target_pairs={{0,24},{16,8},{24,0},{8,16},{1,25},{17,9},{25,1},{9,17},{2,26},{18... | collective-permute-start | bytes 430088 | tf_op jit(solution)/shard_map/ppermute | solution.py:765
  9.1 5.6 %collective-permute-start.3 = (f32[35,8,128]{2,1,0:T(8,128)S(1)}, f32[35,8,128]{2,1,0:T(8,128)S(1)}, u32[]{:S(2)}, u32[]{:S(2)}) collective-permute-start(f32[35,8,128]{2,1,0:T(8,128)S(1)} %get-tuple-element.52), channel_id=1, source_target_pairs={{0,8},{16,24},{8,0},{24,16},{1,9},{17,25},{9,1},{25,17},{2,10},{18... | collective-permute-start | bytes 430088 | tf_op jit(solution)/shard_map/ppermute | solution.py:765
  10.0 9.9 %all-to-all-start = ((f32[32,4,128]{2,1,0:T(4,128)}), f32[32,4,128]{2,1,0:T(4,128)S(1)}, u32[]{:S(2)}, u32[]{:S(2)}) async-start(f32[32,4,128]{2,1,0:T(4,128)} %get-tuple-element.63), calls=%async_computation | async-start | bytes 131072 | tf_op jit(solution)/shard_map/all_to_all | solution.py:811
  13.0 4.8 %collective-permute-start.4 = (f32[18,8,128]{2,1,0:T(8,128)S(1)}, f32[18,8,128]{2,1,0:T(8,128)S(1)}, u32[]{:S(2)}, u32[]{:S(2)}) collective-permute-start(f32[18,8,128]{2,1,0:T(8,128)S(1)} %get-tuple-element.53), channel_id=1, source_target_pairs={{0,24},{16,8},{24,0},{8,16},{1,25},{17,9},{25,1},{9,17},{2,26},{18... | collective-permute-start | bytes 221192 | tf_op jit(solution)/shard_map/ppermute | solution.py:765
  14.2 3.6 %collective-permute-start.5 = (f32[18,8,128]{2,1,0:T(8,128)S(1)}, f32[18,8,128]{2,1,0:T(8,128)S(1)}, u32[]{:S(2)}, u32[]{:S(2)}) collective-permute-start(f32[18,8,128]{2,1,0:T(8,128)S(1)} %get-tuple-element.54), channel_id=1, source_target_pairs={{0,8},{16,24},{8,0},{24,16},{1,9},{17,25},{9,1},{25,17},{2,10},{18... | collective-permute-start | bytes 221192 | tf_op jit(solution)/shard_map/ppermute | solution.py:765
  20.0 6.6 %collective-permute-start.6 = (f32[7,8,128]{2,1,0:T(8,128)S(1)}, f32[7,8,128]{2,1,0:T(8,128)S(1)}, u32[]{:S(2)}, u32[]{:S(2)}) collective-permute-start(f32[7,8,128]{2,1,0:T(8,128)S(1)} %get-tuple-element.65), channel_id=1, source_target_pairs={{0,7},{2,1},{4,3},{6,5},{7,0},{1,2},{3,4},{5,6},{8,15},{10,9},{12,... | collective-permute-start | bytes 86024 | tf_op jit(solution)/shard_map/ppermute | solution.py:765
  22.9 4.0 %collective-permute-start.7 = (f32[7,8,128]{2,1,0:T(8,128)S(1)}, f32[7,8,128]{2,1,0:T(8,128)S(1)}, u32[]{:S(2)}, u32[]{:S(2)}) collective-permute-start(f32[7,8,128]{2,1,0:T(8,128)S(1)} %get-tuple-element.66), channel_id=1, source_target_pairs={{0,1},{2,3},{4,5},{6,7},{1,0},{3,2},{5,4},{7,6},{8,9},{10,11},{12,... | collective-permute-start | bytes 86024 | tf_op jit(solution)/shard_map/ppermute | solution.py:765
  27.5 8.1 %collective-permute-start.8 = (f32[8,8,128]{2,1,0:T(8,128)S(1)}, f32[8,8,128]{2,1,0:T(8,128)S(1)}, u32[]{:S(2)}, u32[]{:S(2)}) collective-permute-start(f32[8,8,128]{2,1,0:T(8,128)S(1)} %get-tuple-element.75), channel_id=1, source_target_pairs={{0,7},{2,1},{4,3},{6,5},{7,0},{1,2},{3,4},{5,6},{8,15},{10,9},{12,... | collective-permute-start | bytes 98312 | tf_op jit(solution)/shard_map/ppermute | solution.py:765
  30.1 5.5 %collective-permute-start.9 = (f32[8,8,128]{2,1,0:T(8,128)S(1)}, f32[8,8,128]{2,1,0:T(8,128)S(1)}, u32[]{:S(2)}, u32[]{:S(2)}) collective-permute-start(f32[8,8,128]{2,1,0:T(8,128)S(1)} %get-tuple-element.76), channel_id=1, source_target_pairs={{0,1},{2,3},{4,5},{6,7},{1,0},{3,2},{5,4},{7,6},{8,9},{10,11},{12,... | collective-permute-start | bytes 98312 | tf_op jit(solution)/shard_map/ppermute | solution.py:765
  30.1 3.7 %collective-permute-start.10 = (f32[3,8,128]{2,1,0:T(8,128)S(1)}, f32[3,8,128]{2,1,0:T(8,128)S(1)}, u32[]{:S(2)}, u32[]{:S(2)}) collective-permute-start(f32[3,8,128]{2,1,0:T(8,128)S(1)} %get-tuple-element.77), channel_id=1, source_target_pairs={{0,2},{1,3},{4,6},{5,7},{2,0},{3,1},{6,4},{7,5},{8,10},{9,11},{12,... | collective-permute-start | bytes 36872 | tf_op jit(solution)/shard_map/ppermute | solution.py:772
  30.1 5.5 %collective-permute-start.11 = (f32[3,8,128]{2,1,0:T(8,128)S(1)}, f32[3,8,128]{2,1,0:T(8,128)S(1)}, u32[]{:S(2)}, u32[]{:S(2)}) collective-permute-start(f32[3,8,128]{2,1,0:T(8,128)S(1)} %get-tuple-element.77), channel_id=1, source_target_pairs={{0,6},{1,7},{4,2},{5,3},{6,0},{7,1},{2,4},{3,5},{8,14},{9,15},{12,... | collective-permute-start | bytes 36872 | tf_op jit(solution)/shard_map/ppermute | solution.py:772

commit v16 on v15

--- a/solution.py
+++ b/solution.py
@@ -368,12 +368,16 @@
     write_spread([fields[i] for i in (0, 1, 4, 5)], coarse, copies)
     copy = pltpu.make_async_copy(copies, spread, sem)
     copy.start()
-    for i in range(6):
-        value = fields[i] if i in fields else field(i)
-        main[i] = value
-        held[i * rows : (i + 1) * rows] = value
-    held[6 * rows : 6 * rows + 2 * OWN + 1] = coarse[...]
-    pack_edges(held, is_even("gx"), first, second)
+
+    @pl.when(lax.axis_index("gx") >= 0)
+    def _():
+        for i in range(6):
+            value = field(i)
+            main[i] = value
+            held[i * rows : (i + 1) * rows] = value
+        held[6 * rows : 6 * rows + 2 * OWN + 1] = coarse[...]
+        pack_edges(held, is_even("gx"), first, second)
+
     copy.wait()
 
 

time: 38.4 us -> 38.3 us (level)
  no operation moved by 1% of the time
where the time goes in v16:
time: 38.3 us; the launch traced here: 38.2 us
  starting transfers between devices  20.2 us (53%)
  waiting for transfers between devices  10.3 us (27%)
  Pallas kernels  7.6 us (20%)
    ppermute x10, starting transfers between devices, swap(): return lax.ppermute(value, axis, pairs + [(j, i) for i, j in pairs])  14.9 us
    pallas_call x10, Pallas kernels, call(): pl.pallas_call(kernel, out_shape=out, in_specs=[pl.BlockSpec(memory_space...  7.6 us
    ppermute x10, waiting for transfers between devices, swap(): return lax.ppermute(value, axis, pairs + [(j, i) for i, j in pairs])  6.31 us
    ppermute x2, waiting for transfers between devices, swap_far(): return lax.ppermute(value, axis, pairs + [(j, i) for i, j in pairs])  2.77 us
    ppermute x2, starting transfers between devices, swap_far(): return lax.ppermute(value, axis, pairs + [(j, i) for i, j in pairs])  2.73 us
    all_to_all x1, starting transfers between devices, body(): spread = lax.all_to_all(spread, ('gx', 'gy'), 0, 0, tiled=True)  2.57 us
    all_to_all x1, waiting for transfers between devices, body(): spread = lax.all_to_all(spread, ('gx', 'gy'), 0, 0, tiled=True)  1.18 us
  transfers between devices with their start and end apart: 13, of which 7 were waited for; matrix products, arithmetic and copies ran while one was open for 0% of the time, Pallas kernels for 8%

profile of v16, /device:TPU:0, one launch (start us, length us, event | category | flops | bytes accessed | tf_op | source)
XLA Modules:
  0.0 38.2 jit_solution(2645188292749814425)
XLA Ops:
  0.0 1.3 %shard_map.46 = (f32[27,8,128]{2,1,0:T(8,128)S(1)}, f32[27,8,128]{2,1,0:T(8,128)S(1)}, f32[9,8,128]{2,1,0:T(8,128)S(1)}, f32[256,128]{1,0:T(8,128)S(1)}, f32[256...) custom-call(f32[256,128]{1,0:T(8,128)} %bitcast.5, f32[256,128]{1,0:T(8,128)} %bitcast.6, ...), custom_call_target="tpu_custom_call" | custom-call | tf_op jit(solution)/shard_map/pallas_call | solution.py:755
  1.3 6.1 %collective-permute-start = (f32[27,8,128]{2,1,0:T(8,128)S(1)}, f32[27,8,128]{2,1,0:T(8,128)S(1)}, u32[]{:S(2)}, u32[]{:S(2)}) collective-permute-start(f32[27,8,128]{2,1,0:T(8,128)S(1)} %get-tuple-element.49), channel_id=1, source_target_pairs={{0,7},{2,1},{4,3},{6,5},{7,0},{1,2},{3,4},{5,6},{8,15},{10,9},{12,... | collective-permute-start | bytes 331784 | tf_op jit(solution)/shard_map/ppermute | solution.py:769
  7.4 0.9 %shard_map.47 = (f32[35,8,128]{2,1,0:T(8,128)S(1)}, f32[35,8,128]{2,1,0:T(8,128)S(1)}, f32[32,4,128]{2,1,0:T(4,128)}, f32[6,16,8,128]{3,2,1,0:T(8,128)S(1)}) custom-call(f32[256,128]{1,0:T(8,128)S(1)} %get-tuple-element.43.state, f32[256,128]{1,0:T(8,128)S(1)} %get-tuple-element.44.previous, f32[128,128]{1,0:T(8,128)S(1)} %get-tuple-element.45.feed, ...), custom_call_target="tpu_custom_call" | custom-call | tf_op jit(solution)/shard_map/pallas_call | solution.py:755
  8.3 0.7 %collective-permute-start.2 = (f32[35,8,128]{2,1,0:T(8,128)S(1)}, f32[35,8,128]{2,1,0:T(8,128)S(1)}, u32[]{:S(2)}, u32[]{:S(2)}) collective-permute-start(f32[35,8,128]{2,1,0:T(8,128)S(1)} %get-tuple-element.51), channel_id=1, source_target_pairs={{0,24},{16,8},{24,0},{8,16},{1,25},{17,9},{25,1},{9,17},{2,26},{18... | collective-permute-start | bytes 430088 | tf_op jit(solution)/shard_map/ppermute | solution.py:769
  9.0 1.0 %collective-permute-start.3 = (f32[35,8,128]{2,1,0:T(8,128)S(1)}, f32[35,8,128]{2,1,0:T(8,128)S(1)}, u32[]{:S(2)}, u32[]{:S(2)}) collective-permute-start(f32[35,8,128]{2,1,0:T(8,128)S(1)} %get-tuple-element.52), channel_id=1, source_target_pairs={{0,8},{16,24},{8,0},{24,16},{1,9},{17,25},{9,1},{25,17},{2,10},{18... | collective-permute-start | bytes 430088 | tf_op jit(solution)/shard_map/ppermute | solution.py:769
  10.0 2.6 %all-to-all-start = ((f32[32,4,128]{2,1,0:T(4,128)}), f32[32,4,128]{2,1,0:T(4,128)S(1)}, u32[]{:S(2)}, u32[]{:S(2)}) async-start(f32[32,4,128]{2,1,0:T(4,128)} %get-tuple-element.63), calls=%async_computation | async-start | bytes 131072 | tf_op jit(solution)/shard_map/all_to_all | solution.py:815
  12.6 0.3 collective-permute-done.1.y_second
  13.0 1.2 %collective-permute-start.4 = (f32[18,8,128]{2,1,0:T(8,128)S(1)}, f32[18,8,128]{2,1,0:T(8,128)S(1)}, u32[]{:S(2)}, u32[]{:S(2)}) collective-permute-start(f32[18,8,128]{2,1,0:T(8,128)S(1)} %get-tuple-element.53), channel_id=1, source_target_pairs={{0,24},{16,8},{24,0},{8,16},{1,25},{17,9},{25,1},{9,17},{2,26},{18... | collective-permute-start | bytes 221192 | tf_op jit(solution)/shard_map/ppermute | solution.py:769
  14.2 0.5 %collective-permute-start.5 = (f32[18,8,128]{2,1,0:T(8,128)S(1)}, f32[18,8,128]{2,1,0:T(8,128)S(1)}, u32[]{:S(2)}, u32[]{:S(2)}) collective-permute-start(f32[18,8,128]{2,1,0:T(8,128)S(1)} %get-tuple-element.54), channel_id=1, source_target_pairs={{0,8},{16,24},{8,0},{24,16},{1,9},{17,25},{9,1},{25,17},{2,10},{18... | collective-permute-start | bytes 221192 | tf_op jit(solution)/shard_map/ppermute | solution.py:769
  14.7 0.9 %shard_map.49 = (f32[6,2,14,8,128]{4,3,2,1,0:T(8,128)S(1)}, f32[2,2,4,8,128]{4,3,2,1,0:T(8,128)S(1)}, f32[2,2,12,8,128]{4,3,2,1,0:T(8,128)S(1)}, f32[2,2,10,8,12...) custom-call(f32[6,16,8,128]{3,2,1,0:T(8,128)S(1)} %get-tuple-element.48.main, ...), custom_call_target="tpu_custom_call" | custom-call | tf_op jit(solution)/shard_map/pallas_call | solution.py:755
  15.6 2.3 %collective-permute-done.4.corner_a = f32[18,8,128]{2,1,0:T(8,128)S(1)} collective-permute-done((f32[18,8,128]{2,1,0:T(8,128)S(1)}, f32[18,8,128]{2,1,0:T(8,128)S(1)}, u32[]{:S(2)}, u32[]{:S(2)}) %collective-permute-start.4) | collective-permute-done | bytes 73760 | tf_op jit(solution)/shard_map/ppermute | solution.py:769
  17.9 0.8 %shard_map.50 = (f32[6,2,8,8,128]{4,3,2,1,0:T(8,128)S(1)}, f32[2,2,4,8,128]{4,3,2,1,0:T(8,128)S(1)}, f32[2,2,6,8,128]{4,3,2,1,0:T(8,128)S(1)}, f32[4,2,4,8,128]{4,3,2,1,0:T(8,128)S(1)}, f32[3,2,7,8,128]{4,3,2,1,0:T(8,128)S(1)}) custom-call(f32[6,16,8,128]{3,2,1,0:T(8,128)S(1)} %get-tuple-element.48.main, f32[27,8,128]{2,1,0:T(8,128)S(1)} %collective-permute-done.y_first, ...), custom_call_target="tpu_custom_call" | custom-call | tf_op jit(solution)/shard_map/pallas_call | solution.py:755
  18.6 1.2 %all-to-all-done.spread = f32[32,4,128]{2,1,0:T(4,128)S(1)} async-done(((f32[32,4,128]{2,1,0:T(4,128)}), f32[32,4,128]{2,1,0:T(4,128)S(1)}, u32[]{:S(2)}, u32[]{:S(2)}) %all-to-all-start) | async-done | bytes 65568 | tf_op jit(solution)/shard_map/all_to_all | solution.py:815
  19.8 0.2 shard_map.51
  20.0 2.9 %collective-permute-start.6 = (f32[7,8,128]{2,1,0:T(8,128)S(1)}, f32[7,8,128]{2,1,0:T(8,128)S(1)}, u32[]{:S(2)}, u32[]{:S(2)}) collective-permute-start(f32[7,8,128]{2,1,0:T(8,128)S(1)} %get-tuple-element.65), channel_id=1, source_target_pairs={{0,7},{2,1},{4,3},{6,5},{7,0},{1,2},{3,4},{5,6},{8,15},{10,9},{12,... | collective-permute-start | bytes 86024 | tf_op jit(solution)/shard_map/ppermute | solution.py:769
  23.0 0.2 shard_map.53
  23.2 3.4 %collective-permute-done.6.first = f32[7,8,128]{2,1,0:T(8,128)S(1)} collective-permute-done((f32[7,8,128]{2,1,0:T(8,128)S(1)}, f32[7,8,128]{2,1,0:T(8,128)S(1)}, u32[]{:S(2)}, u32[]{:S(2)}) %collective-permute-start.6) | collective-permute-done | bytes 28704 | tf_op jit(solution)/shard_map/ppermute | solution.py:769
  26.6 0.3 collective-permute-done.7.second
  26.9 0.5 %shard_map.54 = (f32[1,8,128]{2,1,0:T(8,128)S(1)}, f32[8,8,128]{2,1,0:T(8,128)S(1)}, f32[8,8,128]{2,1,0:T(8,128)S(1)}, f32[3,8,128]{2,1,0:T(8,128)S(1)}, f32[2,2,14,8,128]{4,3,2,1,0:T(8,128)S(1)}) custom-call(f32[2,4,8,128]{3,2,1,0:T(8,128)S(1)} %get-tuple-element.64.own, f32[7,8,128]{2,1,0:T(8,128)S(1)} %collective-permute-done.6.first, ...), custom_call_target="tpu_custom_call" | custom-call | tf_op jit(solution)/shard_map/pallas_call | solution.py:755
  27.4 2.6 %collective-permute-start.8 = (f32[8,8,128]{2,1,0:T(8,128)S(1)}, f32[8,8,128]{2,1,0:T(8,128)S(1)}, u32[]{:S(2)}, u32[]{:S(2)}) collective-permute-start(f32[8,8,128]{2,1,0:T(8,128)S(1)} %get-tuple-element.75), channel_id=1, source_target_pairs={{0,7},{2,1},{4,3},{6,5},{7,0},{1,2},{3,4},{5,6},{8,15},{10,9},{12,... | collective-permute-start | bytes 98312 | tf_op jit(solution)/shard_map/ppermute | solution.py:769
  30.1 2.7 %collective-permute-start.11 = (f32[3,8,128]{2,1,0:T(8,128)S(1)}, f32[3,8,128]{2,1,0:T(8,128)S(1)}, u32[]{:S(2)}, u32[]{:S(2)}) collective-permute-start(f32[3,8,128]{2,1,0:T(8,128)S(1)} %get-tuple-element.77), channel_id=1, source_target_pairs={{0,6},{1,7},{4,2},{5,3},{6,0},{7,1},{2,4},{3,5},{8,14},{9,15},{12,... | collective-permute-start | bytes 36872 | tf_op jit(solution)/shard_map/ppermute | solution.py:776
  32.8 1.0 %collective-permute-done.10.far_a = f32[3,8,128]{2,1,0:T(8,128)S(1)} collective-permute-done((f32[3,8,128]{2,1,0:T(8,128)S(1)}, f32[3,8,128]{2,1,0:T(8,128)S(1)}, u32[]{:S(2)}, u32[]{:S(2)}) %collective-permute-start.10) | collective-permute-done | bytes 12320 | tf_op jit(solution)/shard_map/ppermute | solution.py:776
  33.8 1.8 %collective-permute-done.11.far_b = f32[3,8,128]{2,1,0:T(8,128)S(1)} collective-permute-done((f32[3,8,128]{2,1,0:T(8,128)S(1)}, f32[3,8,128]{2,1,0:T(8,128)S(1)}, u32[]{:S(2)}, u32[]{:S(2)}) %collective-permute-start.11) | collective-permute-done | bytes 12320 | tf_op jit(solution)/shard_map/ppermute | solution.py:776
  35.6 2.6 %shard_map.55 = f32[256,128]{1,0:T(8,128)} custom-call(f32[1,8,128]{2,1,0:T(8,128)S(1)} %get-tuple-element.74.own2, f32[8,8,128]{2,1,0:T(8,128)S(1)} %collective-permute-done.8.near_a, f32[8,8,128]{2,1,0:T(8,128)S(1)} %collective-permute-done.9.near_b, f32[3,8,128]{2,1,0:T(8,128)S(1)} %collective-permute-done.10.far_a, ...), custom_call_target="tpu_custom_call" | custom-call | tf_op jit(solution)/shard_map/pallas_call | solution.py:755
  (12 shorter events, 0.3 us)
Async XLA Ops:
  1.3 11.2 %collective-permute-start = (f32[27,8,128]{2,1,0:T(8,128)S(1)}, f32[27,8,128]{2,1,0:T(8,128)S(1)}, u32[]{:S(2)}, u32[]{:S(2)}) collective-permute-start(f32[27,8,128]{2,1,0:T(8,128)S(1)} %get-tuple-element.49), channel_id=1, source_target_pairs={{0,7},{2,1},{4,3},{6,5},{7,0},{1,2},{3,4},{5,6},{8,15},{10,9},{12,... | collective-permute-start | bytes 331784 | tf_op jit(solution)/shard_map/ppermute | solution.py:769
  7.4 5.4 %collective-permute-start.1 = (f32[27,8,128]{2,1,0:T(8,128)S(1)}, f32[27,8,128]{2,1,0:T(8,128)S(1)}, u32[]{:S(2)}, u32[]{:S(2)}) collective-permute-start(f32[27,8,128]{2,1,0:T(8,128)S(1)} %get-tuple-element.50), channel_id=1, source_target_pairs={{0,1},{2,3},{4,5},{6,7},{1,0},{3,2},{5,4},{7,6},{8,9},{10,11},{12,... | collective-permute-start | bytes 331784 | tf_op jit(solution)/shard_map/ppermute | solution.py:769
  8.3 6.4 %collective-permute-start.2 = (f32[35,8,128]{2,1,0:T(8,128)S(1)}, f32[35,8,128]{2,1,0:T(8,128)S(1)}, u32[]{:S(2)}, u32[]{:S(2)}) collective-permute-start(f32[35,8,128]{2,1,0:T(8,128)S(1)} %get-tuple-element.51), channel_id=1, source_target_pairs={{0,24},{16,8},{24,0},{8,16},{1,25},{17,9},{25,1},{9,17},{2,26},{18... | collective-permute-start | bytes 430088 | tf_op jit(solution)/shard_map/ppermute | solution.py:769
  9.0 5.7 %collective-permute-start.3 = (f32[35,8,128]{2,1,0:T(8,128)S(1)}, f32[35,8,128]{2,1,0:T(8,128)S(1)}, u32[]{:S(2)}, u32[]{:S(2)}) collective-permute-start(f32[35,8,128]{2,1,0:T(8,128)S(1)} %get-tuple-element.52), channel_id=1, source_target_pairs={{0,8},{16,24},{8,0},{24,16},{1,9},{17,25},{9,1},{25,17},{2,10},{18... | collective-permute-start | bytes 430088 | tf_op jit(solution)/shard_map/ppermute | solution.py:769
  10.0 9.9 %all-to-all-start = ((f32[32,4,128]{2,1,0:T(4,128)}), f32[32,4,128]{2,1,0:T(4,128)S(1)}, u32[]{:S(2)}, u32[]{:S(2)}) async-start(f32[32,4,128]{2,1,0:T(4,128)} %get-tuple-element.63), calls=%async_computation | async-start | bytes 131072 | tf_op jit(solution)/shard_map/all_to_all | solution.py:815
  13.0 4.8 %collective-permute-start.4 = (f32[18,8,128]{2,1,0:T(8,128)S(1)}, f32[18,8,128]{2,1,0:T(8,128)S(1)}, u32[]{:S(2)}, u32[]{:S(2)}) collective-permute-start(f32[18,8,128]{2,1,0:T(8,128)S(1)} %get-tuple-element.53), channel_id=1, source_target_pairs={{0,24},{16,8},{24,0},{8,16},{1,25},{17,9},{25,1},{9,17},{2,26},{18... | collective-permute-start | bytes 221192 | tf_op jit(solution)/shard_map/ppermute | solution.py:769
  14.2 3.7 %collective-permute-start.5 = (f32[18,8,128]{2,1,0:T(8,128)S(1)}, f32[18,8,128]{2,1,0:T(8,128)S(1)}, u32[]{:S(2)}, u32[]{:S(2)}) collective-permute-start(f32[18,8,128]{2,1,0:T(8,128)S(1)} %get-tuple-element.54), channel_id=1, source_target_pairs={{0,8},{16,24},{8,0},{24,16},{1,9},{17,25},{9,1},{25,17},{2,10},{18... | collective-permute-start | bytes 221192 | tf_op jit(solution)/shard_map/ppermute | solution.py:769
  20.0 6.6 %collective-permute-start.6 = (f32[7,8,128]{2,1,0:T(8,128)S(1)}, f32[7,8,128]{2,1,0:T(8,128)S(1)}, u32[]{:S(2)}, u32[]{:S(2)}) collective-permute-start(f32[7,8,128]{2,1,0:T(8,128)S(1)} %get-tuple-element.65), channel_id=1, source_target_pairs={{0,7},{2,1},{4,3},{6,5},{7,0},{1,2},{3,4},{5,6},{8,15},{10,9},{12,... | collective-permute-start | bytes 86024 | tf_op jit(solution)/shard_map/ppermute | solution.py:769
  22.9 4.0 %collective-permute-start.7 = (f32[7,8,128]{2,1,0:T(8,128)S(1)}, f32[7,8,128]{2,1,0:T(8,128)S(1)}, u32[]{:S(2)}, u32[]{:S(2)}) collective-permute-start(f32[7,8,128]{2,1,0:T(8,128)S(1)} %get-tuple-element.66), channel_id=1, source_target_pairs={{0,1},{2,3},{4,5},{6,7},{1,0},{3,2},{5,4},{7,6},{8,9},{10,11},{12,... | collective-permute-start | bytes 86024 | tf_op jit(solution)/shard_map/ppermute | solution.py:769
  27.4 8.1 %collective-permute-start.8 = (f32[8,8,128]{2,1,0:T(8,128)S(1)}, f32[8,8,128]{2,1,0:T(8,128)S(1)}, u32[]{:S(2)}, u32[]{:S(2)}) collective-permute-start(f32[8,8,128]{2,1,0:T(8,128)S(1)} %get-tuple-element.75), channel_id=1, source_target_pairs={{0,7},{2,1},{4,3},{6,5},{7,0},{1,2},{3,4},{5,6},{8,15},{10,9},{12,... | collective-permute-start | bytes 98312 | tf_op jit(solution)/shard_map/ppermute | solution.py:769
  30.1 5.5 %collective-permute-start.9 = (f32[8,8,128]{2,1,0:T(8,128)S(1)}, f32[8,8,128]{2,1,0:T(8,128)S(1)}, u32[]{:S(2)}, u32[]{:S(2)}) collective-permute-start(f32[8,8,128]{2,1,0:T(8,128)S(1)} %get-tuple-element.76), channel_id=1, source_target_pairs={{0,1},{2,3},{4,5},{6,7},{1,0},{3,2},{5,4},{7,6},{8,9},{10,11},{12,... | collective-permute-start | bytes 98312 | tf_op jit(solution)/shard_map/ppermute | solution.py:769
  30.1 3.7 %collective-permute-start.10 = (f32[3,8,128]{2,1,0:T(8,128)S(1)}, f32[3,8,128]{2,1,0:T(8,128)S(1)}, u32[]{:S(2)}, u32[]{:S(2)}) collective-permute-start(f32[3,8,128]{2,1,0:T(8,128)S(1)} %get-tuple-element.77), channel_id=1, source_target_pairs={{0,2},{1,3},{4,6},{5,7},{2,0},{3,1},{6,4},{7,5},{8,10},{9,11},{12,... | collective-permute-start | bytes 36872 | tf_op jit(solution)/shard_map/ppermute | solution.py:776
  30.1 5.5 %collective-permute-start.11 = (f32[3,8,128]{2,1,0:T(8,128)S(1)}, f32[3,8,128]{2,1,0:T(8,128)S(1)}, u32[]{:S(2)}, u32[]{:S(2)}) collective-permute-start(f32[3,8,128]{2,1,0:T(8,128)S(1)} %get-tuple-element.77), channel_id=1, source_target_pairs={{0,6},{1,7},{4,2},{5,3},{6,0},{7,1},{2,4},{3,5},{8,14},{9,15},{12,... | collective-permute-start | bytes 36872 | tf_op jit(solution)/shard_map/ppermute | solution.py:776

commit v17 on v15

--- a/solution.py
+++ b/solution.py
@@ -355,26 +355,21 @@
     return out
 
 
-def pack_own_kernel(
-    rows, state, previous, feed, kill, coarse, first, second, spread, main, held, copies, sem
-):
+def spread_kernel(rows, state, feed, kill, coarse, out):
+    inputs = (state, None, feed, kill)
+    fields = [jnp.stack([plane(inputs[j], f, y, rows) for y in range(rows)]) for j, f in ((0, 0), (0, 1), (2, 0), (3, 0))]
+    write_spread(fields, coarse, out)
+
+
+def pack_own_kernel(rows, state, previous, feed, kill, coarse, first, second, main, held):
     inputs = (state, previous, feed, kill)
-
-    def field(i):
-        j, f = SOURCES[i]
-        return jnp.stack([plane(inputs[j], f, y, rows) for y in range(rows)])
-
-    fields = {i: field(i) for i in (0, 1, 4, 5)}
-    write_spread([fields[i] for i in (0, 1, 4, 5)], coarse, copies)
-    copy = pltpu.make_async_copy(copies, spread, sem)
-    copy.start()
-    for i in range(6):
-        value = fields[i] if i in fields else field(i)
-        main[i] = value
-        held[i * rows : (i + 1) * rows] = value
+    for i, (j, f) in enumerate(SOURCES):
+        for y in range(rows):
+            value = plane(inputs[j], f, y, rows)
+            main[i, y] = value
+            held[i * rows + y] = value
     held[6 * rows : 6 * rows + 2 * OWN + 1] = coarse[...]
     pack_edges(held, is_even("gx"), first, second)
-    copy.wait()
 
 
 def pack_corner_kernel(y_first, y_second, first, second, held):
@@ -639,7 +634,7 @@
 
 
 def level1_kernel(
-    own, first, second, edge_a, edge_b, fields2, coef1, gain, packet, to_first, to_second, to_far, keep, y1, d1
+    own, first, second, edge_a, edge_b, fields2, coef1, gain, packet, to_first, to_second, to_far_a, to_far_b, keep, y1, d1
 ):
     b1, x1 = keep.at[0], keep.at[1]
     even = is_even("gy")
@@ -660,10 +655,13 @@
     for t, (c, other, spread) in enumerate(packed_terms(x1, 1 + OWN, OWN, 1)):
         res = b1[t, here] - coef1[2, t, here] * c + coef1[1, t, here] * other + spread
         values.append(restrict_12([res[j : j + 1] for j in range(OWN)]))
-        to_far[1 + t : 2 + t] = fields2[t, 1:2]
+        for ref in (to_far_a, to_far_b):
+            ref[1 + t : 2 + t] = fields2[t, 1:2]
     value = jnp.where((sub_of() & 2) == 0, values[0], values[1])
-    for ref in (packet, to_first, to_second, to_far):
+    for ref in (packet, to_first, to_second, to_far_a, to_far_b):
         ref[0:1] = value
+    for ref in (to_far_a, to_far_b):
+        ref[3:] = jnp.broadcast_to(value, (ref.shape[0] - 3, Z, X))
     to_first[1:] = edge_a[...]
     to_second[1:] = edge_b[...]
 
@@ -798,17 +796,19 @@
     y_packets = exchange(first, second, "gy")
 
     tiles = tiles_for(6 * rows + 2 * OWN + 1)
-    spread_shape = (across * count, Z // 2, X)
-    first, second, spread, main = call(
+    state, _, feed, kill = inputs
+    (spread,) = call(
+        functools.partial(spread_kernel, rows), [(across * count, 6, X)], [], state, feed, kill, coarse
+    )
+    spread = lax.all_to_all(spread, ("gx", "gy"), 0, 0, tiled=True)
+    first, second, main = call(
         functools.partial(pack_own_kernel, rows),
-        [(tiles, Z, X), (tiles, Z, X), spread_shape, (6, rows, Z, X)],
-        [(PER * tiles, Z, X), spread_shape, pltpu.SemaphoreType.DMA],
+        [(tiles, Z, X), (tiles, Z, X), (6, rows, Z, X)],
+        [(PER * tiles, Z, X)],
         *inputs,
         coarse,
-        outs=[pltpu.VMEM, pltpu.VMEM, pltpu.HBM, pltpu.VMEM],
     )
     own_x = exchange(first, second, "gx")
-    spread = lax.all_to_all(spread, ("gx", "gy"), 0, 0, tiled=True)
     tiles = tiles_for(2 * PACKET)
     corner_x = exchange(
         *call(pack_corner_kernel, [(tiles, Z, X), (tiles, Z, X)], [(PER * tiles, Z, X)], *y_packets), "gx"
@@ -874,9 +874,9 @@
 
     one, two, up = (2, SIZE1, Z, X), (2, SIZE2, Z, X), (2, SIZE_UP, Z, X)
     near = (1 + EDGE_TILES, Z, X)
-    packet, first, second, to_far, keep1 = call(
+    packet, first, second, far_a, far_b, keep1 = call(
         level1_kernel,
-        [(1, Z, X), near, near, (3, Z, X), (2, *one)],
+        [(1, Z, X), near, near, (near[0] + 2, Z, X), (near[0] + 1, Z, X), (2, *one)],
         [one, one],
         own,
         *b_packets,
@@ -886,7 +886,7 @@
         coef1,
         gain,
     )
-    far = (swap_far(to_far, "gy", 1), swap_far(to_far, "gy", -1))
+    far = (swap_far(far_a, "gy", 1), swap_far(far_b, "gy", -1))
     near = exchange(first, second, "gy")
 
     (out,) = call(

time: 38.4 us -> 44.5 us (1.16)
  waiting for transfers between devices: 10.3 us -> 16.6 us
  starting transfers between devices: 20.2 us -> 19.6 us
    ppermute x10, waiting for transfers between devices: 6.25 us -> 16.6 us  [swap(): return lax.ppermute(value, axis, pairs + [(j, i) for i, j in pairs])]
    all_to_all x1, starting transfers between devices: 2.57 us -> 7.3 us  [body(): spread = lax.all_to_all(spread, ('gx', 'gy'), 0, 0, tiled=True)]
    ppermute x10, starting transfers between devices: 14.9 us -> 11.7 us  [swap(): return lax.ppermute(value, axis, pairs + [(j, i) for i, j in pairs])]
    ppermute x2, waiting for transfers between devices: 2.77 us -> 0.01 us  [swap_far(): return lax.ppermute(value, axis, pairs + [(j, i) for i, j in pairs])]
    ppermute x2, starting transfers between devices: 2.73 us -> 0.59 us  [swap_far(): return lax.ppermute(value, axis, pairs + [(j, i) for i, j in pairs])]
    all_to_all x1, waiting for transfers between devices: 1.23 us -> 0.01 us  [body(): spread = lax.all_to_all(spread, ('gx', 'gy'), 0, 0, tiled=True)]
    pallas_call x10 -> x11, Pallas kernels: 7.65 us -> 7.94 us  [call(): pl.pallas_call(kernel, out_shape=out, in_specs=[pl.BlockSpec(memory_space...]
  transfers between devices with their start and end apart: 13 -> 13, of which waited for: 7 -> 5; matrix products, arithmetic and copies ran while one was open for 0% -> 0% of each run, Pallas kernels for 8% -> 5%
where the time goes in v17:
time: 44.5 us; the launch traced here: 44.3 us
  starting transfers between devices  19.6 us (44%)
  waiting for transfers between devices  16.6 us (37%)
  Pallas kernels  7.94 us (18%)
    ppermute x10, waiting for transfers between devices, swap(): return lax.ppermute(value, axis, pairs + [(j, i) for i, j in pairs])  16.6 us
    ppermute x10, starting transfers between devices, swap(): return lax.ppermute(value, axis, pairs + [(j, i) for i, j in pairs])  11.7 us
    pallas_call x11, Pallas kernels, call(): pl.pallas_call(kernel, out_shape=out, in_specs=[pl.BlockSpec(memory_space...  7.94 us
    all_to_all x1, starting transfers between devices, body(): spread = lax.all_to_all(spread, ('gx', 'gy'), 0, 0, tiled=True)  7.3 us
  transfers between devices with their start and end apart: 13, of which 5 were waited for; matrix products, arithmetic and copies ran while one was open for 0% of the time, Pallas kernels for 5%

profile of v17, /device:TPU:0, one launch (start us, length us, event | category | flops | bytes accessed | tf_op | source)
XLA Modules:
  0.0 44.3 jit_solution(2444577071243867103)
XLA Ops:
  0.0 1.3 %shard_map.46 = (f32[27,8,128]{2,1,0:T(8,128)S(1)}, f32[27,8,128]{2,1,0:T(8,128)S(1)}, f32[9,8,128]{2,1,0:T(8,128)S(1)}, f32[256,128]{1,0:T(8,128)S(1)}, f32[256...) custom-call(f32[256,128]{1,0:T(8,128)} %bitcast.5, f32[256,128]{1,0:T(8,128)} %bitcast.6, ...), custom_call_target="tpu_custom_call" | custom-call | tf_op jit(solution)/shard_map/pallas_call | solution.py:749
  1.3 0.9 %shard_map.51 = f32[32,6,128]{2,1,0:T(8,128)} custom-call(f32[256,128]{1,0:T(8,128)S(1)} %get-tuple-element.43.state, f32[128,128]{1,0:T(8,128)S(1)} %get-tuple-element.45.feed, f32[128,128]{1,0:T(8,128)S(1)} %get-tuple-element.46.kill, f32[9,8,128]{2,1,0:T(8,128)S(1)} %get-tuple-element.47.coarse), custom_call_target="tpu_custom_call" | custom-call | tf_op jit(solution)/shard_map/pallas_call | solution.py:749
  2.2 7.3 %all-to-all-start = ((f32[32,6,128]{2,1,0:T(8,128)}), f32[32,6,128]{2,1,0:T(8,128)S(1)}, u32[]{:S(2)}, u32[]{:S(2)}) async-start(f32[32,6,128]{2,1,0:T(8,128)} %shard_map.51), calls=%async_computation | async-start | bytes 262144 | tf_op jit(solution)/shard_map/all_to_all | solution.py:803
  9.5 4.6 %collective-permute-start = (f32[27,8,128]{2,1,0:T(8,128)S(1)}, f32[27,8,128]{2,1,0:T(8,128)S(1)}, u32[]{:S(2)}, u32[]{:S(2)}) collective-permute-start(f32[27,8,128]{2,1,0:T(8,128)S(1)} %get-tuple-element.49), channel_id=1, source_target_pairs={{0,7},{2,1},{4,3},{6,5},{7,0},{1,2},{3,4},{5,6},{8,15},{10,9},{12,... | collective-permute-start | bytes 331784 | tf_op jit(solution)/shard_map/ppermute | solution.py:763
  14.2 0.3 shard_map.47
  14.4 1.0 %collective-permute-start.2 = (f32[35,8,128]{2,1,0:T(8,128)S(1)}, f32[35,8,128]{2,1,0:T(8,128)S(1)}, u32[]{:S(2)}, u32[]{:S(2)}) collective-permute-start(f32[35,8,128]{2,1,0:T(8,128)S(1)} %get-tuple-element.51), channel_id=1, source_target_pairs={{0,24},{16,8},{24,0},{8,16},{1,25},{17,9},{25,1},{9,17},{2,26},{18... | collective-permute-start | bytes 430088 | tf_op jit(solution)/shard_map/ppermute | solution.py:763
  15.5 0.6 %collective-permute-start.3 = (f32[35,8,128]{2,1,0:T(8,128)S(1)}, f32[35,8,128]{2,1,0:T(8,128)S(1)}, u32[]{:S(2)}, u32[]{:S(2)}) collective-permute-start(f32[35,8,128]{2,1,0:T(8,128)S(1)} %get-tuple-element.52), channel_id=1, source_target_pairs={{0,8},{16,24},{8,0},{24,16},{1,9},{17,25},{9,1},{25,17},{2,10},{18... | collective-permute-start | bytes 430088 | tf_op jit(solution)/shard_map/ppermute | solution.py:763
  16.1 3.6 %collective-permute-done.y_first = f32[27,8,128]{2,1,0:T(8,128)S(1)} collective-permute-done((f32[27,8,128]{2,1,0:T(8,128)S(1)}, f32[27,8,128]{2,1,0:T(8,128)S(1)}, u32[]{:S(2)}, u32[]{:S(2)}) %collective-permute-start) | collective-permute-done | bytes 110624 | tf_op jit(solution)/shard_map/ppermute | solution.py:763
  19.7 1.8 %collective-permute-done.1.y_second = f32[27,8,128]{2,1,0:T(8,128)S(1)} collective-permute-done((f32[27,8,128]{2,1,0:T(8,128)S(1)}, f32[27,8,128]{2,1,0:T(8,128)S(1)}, u32[]{:S(2)}, u32[]{:S(2)}) %collective-permute-start.1) | collective-permute-done | bytes 110624 | tf_op jit(solution)/shard_map/ppermute | solution.py:763
  21.7 0.6 %collective-permute-start.4 = (f32[18,8,128]{2,1,0:T(8,128)S(1)}, f32[18,8,128]{2,1,0:T(8,128)S(1)}, u32[]{:S(2)}, u32[]{:S(2)}) collective-permute-start(f32[18,8,128]{2,1,0:T(8,128)S(1)} %get-tuple-element.53), channel_id=1, source_target_pairs={{0,24},{16,8},{24,0},{8,16},{1,25},{17,9},{25,1},{9,17},{2,26},{18... | collective-permute-start | bytes 221192 | tf_op jit(solution)/shard_map/ppermute | solution.py:763
  22.2 1.0 %collective-permute-start.5 = (f32[18,8,128]{2,1,0:T(8,128)S(1)}, f32[18,8,128]{2,1,0:T(8,128)S(1)}, u32[]{:S(2)}, u32[]{:S(2)}) collective-permute-start(f32[18,8,128]{2,1,0:T(8,128)S(1)} %get-tuple-element.54), channel_id=1, source_target_pairs={{0,8},{16,24},{8,0},{24,16},{1,9},{17,25},{9,1},{25,17},{2,10},{18... | collective-permute-start | bytes 221192 | tf_op jit(solution)/shard_map/ppermute | solution.py:763
  23.2 0.9 %shard_map.49 = (f32[6,2,14,8,128]{4,3,2,1,0:T(8,128)S(1)}, f32[2,2,4,8,128]{4,3,2,1,0:T(8,128)S(1)}, f32[2,2,12,8,128]{4,3,2,1,0:T(8,128)S(1)}, f32[2,2,10,8,12...) custom-call(f32[6,16,8,128]{3,2,1,0:T(8,128)S(1)} %get-tuple-element.48.main, ...), custom_call_target="tpu_custom_call" | custom-call | tf_op jit(solution)/shard_map/pallas_call | solution.py:749
  24.1 2.1 %collective-permute-done.4.corner_a = f32[18,8,128]{2,1,0:T(8,128)S(1)} collective-permute-done((f32[18,8,128]{2,1,0:T(8,128)S(1)}, f32[18,8,128]{2,1,0:T(8,128)S(1)}, u32[]{:S(2)}, u32[]{:S(2)}) %collective-permute-start.4) | collective-permute-done | bytes 73760 | tf_op jit(solution)/shard_map/ppermute | solution.py:763
  26.3 0.8 %shard_map.50 = (f32[6,2,8,8,128]{4,3,2,1,0:T(8,128)S(1)}, f32[2,2,4,8,128]{4,3,2,1,0:T(8,128)S(1)}, f32[2,2,6,8,128]{4,3,2,1,0:T(8,128)S(1)}, f32[4,2,4,8,128]{4,3,2,1,0:T(8,128)S(1)}, f32[3,2,7,8,128]{4,3,2,1,0:T(8,128)S(1)}) custom-call(f32[6,16,8,128]{3,2,1,0:T(8,128)S(1)} %get-tuple-element.48.main, f32[27,8,128]{2,1,0:T(8,128)S(1)} %collective-permute-done.y_first, ...), custom_call_target="tpu_custom_call" | custom-call | tf_op jit(solution)/shard_map/pallas_call | solution.py:749
  27.0 0.2 shard_map.52
  27.2 0.9 %collective-permute-start.6 = (f32[7,8,128]{2,1,0:T(8,128)S(1)}, f32[7,8,128]{2,1,0:T(8,128)S(1)}, u32[]{:S(2)}, u32[]{:S(2)}) collective-permute-start(f32[7,8,128]{2,1,0:T(8,128)S(1)} %get-tuple-element.64), channel_id=1, source_target_pairs={{0,7},{2,1},{4,3},{6,5},{7,0},{1,2},{3,4},{5,6},{8,15},{10,9},{12,... | collective-permute-start | bytes 86024 | tf_op jit(solution)/shard_map/ppermute | solution.py:763
  28.2 0.2 shard_map.54
  28.4 5.5 %collective-permute-done.6.first = f32[7,8,128]{2,1,0:T(8,128)S(1)} collective-permute-done((f32[7,8,128]{2,1,0:T(8,128)S(1)}, f32[7,8,128]{2,1,0:T(8,128)S(1)}, u32[]{:S(2)}, u32[]{:S(2)}) %collective-permute-start.6) | collective-permute-done | bytes 28704 | tf_op jit(solution)/shard_map/ppermute | solution.py:763
  33.9 0.5 %shard_map.55 = (f32[1,8,128]{2,1,0:T(8,128)S(1)}, f32[8,8,128]{2,1,0:T(8,128)S(1)}, f32[8,8,128]{2,1,0:T(8,128)S(1)}, f32[10,8,128]{2,1,0:T(8,128)S(1)}, f32[9,...) custom-call(f32[2,4,8,128]{3,2,1,0:T(8,128)S(1)} %get-tuple-element.63.own, ...), custom_call_target="tpu_custom_call" | custom-call | tf_op jit(solution)/shard_map/pallas_call | solution.py:749
  34.5 0.5 %collective-permute-start.11 = (f32[9,8,128]{2,1,0:T(8,128)S(1)}, f32[9,8,128]{2,1,0:T(8,128)S(1)}, u32[]{:S(2)}, u32[]{:S(2)}) collective-permute-start(f32[9,8,128]{2,1,0:T(8,128)S(1)} %get-tuple-element.77), channel_id=1, source_target_pairs={{0,6},{1,7},{4,2},{5,3},{6,0},{7,1},{2,4},{3,5},{8,14},{9,15},{12,... | collective-permute-start | bytes 110600 | tf_op jit(solution)/shard_map/ppermute | solution.py:770
  35.1 2.0 %collective-permute-start.8 = (f32[8,8,128]{2,1,0:T(8,128)S(1)}, f32[8,8,128]{2,1,0:T(8,128)S(1)}, u32[]{:S(2)}, u32[]{:S(2)}) collective-permute-start(f32[8,8,128]{2,1,0:T(8,128)S(1)} %get-tuple-element.74), channel_id=1, source_target_pairs={{0,7},{2,1},{4,3},{6,5},{7,0},{1,2},{3,4},{5,6},{8,15},{10,9},{12,... | collective-permute-start | bytes 98312 | tf_op jit(solution)/shard_map/ppermute | solution.py:763
  37.1 0.9 %collective-permute-start.9 = (f32[8,8,128]{2,1,0:T(8,128)S(1)}, f32[8,8,128]{2,1,0:T(8,128)S(1)}, u32[]{:S(2)}, u32[]{:S(2)}) collective-permute-start(f32[8,8,128]{2,1,0:T(8,128)S(1)} %get-tuple-element.75), channel_id=1, source_target_pairs={{0,1},{2,3},{4,5},{6,7},{1,0},{3,2},{5,4},{7,6},{8,9},{10,11},{12,... | collective-permute-start | bytes 98312 | tf_op jit(solution)/shard_map/ppermute | solution.py:763
  38.0 3.7 %collective-permute-done.8.near_a = f32[8,8,128]{2,1,0:T(8,128)S(1)} collective-permute-done((f32[8,8,128]{2,1,0:T(8,128)S(1)}, f32[8,8,128]{2,1,0:T(8,128)S(1)}, u32[]{:S(2)}, u32[]{:S(2)}) %collective-permute-start.8) | collective-permute-done | bytes 32800 | tf_op jit(solution)/shard_map/ppermute | solution.py:763
  41.7 2.6 %shard_map.56 = f32[256,128]{1,0:T(8,128)} custom-call(f32[1,8,128]{2,1,0:T(8,128)S(1)} %get-tuple-element.73.own2, f32[8,8,128]{2,1,0:T(8,128)S(1)} %collective-permute-done.8.near_a, f32[8,8,128]{2,1,0:T(8,128)S(1)} %collective-permute-done.9.near_b, f32[10,8,128]{2,1,0:T(8,128)S(1)} %collective-permute-done.10.far_a, ...), custom_call_target="tpu_custom_call" | custom-call | tf_op jit(solution)/shard_map/pallas_call | solution.py:749
  (13 shorter events, 0.4 us)
Async XLA Ops:
  2.2 24.8 %all-to-all-start = ((f32[32,6,128]{2,1,0:T(8,128)}), f32[32,6,128]{2,1,0:T(8,128)S(1)}, u32[]{:S(2)}, u32[]{:S(2)}) async-start(f32[32,6,128]{2,1,0:T(8,128)} %shard_map.51), calls=%async_computation | async-start | bytes 262144 | tf_op jit(solution)/shard_map/all_to_all | solution.py:803
  9.5 10.2 %collective-permute-start = (f32[27,8,128]{2,1,0:T(8,128)S(1)}, f32[27,8,128]{2,1,0:T(8,128)S(1)}, u32[]{:S(2)}, u32[]{:S(2)}) collective-permute-start(f32[27,8,128]{2,1,0:T(8,128)S(1)} %get-tuple-element.49), channel_id=1, source_target_pairs={{0,7},{2,1},{4,3},{6,5},{7,0},{1,2},{3,4},{5,6},{8,15},{10,9},{12,... | collective-permute-start | bytes 331784 | tf_op jit(solution)/shard_map/ppermute | solution.py:763
  14.2 7.3 %collective-permute-start.1 = (f32[27,8,128]{2,1,0:T(8,128)S(1)}, f32[27,8,128]{2,1,0:T(8,128)S(1)}, u32[]{:S(2)}, u32[]{:S(2)}) collective-permute-start(f32[27,8,128]{2,1,0:T(8,128)S(1)} %get-tuple-element.50), channel_id=1, source_target_pairs={{0,1},{2,3},{4,5},{6,7},{1,0},{3,2},{5,4},{7,6},{8,9},{10,11},{12,... | collective-permute-start | bytes 331784 | tf_op jit(solution)/shard_map/ppermute | solution.py:763
  14.4 8.8 %collective-permute-start.2 = (f32[35,8,128]{2,1,0:T(8,128)S(1)}, f32[35,8,128]{2,1,0:T(8,128)S(1)}, u32[]{:S(2)}, u32[]{:S(2)}) collective-permute-start(f32[35,8,128]{2,1,0:T(8,128)S(1)} %get-tuple-element.51), channel_id=1, source_target_pairs={{0,24},{16,8},{24,0},{8,16},{1,25},{17,9},{25,1},{9,17},{2,26},{18... | collective-permute-start | bytes 430088 | tf_op jit(solution)/shard_map/ppermute | solution.py:763
  15.5 7.8 %collective-permute-start.3 = (f32[35,8,128]{2,1,0:T(8,128)S(1)}, f32[35,8,128]{2,1,0:T(8,128)S(1)}, u32[]{:S(2)}, u32[]{:S(2)}) collective-permute-start(f32[35,8,128]{2,1,0:T(8,128)S(1)} %get-tuple-element.52), channel_id=1, source_target_pairs={{0,8},{16,24},{8,0},{24,16},{1,9},{17,25},{9,1},{25,17},{2,10},{18... | collective-permute-start | bytes 430088 | tf_op jit(solution)/shard_map/ppermute | solution.py:763
  21.7 4.6 %collective-permute-start.4 = (f32[18,8,128]{2,1,0:T(8,128)S(1)}, f32[18,8,128]{2,1,0:T(8,128)S(1)}, u32[]{:S(2)}, u32[]{:S(2)}) collective-permute-start(f32[18,8,128]{2,1,0:T(8,128)S(1)} %get-tuple-element.53), channel_id=1, source_target_pairs={{0,24},{16,8},{24,0},{8,16},{1,25},{17,9},{25,1},{9,17},{2,26},{18... | collective-permute-start | bytes 221192 | tf_op jit(solution)/shard_map/ppermute | solution.py:763
  22.2 4.0 %collective-permute-start.5 = (f32[18,8,128]{2,1,0:T(8,128)S(1)}, f32[18,8,128]{2,1,0:T(8,128)S(1)}, u32[]{:S(2)}, u32[]{:S(2)}) collective-permute-start(f32[18,8,128]{2,1,0:T(8,128)S(1)} %get-tuple-element.54), channel_id=1, source_target_pairs={{0,8},{16,24},{8,0},{24,16},{1,9},{17,25},{9,1},{25,17},{2,10},{18... | collective-permute-start | bytes 221192 | tf_op jit(solution)/shard_map/ppermute | solution.py:763
  27.2 6.7 %collective-permute-start.6 = (f32[7,8,128]{2,1,0:T(8,128)S(1)}, f32[7,8,128]{2,1,0:T(8,128)S(1)}, u32[]{:S(2)}, u32[]{:S(2)}) collective-permute-start(f32[7,8,128]{2,1,0:T(8,128)S(1)} %get-tuple-element.64), channel_id=1, source_target_pairs={{0,7},{2,1},{4,3},{6,5},{7,0},{1,2},{3,4},{5,6},{8,15},{10,9},{12,... | collective-permute-start | bytes 86024 | tf_op jit(solution)/shard_map/ppermute | solution.py:763
  28.1 5.8 %collective-permute-start.7 = (f32[7,8,128]{2,1,0:T(8,128)S(1)}, f32[7,8,128]{2,1,0:T(8,128)S(1)}, u32[]{:S(2)}, u32[]{:S(2)}) collective-permute-start(f32[7,8,128]{2,1,0:T(8,128)S(1)} %get-tuple-element.65), channel_id=1, source_target_pairs={{0,1},{2,3},{4,5},{6,7},{1,0},{3,2},{5,4},{7,6},{8,9},{10,11},{12,... | collective-permute-start | bytes 86024 | tf_op jit(solution)/shard_map/ppermute | solution.py:763
  34.5 7.2 %collective-permute-start.10 = (f32[10,8,128]{2,1,0:T(8,128)S(1)}, f32[10,8,128]{2,1,0:T(8,128)S(1)}, u32[]{:S(2)}, u32[]{:S(2)}) collective-permute-start(f32[10,8,128]{2,1,0:T(8,128)S(1)} %get-tuple-element.76), channel_id=1, source_target_pairs={{0,2},{1,3},{4,6},{5,7},{2,0},{3,1},{6,4},{7,5},{8,10},{9,11},{12,... | collective-permute-start | bytes 122888 | tf_op jit(solution)/shard_map/ppermute | solution.py:770
  34.5 7.1 %collective-permute-start.11 = (f32[9,8,128]{2,1,0:T(8,128)S(1)}, f32[9,8,128]{2,1,0:T(8,128)S(1)}, u32[]{:S(2)}, u32[]{:S(2)}) collective-permute-start(f32[9,8,128]{2,1,0:T(8,128)S(1)} %get-tuple-element.77), channel_id=1, source_target_pairs={{0,6},{1,7},{4,2},{5,3},{6,0},{7,1},{2,4},{3,5},{8,14},{9,15},{12,... | collective-permute-start | bytes 110600 | tf_op jit(solution)/shard_map/ppermute | solution.py:770
  35.1 6.6 %collective-permute-start.8 = (f32[8,8,128]{2,1,0:T(8,128)S(1)}, f32[8,8,128]{2,1,0:T(8,128)S(1)}, u32[]{:S(2)}, u32[]{:S(2)}) collective-permute-start(f32[8,8,128]{2,1,0:T(8,128)S(1)} %get-tuple-element.74), channel_id=1, source_target_pairs={{0,7},{2,1},{4,3},{6,5},{7,0},{1,2},{3,4},{5,6},{8,15},{10,9},{12,... | collective-permute-start | bytes 98312 | tf_op jit(solution)/shard_map/ppermute | solution.py:763
  37.1 4.6 %collective-permute-start.9 = (f32[8,8,128]{2,1,0:T(8,128)S(1)}, f32[8,8,128]{2,1,0:T(8,128)S(1)}, u32[]{:S(2)}, u32[]{:S(2)}) collective-permute-start(f32[8,8,128]{2,1,0:T(8,128)S(1)} %get-tuple-element.75), channel_id=1, source_target_pairs={{0,1},{2,3},{4,5},{6,7},{1,0},{3,2},{5,4},{7,6},{8,9},{10,11},{12,... | collective-permute-start | bytes 98312 | tf_op jit(solution)/shard_map/ppermute | solution.py:763

commit v18 on v17

--- a/solution.py
+++ b/solution.py
@@ -798,7 +798,7 @@
     tiles = tiles_for(6 * rows + 2 * OWN + 1)
     state, _, feed, kill = inputs
     (spread,) = call(
-        functools.partial(spread_kernel, rows), [(across * count, 6, X)], [], state, feed, kill, coarse
+        functools.partial(spread_kernel, rows), [(across * count, 5, X)], [], state, feed, kill, coarse
     )
     spread = lax.all_to_all(spread, ("gx", "gy"), 0, 0, tiled=True)
     first, second, main = call(

time: 44.5 us -> 40.7 us (0.915)
  waiting for transfers between devices: 16.6 us -> 12.9 us
    all_to_all x1, starting transfers between devices: 7.3 us -> 3.31 us  [body(): spread = lax.all_to_all(spread, ('gx', 'gy'), 0, 0, tiled=True)]
    ppermute x10, waiting for transfers between devices: 16.6 us -> 12.9 us  [swap(): return lax.ppermute(value, axis, pairs + [(j, i) for i, j in pairs])]
    ppermute x10, starting transfers between devices: 11.7 us -> 15 us  [swap(): return lax.ppermute(value, axis, pairs + [(j, i) for i, j in pairs])]
    ppermute x2, starting transfers between devices: 0.59 us -> 1.28 us  [swap_far(): return lax.ppermute(value, axis, pairs + [(j, i) for i, j in pairs])]
  transfers between devices with their start and end apart: 13 -> 13, of which waited for: 5 -> 5; matrix products, arithmetic and copies ran while one was open for 0% -> 0% of each run, Pallas kernels for 5% -> 8%
where the time goes in v18:
time: 40.7 us; the launch traced here: 40.6 us
  starting transfers between devices  19.6 us (48%)
  waiting for transfers between devices  12.9 us (32%)
  Pallas kernels  7.94 us (20%)
    ppermute x10, starting transfers between devices, swap(): return lax.ppermute(value, axis, pairs + [(j, i) for i, j in pairs])  15 us
    ppermute x10, waiting for transfers between devices, swap(): return lax.ppermute(value, axis, pairs + [(j, i) for i, j in pairs])  12.9 us
    pallas_call x11, Pallas kernels, call(): pl.pallas_call(kernel, out_shape=out, in_specs=[pl.BlockSpec(memory_space...  7.94 us
    all_to_all x1, starting transfers between devices, body(): spread = lax.all_to_all(spread, ('gx', 'gy'), 0, 0, tiled=True)  3.31 us
    ppermute x2, starting transfers between devices, swap_far(): return lax.ppermute(value, axis, pairs + [(j, i) for i, j in pairs])  1.28 us
  transfers between devices with their start and end apart: 13, of which 5 were waited for; matrix products, arithmetic and copies ran while one was open for 0% of the time, Pallas kernels for 8%

profile of v18, /device:TPU:0, one launch (start us, length us, event | category | flops | bytes accessed | tf_op | source)
XLA Modules:
  0.0 40.6 jit_solution(1884900540558321853)
XLA Ops:
  0.0 1.3 %shard_map.46 = (f32[27,8,128]{2,1,0:T(8,128)S(1)}, f32[27,8,128]{2,1,0:T(8,128)S(1)}, f32[9,8,128]{2,1,0:T(8,128)S(1)}, f32[256,128]{1,0:T(8,128)S(1)}, f32[256...) custom-call(f32[256,128]{1,0:T(8,128)} %bitcast.5, f32[256,128]{1,0:T(8,128)} %bitcast.6, ...), custom_call_target="tpu_custom_call" | custom-call | tf_op jit(solution)/shard_map/pallas_call | solution.py:749
  1.3 6.1 %collective-permute-start = (f32[27,8,128]{2,1,0:T(8,128)S(1)}, f32[27,8,128]{2,1,0:T(8,128)S(1)}, u32[]{:S(2)}, u32[]{:S(2)}) collective-permute-start(f32[27,8,128]{2,1,0:T(8,128)S(1)} %get-tuple-element.49), channel_id=1, source_target_pairs={{0,7},{2,1},{4,3},{6,5},{7,0},{1,2},{3,4},{5,6},{8,15},{10,9},{12,... | collective-permute-start | bytes 331784 | tf_op jit(solution)/shard_map/ppermute | solution.py:763
  7.4 0.9 %shard_map.51 = f32[32,5,128]{2,1,0:T(8,128)} custom-call(f32[256,128]{1,0:T(8,128)S(1)} %get-tuple-element.43.state, f32[128,128]{1,0:T(8,128)S(1)} %get-tuple-element.45.feed, f32[128,128]{1,0:T(8,128)S(1)} %get-tuple-element.46.kill, f32[9,8,128]{2,1,0:T(8,128)S(1)} %get-tuple-element.47.coarse), custom_call_target="tpu_custom_call" | custom-call | tf_op jit(solution)/shard_map/pallas_call | solution.py:749
  8.3 3.3 %all-to-all-start = ((f32[32,5,128]{2,1,0:T(8,128)}), f32[32,5,128]{2,1,0:T(8,128)S(1)}, u32[]{:S(2)}, u32[]{:S(2)}) async-start(f32[32,5,128]{2,1,0:T(8,128)} %shard_map.51), calls=%async_computation | async-start | bytes 262144 | tf_op jit(solution)/shard_map/all_to_all | solution.py:803
  11.6 0.3 shard_map.47
  11.9 1.6 %collective-permute-start.2 = (f32[35,8,128]{2,1,0:T(8,128)S(1)}, f32[35,8,128]{2,1,0:T(8,128)S(1)}, u32[]{:S(2)}, u32[]{:S(2)}) collective-permute-start(f32[35,8,128]{2,1,0:T(8,128)S(1)} %get-tuple-element.51), channel_id=1, source_target_pairs={{0,24},{16,8},{24,0},{8,16},{1,25},{17,9},{25,1},{9,17},{2,26},{18... | collective-permute-start | bytes 430088 | tf_op jit(solution)/shard_map/ppermute | solution.py:763
  13.5 0.4 collective-permute-start.3
  13.9 0.2 shard_map.48
  14.1 0.2 collective-permute-start.4
  14.2 0.5 %collective-permute-start.5 = (f32[18,8,128]{2,1,0:T(8,128)S(1)}, f32[18,8,128]{2,1,0:T(8,128)S(1)}, u32[]{:S(2)}, u32[]{:S(2)}) collective-permute-start(f32[18,8,128]{2,1,0:T(8,128)S(1)} %get-tuple-element.54), channel_id=1, source_target_pairs={{0,8},{16,24},{8,0},{24,16},{1,9},{17,25},{9,1},{25,17},{2,10},{18... | collective-permute-start | bytes 221192 | tf_op jit(solution)/shard_map/ppermute | solution.py:763
  14.7 4.2 %collective-permute-done.2.own_a = f32[35,8,128]{2,1,0:T(8,128)S(1)} collective-permute-done((f32[35,8,128]{2,1,0:T(8,128)S(1)}, f32[35,8,128]{2,1,0:T(8,128)S(1)}, u32[]{:S(2)}, u32[]{:S(2)}) %collective-permute-start.2) | collective-permute-done | bytes 143392 | tf_op jit(solution)/shard_map/ppermute | solution.py:763
  18.9 0.9 %shard_map.49 = (f32[6,2,14,8,128]{4,3,2,1,0:T(8,128)S(1)}, f32[2,2,4,8,128]{4,3,2,1,0:T(8,128)S(1)}, f32[2,2,12,8,128]{4,3,2,1,0:T(8,128)S(1)}, f32[2,2,10,8,12...) custom-call(f32[6,16,8,128]{3,2,1,0:T(8,128)S(1)} %get-tuple-element.48.main, ...), custom_call_target="tpu_custom_call" | custom-call | tf_op jit(solution)/shard_map/pallas_call | solution.py:749
  19.8 0.8 %collective-permute-done.4.corner_a = f32[18,8,128]{2,1,0:T(8,128)S(1)} collective-permute-done((f32[18,8,128]{2,1,0:T(8,128)S(1)}, f32[18,8,128]{2,1,0:T(8,128)S(1)}, u32[]{:S(2)}, u32[]{:S(2)}) %collective-permute-start.4) | collective-permute-done | bytes 73760 | tf_op jit(solution)/shard_map/ppermute | solution.py:763
  20.6 0.8 %shard_map.50 = (f32[6,2,8,8,128]{4,3,2,1,0:T(8,128)S(1)}, f32[2,2,4,8,128]{4,3,2,1,0:T(8,128)S(1)}, f32[2,2,6,8,128]{4,3,2,1,0:T(8,128)S(1)}, f32[4,2,4,8,128]{4,3,2,1,0:T(8,128)S(1)}, f32[3,2,7,8,128]{4,3,2,1,0:T(8,128)S(1)}) custom-call(f32[6,16,8,128]{3,2,1,0:T(8,128)S(1)} %get-tuple-element.48.main, f32[27,8,128]{2,1,0:T(8,128)S(1)} %collective-permute-done.y_first, ...), custom_call_target="tpu_custom_call" | custom-call | tf_op jit(solution)/shard_map/pallas_call | solution.py:749
  21.4 0.2 shard_map.52
  21.6 4.1 %collective-permute-start.6 = (f32[7,8,128]{2,1,0:T(8,128)S(1)}, f32[7,8,128]{2,1,0:T(8,128)S(1)}, u32[]{:S(2)}, u32[]{:S(2)}) collective-permute-start(f32[7,8,128]{2,1,0:T(8,128)S(1)} %get-tuple-element.64), channel_id=1, source_target_pairs={{0,7},{2,1},{4,3},{6,5},{7,0},{1,2},{3,4},{5,6},{8,15},{10,9},{12,... | collective-permute-start | bytes 86024 | tf_op jit(solution)/shard_map/ppermute | solution.py:763
  25.7 0.2 shard_map.54
  26.0 2.2 %collective-permute-done.6.first = f32[7,8,128]{2,1,0:T(8,128)S(1)} collective-permute-done((f32[7,8,128]{2,1,0:T(8,128)S(1)}, f32[7,8,128]{2,1,0:T(8,128)S(1)}, u32[]{:S(2)}, u32[]{:S(2)}) %collective-permute-start.6) | collective-permute-done | bytes 28704 | tf_op jit(solution)/shard_map/ppermute | solution.py:763
  28.2 1.3 %collective-permute-done.7.second = f32[7,8,128]{2,1,0:T(8,128)S(1)} collective-permute-done((f32[7,8,128]{2,1,0:T(8,128)S(1)}, f32[7,8,128]{2,1,0:T(8,128)S(1)}, u32[]{:S(2)}, u32[]{:S(2)}) %collective-permute-start.7) | collective-permute-done | bytes 28704 | tf_op jit(solution)/shard_map/ppermute | solution.py:763
  29.5 0.5 %shard_map.55 = (f32[1,8,128]{2,1,0:T(8,128)S(1)}, f32[8,8,128]{2,1,0:T(8,128)S(1)}, f32[8,8,128]{2,1,0:T(8,128)S(1)}, f32[10,8,128]{2,1,0:T(8,128)S(1)}, f32[9,...) custom-call(f32[2,4,8,128]{3,2,1,0:T(8,128)S(1)} %get-tuple-element.63.own, ...), custom_call_target="tpu_custom_call" | custom-call | tf_op jit(solution)/shard_map/pallas_call | solution.py:749
  30.1 1.2 %collective-permute-start.11 = (f32[9,8,128]{2,1,0:T(8,128)S(1)}, f32[9,8,128]{2,1,0:T(8,128)S(1)}, u32[]{:S(2)}, u32[]{:S(2)}) collective-permute-start(f32[9,8,128]{2,1,0:T(8,128)S(1)} %get-tuple-element.77), channel_id=1, source_target_pairs={{0,6},{1,7},{4,2},{5,3},{6,0},{7,1},{2,4},{3,5},{8,14},{9,15},{12,... | collective-permute-start | bytes 110600 | tf_op jit(solution)/shard_map/ppermute | solution.py:770
  31.3 2.3 %collective-permute-start.8 = (f32[8,8,128]{2,1,0:T(8,128)S(1)}, f32[8,8,128]{2,1,0:T(8,128)S(1)}, u32[]{:S(2)}, u32[]{:S(2)}) collective-permute-start(f32[8,8,128]{2,1,0:T(8,128)S(1)} %get-tuple-element.74), channel_id=1, source_target_pairs={{0,7},{2,1},{4,3},{6,5},{7,0},{1,2},{3,4},{5,6},{8,15},{10,9},{12,... | collective-permute-start | bytes 98312 | tf_op jit(solution)/shard_map/ppermute | solution.py:763
  33.6 4.3 %collective-permute-done.8.near_a = f32[8,8,128]{2,1,0:T(8,128)S(1)} collective-permute-done((f32[8,8,128]{2,1,0:T(8,128)S(1)}, f32[8,8,128]{2,1,0:T(8,128)S(1)}, u32[]{:S(2)}, u32[]{:S(2)}) %collective-permute-start.8) | collective-permute-done | bytes 32800 | tf_op jit(solution)/shard_map/ppermute | solution.py:763
  38.0 2.6 %shard_map.56 = f32[256,128]{1,0:T(8,128)} custom-call(f32[1,8,128]{2,1,0:T(8,128)S(1)} %get-tuple-element.73.own2, f32[8,8,128]{2,1,0:T(8,128)S(1)} %collective-permute-done.8.near_a, f32[8,8,128]{2,1,0:T(8,128)S(1)} %collective-permute-done.9.near_b, f32[10,8,128]{2,1,0:T(8,128)S(1)} %collective-permute-done.10.far_a, ...), custom_call_target="tpu_custom_call" | custom-call | tf_op jit(solution)/shard_map/pallas_call | solution.py:749
  (13 shorter events, 0.2 us)
Async XLA Ops:
  1.3 12.5 %collective-permute-start = (f32[27,8,128]{2,1,0:T(8,128)S(1)}, f32[27,8,128]{2,1,0:T(8,128)S(1)}, u32[]{:S(2)}, u32[]{:S(2)}) collective-permute-start(f32[27,8,128]{2,1,0:T(8,128)S(1)} %get-tuple-element.49), channel_id=1, source_target_pairs={{0,7},{2,1},{4,3},{6,5},{7,0},{1,2},{3,4},{5,6},{8,15},{10,9},{12,... | collective-permute-start | bytes 331784 | tf_op jit(solution)/shard_map/ppermute | solution.py:763
  7.4 6.5 %collective-permute-start.1 = (f32[27,8,128]{2,1,0:T(8,128)S(1)}, f32[27,8,128]{2,1,0:T(8,128)S(1)}, u32[]{:S(2)}, u32[]{:S(2)}) collective-permute-start(f32[27,8,128]{2,1,0:T(8,128)S(1)} %get-tuple-element.50), channel_id=1, source_target_pairs={{0,1},{2,3},{4,5},{6,7},{1,0},{3,2},{5,4},{7,6},{8,9},{10,11},{12,... | collective-permute-start | bytes 331784 | tf_op jit(solution)/shard_map/ppermute | solution.py:763
  8.3 13.1 %all-to-all-start = ((f32[32,5,128]{2,1,0:T(8,128)}), f32[32,5,128]{2,1,0:T(8,128)S(1)}, u32[]{:S(2)}, u32[]{:S(2)}) async-start(f32[32,5,128]{2,1,0:T(8,128)} %shard_map.51), calls=%async_computation | async-start | bytes 262144 | tf_op jit(solution)/shard_map/all_to_all | solution.py:803
  11.9 7.0 %collective-permute-start.2 = (f32[35,8,128]{2,1,0:T(8,128)S(1)}, f32[35,8,128]{2,1,0:T(8,128)S(1)}, u32[]{:S(2)}, u32[]{:S(2)}) collective-permute-start(f32[35,8,128]{2,1,0:T(8,128)S(1)} %get-tuple-element.51), channel_id=1, source_target_pairs={{0,24},{16,8},{24,0},{8,16},{1,25},{17,9},{25,1},{9,17},{2,26},{18... | collective-permute-start | bytes 430088 | tf_op jit(solution)/shard_map/ppermute | solution.py:763
  13.5 5.4 %collective-permute-start.3 = (f32[35,8,128]{2,1,0:T(8,128)S(1)}, f32[35,8,128]{2,1,0:T(8,128)S(1)}, u32[]{:S(2)}, u32[]{:S(2)}) collective-permute-start(f32[35,8,128]{2,1,0:T(8,128)S(1)} %get-tuple-element.52), channel_id=1, source_target_pairs={{0,8},{16,24},{8,0},{24,16},{1,9},{17,25},{9,1},{25,17},{2,10},{18... | collective-permute-start | bytes 430088 | tf_op jit(solution)/shard_map/ppermute | solution.py:763
  14.1 6.6 %collective-permute-start.4 = (f32[18,8,128]{2,1,0:T(8,128)S(1)}, f32[18,8,128]{2,1,0:T(8,128)S(1)}, u32[]{:S(2)}, u32[]{:S(2)}) collective-permute-start(f32[18,8,128]{2,1,0:T(8,128)S(1)} %get-tuple-element.53), channel_id=1, source_target_pairs={{0,24},{16,8},{24,0},{8,16},{1,25},{17,9},{25,1},{9,17},{2,26},{18... | collective-permute-start | bytes 221192 | tf_op jit(solution)/shard_map/ppermute | solution.py:763
  14.2 6.4 %collective-permute-start.5 = (f32[18,8,128]{2,1,0:T(8,128)S(1)}, f32[18,8,128]{2,1,0:T(8,128)S(1)}, u32[]{:S(2)}, u32[]{:S(2)}) collective-permute-start(f32[18,8,128]{2,1,0:T(8,128)S(1)} %get-tuple-element.54), channel_id=1, source_target_pairs={{0,8},{16,24},{8,0},{24,16},{1,9},{17,25},{9,1},{25,17},{2,10},{18... | collective-permute-start | bytes 221192 | tf_op jit(solution)/shard_map/ppermute | solution.py:763
  21.6 6.6 %collective-permute-start.6 = (f32[7,8,128]{2,1,0:T(8,128)S(1)}, f32[7,8,128]{2,1,0:T(8,128)S(1)}, u32[]{:S(2)}, u32[]{:S(2)}) collective-permute-start(f32[7,8,128]{2,1,0:T(8,128)S(1)} %get-tuple-element.64), channel_id=1, source_target_pairs={{0,7},{2,1},{4,3},{6,5},{7,0},{1,2},{3,4},{5,6},{8,15},{10,9},{12,... | collective-permute-start | bytes 86024 | tf_op jit(solution)/shard_map/ppermute | solution.py:763
  25.6 3.9 %collective-permute-start.7 = (f32[7,8,128]{2,1,0:T(8,128)S(1)}, f32[7,8,128]{2,1,0:T(8,128)S(1)}, u32[]{:S(2)}, u32[]{:S(2)}) collective-permute-start(f32[7,8,128]{2,1,0:T(8,128)S(1)} %get-tuple-element.65), channel_id=1, source_target_pairs={{0,1},{2,3},{4,5},{6,7},{1,0},{3,2},{5,4},{7,6},{8,9},{10,11},{12,... | collective-permute-start | bytes 86024 | tf_op jit(solution)/shard_map/ppermute | solution.py:763
  30.1 7.9 %collective-permute-start.10 = (f32[10,8,128]{2,1,0:T(8,128)S(1)}, f32[10,8,128]{2,1,0:T(8,128)S(1)}, u32[]{:S(2)}, u32[]{:S(2)}) collective-permute-start(f32[10,8,128]{2,1,0:T(8,128)S(1)} %get-tuple-element.76), channel_id=1, source_target_pairs={{0,2},{1,3},{4,6},{5,7},{2,0},{3,1},{6,4},{7,5},{8,10},{9,11},{12,... | collective-permute-start | bytes 122888 | tf_op jit(solution)/shard_map/ppermute | solution.py:770
  30.1 7.8 %collective-permute-start.11 = (f32[9,8,128]{2,1,0:T(8,128)S(1)}, f32[9,8,128]{2,1,0:T(8,128)S(1)}, u32[]{:S(2)}, u32[]{:S(2)}) collective-permute-start(f32[9,8,128]{2,1,0:T(8,128)S(1)} %get-tuple-element.77), channel_id=1, source_target_pairs={{0,6},{1,7},{4,2},{5,3},{6,0},{7,1},{2,4},{3,5},{8,14},{9,15},{12,... | collective-permute-start | bytes 110600 | tf_op jit(solution)/shard_map/ppermute | solution.py:770
  31.3 6.6 %collective-permute-start.8 = (f32[8,8,128]{2,1,0:T(8,128)S(1)}, f32[8,8,128]{2,1,0:T(8,128)S(1)}, u32[]{:S(2)}, u32[]{:S(2)}) collective-permute-start(f32[8,8,128]{2,1,0:T(8,128)S(1)} %get-tuple-element.74), channel_id=1, source_target_pairs={{0,7},{2,1},{4,3},{6,5},{7,0},{1,2},{3,4},{5,6},{8,15},{10,9},{12,... | collective-permute-start | bytes 98312 | tf_op jit(solution)/shard_map/ppermute | solution.py:763
  33.6 4.3 %collective-permute-start.9 = (f32[8,8,128]{2,1,0:T(8,128)S(1)}, f32[8,8,128]{2,1,0:T(8,128)S(1)}, u32[]{:S(2)}, u32[]{:S(2)}) collective-permute-start(f32[8,8,128]{2,1,0:T(8,128)S(1)} %get-tuple-element.75), channel_id=1, source_target_pairs={{0,1},{2,3},{4,5},{6,7},{1,0},{3,2},{5,4},{7,6},{8,9},{10,11},{12,... | collective-permute-start | bytes 98312 | tf_op jit(solution)/shard_map/ppermute | solution.py:763

commit v19 on v16

--- a/solution.py
+++ b/solution.py
@@ -643,7 +643,7 @@
 
 
 def level1_kernel(
-    own, first, second, edge_a, edge_b, fields2, coef1, gain, packet, to_first, to_second, to_far, keep, y1, d1
+    own, first, second, edge_a, edge_b, fields2, coef1, gain, packet, to_first, to_second, to_far_a, to_far_b, keep, y1, d1
 ):
     b1, x1 = keep.at[0], keep.at[1]
     even = is_even("gy")
@@ -664,10 +664,13 @@
     for t, (c, other, spread) in enumerate(packed_terms(x1, 1 + OWN, OWN, 1)):
         res = b1[t, here] - coef1[2, t, here] * c + coef1[1, t, here] * other + spread
         values.append(restrict_12([res[j : j + 1] for j in range(OWN)]))
-        to_far[1 + t : 2 + t] = fields2[t, 1:2]
+        for ref in (to_far_a, to_far_b):
+            ref[1 + t : 2 + t] = fields2[t, 1:2]
     value = jnp.where((sub_of() & 2) == 0, values[0], values[1])
-    for ref in (packet, to_first, to_second, to_far):
+    for ref in (packet, to_first, to_second, to_far_a, to_far_b):
         ref[0:1] = value
+    for ref in (to_far_a, to_far_b):
+        ref[3:] = jnp.broadcast_to(value, (ref.shape[0] - 3, Z, X))
     to_first[1:] = edge_a[...]
     to_second[1:] = edge_b[...]
 
@@ -878,9 +881,9 @@
 
     one, two, up = (2, SIZE1, Z, X), (2, SIZE2, Z, X), (2, SIZE_UP, Z, X)
     near = (1 + EDGE_TILES, Z, X)
-    packet, first, second, to_far, keep1 = call(
+    packet, first, second, far_a, far_b, keep1 = call(
         level1_kernel,
-        [(1, Z, X), near, near, (3, Z, X), (2, *one)],
+        [(1, Z, X), near, near, (near[0] + 2, Z, X), (near[0] + 1, Z, X), (2, *one)],
         [one, one],
         own,
         *b_packets,
@@ -890,7 +893,7 @@
         coef1,
         gain,
     )
-    far = (swap_far(to_far, "gy", 1), swap_far(to_far, "gy", -1))
+    far = (swap_far(far_a, "gy", 1), swap_far(far_b, "gy", -1))
     near = exchange(first, second, "gy")
 
     (out,) = call(

time: 38.3 us -> 38 us (level)
  starting transfers between devices: 20.2 us -> 18.4 us
  waiting for transfers between devices: 10.3 us -> 11.7 us
    ppermute x10, waiting for transfers between devices: 6.31 us -> 10.5 us  [swap(): return lax.ppermute(value, axis, pairs + [(j, i) for i, j in pairs])]
    ppermute x2, waiting for transfers between devices: 2.77 us -> 0.01 us  [swap_far(): return lax.ppermute(value, axis, pairs + [(j, i) for i, j in pairs])]
    ppermute x2, starting transfers between devices: 2.73 us -> 1.03 us  [swap_far(): return lax.ppermute(value, axis, pairs + [(j, i) for i, j in pairs])]
  transfers between devices with their start and end apart: 13 -> 13, of which waited for: 7 -> 6; matrix products, arithmetic and copies ran while one was open for 0% -> 0% of each run, Pallas kernels for 8% -> 8%
where the time goes in v19:
time: 38 us; the launch traced here: 37.8 us
  starting transfers between devices  18.4 us (48%)
  waiting for transfers between devices  11.7 us (31%)
  Pallas kernels  7.61 us (20%)
    ppermute x10, starting transfers between devices, swap(): return lax.ppermute(value, axis, pairs + [(j, i) for i, j in pairs])  14.8 us
    ppermute x10, waiting for transfers between devices, swap(): return lax.ppermute(value, axis, pairs + [(j, i) for i, j in pairs])  10.5 us
    pallas_call x10, Pallas kernels, call(): pl.pallas_call(kernel, out_shape=out, in_specs=[pl.BlockSpec(memory_space...  7.61 us
    all_to_all x1, starting transfers between devices, body(): spread = lax.all_to_all(spread, ('gx', 'gy'), 0, 0, tiled=True)  2.57 us
    all_to_all x1, waiting for transfers between devices, body(): spread = lax.all_to_all(spread, ('gx', 'gy'), 0, 0, tiled=True)  1.18 us
    ppermute x2, starting transfers between devices, swap_far(): return lax.ppermute(value, axis, pairs + [(j, i) for i, j in pairs])  1.03 us
  transfers between devices with their start and end apart: 13, of which 6 were waited for; matrix products, arithmetic and copies ran while one was open for 0% of the time, Pallas kernels for 8%

profile of v19, /device:TPU:0, one launch (start us, length us, event | category | flops | bytes accessed | tf_op | source)
XLA Modules:
  0.0 37.8 jit_solution(3385999311830003013)
XLA Ops:
  0.0 1.3 %shard_map.46 = (f32[27,8,128]{2,1,0:T(8,128)S(1)}, f32[27,8,128]{2,1,0:T(8,128)S(1)}, f32[9,8,128]{2,1,0:T(8,128)S(1)}, f32[256,128]{1,0:T(8,128)S(1)}, f32[256...) custom-call(f32[256,128]{1,0:T(8,128)} %bitcast.5, f32[256,128]{1,0:T(8,128)} %bitcast.6, ...), custom_call_target="tpu_custom_call" | custom-call | tf_op jit(solution)/shard_map/pallas_call | solution.py:758
  1.3 6.1 %collective-permute-start = (f32[27,8,128]{2,1,0:T(8,128)S(1)}, f32[27,8,128]{2,1,0:T(8,128)S(1)}, u32[]{:S(2)}, u32[]{:S(2)}) collective-permute-start(f32[27,8,128]{2,1,0:T(8,128)S(1)} %get-tuple-element.50), channel_id=1, source_target_pairs={{0,7},{2,1},{4,3},{6,5},{7,0},{1,2},{3,4},{5,6},{8,15},{10,9},{12,... | collective-permute-start | bytes 331784 | tf_op jit(solution)/shard_map/ppermute | solution.py:772
  7.4 0.9 %shard_map.47 = (f32[35,8,128]{2,1,0:T(8,128)S(1)}, f32[35,8,128]{2,1,0:T(8,128)S(1)}, f32[32,4,128]{2,1,0:T(4,128)}, f32[6,16,8,128]{3,2,1,0:T(8,128)S(1)}) custom-call(f32[256,128]{1,0:T(8,128)S(1)} %get-tuple-element.44.state, f32[256,128]{1,0:T(8,128)S(1)} %get-tuple-element.45.previous, f32[128,128]{1,0:T(8,128)S(1)} %get-tuple-element.46.feed, ...), custom_call_target="tpu_custom_call" | custom-call | tf_op jit(solution)/shard_map/pallas_call | solution.py:758
  8.3 0.7 %collective-permute-start.2 = (f32[35,8,128]{2,1,0:T(8,128)S(1)}, f32[35,8,128]{2,1,0:T(8,128)S(1)}, u32[]{:S(2)}, u32[]{:S(2)}) collective-permute-start(f32[35,8,128]{2,1,0:T(8,128)S(1)} %get-tuple-element.52), channel_id=1, source_target_pairs={{0,24},{16,8},{24,0},{8,16},{1,25},{17,9},{25,1},{9,17},{2,26},{18... | collective-permute-start | bytes 430088 | tf_op jit(solution)/shard_map/ppermute | solution.py:772
  9.0 1.0 %collective-permute-start.3 = (f32[35,8,128]{2,1,0:T(8,128)S(1)}, f32[35,8,128]{2,1,0:T(8,128)S(1)}, u32[]{:S(2)}, u32[]{:S(2)}) collective-permute-start(f32[35,8,128]{2,1,0:T(8,128)S(1)} %get-tuple-element.53), channel_id=1, source_target_pairs={{0,8},{16,24},{8,0},{24,16},{1,9},{17,25},{9,1},{25,17},{2,10},{18... | collective-permute-start | bytes 430088 | tf_op jit(solution)/shard_map/ppermute | solution.py:772
  10.0 2.6 %all-to-all-start = ((f32[32,4,128]{2,1,0:T(4,128)}), f32[32,4,128]{2,1,0:T(4,128)S(1)}, u32[]{:S(2)}, u32[]{:S(2)}) async-start(f32[32,4,128]{2,1,0:T(4,128)} %get-tuple-element.64), calls=%async_computation | async-start | bytes 131072 | tf_op jit(solution)/shard_map/all_to_all | solution.py:818
  12.6 0.3 collective-permute-done.1.y_second
  12.8 0.2 shard_map.48
  13.0 1.2 %collective-permute-start.4 = (f32[18,8,128]{2,1,0:T(8,128)S(1)}, f32[18,8,128]{2,1,0:T(8,128)S(1)}, u32[]{:S(2)}, u32[]{:S(2)}) collective-permute-start(f32[18,8,128]{2,1,0:T(8,128)S(1)} %get-tuple-element.54), channel_id=1, source_target_pairs={{0,24},{16,8},{24,0},{8,16},{1,25},{17,9},{25,1},{9,17},{2,26},{18... | collective-permute-start | bytes 221192 | tf_op jit(solution)/shard_map/ppermute | solution.py:772
  14.2 0.5 %collective-permute-start.5 = (f32[18,8,128]{2,1,0:T(8,128)S(1)}, f32[18,8,128]{2,1,0:T(8,128)S(1)}, u32[]{:S(2)}, u32[]{:S(2)}) collective-permute-start(f32[18,8,128]{2,1,0:T(8,128)S(1)} %get-tuple-element.55), channel_id=1, source_target_pairs={{0,8},{16,24},{8,0},{24,16},{1,9},{17,25},{9,1},{25,17},{2,10},{18... | collective-permute-start | bytes 221192 | tf_op jit(solution)/shard_map/ppermute | solution.py:772
  14.7 0.9 %shard_map.49 = (f32[6,2,14,8,128]{4,3,2,1,0:T(8,128)S(1)}, f32[2,2,4,8,128]{4,3,2,1,0:T(8,128)S(1)}, f32[2,2,12,8,128]{4,3,2,1,0:T(8,128)S(1)}, f32[2,2,10,8,12...) custom-call(f32[6,16,8,128]{3,2,1,0:T(8,128)S(1)} %get-tuple-element.49.main, ...), custom_call_target="tpu_custom_call" | custom-call | tf_op jit(solution)/shard_map/pallas_call | solution.py:758
  15.6 2.3 %collective-permute-done.4.corner_a = f32[18,8,128]{2,1,0:T(8,128)S(1)} collective-permute-done((f32[18,8,128]{2,1,0:T(8,128)S(1)}, f32[18,8,128]{2,1,0:T(8,128)S(1)}, u32[]{:S(2)}, u32[]{:S(2)}) %collective-permute-start.4) | collective-permute-done | bytes 73760 | tf_op jit(solution)/shard_map/ppermute | solution.py:772
  17.9 0.8 %shard_map.50 = (f32[6,2,8,8,128]{4,3,2,1,0:T(8,128)S(1)}, f32[2,2,4,8,128]{4,3,2,1,0:T(8,128)S(1)}, f32[2,2,6,8,128]{4,3,2,1,0:T(8,128)S(1)}, f32[4,2,4,8,128]{4,3,2,1,0:T(8,128)S(1)}, f32[3,2,7,8,128]{4,3,2,1,0:T(8,128)S(1)}) custom-call(f32[6,16,8,128]{3,2,1,0:T(8,128)S(1)} %get-tuple-element.49.main, f32[27,8,128]{2,1,0:T(8,128)S(1)} %collective-permute-done.y_first, ...), custom_call_target="tpu_custom_call" | custom-call | tf_op jit(solution)/shard_map/pallas_call | solution.py:758
  18.6 1.2 %all-to-all-done.spread = f32[32,4,128]{2,1,0:T(4,128)S(1)} async-done(((f32[32,4,128]{2,1,0:T(4,128)}), f32[32,4,128]{2,1,0:T(4,128)S(1)}, u32[]{:S(2)}, u32[]{:S(2)}) %all-to-all-start) | async-done | bytes 65568 | tf_op jit(solution)/shard_map/all_to_all | solution.py:818
  19.8 0.2 shard_map.51
  20.0 2.9 %collective-permute-start.6 = (f32[7,8,128]{2,1,0:T(8,128)S(1)}, f32[7,8,128]{2,1,0:T(8,128)S(1)}, u32[]{:S(2)}, u32[]{:S(2)}) collective-permute-start(f32[7,8,128]{2,1,0:T(8,128)S(1)} %get-tuple-element.66), channel_id=1, source_target_pairs={{0,7},{2,1},{4,3},{6,5},{7,0},{1,2},{3,4},{5,6},{8,15},{10,9},{12,... | collective-permute-start | bytes 86024 | tf_op jit(solution)/shard_map/ppermute | solution.py:772
  23.0 0.2 shard_map.53
  23.2 3.4 %collective-permute-done.6.first = f32[7,8,128]{2,1,0:T(8,128)S(1)} collective-permute-done((f32[7,8,128]{2,1,0:T(8,128)S(1)}, f32[7,8,128]{2,1,0:T(8,128)S(1)}, u32[]{:S(2)}, u32[]{:S(2)}) %collective-permute-start.6) | collective-permute-done | bytes 28704 | tf_op jit(solution)/shard_map/ppermute | solution.py:772
  26.6 0.3 collective-permute-done.7.second
  26.9 0.5 %shard_map.54 = (f32[1,8,128]{2,1,0:T(8,128)S(1)}, f32[8,8,128]{2,1,0:T(8,128)S(1)}, f32[8,8,128]{2,1,0:T(8,128)S(1)}, f32[10,8,128]{2,1,0:T(8,128)S(1)}, f32[9,...) custom-call(f32[2,4,8,128]{3,2,1,0:T(8,128)S(1)} %get-tuple-element.65.own, ...), custom_call_target="tpu_custom_call" | custom-call | tf_op jit(solution)/shard_map/pallas_call | solution.py:758
  27.5 1.0 %collective-permute-start.11 = (f32[9,8,128]{2,1,0:T(8,128)S(1)}, f32[9,8,128]{2,1,0:T(8,128)S(1)}, u32[]{:S(2)}, u32[]{:S(2)}) collective-permute-start(f32[9,8,128]{2,1,0:T(8,128)S(1)} %get-tuple-element.79), channel_id=1, source_target_pairs={{0,6},{1,7},{4,2},{5,3},{6,0},{7,1},{2,4},{3,5},{8,14},{9,15},{12,... | collective-permute-start | bytes 110600 | tf_op jit(solution)/shard_map/ppermute | solution.py:779
  28.5 2.4 %collective-permute-start.8 = (f32[8,8,128]{2,1,0:T(8,128)S(1)}, f32[8,8,128]{2,1,0:T(8,128)S(1)}, u32[]{:S(2)}, u32[]{:S(2)}) collective-permute-start(f32[8,8,128]{2,1,0:T(8,128)S(1)} %get-tuple-element.76), channel_id=1, source_target_pairs={{0,7},{2,1},{4,3},{6,5},{7,0},{1,2},{3,4},{5,6},{8,15},{10,9},{12,... | collective-permute-start | bytes 98312 | tf_op jit(solution)/shard_map/ppermute | solution.py:772
  31.0 4.2 %collective-permute-done.8.near_a = f32[8,8,128]{2,1,0:T(8,128)S(1)} collective-permute-done((f32[8,8,128]{2,1,0:T(8,128)S(1)}, f32[8,8,128]{2,1,0:T(8,128)S(1)}, u32[]{:S(2)}, u32[]{:S(2)}) %collective-permute-start.8) | collective-permute-done | bytes 32800 | tf_op jit(solution)/shard_map/ppermute | solution.py:772
  35.2 2.6 %shard_map.55 = f32[256,128]{1,0:T(8,128)} custom-call(f32[1,8,128]{2,1,0:T(8,128)S(1)} %get-tuple-element.75.own2, f32[8,8,128]{2,1,0:T(8,128)S(1)} %collective-permute-done.8.near_a, f32[8,8,128]{2,1,0:T(8,128)S(1)} %collective-permute-done.9.near_b, f32[10,8,128]{2,1,0:T(8,128)S(1)} %collective-permute-done.10.far_a, ...), custom_call_target="tpu_custom_call" | custom-call | tf_op jit(solution)/shard_map/pallas_call | solution.py:758
  (12 shorter events, 0.2 us)
Async XLA Ops:
  1.3 11.2 %collective-permute-start = (f32[27,8,128]{2,1,0:T(8,128)S(1)}, f32[27,8,128]{2,1,0:T(8,128)S(1)}, u32[]{:S(2)}, u32[]{:S(2)}) collective-permute-start(f32[27,8,128]{2,1,0:T(8,128)S(1)} %get-tuple-element.50), channel_id=1, source_target_pairs={{0,7},{2,1},{4,3},{6,5},{7,0},{1,2},{3,4},{5,6},{8,15},{10,9},{12,... | collective-permute-start | bytes 331784 | tf_op jit(solution)/shard_map/ppermute | solution.py:772
  7.4 5.4 %collective-permute-start.1 = (f32[27,8,128]{2,1,0:T(8,128)S(1)}, f32[27,8,128]{2,1,0:T(8,128)S(1)}, u32[]{:S(2)}, u32[]{:S(2)}) collective-permute-start(f32[27,8,128]{2,1,0:T(8,128)S(1)} %get-tuple-element.51), channel_id=1, source_target_pairs={{0,1},{2,3},{4,5},{6,7},{1,0},{3,2},{5,4},{7,6},{8,9},{10,11},{12,... | collective-permute-start | bytes 331784 | tf_op jit(solution)/shard_map/ppermute | solution.py:772
  8.3 6.4 %collective-permute-start.2 = (f32[35,8,128]{2,1,0:T(8,128)S(1)}, f32[35,8,128]{2,1,0:T(8,128)S(1)}, u32[]{:S(2)}, u32[]{:S(2)}) collective-permute-start(f32[35,8,128]{2,1,0:T(8,128)S(1)} %get-tuple-element.52), channel_id=1, source_target_pairs={{0,24},{16,8},{24,0},{8,16},{1,25},{17,9},{25,1},{9,17},{2,26},{18... | collective-permute-start | bytes 430088 | tf_op jit(solution)/shard_map/ppermute | solution.py:772
  9.0 5.7 %collective-permute-start.3 = (f32[35,8,128]{2,1,0:T(8,128)S(1)}, f32[35,8,128]{2,1,0:T(8,128)S(1)}, u32[]{:S(2)}, u32[]{:S(2)}) collective-permute-start(f32[35,8,128]{2,1,0:T(8,128)S(1)} %get-tuple-element.53), channel_id=1, source_target_pairs={{0,8},{16,24},{8,0},{24,16},{1,9},{17,25},{9,1},{25,17},{2,10},{18... | collective-permute-start | bytes 430088 | tf_op jit(solution)/shard_map/ppermute | solution.py:772
  10.0 9.9 %all-to-all-start = ((f32[32,4,128]{2,1,0:T(4,128)}), f32[32,4,128]{2,1,0:T(4,128)S(1)}, u32[]{:S(2)}, u32[]{:S(2)}) async-start(f32[32,4,128]{2,1,0:T(4,128)} %get-tuple-element.64), calls=%async_computation | async-start | bytes 131072 | tf_op jit(solution)/shard_map/all_to_all | solution.py:818
  13.0 4.8 %collective-permute-start.4 = (f32[18,8,128]{2,1,0:T(8,128)S(1)}, f32[18,8,128]{2,1,0:T(8,128)S(1)}, u32[]{:S(2)}, u32[]{:S(2)}) collective-permute-start(f32[18,8,128]{2,1,0:T(8,128)S(1)} %get-tuple-element.54), channel_id=1, source_target_pairs={{0,24},{16,8},{24,0},{8,16},{1,25},{17,9},{25,1},{9,17},{2,26},{18... | collective-permute-start | bytes 221192 | tf_op jit(solution)/shard_map/ppermute | solution.py:772
  14.2 3.7 %collective-permute-start.5 = (f32[18,8,128]{2,1,0:T(8,128)S(1)}, f32[18,8,128]{2,1,0:T(8,128)S(1)}, u32[]{:S(2)}, u32[]{:S(2)}) collective-permute-start(f32[18,8,128]{2,1,0:T(8,128)S(1)} %get-tuple-element.55), channel_id=1, source_target_pairs={{0,8},{16,24},{8,0},{24,16},{1,9},{17,25},{9,1},{25,17},{2,10},{18... | collective-permute-start | bytes 221192 | tf_op jit(solution)/shard_map/ppermute | solution.py:772
  20.0 6.6 %collective-permute-start.6 = (f32[7,8,128]{2,1,0:T(8,128)S(1)}, f32[7,8,128]{2,1,0:T(8,128)S(1)}, u32[]{:S(2)}, u32[]{:S(2)}) collective-permute-start(f32[7,8,128]{2,1,0:T(8,128)S(1)} %get-tuple-element.66), channel_id=1, source_target_pairs={{0,7},{2,1},{4,3},{6,5},{7,0},{1,2},{3,4},{5,6},{8,15},{10,9},{12,... | collective-permute-start | bytes 86024 | tf_op jit(solution)/shard_map/ppermute | solution.py:772
  22.9 4.0 %collective-permute-start.7 = (f32[7,8,128]{2,1,0:T(8,128)S(1)}, f32[7,8,128]{2,1,0:T(8,128)S(1)}, u32[]{:S(2)}, u32[]{:S(2)}) collective-permute-start(f32[7,8,128]{2,1,0:T(8,128)S(1)} %get-tuple-element.67), channel_id=1, source_target_pairs={{0,1},{2,3},{4,5},{6,7},{1,0},{3,2},{5,4},{7,6},{8,9},{10,11},{12,... | collective-permute-start | bytes 86024 | tf_op jit(solution)/shard_map/ppermute | solution.py:772
  27.4 7.8 %collective-permute-start.10 = (f32[10,8,128]{2,1,0:T(8,128)S(1)}, f32[10,8,128]{2,1,0:T(8,128)S(1)}, u32[]{:S(2)}, u32[]{:S(2)}) collective-permute-start(f32[10,8,128]{2,1,0:T(8,128)S(1)} %get-tuple-element.78), channel_id=1, source_target_pairs={{0,2},{1,3},{4,6},{5,7},{2,0},{3,1},{6,4},{7,5},{8,10},{9,11},{12,... | collective-permute-start | bytes 122888 | tf_op jit(solution)/shard_map/ppermute | solution.py:779
  27.5 7.7 %collective-permute-start.11 = (f32[9,8,128]{2,1,0:T(8,128)S(1)}, f32[9,8,128]{2,1,0:T(8,128)S(1)}, u32[]{:S(2)}, u32[]{:S(2)}) collective-permute-start(f32[9,8,128]{2,1,0:T(8,128)S(1)} %get-tuple-element.79), channel_id=1, source_target_pairs={{0,6},{1,7},{4,2},{5,3},{6,0},{7,1},{2,4},{3,5},{8,14},{9,15},{12,... | collective-permute-start | bytes 110600 | tf_op jit(solution)/shard_map/ppermute | solution.py:779
  28.5 6.7 %collective-permute-start.8 = (f32[8,8,128]{2,1,0:T(8,128)S(1)}, f32[8,8,128]{2,1,0:T(8,128)S(1)}, u32[]{:S(2)}, u32[]{:S(2)}) collective-permute-start(f32[8,8,128]{2,1,0:T(8,128)S(1)} %get-tuple-element.76), channel_id=1, source_target_pairs={{0,7},{2,1},{4,3},{6,5},{7,0},{1,2},{3,4},{5,6},{8,15},{10,9},{12,... | collective-permute-start | bytes 98312 | tf_op jit(solution)/shard_map/ppermute | solution.py:772
  30.9 4.3 %collective-permute-start.9 = (f32[8,8,128]{2,1,0:T(8,128)S(1)}, f32[8,8,128]{2,1,0:T(8,128)S(1)}, u32[]{:S(2)}, u32[]{:S(2)}) collective-permute-start(f32[8,8,128]{2,1,0:T(8,128)S(1)} %get-tuple-element.77), channel_id=1, source_target_pairs={{0,1},{2,3},{4,5},{6,7},{1,0},{3,2},{5,4},{7,6},{8,9},{10,11},{12,... | collective-permute-start | bytes 98312 | tf_op jit(solution)/shard_map/ppermute | solution.py:772

commit v20 on v19

--- a/solution.py
+++ b/solution.py
@@ -671,7 +671,8 @@
         ref[0:1] = value
     for ref in (to_far_a, to_far_b):
         ref[3:] = jnp.broadcast_to(value, (ref.shape[0] - 3, Z, X))
-    to_first[1:] = edge_a[...]
+    to_first[1 : 1 + EDGE_TILES] = edge_a[...]
+    to_first[1 + EDGE_TILES :] = jnp.broadcast_to(value, (to_first.shape[0] - 1 - EDGE_TILES, Z, X))
     to_second[1:] = edge_b[...]
 
 
@@ -883,7 +884,7 @@
     near = (1 + EDGE_TILES, Z, X)
     packet, first, second, far_a, far_b, keep1 = call(
         level1_kernel,
-        [(1, Z, X), near, near, (near[0] + 2, Z, X), (near[0] + 1, Z, X), (2, *one)],
+        [(1, Z, X), (near[0] + 2, Z, X), near, (near[0] + 3, Z, X), (near[0] + 1, Z, X), (2, *one)],
         [one, one],
         own,
         *b_packets,

time: 38 us -> 38.8 us (1.021)
  starting transfers between devices: 18.4 us -> 20.3 us
  waiting for transfers between devices: 11.7 us -> 10.6 us
    ppermute x10, waiting for transfers between devices: 10.5 us -> 9.44 us  [swap(): return lax.ppermute(value, axis, pairs + [(j, i) for i, j in pairs])]
    ppermute x2, starting transfers between devices: 1.03 us -> 2.02 us  [swap_far(): return lax.ppermute(value, axis, pairs + [(j, i) for i, j in pairs])]
    ppermute x10, starting transfers between devices: 14.8 us -> 15.7 us  [swap(): return lax.ppermute(value, axis, pairs + [(j, i) for i, j in pairs])]
where the time goes in v20:
time: 38.8 us; the launch traced here: 38.6 us
  starting transfers between devices  20.3 us (52%)
  waiting for transfers between devices  10.6 us (27%)
  Pallas kernels  7.61 us (20%)
    ppermute x10, starting transfers between devices, swap(): return lax.ppermute(value, axis, pairs + [(j, i) for i, j in pairs])  15.7 us
    ppermute x10, waiting for transfers between devices, swap(): return lax.ppermute(value, axis, pairs + [(j, i) for i, j in pairs])  9.44 us
    pallas_call x10, Pallas kernels, call(): pl.pallas_call(kernel, out_shape=out, in_specs=[pl.BlockSpec(memory_space...  7.61 us
    all_to_all x1, starting transfers between devices, body(): spread = lax.all_to_all(spread, ('gx', 'gy'), 0, 0, tiled=True)  2.57 us
    ppermute x2, starting transfers between devices, swap_far(): return lax.ppermute(value, axis, pairs + [(j, i) for i, j in pairs])  2.02 us
    all_to_all x1, waiting for transfers between devices, body(): spread = lax.all_to_all(spread, ('gx', 'gy'), 0, 0, tiled=True)  1.18 us
  transfers between devices with their start and end apart: 13, of which 6 were waited for; matrix products, arithmetic and copies ran while one was open for 0% of the time, Pallas kernels for 8%

profile of v20, /device:TPU:0, one launch (start us, length us, event | category | flops | bytes accessed | tf_op | source)
XLA Modules:
  0.0 38.6 jit_solution(14394496456302525738)
XLA Ops:
  0.0 1.3 %shard_map.46 = (f32[27,8,128]{2,1,0:T(8,128)S(1)}, f32[27,8,128]{2,1,0:T(8,128)S(1)}, f32[9,8,128]{2,1,0:T(8,128)S(1)}, f32[256,128]{1,0:T(8,128)S(1)}, f32[256...) custom-call(f32[256,128]{1,0:T(8,128)} %bitcast.5, f32[256,128]{1,0:T(8,128)} %bitcast.6, ...), custom_call_target="tpu_custom_call" | custom-call | tf_op jit(solution)/shard_map/pallas_call | solution.py:759
  1.3 6.1 %collective-permute-start = (f32[27,8,128]{2,1,0:T(8,128)S(1)}, f32[27,8,128]{2,1,0:T(8,128)S(1)}, u32[]{:S(2)}, u32[]{:S(2)}) collective-permute-start(f32[27,8,128]{2,1,0:T(8,128)S(1)} %get-tuple-element.50), channel_id=1, source_target_pairs={{0,7},{2,1},{4,3},{6,5},{7,0},{1,2},{3,4},{5,6},{8,15},{10,9},{12,... | collective-permute-start | bytes 331784 | tf_op jit(solution)/shard_map/ppermute | solution.py:773
  7.4 0.9 %shard_map.47 = (f32[35,8,128]{2,1,0:T(8,128)S(1)}, f32[35,8,128]{2,1,0:T(8,128)S(1)}, f32[32,4,128]{2,1,0:T(4,128)}, f32[6,16,8,128]{3,2,1,0:T(8,128)S(1)}) custom-call(f32[256,128]{1,0:T(8,128)S(1)} %get-tuple-element.44.state, f32[256,128]{1,0:T(8,128)S(1)} %get-tuple-element.45.previous, f32[128,128]{1,0:T(8,128)S(1)} %get-tuple-element.46.feed, ...), custom_call_target="tpu_custom_call" | custom-call | tf_op jit(solution)/shard_map/pallas_call | solution.py:759
  8.3 0.7 %collective-permute-start.2 = (f32[35,8,128]{2,1,0:T(8,128)S(1)}, f32[35,8,128]{2,1,0:T(8,128)S(1)}, u32[]{:S(2)}, u32[]{:S(2)}) collective-permute-start(f32[35,8,128]{2,1,0:T(8,128)S(1)} %get-tuple-element.52), channel_id=1, source_target_pairs={{0,24},{16,8},{24,0},{8,16},{1,25},{17,9},{25,1},{9,17},{2,26},{18... | collective-permute-start | bytes 430088 | tf_op jit(solution)/shard_map/ppermute | solution.py:773
  9.0 1.0 %collective-permute-start.3 = (f32[35,8,128]{2,1,0:T(8,128)S(1)}, f32[35,8,128]{2,1,0:T(8,128)S(1)}, u32[]{:S(2)}, u32[]{:S(2)}) collective-permute-start(f32[35,8,128]{2,1,0:T(8,128)S(1)} %get-tuple-element.53), channel_id=1, source_target_pairs={{0,8},{16,24},{8,0},{24,16},{1,9},{17,25},{9,1},{25,17},{2,10},{18... | collective-permute-start | bytes 430088 | tf_op jit(solution)/shard_map/ppermute | solution.py:773
  10.0 2.6 %all-to-all-start = ((f32[32,4,128]{2,1,0:T(4,128)}), f32[32,4,128]{2,1,0:T(4,128)S(1)}, u32[]{:S(2)}, u32[]{:S(2)}) async-start(f32[32,4,128]{2,1,0:T(4,128)} %get-tuple-element.64), calls=%async_computation | async-start | bytes 131072 | tf_op jit(solution)/shard_map/all_to_all | solution.py:819
  12.6 0.3 collective-permute-done.1.y_second
  13.0 1.2 %collective-permute-start.4 = (f32[18,8,128]{2,1,0:T(8,128)S(1)}, f32[18,8,128]{2,1,0:T(8,128)S(1)}, u32[]{:S(2)}, u32[]{:S(2)}) collective-permute-start(f32[18,8,128]{2,1,0:T(8,128)S(1)} %get-tuple-element.54), channel_id=1, source_target_pairs={{0,24},{16,8},{24,0},{8,16},{1,25},{17,9},{25,1},{9,17},{2,26},{18... | collective-permute-start | bytes 221192 | tf_op jit(solution)/shard_map/ppermute | solution.py:773
  14.2 0.5 %collective-permute-start.5 = (f32[18,8,128]{2,1,0:T(8,128)S(1)}, f32[18,8,128]{2,1,0:T(8,128)S(1)}, u32[]{:S(2)}, u32[]{:S(2)}) collective-permute-start(f32[18,8,128]{2,1,0:T(8,128)S(1)} %get-tuple-element.55), channel_id=1, source_target_pairs={{0,8},{16,24},{8,0},{24,16},{1,9},{17,25},{9,1},{25,17},{2,10},{18... | collective-permute-start | bytes 221192 | tf_op jit(solution)/shard_map/ppermute | solution.py:773
  14.7 0.9 %shard_map.49 = (f32[6,2,14,8,128]{4,3,2,1,0:T(8,128)S(1)}, f32[2,2,4,8,128]{4,3,2,1,0:T(8,128)S(1)}, f32[2,2,12,8,128]{4,3,2,1,0:T(8,128)S(1)}, f32[2,2,10,8,12...) custom-call(f32[6,16,8,128]{3,2,1,0:T(8,128)S(1)} %get-tuple-element.49.main, ...), custom_call_target="tpu_custom_call" | custom-call | tf_op jit(solution)/shard_map/pallas_call | solution.py:759
  15.6 2.3 %collective-permute-done.4.corner_a = f32[18,8,128]{2,1,0:T(8,128)S(1)} collective-permute-done((f32[18,8,128]{2,1,0:T(8,128)S(1)}, f32[18,8,128]{2,1,0:T(8,128)S(1)}, u32[]{:S(2)}, u32[]{:S(2)}) %collective-permute-start.4) | collective-permute-done | bytes 73760 | tf_op jit(solution)/shard_map/ppermute | solution.py:773
  17.9 0.8 %shard_map.50 = (f32[6,2,8,8,128]{4,3,2,1,0:T(8,128)S(1)}, f32[2,2,4,8,128]{4,3,2,1,0:T(8,128)S(1)}, f32[2,2,6,8,128]{4,3,2,1,0:T(8,128)S(1)}, f32[4,2,4,8,128]{4,3,2,1,0:T(8,128)S(1)}, f32[3,2,7,8,128]{4,3,2,1,0:T(8,128)S(1)}) custom-call(f32[6,16,8,128]{3,2,1,0:T(8,128)S(1)} %get-tuple-element.49.main, f32[27,8,128]{2,1,0:T(8,128)S(1)} %collective-permute-done.y_first, ...), custom_call_target="tpu_custom_call" | custom-call | tf_op jit(solution)/shard_map/pallas_call | solution.py:759
  18.6 1.2 %all-to-all-done.spread = f32[32,4,128]{2,1,0:T(4,128)S(1)} async-done(((f32[32,4,128]{2,1,0:T(4,128)}), f32[32,4,128]{2,1,0:T(4,128)S(1)}, u32[]{:S(2)}, u32[]{:S(2)}) %all-to-all-start) | async-done | bytes 65568 | tf_op jit(solution)/shard_map/all_to_all | solution.py:819
  19.8 0.2 shard_map.51
  20.0 2.9 %collective-permute-start.6 = (f32[7,8,128]{2,1,0:T(8,128)S(1)}, f32[7,8,128]{2,1,0:T(8,128)S(1)}, u32[]{:S(2)}, u32[]{:S(2)}) collective-permute-start(f32[7,8,128]{2,1,0:T(8,128)S(1)} %get-tuple-element.66), channel_id=1, source_target_pairs={{0,7},{2,1},{4,3},{6,5},{7,0},{1,2},{3,4},{5,6},{8,15},{10,9},{12,... | collective-permute-start | bytes 86024 | tf_op jit(solution)/shard_map/ppermute | solution.py:773
  23.0 0.2 shard_map.53
  23.2 3.4 %collective-permute-done.6.first = f32[7,8,128]{2,1,0:T(8,128)S(1)} collective-permute-done((f32[7,8,128]{2,1,0:T(8,128)S(1)}, f32[7,8,128]{2,1,0:T(8,128)S(1)}, u32[]{:S(2)}, u32[]{:S(2)}) %collective-permute-start.6) | collective-permute-done | bytes 28704 | tf_op jit(solution)/shard_map/ppermute | solution.py:773
  26.6 0.3 collective-permute-done.7.second
  26.9 0.5 %shard_map.54 = (f32[1,8,128]{2,1,0:T(8,128)S(1)}, f32[10,8,128]{2,1,0:T(8,128)S(1)}, f32[8,8,128]{2,1,0:T(8,128)S(1)}, f32[11,8,128]{2,1,0:T(8,128)S(1)}, f32[9...) custom-call(f32[2,4,8,128]{3,2,1,0:T(8,128)S(1)} %get-tuple-element.65.own, ...), custom_call_target="tpu_custom_call" | custom-call | tf_op jit(solution)/shard_map/pallas_call | solution.py:759
  27.5 2.6 %collective-permute-start.8 = (f32[10,8,128]{2,1,0:T(8,128)S(1)}, f32[10,8,128]{2,1,0:T(8,128)S(1)}, u32[]{:S(2)}, u32[]{:S(2)}) collective-permute-start(f32[10,8,128]{2,1,0:T(8,128)S(1)} %get-tuple-element.76), channel_id=1, source_target_pairs={{0,7},{2,1},{4,3},{6,5},{7,0},{1,2},{3,4},{5,6},{8,15},{10,9},{12,... | collective-permute-start | bytes 122888 | tf_op jit(solution)/shard_map/ppermute | solution.py:773
  30.1 1.9 %collective-permute-start.11 = (f32[9,8,128]{2,1,0:T(8,128)S(1)}, f32[9,8,128]{2,1,0:T(8,128)S(1)}, u32[]{:S(2)}, u32[]{:S(2)}) collective-permute-start(f32[9,8,128]{2,1,0:T(8,128)S(1)} %get-tuple-element.79), channel_id=1, source_target_pairs={{0,6},{1,7},{4,2},{5,3},{6,0},{7,1},{2,4},{3,5},{8,14},{9,15},{12,... | collective-permute-start | bytes 110600 | tf_op jit(solution)/shard_map/ppermute | solution.py:780
  32.1 0.8 %collective-permute-start.9 = (f32[8,8,128]{2,1,0:T(8,128)S(1)}, f32[8,8,128]{2,1,0:T(8,128)S(1)}, u32[]{:S(2)}, u32[]{:S(2)}) collective-permute-start(f32[8,8,128]{2,1,0:T(8,128)S(1)} %get-tuple-element.77), channel_id=1, source_target_pairs={{0,1},{2,3},{4,5},{6,7},{1,0},{3,2},{5,4},{7,6},{8,9},{10,11},{12,... | collective-permute-start | bytes 98312 | tf_op jit(solution)/shard_map/ppermute | solution.py:773
  32.9 3.1 %collective-permute-done.9.near_b = f32[8,8,128]{2,1,0:T(8,128)S(1)} collective-permute-done((f32[8,8,128]{2,1,0:T(8,128)S(1)}, f32[8,8,128]{2,1,0:T(8,128)S(1)}, u32[]{:S(2)}, u32[]{:S(2)}) %collective-permute-start.9) | collective-permute-done | bytes 32800 | tf_op jit(solution)/shard_map/ppermute | solution.py:773
  36.0 2.6 %shard_map.55 = f32[256,128]{1,0:T(8,128)} custom-call(f32[1,8,128]{2,1,0:T(8,128)S(1)} %get-tuple-element.75.own2, f32[10,8,128]{2,1,0:T(8,128)S(1)} %collective-permute-done.8.near_a, f32[8,8,128]{2,1,0:T(8,128)S(1)} %collective-permute-done.9.near_b, f32[11,8,128]{2,1,0:T(8,128)S(1)} %collective-permute-done.10.far_a, ...), custom_call_target="tpu_custom_call" | custom-call | tf_op jit(solution)/shard_map/pallas_call | solution.py:759
  (12 shorter events, 0.3 us)
Async XLA Ops:
  1.3 11.2 %collective-permute-start = (f32[27,8,128]{2,1,0:T(8,128)S(1)}, f32[27,8,128]{2,1,0:T(8,128)S(1)}, u32[]{:S(2)}, u32[]{:S(2)}) collective-permute-start(f32[27,8,128]{2,1,0:T(8,128)S(1)} %get-tuple-element.50), channel_id=1, source_target_pairs={{0,7},{2,1},{4,3},{6,5},{7,0},{1,2},{3,4},{5,6},{8,15},{10,9},{12,... | collective-permute-start | bytes 331784 | tf_op jit(solution)/shard_map/ppermute | solution.py:773
  7.4 5.4 %collective-permute-start.1 = (f32[27,8,128]{2,1,0:T(8,128)S(1)}, f32[27,8,128]{2,1,0:T(8,128)S(1)}, u32[]{:S(2)}, u32[]{:S(2)}) collective-permute-start(f32[27,8,128]{2,1,0:T(8,128)S(1)} %get-tuple-element.51), channel_id=1, source_target_pairs={{0,1},{2,3},{4,5},{6,7},{1,0},{3,2},{5,4},{7,6},{8,9},{10,11},{12,... | collective-permute-start | bytes 331784 | tf_op jit(solution)/shard_map/ppermute | solution.py:773
  8.3 6.4 %collective-permute-start.2 = (f32[35,8,128]{2,1,0:T(8,128)S(1)}, f32[35,8,128]{2,1,0:T(8,128)S(1)}, u32[]{:S(2)}, u32[]{:S(2)}) collective-permute-start(f32[35,8,128]{2,1,0:T(8,128)S(1)} %get-tuple-element.52), channel_id=1, source_target_pairs={{0,24},{16,8},{24,0},{8,16},{1,25},{17,9},{25,1},{9,17},{2,26},{18... | collective-permute-start | bytes 430088 | tf_op jit(solution)/shard_map/ppermute | solution.py:773
  9.0 5.7 %collective-permute-start.3 = (f32[35,8,128]{2,1,0:T(8,128)S(1)}, f32[35,8,128]{2,1,0:T(8,128)S(1)}, u32[]{:S(2)}, u32[]{:S(2)}) collective-permute-start(f32[35,8,128]{2,1,0:T(8,128)S(1)} %get-tuple-element.53), channel_id=1, source_target_pairs={{0,8},{16,24},{8,0},{24,16},{1,9},{17,25},{9,1},{25,17},{2,10},{18... | collective-permute-start | bytes 430088 | tf_op jit(solution)/shard_map/ppermute | solution.py:773
  10.0 9.9 %all-to-all-start = ((f32[32,4,128]{2,1,0:T(4,128)}), f32[32,4,128]{2,1,0:T(4,128)S(1)}, u32[]{:S(2)}, u32[]{:S(2)}) async-start(f32[32,4,128]{2,1,0:T(4,128)} %get-tuple-element.64), calls=%async_computation | async-start | bytes 131072 | tf_op jit(solution)/shard_map/all_to_all | solution.py:819
  13.0 4.8 %collective-permute-start.4 = (f32[18,8,128]{2,1,0:T(8,128)S(1)}, f32[18,8,128]{2,1,0:T(8,128)S(1)}, u32[]{:S(2)}, u32[]{:S(2)}) collective-permute-start(f32[18,8,128]{2,1,0:T(8,128)S(1)} %get-tuple-element.54), channel_id=1, source_target_pairs={{0,24},{16,8},{24,0},{8,16},{1,25},{17,9},{25,1},{9,17},{2,26},{18... | collective-permute-start | bytes 221192 | tf_op jit(solution)/shard_map/ppermute | solution.py:773
  14.2 3.7 %collective-permute-start.5 = (f32[18,8,128]{2,1,0:T(8,128)S(1)}, f32[18,8,128]{2,1,0:T(8,128)S(1)}, u32[]{:S(2)}, u32[]{:S(2)}) collective-permute-start(f32[18,8,128]{2,1,0:T(8,128)S(1)} %get-tuple-element.55), channel_id=1, source_target_pairs={{0,8},{16,24},{8,0},{24,16},{1,9},{17,25},{9,1},{25,17},{2,10},{18... | collective-permute-start | bytes 221192 | tf_op jit(solution)/shard_map/ppermute | solution.py:773
  20.0 6.6 %collective-permute-start.6 = (f32[7,8,128]{2,1,0:T(8,128)S(1)}, f32[7,8,128]{2,1,0:T(8,128)S(1)}, u32[]{:S(2)}, u32[]{:S(2)}) collective-permute-start(f32[7,8,128]{2,1,0:T(8,128)S(1)} %get-tuple-element.66), channel_id=1, source_target_pairs={{0,7},{2,1},{4,3},{6,5},{7,0},{1,2},{3,4},{5,6},{8,15},{10,9},{12,... | collective-permute-start | bytes 86024 | tf_op jit(solution)/shard_map/ppermute | solution.py:773
  22.9 4.0 %collective-permute-start.7 = (f32[7,8,128]{2,1,0:T(8,128)S(1)}, f32[7,8,128]{2,1,0:T(8,128)S(1)}, u32[]{:S(2)}, u32[]{:S(2)}) collective-permute-start(f32[7,8,128]{2,1,0:T(8,128)S(1)} %get-tuple-element.67), channel_id=1, source_target_pairs={{0,1},{2,3},{4,5},{6,7},{1,0},{3,2},{5,4},{7,6},{8,9},{10,11},{12,... | collective-permute-start | bytes 86024 | tf_op jit(solution)/shard_map/ppermute | solution.py:773
  27.4 8.6 %collective-permute-start.10 = (f32[11,8,128]{2,1,0:T(8,128)S(1)}, f32[11,8,128]{2,1,0:T(8,128)S(1)}, u32[]{:S(2)}, u32[]{:S(2)}) collective-permute-start(f32[11,8,128]{2,1,0:T(8,128)S(1)} %get-tuple-element.78), channel_id=1, source_target_pairs={{0,2},{1,3},{4,6},{5,7},{2,0},{3,1},{6,4},{7,5},{8,10},{9,11},{12,... | collective-permute-start | bytes 135176 | tf_op jit(solution)/shard_map/ppermute | solution.py:780
  27.5 8.5 %collective-permute-start.8 = (f32[10,8,128]{2,1,0:T(8,128)S(1)}, f32[10,8,128]{2,1,0:T(8,128)S(1)}, u32[]{:S(2)}, u32[]{:S(2)}) collective-permute-start(f32[10,8,128]{2,1,0:T(8,128)S(1)} %get-tuple-element.76), channel_id=1, source_target_pairs={{0,7},{2,1},{4,3},{6,5},{7,0},{1,2},{3,4},{5,6},{8,15},{10,9},{12,... | collective-permute-start | bytes 122888 | tf_op jit(solution)/shard_map/ppermute | solution.py:773
  30.1 5.9 %collective-permute-start.11 = (f32[9,8,128]{2,1,0:T(8,128)S(1)}, f32[9,8,128]{2,1,0:T(8,128)S(1)}, u32[]{:S(2)}, u32[]{:S(2)}) collective-permute-start(f32[9,8,128]{2,1,0:T(8,128)S(1)} %get-tuple-element.79), channel_id=1, source_target_pairs={{0,6},{1,7},{4,2},{5,3},{6,0},{7,1},{2,4},{3,5},{8,14},{9,15},{12,... | collective-permute-start | bytes 110600 | tf_op jit(solution)/shard_map/ppermute | solution.py:780
  32.1 3.9 %collective-permute-start.9 = (f32[8,8,128]{2,1,0:T(8,128)S(1)}, f32[8,8,128]{2,1,0:T(8,128)S(1)}, u32[]{:S(2)}, u32[]{:S(2)}) collective-permute-start(f32[8,8,128]{2,1,0:T(8,128)S(1)} %get-tuple-element.77), channel_id=1, source_target_pairs={{0,1},{2,3},{4,5},{6,7},{1,0},{3,2},{5,4},{7,6},{8,9},{10,11},{12,... | collective-permute-start | bytes 98312 | tf_op jit(solution)/shard_map/ppermute | solution.py:773

commit v21 on v19

--- a/solution.py
+++ b/solution.py
@@ -883,7 +883,7 @@
     near = (1 + EDGE_TILES, Z, X)
     packet, first, second, far_a, far_b, keep1 = call(
         level1_kernel,
-        [(1, Z, X), near, near, (near[0] + 2, Z, X), (near[0] + 1, Z, X), (2, *one)],
+        [(1, Z, X), near, near, (near[0] + 1, Z, X), (near[0] + 2, Z, X), (2, *one)],
         [one, one],
         own,
         *b_packets,

time: 38 us -> 37.7 us (level)
  waiting for transfers between devices: 11.7 us -> 10.9 us
  starting transfers between devices: 18.4 us -> 18.9 us
    ppermute x10, starting transfers between devices: 14.8 us -> 15.8 us  [swap(): return lax.ppermute(value, axis, pairs + [(j, i) for i, j in pairs])]
    ppermute x10, waiting for transfers between devices: 10.5 us -> 9.7 us  [swap(): return lax.ppermute(value, axis, pairs + [(j, i) for i, j in pairs])]
    ppermute x2, starting transfers between devices: 1.03 us -> 0.56 us  [swap_far(): return lax.ppermute(value, axis, pairs + [(j, i) for i, j in pairs])]
  transfers between devices with their start and end apart: 13 -> 13, of which waited for: 6 -> 7; matrix products, arithmetic and copies ran while one was open for 0% -> 0% of each run, Pallas kernels for 8% -> 8%
where the time goes in v21:
time: 37.7 us; the launch traced here: 37.5 us
  starting transfers between devices  18.9 us (50%)
  waiting for transfers between devices  10.9 us (29%)
  Pallas kernels  7.61 us (20%)
    ppermute x10, starting transfers between devices, swap(): return lax.ppermute(value, axis, pairs + [(j, i) for i, j in pairs])  15.8 us
    ppermute x10, waiting for transfers between devices, swap(): return lax.ppermute(value, axis, pairs + [(j, i) for i, j in pairs])  9.7 us
    pallas_call x10, Pallas kernels, call(): pl.pallas_call(kernel, out_shape=out, in_specs=[pl.BlockSpec(memory_space...  7.61 us
    all_to_all x1, starting transfers between devices, body(): spread = lax.all_to_all(spread, ('gx', 'gy'), 0, 0, tiled=True)  2.57 us
    all_to_all x1, waiting for transfers between devices, body(): spread = lax.all_to_all(spread, ('gx', 'gy'), 0, 0, tiled=True)  1.18 us
  transfers between devices with their start and end apart: 13, of which 7 were waited for; matrix products, arithmetic and copies ran while one was open for 0% of the time, Pallas kernels for 8%

profile of v21, /device:TPU:0, one launch (start us, length us, event | category | flops | bytes accessed | tf_op | source)
XLA Modules:
  0.0 37.5 jit_solution(11440126369455734014)
XLA Ops:
  0.0 1.3 %shard_map.46 = (f32[27,8,128]{2,1,0:T(8,128)S(1)}, f32[27,8,128]{2,1,0:T(8,128)S(1)}, f32[9,8,128]{2,1,0:T(8,128)S(1)}, f32[256,128]{1,0:T(8,128)S(1)}, f32[256...) custom-call(f32[256,128]{1,0:T(8,128)} %bitcast.5, f32[256,128]{1,0:T(8,128)} %bitcast.6, ...), custom_call_target="tpu_custom_call" | custom-call | tf_op jit(solution)/shard_map/pallas_call | solution.py:758
  1.3 6.1 %collective-permute-start = (f32[27,8,128]{2,1,0:T(8,128)S(1)}, f32[27,8,128]{2,1,0:T(8,128)S(1)}, u32[]{:S(2)}, u32[]{:S(2)}) collective-permute-start(f32[27,8,128]{2,1,0:T(8,128)S(1)} %get-tuple-element.50), channel_id=1, source_target_pairs={{0,7},{2,1},{4,3},{6,5},{7,0},{1,2},{3,4},{5,6},{8,15},{10,9},{12,... | collective-permute-start | bytes 331784 | tf_op jit(solution)/shard_map/ppermute | solution.py:772
  7.4 0.9 %shard_map.47 = (f32[35,8,128]{2,1,0:T(8,128)S(1)}, f32[35,8,128]{2,1,0:T(8,128)S(1)}, f32[32,4,128]{2,1,0:T(4,128)}, f32[6,16,8,128]{3,2,1,0:T(8,128)S(1)}) custom-call(f32[256,128]{1,0:T(8,128)S(1)} %get-tuple-element.44.state, f32[256,128]{1,0:T(8,128)S(1)} %get-tuple-element.45.previous, f32[128,128]{1,0:T(8,128)S(1)} %get-tuple-element.46.feed, ...), custom_call_target="tpu_custom_call" | custom-call | tf_op jit(solution)/shard_map/pallas_call | solution.py:758
  8.3 0.7 %collective-permute-start.2 = (f32[35,8,128]{2,1,0:T(8,128)S(1)}, f32[35,8,128]{2,1,0:T(8,128)S(1)}, u32[]{:S(2)}, u32[]{:S(2)}) collective-permute-start(f32[35,8,128]{2,1,0:T(8,128)S(1)} %get-tuple-element.52), channel_id=1, source_target_pairs={{0,24},{16,8},{24,0},{8,16},{1,25},{17,9},{25,1},{9,17},{2,26},{18... | collective-permute-start | bytes 430088 | tf_op jit(solution)/shard_map/ppermute | solution.py:772
  9.0 1.0 %collective-permute-start.3 = (f32[35,8,128]{2,1,0:T(8,128)S(1)}, f32[35,8,128]{2,1,0:T(8,128)S(1)}, u32[]{:S(2)}, u32[]{:S(2)}) collective-permute-start(f32[35,8,128]{2,1,0:T(8,128)S(1)} %get-tuple-element.53), channel_id=1, source_target_pairs={{0,8},{16,24},{8,0},{24,16},{1,9},{17,25},{9,1},{25,17},{2,10},{18... | collective-permute-start | bytes 430088 | tf_op jit(solution)/shard_map/ppermute | solution.py:772
  10.0 2.6 %all-to-all-start = ((f32[32,4,128]{2,1,0:T(4,128)}), f32[32,4,128]{2,1,0:T(4,128)S(1)}, u32[]{:S(2)}, u32[]{:S(2)}) async-start(f32[32,4,128]{2,1,0:T(4,128)} %get-tuple-element.64), calls=%async_computation | async-start | bytes 131072 | tf_op jit(solution)/shard_map/all_to_all | solution.py:818
  12.6 0.3 collective-permute-done.1.y_second
  13.0 1.2 %collective-permute-start.4 = (f32[18,8,128]{2,1,0:T(8,128)S(1)}, f32[18,8,128]{2,1,0:T(8,128)S(1)}, u32[]{:S(2)}, u32[]{:S(2)}) collective-permute-start(f32[18,8,128]{2,1,0:T(8,128)S(1)} %get-tuple-element.54), channel_id=1, source_target_pairs={{0,24},{16,8},{24,0},{8,16},{1,25},{17,9},{25,1},{9,17},{2,26},{18... | collective-permute-start | bytes 221192 | tf_op jit(solution)/shard_map/ppermute | solution.py:772
  14.2 0.5 %collective-permute-start.5 = (f32[18,8,128]{2,1,0:T(8,128)S(1)}, f32[18,8,128]{2,1,0:T(8,128)S(1)}, u32[]{:S(2)}, u32[]{:S(2)}) collective-permute-start(f32[18,8,128]{2,1,0:T(8,128)S(1)} %get-tuple-element.55), channel_id=1, source_target_pairs={{0,8},{16,24},{8,0},{24,16},{1,9},{17,25},{9,1},{25,17},{2,10},{18... | collective-permute-start | bytes 221192 | tf_op jit(solution)/shard_map/ppermute | solution.py:772
  14.7 0.9 %shard_map.49 = (f32[6,2,14,8,128]{4,3,2,1,0:T(8,128)S(1)}, f32[2,2,4,8,128]{4,3,2,1,0:T(8,128)S(1)}, f32[2,2,12,8,128]{4,3,2,1,0:T(8,128)S(1)}, f32[2,2,10,8,12...) custom-call(f32[6,16,8,128]{3,2,1,0:T(8,128)S(1)} %get-tuple-element.49.main, ...), custom_call_target="tpu_custom_call" | custom-call | tf_op jit(solution)/shard_map/pallas_call | solution.py:758
  15.6 2.3 %collective-permute-done.4.corner_a = f32[18,8,128]{2,1,0:T(8,128)S(1)} collective-permute-done((f32[18,8,128]{2,1,0:T(8,128)S(1)}, f32[18,8,128]{2,1,0:T(8,128)S(1)}, u32[]{:S(2)}, u32[]{:S(2)}) %collective-permute-start.4) | collective-permute-done | bytes 73760 | tf_op jit(solution)/shard_map/ppermute | solution.py:772
  17.9 0.8 %shard_map.50 = (f32[6,2,8,8,128]{4,3,2,1,0:T(8,128)S(1)}, f32[2,2,4,8,128]{4,3,2,1,0:T(8,128)S(1)}, f32[2,2,6,8,128]{4,3,2,1,0:T(8,128)S(1)}, f32[4,2,4,8,128]{4,3,2,1,0:T(8,128)S(1)}, f32[3,2,7,8,128]{4,3,2,1,0:T(8,128)S(1)}) custom-call(f32[6,16,8,128]{3,2,1,0:T(8,128)S(1)} %get-tuple-element.49.main, f32[27,8,128]{2,1,0:T(8,128)S(1)} %collective-permute-done.y_first, ...), custom_call_target="tpu_custom_call" | custom-call | tf_op jit(solution)/shard_map/pallas_call | solution.py:758
  18.6 1.2 %all-to-all-done.spread = f32[32,4,128]{2,1,0:T(4,128)S(1)} async-done(((f32[32,4,128]{2,1,0:T(4,128)}), f32[32,4,128]{2,1,0:T(4,128)S(1)}, u32[]{:S(2)}, u32[]{:S(2)}) %all-to-all-start) | async-done | bytes 65568 | tf_op jit(solution)/shard_map/all_to_all | solution.py:818
  19.8 0.2 shard_map.51
  20.0 2.9 %collective-permute-start.6 = (f32[7,8,128]{2,1,0:T(8,128)S(1)}, f32[7,8,128]{2,1,0:T(8,128)S(1)}, u32[]{:S(2)}, u32[]{:S(2)}) collective-permute-start(f32[7,8,128]{2,1,0:T(8,128)S(1)} %get-tuple-element.66), channel_id=1, source_target_pairs={{0,7},{2,1},{4,3},{6,5},{7,0},{1,2},{3,4},{5,6},{8,15},{10,9},{12,... | collective-permute-start | bytes 86024 | tf_op jit(solution)/shard_map/ppermute | solution.py:772
  23.0 0.2 shard_map.53
  23.2 3.4 %collective-permute-done.6.first = f32[7,8,128]{2,1,0:T(8,128)S(1)} collective-permute-done((f32[7,8,128]{2,1,0:T(8,128)S(1)}, f32[7,8,128]{2,1,0:T(8,128)S(1)}, u32[]{:S(2)}, u32[]{:S(2)}) %collective-permute-start.6) | collective-permute-done | bytes 28704 | tf_op jit(solution)/shard_map/ppermute | solution.py:772
  26.6 0.3 collective-permute-done.7.second
  26.9 0.5 %shard_map.54 = (f32[1,8,128]{2,1,0:T(8,128)S(1)}, f32[8,8,128]{2,1,0:T(8,128)S(1)}, f32[8,8,128]{2,1,0:T(8,128)S(1)}, f32[9,8,128]{2,1,0:T(8,128)S(1)}, f32[10,...) custom-call(f32[2,4,8,128]{3,2,1,0:T(8,128)S(1)} %get-tuple-element.65.own, ...), custom_call_target="tpu_custom_call" | custom-call | tf_op jit(solution)/shard_map/pallas_call | solution.py:758
  27.4 0.6 %collective-permute-start.11 = (f32[10,8,128]{2,1,0:T(8,128)S(1)}, f32[10,8,128]{2,1,0:T(8,128)S(1)}, u32[]{:S(2)}, u32[]{:S(2)}) collective-permute-start(f32[10,8,128]{2,1,0:T(8,128)S(1)} %get-tuple-element.79), channel_id=1, source_target_pairs={{0,6},{1,7},{4,2},{5,3},{6,0},{7,1},{2,4},{3,5},{8,14},{9,15},{12,... | collective-permute-start | bytes 122888 | tf_op jit(solution)/shard_map/ppermute | solution.py:779
  28.0 2.6 %collective-permute-start.8 = (f32[8,8,128]{2,1,0:T(8,128)S(1)}, f32[8,8,128]{2,1,0:T(8,128)S(1)}, u32[]{:S(2)}, u32[]{:S(2)}) collective-permute-start(f32[8,8,128]{2,1,0:T(8,128)S(1)} %get-tuple-element.76), channel_id=1, source_target_pairs={{0,7},{2,1},{4,3},{6,5},{7,0},{1,2},{3,4},{5,6},{8,15},{10,9},{12,... | collective-permute-start | bytes 98312 | tf_op jit(solution)/shard_map/ppermute | solution.py:772
  30.6 0.9 %collective-permute-start.9 = (f32[8,8,128]{2,1,0:T(8,128)S(1)}, f32[8,8,128]{2,1,0:T(8,128)S(1)}, u32[]{:S(2)}, u32[]{:S(2)}) collective-permute-start(f32[8,8,128]{2,1,0:T(8,128)S(1)} %get-tuple-element.77), channel_id=1, source_target_pairs={{0,1},{2,3},{4,5},{6,7},{1,0},{3,2},{5,4},{7,6},{8,9},{10,11},{12,... | collective-permute-start | bytes 98312 | tf_op jit(solution)/shard_map/ppermute | solution.py:772
  31.5 3.2 %collective-permute-done.8.near_a = f32[8,8,128]{2,1,0:T(8,128)S(1)} collective-permute-done((f32[8,8,128]{2,1,0:T(8,128)S(1)}, f32[8,8,128]{2,1,0:T(8,128)S(1)}, u32[]{:S(2)}, u32[]{:S(2)}) %collective-permute-start.8) | collective-permute-done | bytes 32800 | tf_op jit(solution)/shard_map/ppermute | solution.py:772
  34.9 2.6 %shard_map.55 = f32[256,128]{1,0:T(8,128)} custom-call(f32[1,8,128]{2,1,0:T(8,128)S(1)} %get-tuple-element.75.own2, f32[8,8,128]{2,1,0:T(8,128)S(1)} %collective-permute-done.8.near_a, f32[8,8,128]{2,1,0:T(8,128)S(1)} %collective-permute-done.9.near_b, f32[9,8,128]{2,1,0:T(8,128)S(1)} %collective-permute-done.10.far_a, ...), custom_call_target="tpu_custom_call" | custom-call | tf_op jit(solution)/shard_map/pallas_call | solution.py:758
  (12 shorter events, 0.4 us)
Async XLA Ops:
  1.3 11.2 %collective-permute-start = (f32[27,8,128]{2,1,0:T(8,128)S(1)}, f32[27,8,128]{2,1,0:T(8,128)S(1)}, u32[]{:S(2)}, u32[]{:S(2)}) collective-permute-start(f32[27,8,128]{2,1,0:T(8,128)S(1)} %get-tuple-element.50), channel_id=1, source_target_pairs={{0,7},{2,1},{4,3},{6,5},{7,0},{1,2},{3,4},{5,6},{8,15},{10,9},{12,... | collective-permute-start | bytes 331784 | tf_op jit(solution)/shard_map/ppermute | solution.py:772
  7.4 5.4 %collective-permute-start.1 = (f32[27,8,128]{2,1,0:T(8,128)S(1)}, f32[27,8,128]{2,1,0:T(8,128)S(1)}, u32[]{:S(2)}, u32[]{:S(2)}) collective-permute-start(f32[27,8,128]{2,1,0:T(8,128)S(1)} %get-tuple-element.51), channel_id=1, source_target_pairs={{0,1},{2,3},{4,5},{6,7},{1,0},{3,2},{5,4},{7,6},{8,9},{10,11},{12,... | collective-permute-start | bytes 331784 | tf_op jit(solution)/shard_map/ppermute | solution.py:772
  8.3 6.4 %collective-permute-start.2 = (f32[35,8,128]{2,1,0:T(8,128)S(1)}, f32[35,8,128]{2,1,0:T(8,128)S(1)}, u32[]{:S(2)}, u32[]{:S(2)}) collective-permute-start(f32[35,8,128]{2,1,0:T(8,128)S(1)} %get-tuple-element.52), channel_id=1, source_target_pairs={{0,24},{16,8},{24,0},{8,16},{1,25},{17,9},{25,1},{9,17},{2,26},{18... | collective-permute-start | bytes 430088 | tf_op jit(solution)/shard_map/ppermute | solution.py:772
  9.0 5.7 %collective-permute-start.3 = (f32[35,8,128]{2,1,0:T(8,128)S(1)}, f32[35,8,128]{2,1,0:T(8,128)S(1)}, u32[]{:S(2)}, u32[]{:S(2)}) collective-permute-start(f32[35,8,128]{2,1,0:T(8,128)S(1)} %get-tuple-element.53), channel_id=1, source_target_pairs={{0,8},{16,24},{8,0},{24,16},{1,9},{17,25},{9,1},{25,17},{2,10},{18... | collective-permute-start | bytes 430088 | tf_op jit(solution)/shard_map/ppermute | solution.py:772
  10.0 9.9 %all-to-all-start = ((f32[32,4,128]{2,1,0:T(4,128)}), f32[32,4,128]{2,1,0:T(4,128)S(1)}, u32[]{:S(2)}, u32[]{:S(2)}) async-start(f32[32,4,128]{2,1,0:T(4,128)} %get-tuple-element.64), calls=%async_computation | async-start | bytes 131072 | tf_op jit(solution)/shard_map/all_to_all | solution.py:818
  13.0 4.8 %collective-permute-start.4 = (f32[18,8,128]{2,1,0:T(8,128)S(1)}, f32[18,8,128]{2,1,0:T(8,128)S(1)}, u32[]{:S(2)}, u32[]{:S(2)}) collective-permute-start(f32[18,8,128]{2,1,0:T(8,128)S(1)} %get-tuple-element.54), channel_id=1, source_target_pairs={{0,24},{16,8},{24,0},{8,16},{1,25},{17,9},{25,1},{9,17},{2,26},{18... | collective-permute-start | bytes 221192 | tf_op jit(solution)/shard_map/ppermute | solution.py:772
  14.2 3.7 %collective-permute-start.5 = (f32[18,8,128]{2,1,0:T(8,128)S(1)}, f32[18,8,128]{2,1,0:T(8,128)S(1)}, u32[]{:S(2)}, u32[]{:S(2)}) collective-permute-start(f32[18,8,128]{2,1,0:T(8,128)S(1)} %get-tuple-element.55), channel_id=1, source_target_pairs={{0,8},{16,24},{8,0},{24,16},{1,9},{17,25},{9,1},{25,17},{2,10},{18... | collective-permute-start | bytes 221192 | tf_op jit(solution)/shard_map/ppermute | solution.py:772
  20.0 6.6 %collective-permute-start.6 = (f32[7,8,128]{2,1,0:T(8,128)S(1)}, f32[7,8,128]{2,1,0:T(8,128)S(1)}, u32[]{:S(2)}, u32[]{:S(2)}) collective-permute-start(f32[7,8,128]{2,1,0:T(8,128)S(1)} %get-tuple-element.66), channel_id=1, source_target_pairs={{0,7},{2,1},{4,3},{6,5},{7,0},{1,2},{3,4},{5,6},{8,15},{10,9},{12,... | collective-permute-start | bytes 86024 | tf_op jit(solution)/shard_map/ppermute | solution.py:772
  22.9 4.0 %collective-permute-start.7 = (f32[7,8,128]{2,1,0:T(8,128)S(1)}, f32[7,8,128]{2,1,0:T(8,128)S(1)}, u32[]{:S(2)}, u32[]{:S(2)}) collective-permute-start(f32[7,8,128]{2,1,0:T(8,128)S(1)} %get-tuple-element.67), channel_id=1, source_target_pairs={{0,1},{2,3},{4,5},{6,7},{1,0},{3,2},{5,4},{7,6},{8,9},{10,11},{12,... | collective-permute-start | bytes 86024 | tf_op jit(solution)/shard_map/ppermute | solution.py:772
  27.4 7.5 %collective-permute-start.11 = (f32[10,8,128]{2,1,0:T(8,128)S(1)}, f32[10,8,128]{2,1,0:T(8,128)S(1)}, u32[]{:S(2)}, u32[]{:S(2)}) collective-permute-start(f32[10,8,128]{2,1,0:T(8,128)S(1)} %get-tuple-element.79), channel_id=1, source_target_pairs={{0,6},{1,7},{4,2},{5,3},{6,0},{7,1},{2,4},{3,5},{8,14},{9,15},{12,... | collective-permute-start | bytes 122888 | tf_op jit(solution)/shard_map/ppermute | solution.py:779
  28.0 6.9 %collective-permute-start.10 = (f32[9,8,128]{2,1,0:T(8,128)S(1)}, f32[9,8,128]{2,1,0:T(8,128)S(1)}, u32[]{:S(2)}, u32[]{:S(2)}) collective-permute-start(f32[9,8,128]{2,1,0:T(8,128)S(1)} %get-tuple-element.78), channel_id=1, source_target_pairs={{0,2},{1,3},{4,6},{5,7},{2,0},{3,1},{6,4},{7,5},{8,10},{9,11},{12,... | collective-permute-start | bytes 110600 | tf_op jit(solution)/shard_map/ppermute | solution.py:779
  28.0 6.7 %collective-permute-start.8 = (f32[8,8,128]{2,1,0:T(8,128)S(1)}, f32[8,8,128]{2,1,0:T(8,128)S(1)}, u32[]{:S(2)}, u32[]{:S(2)}) collective-permute-start(f32[8,8,128]{2,1,0:T(8,128)S(1)} %get-tuple-element.76), channel_id=1, source_target_pairs={{0,7},{2,1},{4,3},{6,5},{7,0},{1,2},{3,4},{5,6},{8,15},{10,9},{12,... | collective-permute-start | bytes 98312 | tf_op jit(solution)/shard_map/ppermute | solution.py:772
  30.6 4.3 %collective-permute-start.9 = (f32[8,8,128]{2,1,0:T(8,128)S(1)}, f32[8,8,128]{2,1,0:T(8,128)S(1)}, u32[]{:S(2)}, u32[]{:S(2)}) collective-permute-start(f32[8,8,128]{2,1,0:T(8,128)S(1)} %get-tuple-element.77), channel_id=1, source_target_pairs={{0,1},{2,3},{4,5},{6,7},{1,0},{3,2},{5,4},{7,6},{8,9},{10,11},{12,... | collective-permute-start | bytes 98312 | tf_op jit(solution)/shard_map/ppermute | solution.py:772
